TPU v7x, 32 devices: a whole 2x2x4 slice. The times are simulated.
32 devices in a mesh: cell: 8 (over y, x, core), cls: 4 (over z).
Axes of the slice: x: 2, y: 2, z: 4, core: 2. Of those that a mesh axis runs over, the one named last changes fastest.
Arguments:
- melt: float32 [64, 32, 8192], P(None, 'cls', 'cell'), may hold values from 0 to 1
- counts: int32 [32, 8192], P('cls', 'cell'), may hold values from 0 to 800, as said below
- pressure: float32 [32, 256], P(('cell', 'cls')), may hold values from 0.5 to 2
- propagator: float32 [32, 64, 64], replicated, as said below
- coupling: float32 [32, 64], replicated, may hold values from 0.05 to 0.5
- flux_weights: float32 [32, 64], replicated, may hold values from 0.002 to 0.2
Outputs:
- shells_out: float32 [64, 32, 8192], P(None, 'cls', 'cell')
- pressure_out: float32 [32, 256], P(('cell', 'cls'))
Inputs may be any that keep to these rules, and one draw needn't show every extreme that they name: counts in layer l are non-negative and below 201 + (600 * l) // 31. Each propagator matrix has a dominant diagonal.
All inputs are finite; a program needn't handle non-finite values.
Results may differ from a plain program's by a relative error of at most 0.0001.
Values sent between devices are 32-bit elements; how exact they have to be, the bound alone decides.
No kernel may reach another device: no remote copies, remote signals or barrier semaphores. Data moves between devices by JAX's collectives and lax.ppermute only.
A program may use at most 64 MiB of HBM per device.

v0:
```python
import jax
import jax.numpy as jnp
from jax import lax
from jax.sharding import PartitionSpec as P

CLASSES = 32
SIDE = 16
SUBSTEPS = 4


count_scale = 400.0


def extended_2(block, sides, width):
    for axis, dim in sides:
        count = lax.axis_size(axis)
        forward = [(i, i + 1) for i in range(count - 1)]
        backward = [(target, source) for source, target in forward]
        low = lax.ppermute(
            lax.slice_in_dim(block, block.shape[dim] - width, None, axis=dim), axis, forward
        )
        high = lax.ppermute(lax.slice_in_dim(block, 0, width, axis=dim), axis, backward)
        block = jnp.concatenate([low, block, high], axis=dim)
    return block


def shell_update(shells, counts_f, propagator, coupling, flux_weights, wall):
    shells = (
        jnp.einsum("kij,jkc->ikc", propagator, shells, precision=lax.Precision.HIGHEST)
        + coupling.T[:, :, None] * wall[None, None, :]
    )
    flux = jnp.einsum("ki,ikc->kc", flux_weights, shells, precision=lax.Precision.HIGHEST)
    partial_gas = jnp.sum(counts_f * flux, axis=0) / (count_scale * CLASSES)
    return (shells, partial_gas)


def pressure_update(tile, gas_tile):
    total = lax.psum(jnp.sum(gas_tile), ("cell", "cls"))
    all_cells = gas_tile.shape[0] * lax.axis_size("cell") * lax.axis_size("cls")
    chamber = 1.5 - 0.5 * total / all_cells
    layer_count = tile.shape[0]
    field = tile.reshape(layer_count, SIDE, SIDE)
    extended = extended_2(field, ((("cell", "cls"), 0),), 1)
    extended = jnp.pad(extended, ((0, 0), (1, 1), (1, 1)))
    lap = (
        extended[2:, 1:-1, 1:-1]
        + extended[:-2, 1:-1, 1:-1]
        + extended[1:-1, 2:, 1:-1]
        + extended[1:-1, :-2, 1:-1]
        + extended[1:-1, 1:-1, 2:]
        + extended[1:-1, 1:-1, :-2]
        - 6.0 * field
    )
    field = field + 0.15 * lap + 0.1 * gas_tile.reshape(field.shape) + 0.2 * (chamber - field)
    return field.reshape(tile.shape)


def shards(melt, counts, pressure, propagator, coupling, flux_weights):
    tile = pressure
    class_count = melt.shape[1]
    start = lax.axis_index("cls") * class_count
    local_prop = lax.dynamic_slice_in_dim(propagator, start, class_count, 0)
    local_coupling = lax.dynamic_slice_in_dim(coupling, start, class_count, 0)
    local_flux = lax.dynamic_slice_in_dim(flux_weights, start, class_count, 0)
    counts_f = counts.astype(jnp.float32)
    shells = melt
    for step in range(SUBSTEPS):
        block_pressure = lax.all_gather(tile.reshape(-1), "cls", axis=0, tiled=True)
        shells, partial_gas = shell_update(
            shells, counts_f, local_prop, local_coupling, local_flux, 0.5 * block_pressure
        )
        gas_tile = lax.psum_scatter(partial_gas, "cls", scatter_dimension=0, tiled=True)
        tile = pressure_update(tile, gas_tile)
    return (shells, tile)


def solution(mesh):
    placed = (P(None, "cls", "cell"), P("cls", "cell"), P(("cell", "cls"), None), P(), P(), P())
    return jax.shard_map(
        shards,
        mesh=mesh,
        in_specs=placed,
        out_specs=(P(None, "cls", "cell"), P(("cell", "cls"), None)),
        check_vma=False,
    )
```

profile of v0, /device:TPU:0, one launch (start us, length us, event | category | flops | bytes accessed | tf_op | source)
XLA Modules:
  0.0 306.2 jit_solution(662261884696256593)
XLA Ops:
  1.2 1.5 reduce.3
  2.7 4.9 %collective-permute-start.1 = (f32[1,16,16]{2,1,0:T(8,128)S(1)}, f32[1,16,16]{2,1,0:T(8,128)S(1)}, u32[]{:S(2)}, u32[]{:S(2)}) collective-permute-start(f32[1,16,16]{2,1,0:T(8,128)S(1)} %reshape.107), channel_id=1, source_target_pairs={{0,1},{1,2},{2,3},{3,4},{4,5},{5,6},{6,7},{7,8},{8,9},{9,10},{10,1... | collective-permute-start | bytes 3080 | tf_op jit(solution)/shard_map/ppermute | solution.py:19
  8.9 12.5 %all-gather = f32[1,1024]{1,0:T(1,128)S(1)} all-gather(f32[1,256]{1,0:T(1,128)} %param.8), channel_id=2, replica_groups=mesh['cell'=8,'cls'=4] {'cls'}, dimensions={1}, use_global_device_ids=true | all-gather | bytes 5120 | tf_op jit(solution)/shard_map/all_gather | solution.py:68
  22.1 4.0 %fusion = f32[8,64,1024]{2,1,0:T(8,128)S(1)} fusion(f32[64,8,1024]{2,1,0:T(8,128)S(1)} %copy-done, f32[32,64,64]{2,1,0:T(8,128)} %param.9, s32[]{:T(128)S(6)} %select_n.2), kind=kOutput, calls=%fused_computation.4 | convolution fusion | flops 402653184 | bytes 4456452 | tf_op jit(solution)/shard_map/kij,jkc->ikc/dot_general | solution.py:29
  28.8 8.4 %all-reduce.4 = f32[1024]{0:T(1024)S(1)} all-reduce(f32[1024]{0:T(1024)S(1)} %broadcast_multiply_fusion.7), channel_id=3, replica_groups=mesh['cell'=8,'cls'=4] {'cls'}, use_global_device_ids=true, to_apply=%region_1.0.clone | all-reduce | flops 1024 | bytes 8192
  39.1 40.9 %psum.28 = f32[]{:T(128)} all-reduce(f32[]{:T(128)} %get-tuple-element.12), channel_id=1, replica_groups=mesh['cell'=8,'cls'=4] {'cell','cls'}, use_global_device_ids=true, to_apply=%region_3.0 | all-reduce | flops 1 | bytes 8 | tf_op jit(solution)/shard_map/psum | solution.py:38
  81.0 2.8 collective-permute-start.3
  85.1 10.9 %all-gather.1 = f32[4,1,256]{2,1,0:T(1,128)S(1)} all-gather(f32[1,1,256]{2,1,0:T(1,128)S(1)} %reshape.112), channel_id=1, replica_groups=mesh['cell'=8,'cls'=4] {'cls'}, dimensions={0}, use_global_device_ids=true | all-gather | bytes 5120 | tf_op jit(solution)/shard_map/all_gather | solution.py:68
  95.9 3.9 %bitcast_add_fusion.2 = f32[64,8,1024]{2,0,1:T(8,128)S(1)} fusion(f32[8,64,1024]{2,1,0:T(8,128)} %copy-done.1, f32[1024]{0:T(1024)S(1)} %bitcast.58, f32[1024]{0:T(1024)S(1)} %bitcast.54, f32[64,8]{0,1:T(8,128)S(1)} %get-tuple-element.14, f32[32,64,64]{2,1,0:T(8,128)S(1)} %copy-done.3, s32[]{:T(128)S(6)} %select_n.2), kind=kOutput, calls=%fused_computation.2 | convolution fusion | flops 404750336 | bytes 4472836 | tf_op jit(solution)/shard_map/kij,jkc->ikc/dot_general | solution.py:29
  101.0 3.3 %fusion.15 = f32[8,1024,64]{1,2,0:T(8,128)} fusion(f32[64,8,1024]{2,0,1:T(8,128)S(1)} %bitcast_add_fusion.2, f32[32,64,64]{2,1,0:T(8,128)S(1)} %copy-done.3, s32[]{:T(128)S(6)} %select_n.2), kind=kOutput, calls=%fused_computation.19 | convolution fusion | flops 402653184 | bytes 4456452 | tf_op jit(solution)/shard_map/kij,jkc->ikc/dot_general | solution.py:29
  104.3 8.4 %all-reduce.5 = f32[1024]{0:T(1024)S(1)} all-reduce(f32[1024]{0:T(1024)S(1)} %broadcast_multiply_fusion.6), channel_id=4, replica_groups=mesh['cell'=8,'cls'=4] {'cls'}, use_global_device_ids=true, to_apply=%region_5.6.clone | all-reduce | flops 1024 | bytes 8192
  113.4 42.4 %psum.29 = f32[]{:T(128)} all-reduce(f32[]{:T(128)} %get-tuple-element.10), channel_id=1, replica_groups=mesh['cell'=8,'cls'=4] {'cell','cls'}, use_global_device_ids=true, to_apply=%region_7.8 | all-reduce | flops 1 | bytes 8 | tf_op jit(solution)/shard_map/psum | solution.py:38
  156.8 3.8 %collective-permute-start.5 = (f32[1,16,16]{2,1,0:T(8,128)S(1)}, f32[1,16,16]{2,1,0:T(8,128)S(1)}, u32[]{:S(2)}, u32[]{:S(2)}) collective-permute-start(f32[1,16,16]{2,1,0:T(8,128)S(1)} %fusion.40), channel_id=1, source_target_pairs={{0,1},{1,2},{2,3},{3,4},{4,5},{5,6},{6,7},{7,8},{8,9},{9,10},{10,1... | collective-permute-start | bytes 3080 | tf_op jit(solution)/shard_map/ppermute | solution.py:19
  161.9 10.2 %all-gather.2 = f32[4,1,256]{2,1,0:T(1,128)S(1)} all-gather(f32[1,1,256]{2,1,0:T(1,128)S(1)} %reshape.114), channel_id=1, replica_groups=mesh['cell'=8,'cls'=4] {'cls'}, dimensions={0}, use_global_device_ids=true | all-gather | bytes 5120 | tf_op jit(solution)/shard_map/all_gather | solution.py:68
  172.2 2.9 fusion.4
  175.1 8.4 %all-reduce.6 = f32[1024]{0:T(1024)S(1)} all-reduce(f32[1024]{0:T(1024)S(1)} %broadcast_multiply_fusion.5), channel_id=5, replica_groups=mesh['cell'=8,'cls'=4] {'cls'}, use_global_device_ids=true, to_apply=%region_9.10.clone | all-reduce | flops 1024 | bytes 8192
  184.1 42.7 %psum.30 = f32[]{:T(128)} all-reduce(f32[]{:T(128)} %get-tuple-element.8), channel_id=1, replica_groups=mesh['cell'=8,'cls'=4] {'cell','cls'}, use_global_device_ids=true, to_apply=%region_11.12 | all-reduce | flops 1 | bytes 8 | tf_op jit(solution)/shard_map/psum | solution.py:38
  227.8 4.0 %collective-permute-start.7 = (f32[1,16,16]{2,1,0:T(8,128)S(1)}, f32[1,16,16]{2,1,0:T(8,128)S(1)}, u32[]{:S(2)}, u32[]{:S(2)}) collective-permute-start(f32[1,16,16]{2,1,0:T(8,128)S(1)} %fusion.35), channel_id=1, source_target_pairs={{0,1},{1,2},{2,3},{3,4},{4,5},{5,6},{6,7},{7,8},{8,9},{9,10},{10,1... | collective-permute-start | bytes 3080 | tf_op jit(solution)/shard_map/ppermute | solution.py:19
  233.1 10.2 %all-gather.3 = f32[4,1,256]{2,1,0:T(1,128)S(1)} all-gather(f32[1,1,256]{2,1,0:T(1,128)S(1)} %reshape.116), channel_id=1, replica_groups=mesh['cell'=8,'cls'=4] {'cls'}, dimensions={0}, use_global_device_ids=true | all-gather | bytes 5120 | tf_op jit(solution)/shard_map/all_gather | solution.py:68
  243.3 3.9 %bitcast_add_fusion = f32[64,8,1024]{2,0,1:T(8,128)S(1)} fusion(f32[8,1024,64]{1,2,0:T(8,128)} %fusion.15, f32[1024]{0:T(1024)S(1)} %bitcast.57, f32[1024]{0:T(1024)S(1)} %bitcast.56, f32[64,8]{0,1:T(8,128)S(1)} %get-tuple-element.14, f32[32,64,64]{2,1,0:T(8,128)S(1)} %copy-done.3, s32[]{:T(128)S(6)} %select_n.2), kind=kOutput, calls=%fused_computation | convolution fusion | flops 404750336 | bytes 4472836 | tf_op jit(solution)/shard_map/kij,jkc->ikc/dot_general | solution.py:29
  247.2 1.3 copy-done.2
  249.7 8.4 %all-reduce.7 = f32[1024]{0:T(1024)S(1)} all-reduce(f32[1024]{0:T(1024)S(1)} %broadcast_multiply_fusion.4), channel_id=6, replica_groups=mesh['cell'=8,'cls'=4] {'cls'}, use_global_device_ids=true, to_apply=%region_13.14.clone | all-reduce | flops 1024 | bytes 8192
  258.8 41.8 %psum.31 = f32[]{:T(128)} all-reduce(f32[]{:T(128)} %get-tuple-element.6), channel_id=1, replica_groups=mesh['cell'=8,'cls'=4] {'cell','cls'}, use_global_device_ids=true, to_apply=%region_15.16 | all-reduce | flops 1 | bytes 8 | tf_op jit(solution)/shard_map/psum | solution.py:38
  300.5 4.1 %copy.11 = f32[64,8,1024]{2,1,0:T(8,128)} copy(f32[64,8,1024]{2,0,1:T(8,128)} %copy-done.2) | data formatting | bytes 4194304
  (62 shorter events, 16.6 us)
Async XLA Ops:
  0.6 21.5 %copy-start = (f32[64,8,1024]{2,1,0:T(8,128)S(1)}, f32[64,8,1024]{2,1,0:T(8,128)}, u32[]{:S(2)}) copy-start(f32[64,8,1024]{2,1,0:T(8,128)} %param.6) | copy-start | bytes 6291460
  2.7 78.0 %collective-permute-start.1 = (f32[1,16,16]{2,1,0:T(8,128)S(1)}, f32[1,16,16]{2,1,0:T(8,128)S(1)}, u32[]{:S(2)}, u32[]{:S(2)}) collective-permute-start(f32[1,16,16]{2,1,0:T(8,128)S(1)} %reshape.107), channel_id=1, source_target_pairs={{0,1},{1,2},{2,3},{3,4},{4,5},{5,6},{6,7},{7,8},{8,9},{9,10},{10,1... | collective-permute-start | bytes 3080 | tf_op jit(solution)/shard_map/ppermute | solution.py:19
  7.6 73.1 %collective-permute-start = (f32[1,16,16]{2,1,0:T(8,128)S(1)}, f32[1,16,16]{2,1,0:T(8,128)S(1)}, u32[]{:S(2)}, u32[]{:S(2)}) collective-permute-start(f32[1,16,16]{2,1,0:T(8,128)S(1)} %reshape.107), channel_id=1, source_target_pairs={{1,0},{2,1},{3,2},{4,3},{5,4},{6,5},{7,6},{8,7},{9,8},{10,9},{11,1... | collective-permute-start | bytes 3080 | tf_op jit(solution)/shard_map/ppermute | solution.py:22
  26.1 1.3 copy-start.1
  26.1 2.6 copy-start.4
  26.1 11.0 %copy-start.5 = (u32[32]{0:T(128)S(1)}, u32[32]{0:T(128)}, u32[]{:S(2)}) copy-start(u32[32]{0:T(128)} %constant.53) | copy-start | bytes 388
  26.2 69.8 %copy-start.3 = (f32[32,64,64]{2,1,0:T(8,128)S(1)}, f32[32,64,64]{2,1,0:T(8,128)}, u32[]{:S(2)}) copy-start(f32[32,64,64]{2,1,0:T(8,128)} %param.9) | copy-start | bytes 1572868
  81.0 75.6 %collective-permute-start.3 = (f32[1,16,16]{2,1,0:T(8,128)S(1)}, f32[1,16,16]{2,1,0:T(8,128)S(1)}, u32[]{:S(2)}, u32[]{:S(2)}) collective-permute-start(f32[1,16,16]{2,1,0:T(8,128)S(1)} %fusion.45), channel_id=1, source_target_pairs={{0,1},{1,2},{2,3},{3,4},{4,5},{5,6},{6,7},{7,8},{8,9},{9,10},{10,1... | collective-permute-start | bytes 3080 | tf_op jit(solution)/shard_map/ppermute | solution.py:19
  83.8 72.8 %collective-permute-start.2 = (f32[1,16,16]{2,1,0:T(8,128)S(1)}, f32[1,16,16]{2,1,0:T(8,128)S(1)}, u32[]{:S(2)}, u32[]{:S(2)}) collective-permute-start(f32[1,16,16]{2,1,0:T(8,128)S(1)} %fusion.45), channel_id=1, source_target_pairs={{1,0},{2,1},{3,2},{4,3},{5,4},{6,5},{7,6},{8,7},{9,8},{10,9},{11,1... | collective-permute-start | bytes 3080 | tf_op jit(solution)/shard_map/ppermute | solution.py:22
  156.8 70.7 %collective-permute-start.5 = (f32[1,16,16]{2,1,0:T(8,128)S(1)}, f32[1,16,16]{2,1,0:T(8,128)S(1)}, u32[]{:S(2)}, u32[]{:S(2)}) collective-permute-start(f32[1,16,16]{2,1,0:T(8,128)S(1)} %fusion.40), channel_id=1, source_target_pairs={{0,1},{1,2},{2,3},{3,4},{4,5},{5,6},{6,7},{7,8},{8,9},{9,10},{10,1... | collective-permute-start | bytes 3080 | tf_op jit(solution)/shard_map/ppermute | solution.py:19
  160.6 66.9 %collective-permute-start.4 = (f32[1,16,16]{2,1,0:T(8,128)S(1)}, f32[1,16,16]{2,1,0:T(8,128)S(1)}, u32[]{:S(2)}, u32[]{:S(2)}) collective-permute-start(f32[1,16,16]{2,1,0:T(8,128)S(1)} %fusion.40), channel_id=1, source_target_pairs={{1,0},{2,1},{3,2},{4,3},{5,4},{6,5},{7,6},{8,7},{9,8},{10,9},{11,1... | collective-permute-start | bytes 3080 | tf_op jit(solution)/shard_map/ppermute | solution.py:22
  227.8 77.6 %collective-permute-start.7 = (f32[1,16,16]{2,1,0:T(8,128)S(1)}, f32[1,16,16]{2,1,0:T(8,128)S(1)}, u32[]{:S(2)}, u32[]{:S(2)}) collective-permute-start(f32[1,16,16]{2,1,0:T(8,128)S(1)} %fusion.35), channel_id=1, source_target_pairs={{0,1},{1,2},{2,3},{3,4},{4,5},{5,6},{6,7},{7,8},{8,9},{9,10},{10,1... | collective-permute-start | bytes 3080 | tf_op jit(solution)/shard_map/ppermute | solution.py:19
  231.8 73.6 %collective-permute-start.6 = (f32[1,16,16]{2,1,0:T(8,128)S(1)}, f32[1,16,16]{2,1,0:T(8,128)S(1)}, u32[]{:S(2)}, u32[]{:S(2)}) collective-permute-start(f32[1,16,16]{2,1,0:T(8,128)S(1)} %fusion.35), channel_id=1, source_target_pairs={{1,0},{2,1},{3,2},{4,3},{5,4},{6,5},{7,6},{8,7},{9,8},{10,9},{11,1... | collective-permute-start | bytes 3080 | tf_op jit(solution)/shard_map/ppermute | solution.py:22
  247.2 1.4 copy-start.2
where the time goes:
time: 308 us; the launch traced here: 306 us
  blocking collectives  245 us (80%)
  matrix products  21.5 us (7%)
  starting transfers between devices  20.7 us (7%)
  local copies, waits for them, and re-layouts  9.86 us (3%)
  other arithmetic  4.92 us (2%)
  between operations  4.19 us (1%)
    psum x4, blocking collectives, pressure_update(): total = lax.psum(jnp.sum(gas_tile), ('cell', 'cls'))  168 us
    all_gather x4, blocking collectives, shards(): block_pressure = lax.all_gather(tile.reshape(-1), 'cls', axis=0, tiled=True)  43.7 us
    unnamed x4, blocking collectives  33.5 us
    ppermute x4, starting transfers between devices, extended_2(): lax.ppermute(lax.slice_in_dim(block, block.shape[dim] - width, None, axis...  15.5 us
    dot_general x4, matrix products, shell_update(): jnp.einsum('kij,jkc->ikc', propagator, shells, precision=lax.Precision.HI...  15.2 us
    unnamed x18, local copies, waits for them, and re-layouts  8.12 us
    dot_general x4, matrix products, shell_update(): jnp.einsum('ki,ikc->kc', flux_weights, shells, precision=lax.Precision.HI...  6.4 us
  transfers between devices with their start and end apart: 8, of which 0 were waited for; matrix products, arithmetic and copies ran while one was open for 10% of the time, Pallas kernels for 0%

commit v1 on v0

v1 whole, which is shorter than its diff:
```python
import jax
import jax.numpy as jnp
from jax import lax
from jax.sharding import PartitionSpec as P

CLASSES = 32
SIDE = 16
SUBSTEPS = 4
COUNT_SCALE = 400.0

HIGHEST = lax.Precision.HIGHEST


def chains(prop, coupling, flux_weights):
    scale = jnp.maximum(1.0, jnp.max(jnp.abs(prop), axis=(1, 2)))
    unit = prop / scale[:, None, None]
    square = jnp.einsum("kij,kjl->kil", unit, unit, precision=HIGHEST)
    fourth = jnp.einsum("kij,kjl->kil", square, square, precision=HIGHEST)
    rows = [flux_weights]
    columns = [coupling]
    for _ in range(SUBSTEPS):
        rows.append(jnp.einsum("ki,kij->kj", rows[-1], unit, precision=HIGHEST))
    for _ in range(SUBSTEPS - 1):
        columns.append(jnp.einsum("kij,kj->ki", unit, columns[-1], precision=HIGHEST))
    return scale, fourth, rows[1:], columns


def grow(value, factor, times):
    for _ in range(times):
        value = value * factor
    return value


def partial_fields(melt, counts_n, scale, rows, columns, flux_weights):
    fields = []
    for t in range(SUBSTEPS):
        flux = jnp.einsum("ki,ikc->kc", rows[t], melt, precision=HIGHEST)
        fields.append(jnp.sum(grow(counts_n * flux, scale[:, None], t + 1), axis=0))
    for d in range(SUBSTEPS):
        response = grow(jnp.sum(flux_weights * columns[d], axis=1), scale, d)
        fields.append(jnp.sum(counts_n * response[:, None], axis=0))
    return fields


def laplacian(field):
    padded = jnp.pad(field, 1)
    return (
        padded[2:, 1:-1, 1:-1]
        + padded[:-2, 1:-1, 1:-1]
        + padded[1:-1, 2:, 1:-1]
        + padded[1:-1, :-2, 1:-1]
        + padded[1:-1, 1:-1, 2:]
        + padded[1:-1, 1:-1, :-2]
        - 6.0 * field
    )


def evolve(own, response, field):
    walls = []
    for t in range(SUBSTEPS):
        walls.append(0.5 * field)
        gas = own[t]
        for s in range(t + 1):
            gas = gas + response[t - s] * walls[s]
        chamber = 1.5 - 0.5 * jnp.sum(gas) / gas.size
        field = field + 0.15 * laplacian(field) + 0.1 * gas + 0.2 * (chamber - field)
    return walls, field


def shards(melt, counts, pressure, propagator, coupling, flux_weights):
    nodes, class_count, cells = melt.shape
    plane = pressure.shape[1]
    layers = cells // plane
    cls = lax.axis_index("cls")
    cell = lax.axis_index("cell")
    start = cls * class_count
    prop = lax.dynamic_slice_in_dim(propagator, start, class_count, 0)
    couple = lax.dynamic_slice_in_dim(coupling, start, class_count, 0)
    flux_w = lax.dynamic_slice_in_dim(flux_weights, start, class_count, 0)
    counts_n = counts.astype(jnp.float32) / (COUNT_SCALE * CLASSES)
    scale, fourth, rows, columns = chains(prop, couple, flux_w)
    fields = partial_fields(melt, counts_n, scale, rows, columns, flux_w)
    own_pressure = lax.dynamic_update_slice_in_dim(
        jnp.zeros((cells,), jnp.float32), pressure.reshape(-1), cls * plane * pressure.shape[0], 0
    )
    packed = jnp.stack(fields + [own_pressure])
    shells = grow(
        jnp.einsum("kij,jkc->ikc", fourth, melt, precision=HIGHEST), scale[None, :, None], SUBSTEPS
    )
    packed = lax.psum(packed, "cls")
    window = lax.all_gather(packed, "cell", axis=0)
    window = jnp.moveaxis(window, 1, 0).reshape(packed.shape[0], -1, SIDE, plane // SIDE)
    walls, field = evolve(window[:SUBSTEPS], window[SUBSTEPS : 2 * SUBSTEPS], window[2 * SUBSTEPS])
    for s in range(SUBSTEPS):
        own = lax.dynamic_slice_in_dim(walls[s], cell * layers, layers, 0).reshape(-1)
        column = grow(columns[SUBSTEPS - 1 - s], scale[:, None], SUBSTEPS - 1 - s)
        shells = shells + column.T[:, :, None] * own[None, None, :]
    tile = lax.dynamic_slice_in_dim(
        field, cell * layers + cls * pressure.shape[0], pressure.shape[0], 0
    )
    return shells, tile.reshape(pressure.shape)


def solution(mesh):
    placed = (P(None, "cls", "cell"), P("cls", "cell"), P(("cell", "cls"), None), P(), P(), P())
    return jax.shard_map(
        shards,
        mesh=mesh,
        in_specs=placed,
        out_specs=(P(None, "cls", "cell"), P(("cell", "cls"), None)),
        check_vma=False,
    )
```

time: 308 us -> 80.6 us (0.26)
  blocking collectives: 245 us -> 31.3 us
  starting transfers between devices: 20.7 us -> 0 us
  other arithmetic: 4.92 us -> 14.9 us
  matrix products: 21.5 us -> 17.8 us
    psum x4 -> x1, blocking collectives: 168 us -> 21.4 us  [shards(): packed = lax.psum(packed, 'cls')]
    all_gather x4 -> x1, blocking collectives: 43.7 us -> 9.87 us  [shards(): window = lax.all_gather(packed, 'cell', axis=0)]
    unnamed x4 -> x0, blocking collectives: 33.5 us -> none
    ppermute x8 -> x0, starting transfers between devices: 20.7 us -> none  [the longest x4 15.5 us: extended_2(): lax.ppermute(lax.slice_in_dim(block, block.shape[dim] - width, None, axis...]
    unnamed x18 -> x7, local copies, waits for them, and re-layouts: 8.12 us -> 3.27 us
    squeeze x0 -> x9, local copies, waits for them, and re-layouts: none -> 4.64 us  [the longest x4 2.62 us: evolve(): gas = own[t]]
    reduce_sum x8 -> x4, other arithmetic: 2.76 us -> 6.7 us  [the longest x2 5.62 us: evolve(): chamber = 1.5 - 0.5 * jnp.sum(gas) / gas.size]
    dot_general x8 -> x14, matrix products: 21.5 us -> 17.8 us  [the longest x4 8.91 us: partial_fields(): flux = jnp.einsum('ki,ikc->kc', rows[t], melt, precision=HIGHEST)]
  transfers between devices with their start and end apart: 8 -> 0, of which waited for: 0 -> 0; matrix products, arithmetic and copies ran while one was open for 10% -> 0% of each run, Pallas kernels for 0% -> 0%
where the time goes in v1:
time: 80.6 us; the launch traced here: 80 us
  blocking collectives  31.3 us (39%)
  matrix products  17.8 us (22%)
  other arithmetic  14.9 us (18%)
  local copies, waits for them, and re-layouts  12.6 us (16%)
  between operations  3.38 us (4%)
    psum x1, blocking collectives, shards(): packed = lax.psum(packed, 'cls')  21.4 us
    all_gather x1, blocking collectives, shards(): window = lax.all_gather(packed, 'cell', axis=0)  9.87 us
    dot_general x4, matrix products, partial_fields(): flux = jnp.einsum('ki,ikc->kc', rows[t], melt, precision=HIGHEST)  8.91 us
    reduce_sum x2, other arithmetic, evolve(): chamber = 1.5 - 0.5 * jnp.sum(gas) / gas.size  5.62 us
    dot_general x1, matrix products, shards(): jnp.einsum('kij,jkc->ikc', fourth, melt, precision=HIGHEST)  4.58 us
    mul x3, other arithmetic, evolve(): walls.append(0.5 * field)  3.63 us
    unnamed x7, local copies, waits for them, and re-layouts  3.27 us
    squeeze x4, local copies, waits for them, and re-layouts, evolve(): gas = own[t]  2.62 us

profile of v1, /device:TPU:0, one launch (start us, length us, event | category | flops | bytes accessed | tf_op | source)
XLA Modules:
  0.0 80.0 jit_solution(6019761665383487082)
XLA Ops:
  0.7 1.3 %abs_reduce_fusion = f32[8]{0:T(128)S(1)} fusion(f32[32,64,64]{2,1,0:T(8,128)} %param.9, s32[]{:T(128)S(6)} %select_n.8), kind=kLoop, calls=%fused_computation.78 | loop fusion | flops 65528 | bytes 131108 | tf_op jit(solution)/shard_map/reduce_max | solution.py:15
  4.0 1.0 %dynamic-slice_divide_fusion = f32[8,64,64]{2,1,0:T(8,128)S(1)} fusion(f32[32,64,64]{2,1,0:T(8,128)} %param.9, s32[]{:T(128)S(6)} %select_n.8, f32[8]{0:T(128)S(1)} %broadcast_maximum_fusion), kind=kLoop, calls=%fused_computation.79 | loop fusion | flops 32768 | bytes 262180 | tf_op jit(solution)/shard_map/div | solution.py:16
  6.6 0.9 %multiply_reduce_fusion.4 = (f32[8]{0:T(128)S(1)}, f32[8]{0:T(128)S(1)}, f32[8]{0:T(128)S(1)}, f32[8]{0:T(128)S(1)}, f32[8,64]{1,0:T(8,128)S(1)}, /*index=5*/f32...) fusion(f32[8,64]{1,0:T(8,128)S(1)} %bitcast.134, f32[8,64]{1,0:T(8,128)S(1)} %bitcast.132, ...), kind=kLoop, calls=%fused_computation.130 | loop fusion | flops 7136 | bytes 18596 | tf_op jit(solution)/shard_map/reduce_sum | solution.py:40
  9.2 1.1 %fusion.78 = f32[8,64,64]{2,1,0:T(8,128)} fusion(f32[8,64,64]{2,1,0:T(8,128)S(1)} %fusion.77), kind=kOutput, calls=%fused_computation.153 | convolution fusion | flops 25165824 | bytes 262144 | tf_op jit(solution)/shard_map/kij,kjl->kil/dot_general | solution.py:18
  10.3 2.2 %fusion.5 = f32[8,1,1024]{2,1,0:T(1,128)S(1)} fusion(f32[8,64,1]{1,2,0:T(1,128)S(1)} %convolution_bitcast_fusion.1, f32[64,8,1024]{2,1,0:T(8,128)S(1)} %copy-done), kind=kOutput, calls=%fused_computation.6 | convolution fusion | flops 6291456 | bytes 2131968 | tf_op jit(solution)/shard_map/ki,ikc->kc/dot_general | solution.py:37
  12.5 2.2 %fusion.3 = f32[8,1,1024]{2,1,0:T(1,128)S(1)} fusion(f32[8,64,1]{1,2,0:T(1,128)S(1)} %convolution_bitcast_fusion, f32[64,8,1024]{2,1,0:T(8,128)S(1)} %copy-done), kind=kOutput, calls=%fused_computation.4 | convolution fusion | flops 6291456 | bytes 2131968 | tf_op jit(solution)/shard_map/ki,ikc->kc/dot_general | solution.py:37
  14.8 2.2 %fusion.7 = f32[8,1,1024]{2,1,0:T(1,128)S(1)} fusion(f32[8,64,1]{1,2,0:T(1,128)S(1)} %convolution_bitcast_fusion.2, f32[64,8,1024]{2,1,0:T(8,128)S(1)} %copy-done), kind=kOutput, calls=%fused_computation.8 | convolution fusion | flops 6291456 | bytes 2131968 | tf_op jit(solution)/shard_map/ki,ikc->kc/dot_general | solution.py:37
  17.0 2.2 %fusion.9 = f32[8,1,1024]{2,1,0:T(1,128)S(1)} fusion(f32[8,64,1]{1,2,0:T(1,128)S(1)} %convolution_bitcast_fusion.3, f32[64,8,1024]{2,1,0:T(8,128)S(1)} %copy-done), kind=kOutput, calls=%fused_computation.10 | convolution fusion | flops 6291456 | bytes 2131968 | tf_op jit(solution)/shard_map/ki,ikc->kc/dot_general | solution.py:37
  19.5 21.4 %psum.7 = f32[1,9,1024]{2,1,0:T(8,128)S(1)} all-reduce(f32[1,9,1024]{2,1,0:T(8,128)S(1)} %bitcast.130), channel_id=1, replica_groups=mesh['cell'=8,'cls'=4] {'cls'}, use_global_device_ids=true, to_apply=%region_13.0 | all-reduce | flops 9216 | bytes 73728 | tf_op jit(solution)/shard_map/psum | solution.py:90
  40.9 9.9 %all_gather.7 = f32[8,9,1024]{2,1,0:T(8,128)S(1)} all-gather(f32[1,9,1024]{2,1,0:T(8,128)S(1)} %psum.7), channel_id=1, replica_groups=mesh['cell'=8,'cls'=4] {'cell'}, dimensions={0}, use_global_device_ids=true | all-gather | bytes 331776 | tf_op jit(solution)/shard_map/all_gather | solution.py:91
  50.8 1.4 %slice_reduce_fusion = (f32[8,1024]{1,0:T(8,128)S(1)}, f32[]{:T(128)}, f32[8,1024]{1,0:T(8,128)S(1)}, f32[8,1024]{1,0:T(8,128)S(1)}, f32[8,1024]{1,0:T(8,128)S(1...) fusion(f32[9,8,1024]{2,0,1:T(8,128)S(1)} %bitcast.129), kind=kLoop, calls=%fused_computation.84 | loop fusion | flops 32767 | bytes 589828 | tf_op jit(solution)/shard_map/slice | solution.py:64
  52.8 0.8 %squeeze.41 = f32[32,16,16]{2,1,0:T(8,128)} reshape(f32[8,1024]{1,0:T(8,128)S(1)} %get-tuple-element.8) | data formatting | bytes 65536 | tf_op jit(solution)/shard_map/squeeze | solution.py:64
  54.0 0.8 %squeeze.39 = f32[32,16,16]{2,1,0:T(8,128)} reshape(f32[8,1024]{1,0:T(8,128)S(1)} %get-tuple-element.11) | data formatting | bytes 65536 | tf_op jit(solution)/shard_map/squeeze | solution.py:64
  54.9 0.8 %squeeze.38 = f32[32,16,16]{2,1,0:T(8,128)} reshape(f32[8,1024]{1,0:T(8,128)S(1)} %get-tuple-element.12) | data formatting | bytes 65536 | tf_op jit(solution)/shard_map/squeeze | solution.py:62
  55.8 0.8 %squeeze.40 = f32[32,16,16]{2,1,0:T(8,128)} reshape(f32[8,1024]{1,0:T(8,128)S(1)} %get-tuple-element.10) | data formatting | bytes 65536 | tf_op jit(solution)/shard_map/squeeze | solution.py:62
  56.6 0.8 %squeeze.34 = f32[32,16,16]{2,1,0:T(8,128)} reshape(f32[8,1024]{1,0:T(8,128)S(1)} %get-tuple-element.16) | data formatting | bytes 65536 | tf_op jit(solution)/shard_map/squeeze | solution.py:62
  57.5 1.2 %broadcast_multiply_fusion.2 = (f32[32,16,16]{2,1,0:T(8,128)S(1)}, f32[32,16,16]{2,1,0:T(8,128)S(1)}) fusion(f32[32,16,16]{2,1,0:T(8,128)S(1)} %squeeze.33, f32[]{:T(128)S(6)} %sub.49, f32[32,16,16]{2,1,0:T(8,128)} %squeeze.34, f32[32,16,16]{2,1,0:T(8,128)S(1)} %squeeze.35), kind=kLoop, calls=%fused_computation.82 | loop fusion | flops 147456 | bytes 163844 | tf_op jit(solution)/shard_map/mul | solution.py:61
  58.8 1.4 %broadcast_multiply_fusion.3 = (f32[32,16,16]{2,1,0:T(8,128)}, f32[]{:T(128)}) fusion(f32[32,16,16]{2,1,0:T(8,128)S(1)} %squeeze.33, f32[32,16,16]{2,1,0:T(8,128)S(1)} %squeeze.35, f32[32,16,16]{2,1,0:T(8,128)S(1)} %get-tuple-element.34, f32[32,16,16]{2,1,0:T(8,128)S(1)} %squeeze.36, f32[32,16,16]{2,1,0:T(8,128)S(1)} %squeeze.37), kind=kLoop, calls=%fused_computation.83 | loop fusion | flops 57343 | bytes 196612 | tf_op jit(solution)/shard_map/mul | solution.py:61
  60.9 0.8 constant_dynamic-slice_fusion.3
  61.7 1.0 %broadcast_multiply_fusion.1 = (f32[32,16,16]{2,1,0:T(8,128)}, f32[32,16,16]{2,1,0:T(8,128)S(1)}) fusion(f32[32,16,16]{2,1,0:T(8,128)S(1)} %get-tuple-element.34, f32[]{:T(128)S(6)} %sub.53, f32[32,16,16]{2,1,0:T(8,128)S(1)} %squeeze.35, f32[32,16,16]{2,1,0:T(8,128)S(1)} %squeeze.36, f32[32,16,16]{2,1,0:T(8,128)S(1)} %squeeze.37, f32[32,16,16]{2,1,0:T(8,128)S(1)} %squeeze.33), kind=kLoop, calls=%fused_computation.81 | loop fusion | flops 172032 | bytes 229380 | tf_op jit(solution)/shard_map/mul | solution.py:61
  63.4 1.7 %fusion.72 = f32[]{:T(128)} fusion(f32[32,16,16]{2,1,0:T(8,128)S(1)} %squeeze.35, f32[32,16,16]{2,1,0:T(8,128)S(1)} %get-tuple-element.36, f32[32,16,16]{2,1,0:T(8,128)S(1)} %squeeze.37, f32[32,16,16]{2,1,0:T(8,128)S(1)} %get-tuple-element.34, f32[32,16,16]{2,1,0:T(8,128)} %squeeze.38, f32[32,16,16]{2,1,0:T(8,128)} %squeeze.39, f32[32,16,16]{2,1,0:T(8,128)S(1)} %squeeze.33), kind=kLoop, calls=%fused_computation.150 | loop fusion | flops 81919 | bytes 229380 | tf_op jit(solution)/shard_map/reduce_sum | solution.py:65
  65.8 3.9 %fusion.73 = (f32[]{:T(128)}, f32[32,16,16]{2,1,0:T(8,128)}, f32[32,16,16]{2,1,0:T(8,128)S(1)}) fusion(f32[32,16,16]{2,1,0:T(8,128)S(1)} %squeeze.35, f32[32,16,16]{2,1,0:T(8,128)S(1)} %squeeze.37, f32[32,16,16]{2,1,0:T(8,128)} %copy-done.1, f32[32,16,16]{2,1,0:T(8,128)} %squeeze.39, f32[32,16,16]{2,1,0:T(8,128)S(1)} %get-tuple-element.34, ...), kind=kLoop, calls=%fused_computation.151 | loop fusion | flops 270335 | bytes 360456 | tf_op jit(solution)/shard_map/reduce_sum | solution.py:65
  72.9 4.6 %fusion.2 = f32[64,8,1024]{2,0,1:T(8,128)S(1)} fusion(f32[8,64,64]{2,1,0:T(8,128)} %fusion.78, f32[64,8,1024]{2,1,0:T(8,128)S(1)} %copy-done, f32[1024]{0:T(1024)S(1)} %mul.525, f32[64,8]{0,1:T(8,128)S(1)} %fusion.101, f32[1024]{0:T(1024)S(1)} %mul.513, f32[64,8]{0,1:T(8,128)S(1)} %get-tuple-element.45, f32[1024]{0:T(1024)S(1)} %mul.500, ...), kind=kOutput, calls=%fused_computation.3 | convolution fusion | flops 408944640 | bytes 4349984 | tf_op jit(solution)/shard_map/kij,jkc->ikc/dot_general | solution.py:88
  77.4 2.5 %copy.13 = f32[64,8,1024]{2,1,0:T(8,128)} copy(f32[64,8,1024]{2,0,1:T(8,128)S(1)} %fusion.2) | data formatting | bytes 4194304
  (36 shorter events, 9.4 us)
Async XLA Ops:
  0.6 9.7 %copy-start = (f32[64,8,1024]{2,1,0:T(8,128)S(1)}, f32[64,8,1024]{2,1,0:T(8,128)}, u32[]{:S(2)}) copy-start(f32[64,8,1024]{2,1,0:T(8,128)} %param.6) | copy-start | bytes 6291460
  14.8 4.5 %copy-start.2 = (s32[8,1024]{1,0:T(8,128)S(1)}, s32[8,1024]{1,0:T(8,128)}, u32[]{:S(2)}) copy-start(s32[8,1024]{1,0:T(8,128)} %param.7) | copy-start | bytes 98308
  62.7 0.7 copy-start.1

commit v2 on v0

v2 whole, which is shorter than its diff:
```python
import functools

import jax
import jax.numpy as jnp
from jax import lax
from jax.experimental import pallas as pl
from jax.experimental.pallas import tpu as pltpu
from jax.sharding import PartitionSpec as P

CLASSES = 32
SIDE = 16
SUBSTEPS = 4
COUNT_SCALE = 400.0
LANES = 128
GROUP = 8
FIELDS = 2 * SUBSTEPS + 1

HIGHEST = lax.Precision.HIGHEST


def grow(value, factor, times):
    for _ in range(times):
        value = value * factor
    return value


def iota(shape, dim):
    return lax.broadcasted_iota(jnp.int32, shape, dim)


def class_scale(prop):
    rows = [jnp.max(jnp.abs(prop[k]), axis=0, keepdims=True) for k in range(prop.shape[0])]
    return jnp.maximum(1.0, jnp.max(jnp.concatenate(rows, axis=0), axis=1, keepdims=True))


def param_copies(prop_any, coup_any, flux_any, prop, coup, flux, sems):
    own = pl.ds(lax.axis_index("cls") * prop.shape[0], prop.shape[0])
    copies = [
        pltpu.make_async_copy(prop_any.at[own], prop, sems.at[0]),
        pltpu.make_async_copy(coup_any.at[own], coup, sems.at[1]),
    ]
    if flux is not None:
        copies.append(pltpu.make_async_copy(flux_any.at[own], flux, sems.at[2]))
    return copies


def fields_kernel(
    copies_out, melt_any, counts, pressure, prop_any, coup_any, flux_any, out, melt, prop, coup, flux, sems, param_sems
):
    nodes, classes, cells = melt.shape
    params = param_copies(prop_any, coup_any, flux_any, prop, coup, flux, param_sems)
    for copy in params:
        copy.start()
    parts = nodes // GROUP
    pieces = [
        pltpu.make_async_copy(
            melt_any.at[pl.ds(g * GROUP, GROUP)], melt.at[pl.ds(g * GROUP, GROUP)], sems.at[g]
        )
        for g in range(parts)
    ]
    for piece in pieces:
        piece.start()
    for copy in params:
        copy.wait()
    scale = class_scale(prop)
    table = prop[...].reshape(classes * nodes, nodes)
    mask = iota((classes, classes * nodes), 1) // nodes == iota((classes, classes * nodes), 0)
    rows = [flux[...]]
    for _ in range(SUBSTEPS):
        wide = jnp.where(mask, jnp.concatenate([rows[-1]] * classes, axis=1), 0.0)
        rows.append(jnp.dot(wide, table, precision=HIGHEST, preferred_element_type=jnp.float32) / scale)
    counts_n = counts[...].astype(jnp.float32) / (COUNT_SCALE * CLASSES)
    chunks = cells // LANES
    spread = [
        grow(jnp.sum(rows[d] * coup[...], axis=1, keepdims=True), scale, d) for d in range(SUBSTEPS)
    ]
    sums = [[jnp.zeros((classes, LANES), jnp.float32) for _ in range(chunks)] for _ in range(SUBSTEPS)]
    for g in range(parts):
        pieces[g].wait()
        for j in range(g * GROUP, (g + 1) * GROUP):
            weights = [
                jnp.broadcast_to(rows[t + 1][:, j : j + 1], (classes, LANES)) for t in range(SUBSTEPS)
            ]
            for r in range(chunks):
                value = melt[j, :, r * LANES : (r + 1) * LANES]
                for t in range(SUBSTEPS):
                    sums[t][r] = sums[t][r] + weights[t] * value
    tile = pressure.shape[0] * pressure.shape[1] // LANES
    for n in range(copies_out):
        out[n, 2 * SUBSTEPS] = jnp.zeros((chunks, LANES), jnp.float32)
    for r in range(chunks):
        here = counts_n[:, r * LANES : (r + 1) * LANES]
        for t in range(SUBSTEPS):
            row = jnp.sum(grow(here * sums[t][r], scale, t + 1), axis=0, keepdims=True)
            for n in range(copies_out):
                out[n, t, r : r + 1, :] = row
        for d in range(SUBSTEPS):
            row = jnp.sum(here * spread[d], axis=0, keepdims=True)
            for n in range(copies_out):
                out[n, SUBSTEPS + d, r : r + 1, :] = row
    at = lax.axis_index("cls") * tile
    per = pressure.shape[1] // LANES
    for i in range(tile):
        row = pressure[i // per : i // per + 1, (i % per) * LANES : (i % per + 1) * LANES]
        for n in range(copies_out):
            out[n, 2 * SUBSTEPS, pl.ds(at + i, 1), :] = row


def power_kernel(melt_any, prop_any, coup_any, out, columns, melt, prop, coup, sems, param_sems):
    chunks = out.shape[0]
    classes, nodes = prop.shape[:2]
    params = param_copies(prop_any, coup_any, None, prop, coup, None, param_sems)
    for copy in params:
        copy.start()
    loads = [
        pltpu.make_async_copy(
            melt_any.at[:, pl.ds(r * LANES, LANES)], melt.at[r], sems.at[r]
        )
        for r in range(chunks)
    ]
    for load in loads:
        load.start()
    for copy in params:
        copy.wait()
    scale = class_scale(prop)
    unit = [prop[k] / scale[k : k + 1, :] for k in range(classes)]
    table = jnp.concatenate(unit, axis=0)
    column = coup[...]
    columns[0] = column
    for d in range(1, SUBSTEPS):
        pairs = lax.dot_general(
            column, table, (((1,), (1,)), ((), ())), precision=HIGHEST, preferred_element_type=jnp.float32
        )
        column = jnp.concatenate(
            [pairs[k : k + 1, k * nodes : (k + 1) * nodes] for k in range(classes)], axis=0
        )
        columns[d] = grow(column, scale, d)
    for load in loads:
        load.wait()
    together = 4
    width = together * nodes
    mask = iota((width, width), 0) // nodes == iota((width, width), 1) // nodes
    for first in range(0, classes, together):
        some = jnp.concatenate(unit[first : first + together], axis=0)
        block = jnp.where(mask, jnp.concatenate([some] * together, axis=1), 0.0)
        for _ in range(2):
            block = jnp.dot(block, block, precision=HIGHEST, preferred_element_type=jnp.float32)
        x = jnp.concatenate(
            [
                jnp.concatenate(
                    [
                        melt[r, pl.ds(first + k, nodes, stride=classes), :]
                        for k in range(together)
                    ],
                    axis=0,
                )
                for r in range(chunks)
            ],
            axis=1,
        )
        y = jnp.dot(block, x, precision=HIGHEST, preferred_element_type=jnp.float32)
        for k in range(together):
            part = grow(
                y[k * nodes : (k + 1) * nodes], scale[first + k : first + k + 1, :], SUBSTEPS
            )
            for r in range(chunks):
                out[r, pl.ds(first + k, nodes, stride=classes), :] = part[
                    :, r * LANES : (r + 1) * LANES
                ]


def laplacian(x, plane):
    rows = x.shape[0]
    row = iota(x.shape, 0)
    lane = iota(x.shape, 1)
    per = plane // LANES
    inside = row % per * LANES + lane
    col = lane % SIDE
    total = jnp.where(col == 0, 0.0, pltpu.roll(x, 1, 1))
    total += jnp.where(col == SIDE - 1, 0.0, pltpu.roll(x, LANES - 1, 1))
    up = pltpu.roll(x, SIDE, 1)
    up = jnp.where(lane < SIDE, pltpu.roll(up, 1, 0), up)
    total += jnp.where(inside < SIDE, 0.0, up)
    down = pltpu.roll(x, LANES - SIDE, 1)
    down = jnp.where(lane >= LANES - SIDE, pltpu.roll(down, rows - 1, 0), down)
    total += jnp.where(inside >= plane - SIDE, 0.0, down)
    total += jnp.where(row < per, 0.0, pltpu.roll(x, per, 0))
    total += jnp.where(row >= rows - per, 0.0, pltpu.roll(x, rows - per, 0))
    return total - 6.0 * x


def finish_kernel(window, shells_any, columns, out_any, pressure_out, shells, out, walls_all, last, sems, out_sems):
    nodes, classes, cells = out.shape
    chunks = cells // LANES
    parts = nodes // GROUP

    def piece(g):
        return pl.ds(g * GROUP, GROUP)

    loads = [
        pltpu.make_async_copy(
            shells_any.at[:, pl.ds(g * GROUP * classes, GROUP * classes)],
            shells.at[:, pl.ds(g * GROUP * classes, GROUP * classes)],
            sems.at[g],
        )
        for g in range(parts)
    ]
    for load in loads:
        load.start()
    plane = pressure_out.shape[1]
    blocks = window.shape[0]
    rows = blocks * chunks

    def field_of(f):
        return window[:, f].reshape(rows, LANES)

    field = field_of(2 * SUBSTEPS)
    walls = []
    for t in range(SUBSTEPS):
        walls.append(0.5 * field)
        walls_all[t] = walls[t]
        gas = field_of(t)
        for s in range(t + 1):
            gas = gas + field_of(SUBSTEPS + t - s) * walls[s]
        chamber = 1.5 - 0.5 * jnp.sum(gas) / (rows * LANES)
        field = field + 0.15 * laplacian(field, plane) + 0.1 * gas + 0.2 * (chamber - field)
    last[...] = field
    cell = lax.axis_index("cell")
    first = cell * chunks
    tile = pressure_out.shape[0] * plane // LANES
    per = plane // LANES
    at = first + lax.axis_index("cls") * tile
    for i in range(tile):
        pressure_out[i // per : i // per + 1, (i % per) * LANES : (i % per + 1) * LANES] = last[
            pl.ds(at + i, 1), :
        ]
    walls_here = [
        [
            jnp.broadcast_to(walls_all[s, pl.ds(first + r, 1), :], (classes, LANES))
            for r in range(chunks)
        ]
        for s in range(SUBSTEPS)
    ]
    stores = [
        pltpu.make_async_copy(out.at[piece(g)], out_any.at[piece(g)], out_sems.at[g]) for g in range(parts)
    ]
    cols = [columns[SUBSTEPS - 1 - s] for s in range(SUBSTEPS)]
    for g in range(parts):
        loads[g].wait()
        for i in range(g * GROUP, (g + 1) * GROUP):
            weights = [jnp.broadcast_to(cols[s][:, i : i + 1], (classes, LANES)) for s in range(SUBSTEPS)]
            for r in range(chunks):
                value = shells[r, i * classes : (i + 1) * classes, :]
                for s in range(SUBSTEPS):
                    value = value + weights[s] * walls_here[s][r]
                out[i, :, r * LANES : (r + 1) * LANES] = value
        stores[g].start()
    for store in stores:
        store.wait()


ANY = pl.BlockSpec(memory_space=pl.ANY)
VMEM = pl.BlockSpec(memory_space=pltpu.VMEM)
DMA = pltpu.SemaphoreType.DMA


def exchange(copies, axis):
    return lax.all_to_all(copies, axis, split_axis=0, concat_axis=0, tiled=True)


def shards(melt, counts, pressure, propagator, coupling, flux_weights):
    nodes, classes, cells = melt.shape
    chunks = cells // LANES
    f32 = jnp.float32
    split = (chunks, nodes * classes, LANES)
    params = pltpu.CompilerParams(vmem_limit_bytes=32 * 2**20)
    cls_count = lax.axis_size("cls")
    cell_count = lax.axis_size("cell")
    prop_v = pltpu.VMEM((classes, nodes, nodes), f32)
    small = pltpu.VMEM((classes, nodes), f32)
    parts = nodes // GROUP
    packed = pl.pallas_call(
        functools.partial(fields_kernel, cls_count),
        out_shape=jax.ShapeDtypeStruct((cls_count, FIELDS, chunks, LANES), f32),
        in_specs=[ANY, VMEM, VMEM, ANY, ANY, ANY],
        out_specs=VMEM,
        scratch_shapes=[pltpu.VMEM(melt.shape, f32), prop_v, small, small, DMA((parts,)), DMA((3,))],
        compiler_params=params,
        name="fields",
    )(melt, counts, pressure, propagator, coupling, flux_weights)
    shells, columns = pl.pallas_call(
        power_kernel,
        out_shape=[
            jax.ShapeDtypeStruct(split, f32),
            jax.ShapeDtypeStruct((SUBSTEPS, classes, nodes), f32),
        ],
        in_specs=[ANY, ANY, ANY],
        out_specs=[VMEM, VMEM],
        scratch_shapes=[pltpu.VMEM(split, f32), prop_v, small, DMA((chunks,)), DMA((2,))],
        compiler_params=params,
        name="power",
    )(melt.reshape(nodes * classes, cells), propagator, coupling)
    packed = jnp.sum(exchange(packed, "cls"), axis=0)
    window = exchange(jnp.broadcast_to(packed[None], (cell_count,) + packed.shape), "cell")
    rows = cell_count * chunks
    return pl.pallas_call(
        finish_kernel,
        out_shape=[jax.ShapeDtypeStruct(melt.shape, f32), jax.ShapeDtypeStruct(pressure.shape, f32)],
        in_specs=[VMEM, ANY, VMEM],
        out_specs=[ANY, VMEM],
        scratch_shapes=[
            pltpu.VMEM(split, f32),
            pltpu.VMEM(melt.shape, f32),
            pltpu.VMEM((SUBSTEPS, rows, LANES), f32),
            pltpu.VMEM((rows, LANES), f32),
            DMA((parts,)),
            DMA((parts,)),
        ],
        compiler_params=params,
        name="finish",
    )(window, shells, columns)


def solution(mesh):
    placed = (P(None, "cls", "cell"), P("cls", "cell"), P(("cell", "cls"), None), P(), P(), P())
    return jax.shard_map(
        shards,
        mesh=mesh,
        in_specs=placed,
        out_specs=(P(None, "cls", "cell"), P(("cell", "cls"), None)),
        check_vma=False,
    )
```

time: 308 us -> 39 us (0.13)
  blocking collectives: 245 us -> 12.8 us
  matrix products: 21.5 us -> 0 us
  starting transfers between devices: 20.7 us -> 3.72 us
  Pallas kernels: 0 us -> 11.8 us
  other arithmetic: 4.92 us -> 0.01 us
  between operations: 4.19 us -> 0.7 us
    psum x4 -> x0, blocking collectives: 168 us -> none  [pressure_update(): total = lax.psum(jnp.sum(gas_tile), ('cell', 'cls'))]
    all_gather x4 -> x0, blocking collectives: 43.7 us -> none  [shards(): block_pressure = lax.all_gather(tile.reshape(-1), 'cls', axis=0, tiled=True)]
    unnamed x4 -> x0, blocking collectives: 33.5 us -> none
    dot_general x8 -> x0, matrix products: 21.5 us -> none  [the longest x4 15.2 us: shell_update(): jnp.einsum('kij,jkc->ikc', propagator, shells, precision=lax.Precision.HI...]
    ppermute x8 -> x0, starting transfers between devices: 20.7 us -> none  [the longest x4 15.5 us: extended_2(): lax.ppermute(lax.slice_in_dim(block, block.shape[dim] - width, None, axis...]
    all_to_all x0 -> x1, blocking collectives: none -> 12.8 us  [exchange(): return lax.all_to_all(copies, axis, split_axis=0, concat_axis=0, tiled=True)]
    pallas_call x0 -> x3, Pallas kernels: none -> 11.8 us  [the longest x1 6.03 us: shards(): pl.pallas_call(power_kernel, out_shape=[jax.ShapeDtypeStruct(split, f32),...]
    all_to_all x0 -> x1, starting transfers between devices: none -> 3.72 us  [exchange(): return lax.all_to_all(copies, axis, split_axis=0, concat_axis=0, tiled=True)]
  transfers between devices with their start and end apart: 8 -> 1, of which waited for: 0 -> 0; matrix products, arithmetic and copies ran while one was open for 10% -> 0% of each run, Pallas kernels for 0% -> 16%
where the time goes in v2:
time: 39 us; the launch traced here: 38.4 us
  blocking collectives  12.8 us (33%)
  Pallas kernels  11.8 us (30%)
  local copies, waits for them, and re-layouts  9.32 us (24%)
  starting transfers between devices  3.72 us (10%)
  between operations  0.7 us (2%)
    all_to_all x1, blocking collectives, exchange(): return lax.all_to_all(copies, axis, split_axis=0, concat_axis=0, tiled=True)  12.8 us
    unnamed x22, local copies, waits for them, and re-layouts  8.59 us
    pallas_call x1, Pallas kernels, shards(): pl.pallas_call(power_kernel, out_shape=[jax.ShapeDtypeStruct(split, f32),...  6.03 us
    all_to_all x1, starting transfers between devices, exchange(): return lax.all_to_all(copies, axis, split_axis=0, concat_axis=0, tiled=True)  3.72 us
    pallas_call x1, Pallas kernels, shards(): pl.pallas_call(finish_kernel, out_shape=[jax.ShapeDtypeStruct(melt.shape,...  3.25 us
    pallas_call x1, Pallas kernels, shards(): pl.pallas_call(functools.partial(fields_kernel, cls_count), out_shape=jax...  2.54 us
  transfers between devices with their start and end apart: 1, of which 0 were waited for; matrix products, arithmetic and copies ran while one was open for 0% of the time, Pallas kernels for 16%

profile of v2, /device:TPU:0, one launch (start us, length us, event | category | flops | bytes accessed | tf_op | source)
XLA Modules:
  0.0 38.4 jit_solution(7630559119860848439)
XLA Ops:
  0.6 0.0 copy-start
  0.6 1.6 %copy-done = f32[64,8,1024]{2,1,0:T(8,128)S(1)} copy-done((f32[64,8,1024]{2,1,0:T(8,128)S(1)}, f32[64,8,1024]{2,1,0:T(8,128)}, u32[]{:S(2)}) %copy-start) | copy-done | bytes 2097176
  2.2 0.0 copy-start.2
  2.2 1.2 %copy-done.2 = f32[32,64,64]{2,1,0:T(8,128)S(1)} copy-done((f32[32,64,64]{2,1,0:T(8,128)S(1)}, f32[32,64,64]{2,1,0:T(8,128)}, u32[]{:S(2)}) %copy-start.2) | copy-done | bytes 524312
  3.4 0.0 copy-start.6
  3.5 0.7 %copy-done.6 = f32[32,64]{1,0:T(8,128)S(1)} copy-done((f32[32,64]{1,0:T(8,128)S(1)}, f32[32,64]{1,0:T(8,128)}, u32[]{:S(2)}) %copy-start.6) | copy-done | bytes 8216
  4.2 0.0 copy-start.8
  4.2 0.8 %copy-done.8 = s32[8,1024]{1,0:T(8,128)S(1)} copy-done((s32[8,1024]{1,0:T(8,128)S(1)}, s32[8,1024]{1,0:T(8,128)}, u32[]{:S(2)}) %copy-start.8) | copy-done | bytes 32792
  4.9 0.7 %copy-done.9 = f32[32,64]{1,0:T(8,128)S(1)} copy-done((f32[32,64]{1,0:T(8,128)S(1)}, f32[32,64]{1,0:T(8,128)}, u32[]{:S(2)}) %copy-start.9) | copy-done | bytes 8216
  5.6 0.0 copy-start.10
  5.6 0.7 %copy-done.10 = f32[1,256]{1,0:T(1,128)S(1)} copy-done((f32[1,256]{1,0:T(1,128)S(1)}, f32[1,256]{1,0:T(1,128)}, u32[]{:S(2)}) %copy-start.10) | copy-done | bytes 1048
  6.3 2.5 %fields.1 = f32[4,9,8,128]{3,2,1,0:T(8,128)S(1)} custom-call(f32[64,8,1024]{2,1,0:T(8,128)S(1)} %copy-done, s32[8,1024]{1,0:T(8,128)S(1)} %copy-done.8, f32[1,256]{1,0:T(1,128)S(1)} %copy-done.10, f32[32,64,64]{2,1,0:T(8,128)S(1)} %copy-done.2, f32[32,64]{1,0:T(8,128)S(1)} %copy-done.6, f32[32,64]{1,0:T(8,128)S(1)} %copy-done.9), custom_call_target="tpu_custom_call" | custom-call | tf_op jit(solution)/shard_map/fields/pallas_call | solution.py:282
  8.9 12.8 %all_to_all.10 = f32[4,9,8,128]{3,2,1,0:T(8,128)S(1)} all-to-all(f32[4,9,8,128]{3,2,1,0:T(8,128)S(1)} %fields.1), channel_id=1, replica_groups=mesh['cell'=8,'cls'=4] {'cls'}, dimensions={0} | all-to-all | bytes 294912 | tf_op jit(solution)/shard_map/all_to_all | solution.py:268
  21.7 0.7 %broadcast_in_dim.2 = f32[8,9,8,128]{3,2,1,0:T(8,128)} broadcast(f32[9,8,128]{2,1,0:T(8,128)S(1)} %reduce_sum.9), dimensions={1,2,3} | broadcast | bytes 331776 | tf_op jit(solution)/shard_map/broadcast_in_dim | solution.py:304
  22.4 3.7 %all-to-all-start.1 = ((f32[8,9,8,128]{3,2,1,0:T(8,128)}), f32[8,9,8,128]{3,2,1,0:T(8,128)S(1)}, u32[]{:S(2)}, u32[]{:S(2)}) async-start(f32[8,9,8,128]{3,2,1,0:T(8,128)} %broadcast_in_dim.2), calls=%async_computation.1 | async-start | bytes 589824 | tf_op jit(solution)/shard_map/all_to_all | solution.py:268
  26.1 0.0 copy-done.1
  26.1 0.0 copy-done.3
  26.1 0.0 copy-done.7
  26.2 6.0 %power.1 = (f32[8,512,128]{2,1,0:T(8,128)S(1)}, f32[4,8,64]{2,1,0:T(8,128)S(1)}) custom-call(f32[512,1024]{1,0:T(8,128)S(1)} %bitcast.1, f32[32,64,64]{2,1,0:T(8,128)S(1)} %copy-done.3, f32[32,64]{1,0:T(8,128)S(1)} %copy-done.7), custom_call_target="tpu_custom_call" | custom-call | tf_op jit(solution)/shard_map/power/pallas_call | solution.py:291
  32.2 0.0 copy-start.4
  32.2 1.3 %copy-done.4 = f32[8,512,128]{2,1,0:T(8,128)} copy-done((f32[8,512,128]{2,1,0:T(8,128)}, f32[8,512,128]{2,1,0:T(8,128)S(1)}, u32[]{:S(2)}) %copy-start.4) | copy-done | bytes 2097176
  33.5 0.0 all-to-all-done.1.window
  33.5 1.6 %copy-done.5 = f32[8,512,128]{2,1,0:T(8,128)S(1)} copy-done((f32[8,512,128]{2,1,0:T(8,128)S(1)}, f32[8,512,128]{2,1,0:T(8,128)}, u32[]{:S(2)}) %copy-start.5) | copy-done | bytes 2097176
  35.1 3.3 %finish.1 = (f32[64,8,1024]{2,1,0:T(8,128)}, f32[1,256]{1,0:T(1,128)}) custom-call(f32[8,9,8,128]{3,2,1,0:T(8,128)S(1)} %all-to-all-done.1.window, f32[8,512,128]{2,1,0:T(8,128)S(1)} %copy-done.5, f32[4,8,64]{2,1,0:T(8,128)S(1)} %get-tuple-element.5.columns), custom_call_target="tpu_custom_call" | custom-call | tf_op jit(solution)/shard_map/finish/pallas_call | solution.py:306
  (6 shorter events, 0.0 us)
Async XLA Ops:
  0.6 1.6 %copy-start = (f32[64,8,1024]{2,1,0:T(8,128)S(1)}, f32[64,8,1024]{2,1,0:T(8,128)}, u32[]{:S(2)}) copy-start(f32[64,8,1024]{2,1,0:T(8,128)} %melt_any.1) | copy-start | bytes 6291460
  2.2 1.2 %copy-start.2 = (f32[32,64,64]{2,1,0:T(8,128)S(1)}, f32[32,64,64]{2,1,0:T(8,128)}, u32[]{:S(2)}) copy-start(f32[32,64,64]{2,1,0:T(8,128)} %prop_any.3) | copy-start | bytes 1572868
  3.4 0.7 %copy-start.6 = (f32[32,64]{1,0:T(8,128)S(1)}, f32[32,64]{1,0:T(8,128)}, u32[]{:S(2)}) copy-start(f32[32,64]{1,0:T(8,128)} %coup_any.3) | copy-start | bytes 24580
  4.2 0.8 %copy-start.8 = (s32[8,1024]{1,0:T(8,128)S(1)}, s32[8,1024]{1,0:T(8,128)}, u32[]{:S(2)}) copy-start(s32[8,1024]{1,0:T(8,128)} %counts.1) | copy-start | bytes 98308
  4.9 0.7 %copy-start.9 = (f32[32,64]{1,0:T(8,128)S(1)}, f32[32,64]{1,0:T(8,128)}, u32[]{:S(2)}) copy-start(f32[32,64]{1,0:T(8,128)} %flux_any.1) | copy-start | bytes 24580
  5.6 0.7 %copy-start.10 = (f32[1,256]{1,0:T(1,128)S(1)}, f32[1,256]{1,0:T(1,128)}, u32[]{:S(2)}) copy-start(f32[1,256]{1,0:T(1,128)} %pressure.1) | copy-start | bytes 3076
  6.3 19.8 %copy-start.1 = (f32[64,8,1024]{2,1,0:T(8,128)S(1)}, f32[64,8,1024]{2,1,0:T(8,128)}, u32[]{:S(2)}) copy-start(f32[64,8,1024]{2,1,0:T(8,128)} %melt_any.1) | copy-start | bytes 6291460
  6.3 19.8 %copy-start.3 = (f32[32,64,64]{2,1,0:T(8,128)S(1)}, f32[32,64,64]{2,1,0:T(8,128)}, u32[]{:S(2)}) copy-start(f32[32,64,64]{2,1,0:T(8,128)} %prop_any.3) | copy-start | bytes 1572868
  6.3 19.8 %copy-start.7 = (f32[32,64]{1,0:T(8,128)S(1)}, f32[32,64]{1,0:T(8,128)}, u32[]{:S(2)}) copy-start(f32[32,64]{1,0:T(8,128)} %coup_any.3) | copy-start | bytes 24580
  22.4 11.1 %all-to-all-start.1 = ((f32[8,9,8,128]{3,2,1,0:T(8,128)}), f32[8,9,8,128]{3,2,1,0:T(8,128)S(1)}, u32[]{:S(2)}, u32[]{:S(2)}) async-start(f32[8,9,8,128]{3,2,1,0:T(8,128)} %broadcast_in_dim.2), calls=%async_computation.1 | async-start | bytes 589824 | tf_op jit(solution)/shard_map/all_to_all | solution.py:268
  32.2 1.3 %copy-start.4 = (f32[8,512,128]{2,1,0:T(8,128)}, f32[8,512,128]{2,1,0:T(8,128)S(1)}, u32[]{:S(2)}) copy-start(f32[8,512,128]{2,1,0:T(8,128)S(1)} %get-tuple-element.4.shells_any) | copy-start | bytes 6291460
  33.5 1.6 %copy-start.5 = (f32[8,512,128]{2,1,0:T(8,128)S(1)}, f32[8,512,128]{2,1,0:T(8,128)}, u32[]{:S(2)}) copy-start(f32[8,512,128]{2,1,0:T(8,128)} %copy-done.4) | copy-start | bytes 6291460

commit v3 on v2

v3 whole, which is shorter than its diff:
```python
import functools

import jax
import jax.numpy as jnp
from jax import lax
from jax.experimental import pallas as pl
from jax.experimental.pallas import tpu as pltpu
from jax.sharding import PartitionSpec as P

CLASSES = 32
SIDE = 16
SUBSTEPS = 4
COUNT_SCALE = 400.0
LANES = 128
GROUP = 8
FIELDS = 2 * SUBSTEPS + 1

HIGHEST = lax.Precision.HIGHEST


def grow(value, factor, times):
    for _ in range(times):
        value = value * factor
    return value


def iota(shape, dim):
    return lax.broadcasted_iota(jnp.int32, shape, dim)


def split3(x):
    high = x.astype(jnp.bfloat16)
    rest = x - high.astype(jnp.float32)
    middle = rest.astype(jnp.bfloat16)
    low = (rest - middle.astype(jnp.float32)).astype(jnp.bfloat16)
    return high, middle, low


def split2(x):
    high = x.astype(jnp.bfloat16)
    return high, (x - high.astype(jnp.float32)).astype(jnp.bfloat16)


def dot(a, b):
    return jnp.dot(a, b, preferred_element_type=jnp.float32)


def square(a):
    high, middle, low = split3(a)
    left = jnp.concatenate([high, high, middle, high, low, middle], axis=1)
    right = jnp.concatenate([high, middle, high, low, high, middle], axis=0)
    return dot(left, right)


def class_scale(prop):
    rows = [jnp.max(jnp.abs(prop[k]), axis=0, keepdims=True) for k in range(prop.shape[0])]
    return jnp.maximum(1.0, jnp.max(jnp.concatenate(rows, axis=0), axis=1, keepdims=True))


def param_copies(pairs, sems):
    copies = []
    for n, (source, target) in enumerate(pairs):
        own = pl.ds(lax.axis_index("cls") * target.shape[0], target.shape[0])
        copies.append(pltpu.make_async_copy(source.at[own], target, sems.at[n]))
    return copies


def fields_kernel(
    melt_hbm, counts_hbm, pressure_hbm, prop_hbm, coup_hbm, flux_hbm, out, melt, counts, pressure, prop, coup, flux, sems, other_sems
):
    nodes, classes, cells = melt.shape
    first = param_copies([(prop_hbm, prop), (flux_hbm, flux), (coup_hbm, coup)], other_sems)
    for copy in first:
        copy.start()
    parts = nodes // GROUP
    pieces = [
        pltpu.make_async_copy(
            melt_hbm.at[pl.ds(g * GROUP, GROUP)], melt.at[pl.ds(g * GROUP, GROUP)], sems.at[g]
        )
        for g in range(parts)
    ]
    for piece in pieces:
        piece.start()
    rest = [
        pltpu.make_async_copy(counts_hbm, counts, other_sems.at[3]),
        pltpu.make_async_copy(pressure_hbm, pressure, other_sems.at[4]),
    ]
    for copy in rest:
        copy.start()
    for copy in first:
        copy.wait()
    scale = class_scale(prop)
    width = classes * nodes
    table = jnp.concatenate(split3(prop[...].reshape(width, nodes)), axis=1)
    mask = iota((classes, width), 1) // nodes == iota((classes, width), 0)
    rows = [flux[...]]
    for _ in range(SUBSTEPS):
        wide = jnp.where(mask, jnp.concatenate([rows[-1]] * classes, axis=1), 0.0)
        pairs = dot(jnp.concatenate(split3(wide), axis=0), table)
        row = pairs[:classes] + pairs[classes : 2 * classes] + pairs[2 * classes :]
        rows.append((row[:, :nodes] + row[:, nodes : 2 * nodes] + row[:, 2 * nodes :]) / scale)
    spread = [
        grow(jnp.sum(rows[d] * coup[...], axis=1, keepdims=True), scale, d) for d in range(SUBSTEPS)
    ]
    for copy in rest:
        copy.wait()
    counts_n = counts[...].astype(jnp.float32) / (COUNT_SCALE * CLASSES)
    chunks = cells // LANES
    sums = [[jnp.zeros((classes, LANES), jnp.float32) for _ in range(chunks)] for _ in range(SUBSTEPS)]
    for g in range(parts):
        pieces[g].wait()
        for j in range(g * GROUP, (g + 1) * GROUP):
            weights = [
                jnp.broadcast_to(rows[t + 1][:, j : j + 1], (classes, LANES)) for t in range(SUBSTEPS)
            ]
            for r in range(chunks):
                value = melt[j, :, r * LANES : (r + 1) * LANES]
                for t in range(SUBSTEPS):
                    sums[t][r] = sums[t][r] + weights[t] * value
    out[2 * SUBSTEPS] = jnp.zeros((chunks, LANES), jnp.float32)
    for r in range(chunks):
        here = counts_n[:, r * LANES : (r + 1) * LANES]
        for t in range(SUBSTEPS):
            out[t, r : r + 1, :] = jnp.sum(grow(here * sums[t][r], scale, t + 1), axis=0, keepdims=True)
        for d in range(SUBSTEPS):
            out[SUBSTEPS + d, r : r + 1, :] = jnp.sum(here * spread[d], axis=0, keepdims=True)
    per = pressure.shape[1] // LANES
    tile = pressure.shape[0] * per
    at = lax.axis_index("cls") * tile
    for i in range(tile):
        out[2 * SUBSTEPS, pl.ds(at + i, 1), :] = pressure[
            i // per : i // per + 1, (i % per) * LANES : (i % per + 1) * LANES
        ]


def power_kernel(melt_hbm, prop_hbm, coup_hbm, out_hbm, columns, melt, out, prop, coup, sems, out_sems, param_sems):
    chunks = out.shape[0]
    classes, nodes = prop.shape[:2]
    params = param_copies([(prop_hbm, prop), (coup_hbm, coup)], param_sems)
    for copy in params:
        copy.start()
    loads = [
        pltpu.make_async_copy(melt_hbm.at[:, pl.ds(r * LANES, LANES)], melt.at[r], sems.at[r])
        for r in range(chunks)
    ]
    stores = [pltpu.make_async_copy(out.at[r], out_hbm.at[r], out_sems.at[r]) for r in range(chunks)]
    for load in loads:
        load.start()
    for copy in params:
        copy.wait()
    scale = class_scale(prop)
    unit = [prop[k] / scale[k : k + 1, :] for k in range(classes)]
    table = jnp.concatenate(unit, axis=0)
    column = coup[...]
    columns[0] = column
    for d in range(1, SUBSTEPS):
        pairs = lax.dot_general(
            column, table, (((1,), (1,)), ((), ())), precision=HIGHEST, preferred_element_type=jnp.float32
        )
        column = jnp.concatenate(
            [pairs[k : k + 1, k * nodes : (k + 1) * nodes] for k in range(classes)], axis=0
        )
        columns[d] = grow(column, scale, d)
    lefts = []
    for k in range(classes):
        high, low = split2(square(square(unit[k])))
        lefts.append(jnp.concatenate([high, high, low], axis=1))
    together = 2 if chunks % 2 == 0 else 1
    for r in range(0, chunks, together):
        for n in range(together):
            loads[r + n].wait()
        for k in range(classes):
            own = pl.ds(k, nodes, stride=classes)
            high, low = split2(jnp.concatenate([melt[r + n, own, :] for n in range(together)], axis=1))
            part = dot(lefts[k], jnp.concatenate([high, low, high], axis=0))
            part = grow(part, scale[k : k + 1, :], SUBSTEPS)
            for n in range(together):
                out[r + n, own, :] = part[:, n * LANES : (n + 1) * LANES]
        for n in range(together):
            stores[r + n].start()
    for store in stores:
        store.wait()


def combine_kernel(mine, theirs, out):
    total = mine[...] + theirs[...]
    wall = 0.5 * total[2 * SUBSTEPS]
    for n in range(out.shape[0]):
        for t in range(SUBSTEPS):
            out[n, t] = total[t] + total[SUBSTEPS + t] * wall
        for d in range(SUBSTEPS - 1):
            out[n, SUBSTEPS + d] = total[SUBSTEPS + d]
        out[n, 2 * SUBSTEPS - 1] = total[2 * SUBSTEPS]


def laplacian(x, plane):
    rows = x.shape[0]
    row = iota(x.shape, 0)
    lane = iota(x.shape, 1)
    per = plane // LANES
    inside = row % per * LANES + lane
    col = lane % SIDE
    total = jnp.where(col == 0, 0.0, pltpu.roll(x, 1, 1))
    total += jnp.where(col == SIDE - 1, 0.0, pltpu.roll(x, LANES - 1, 1))
    up = pltpu.roll(x, SIDE, 1)
    up = jnp.where(lane < SIDE, pltpu.roll(up, 1, 0), up)
    total += jnp.where(inside < SIDE, 0.0, up)
    down = pltpu.roll(x, LANES - SIDE, 1)
    down = jnp.where(lane >= LANES - SIDE, pltpu.roll(down, rows - 1, 0), down)
    total += jnp.where(inside >= plane - SIDE, 0.0, down)
    total += jnp.where(row < per, 0.0, pltpu.roll(x, per, 0))
    total += jnp.where(row >= rows - per, 0.0, pltpu.roll(x, rows - per, 0))
    return total - 6.0 * x


def finish_kernel(window, shells_hbm, columns, out_hbm, pressure_out, shells, out, walls_all, last, sems, out_sems):
    nodes, classes, cells = out.shape
    chunks = cells // LANES
    parts = nodes // GROUP

    def piece(g):
        return pl.ds(g * GROUP, GROUP)

    loads = [
        pltpu.make_async_copy(
            shells_hbm.at[:, pl.ds(g * GROUP * classes, GROUP * classes)],
            shells.at[:, pl.ds(g * GROUP * classes, GROUP * classes)],
            sems.at[g],
        )
        for g in range(parts)
    ]
    for load in loads:
        load.start()
    plane = pressure_out.shape[1]
    blocks = window.shape[0]
    rows = blocks * chunks

    def field_of(f):
        return window[:, f].reshape(rows, LANES)

    field = field_of(2 * SUBSTEPS - 1)
    walls = []
    for t in range(SUBSTEPS):
        walls.append(0.5 * field)
        walls_all[t] = walls[t]
        gas = field_of(t)
        for s in range(1, t + 1):
            gas = gas + field_of(SUBSTEPS + t - s) * walls[s]
        chamber = 1.5 - 0.5 * jnp.sum(gas) / (rows * LANES)
        field = field + 0.15 * laplacian(field, plane) + 0.1 * gas + 0.2 * (chamber - field)
    last[...] = field
    cell = lax.axis_index("cell")
    first = cell * chunks
    tile = pressure_out.shape[0] * plane // LANES
    per = plane // LANES
    at = first + lax.axis_index("cls") * tile
    for i in range(tile):
        pressure_out[i // per : i // per + 1, (i % per) * LANES : (i % per + 1) * LANES] = last[
            pl.ds(at + i, 1), :
        ]
    walls_here = [
        [
            jnp.broadcast_to(walls_all[s, pl.ds(first + r, 1), :], (classes, LANES))
            for r in range(chunks)
        ]
        for s in range(SUBSTEPS)
    ]
    stores = [
        pltpu.make_async_copy(out.at[piece(g)], out_hbm.at[piece(g)], out_sems.at[g]) for g in range(parts)
    ]
    cols = [columns[SUBSTEPS - 1 - s] for s in range(SUBSTEPS)]
    for g in range(parts):
        loads[g].wait()
        for i in range(g * GROUP, (g + 1) * GROUP):
            weights = [jnp.broadcast_to(cols[s][:, i : i + 1], (classes, LANES)) for s in range(SUBSTEPS)]
            for r in range(chunks):
                value = shells[r, i * classes : (i + 1) * classes, :]
                for s in range(SUBSTEPS):
                    value = value + weights[s] * walls_here[s][r]
                out[i, :, r * LANES : (r + 1) * LANES] = value
        stores[g].start()
    for store in stores:
        store.wait()


HBM = pl.BlockSpec(memory_space=pltpu.HBM)
VMEM = pl.BlockSpec(memory_space=pltpu.VMEM)
DMA = pltpu.SemaphoreType.DMA


def partner(value, axis, distance):
    count = lax.axis_size(axis)
    return lax.ppermute(value, axis, [(i, i ^ distance) for i in range(count)])


def shards(melt, counts, pressure, propagator, coupling, flux_weights):
    nodes, classes, cells = melt.shape
    chunks = cells // LANES
    f32 = jnp.float32
    split = (chunks, nodes * classes, LANES)
    params = pltpu.CompilerParams(vmem_limit_bytes=32 * 2**20)
    cls_count = lax.axis_size("cls")
    cell_count = lax.axis_size("cell")
    prop_v = pltpu.VMEM((classes, nodes, nodes), f32)
    small = pltpu.VMEM((classes, nodes), f32)
    parts = nodes // GROUP
    packed = pl.pallas_call(
        fields_kernel,
        out_shape=jax.ShapeDtypeStruct((FIELDS, chunks, LANES), f32),
        in_specs=[HBM] * 6,
        out_specs=VMEM,
        scratch_shapes=[
            pltpu.VMEM(melt.shape, f32),
            pltpu.VMEM(counts.shape, counts.dtype),
            pltpu.VMEM(pressure.shape, f32),
            prop_v,
            small,
            small,
            DMA((parts,)),
            DMA((5,)),
        ],
        compiler_params=params,
        name="fields",
    )(melt, counts, pressure, propagator, coupling, flux_weights)
    shells, columns = pl.pallas_call(
        power_kernel,
        out_shape=[
            jax.ShapeDtypeStruct(split, f32),
            jax.ShapeDtypeStruct((SUBSTEPS, classes, nodes), f32),
        ],
        in_specs=[HBM] * 3,
        out_specs=[HBM, VMEM],
        scratch_shapes=[
            pltpu.VMEM(split, f32),
            pltpu.VMEM(split, f32),
            prop_v,
            small,
            DMA((chunks,)),
            DMA((chunks,)),
            DMA((2,)),
        ],
        compiler_params=params,
        cost_estimate=pl.CostEstimate(flops=2 * 10**9, bytes_accessed=2 * melt.size * 4, transcendentals=0),
        name="power",
    )(melt.reshape(nodes * classes, cells), propagator, coupling)
    distance = 1
    theirs = partner(packed, "cls", distance)
    while 2 * distance < cls_count:
        distance *= 2
        packed = packed + theirs
        theirs = partner(packed, "cls", distance)
    copies = pl.pallas_call(
        combine_kernel,
        out_shape=jax.ShapeDtypeStruct((cell_count, FIELDS - 1, chunks, LANES), f32),
        in_specs=[VMEM, VMEM],
        out_specs=VMEM,
        compiler_params=params,
        name="combine",
    )(packed, theirs)
    window = lax.all_to_all(copies, "cell", split_axis=0, concat_axis=0, tiled=True)
    rows = cell_count * chunks
    return pl.pallas_call(
        finish_kernel,
        out_shape=[jax.ShapeDtypeStruct(melt.shape, f32), jax.ShapeDtypeStruct(pressure.shape, f32)],
        in_specs=[VMEM, HBM, VMEM],
        out_specs=[HBM, VMEM],
        scratch_shapes=[
            pltpu.VMEM(split, f32),
            pltpu.VMEM(melt.shape, f32),
            pltpu.VMEM((SUBSTEPS, rows, LANES), f32),
            pltpu.VMEM((rows, LANES), f32),
            DMA((parts,)),
            DMA((parts,)),
        ],
        compiler_params=params,
        name="finish",
    )(window, shells, columns)


def solution(mesh):
    placed = (P(None, "cls", "cell"), P("cls", "cell"), P(("cell", "cls"), None), P(), P(), P())
    return jax.shard_map(
        shards,
        mesh=mesh,
        in_specs=placed,
        out_specs=(P(None, "cls", "cell"), P(("cell", "cls"), None)),
        check_vma=False,
    )
```

time: 39 us -> 34.5 us (0.88)
  blocking collectives: 12.8 us -> 0 us
  starting transfers between devices: 3.72 us -> 10.2 us
  waiting for transfers between devices: 0.01 us -> 4.41 us
  local copies, waits for them, and re-layouts: 9.32 us -> 7.27 us
    all_to_all x1 -> x0, blocking collectives: 12.8 us -> none  [exchange(): return lax.all_to_all(copies, axis, split_axis=0, concat_axis=0, tiled=True)]
    ppermute x0 -> x2, starting transfers between devices: none -> 6.12 us  [partner(): return lax.ppermute(value, axis, [(i, i ^ distance) for i in range(count)])]
    ppermute x0 -> x2, waiting for transfers between devices: none -> 3.87 us  [partner(): return lax.ppermute(value, axis, [(i, i ^ distance) for i in range(count)])]
    unnamed x22 -> x18, local copies, waits for them, and re-layouts: 8.59 us -> 7.27 us
    pallas_call x1, Pallas kernels: 6.03 us -> 4.78 us  [shards(): pl.pallas_call(power_kernel, out_shape=[jax.ShapeDtypeStruct(split, f32),...]
    pallas_call x1 -> x2, Pallas kernels: 2.54 us -> 3.45 us  [the longest x1 2.72 us: shards(): pl.pallas_call(fields_kernel, out_shape=jax.ShapeDtypeStruct((FIELDS, chu...]
    broadcast_in_dim x1 -> x0, local copies, waits for them, and re-layouts: 0.73 us -> none  [shards(): jnp.broadcast_to(packed[None], (cell_count,) + packed.shape)]
    all_to_all x1, waiting for transfers between devices: 0.01 us -> 0.54 us  [shards(): lax.all_to_all(copies, 'cell', split_axis=0, concat_axis=0, tiled=True)]
  transfers between devices with their start and end apart: 1 -> 3, of which waited for: 0 -> 3; matrix products, arithmetic and copies ran while one was open for 0% -> 0% of each run, Pallas kernels for 16% -> 14%
where the time goes in v3:
time: 34.5 us; the launch traced here: 34 us
  Pallas kernels  11.5 us (33%)
  starting transfers between devices  10.2 us (30%)
  local copies, waits for them, and re-layouts  7.27 us (21%)
  waiting for transfers between devices  4.41 us (13%)
  between operations  0.69 us (2%)
    unnamed x18, local copies, waits for them, and re-layouts  7.27 us
    ppermute x2, starting transfers between devices, partner(): return lax.ppermute(value, axis, [(i, i ^ distance) for i in range(count)])  6.12 us
    pallas_call x1, Pallas kernels, shards(): pl.pallas_call(power_kernel, out_shape=[jax.ShapeDtypeStruct(split, f32),...  4.78 us
    all_to_all x1, starting transfers between devices, shards(): lax.all_to_all(copies, 'cell', split_axis=0, concat_axis=0, tiled=True)  4.06 us
    ppermute x2, waiting for transfers between devices, partner(): return lax.ppermute(value, axis, [(i, i ^ distance) for i in range(count)])  3.87 us
    pallas_call x1, Pallas kernels, shards(): pl.pallas_call(finish_kernel, out_shape=[jax.ShapeDtypeStruct(melt.shape,...  3.25 us
    pallas_call x1, Pallas kernels, shards(): pl.pallas_call(fields_kernel, out_shape=jax.ShapeDtypeStruct((FIELDS, chu...  2.72 us
    pallas_call x1, Pallas kernels, shards(): pl.pallas_call(combine_kernel, out_shape=jax.ShapeDtypeStruct((cell_count...  0.73 us
  transfers between devices with their start and end apart: 3, of which 3 were waited for; matrix products, arithmetic and copies ran while one was open for 0% of the time, Pallas kernels for 14%

profile of v3, /device:TPU:0, one launch (start us, length us, event | category | flops | bytes accessed | tf_op | source)
XLA Modules:
  0.0 34.0 jit_solution(1612020244812769306)
XLA Ops:
  0.6 0.0 copy-start
  0.6 1.6 %copy-done = f32[64,8,1024]{2,1,0:T(8,128)S(1)} copy-done((f32[64,8,1024]{2,1,0:T(8,128)S(1)}, f32[64,8,1024]{2,1,0:T(8,128)}, u32[]{:S(2)}) %copy-start) | copy-done | bytes 2097176
  2.2 0.0 copy-start.2
  2.2 1.2 %copy-done.2 = f32[32,64,64]{2,1,0:T(8,128)S(1)} copy-done((f32[32,64,64]{2,1,0:T(8,128)S(1)}, f32[32,64,64]{2,1,0:T(8,128)}, u32[]{:S(2)}) %copy-start.2) | copy-done | bytes 524312
  3.5 0.0 copy-start.4
  3.5 0.8 %copy-done.4 = s32[8,1024]{1,0:T(8,128)S(1)} copy-done((s32[8,1024]{1,0:T(8,128)S(1)}, s32[8,1024]{1,0:T(8,128)}, u32[]{:S(2)}) %copy-start.4) | copy-done | bytes 32792
  4.2 0.0 copy-start.5
  4.2 0.7 %copy-done.5 = f32[32,64]{1,0:T(8,128)S(1)} copy-done((f32[32,64]{1,0:T(8,128)S(1)}, f32[32,64]{1,0:T(8,128)}, u32[]{:S(2)}) %copy-start.5) | copy-done | bytes 8216
  4.9 0.7 %copy-done.6 = f32[32,64]{1,0:T(8,128)S(1)} copy-done((f32[32,64]{1,0:T(8,128)S(1)}, f32[32,64]{1,0:T(8,128)}, u32[]{:S(2)}) %copy-start.6) | copy-done | bytes 8216
  5.6 0.7 %copy-done.8 = f32[1,256]{1,0:T(1,128)S(1)} copy-done((f32[1,256]{1,0:T(1,128)S(1)}, f32[1,256]{1,0:T(1,128)}, u32[]{:S(2)}) %copy-start.8) | copy-done | bytes 1048
  6.3 2.7 %fields.1 = f32[9,8,128]{2,1,0:T(8,128)S(1)} custom-call(f32[64,8,1024]{2,1,0:T(8,128)S(1)} %copy-done, s32[8,1024]{1,0:T(8,128)S(1)} %copy-done.4, f32[1,256]{1,0:T(1,128)S(1)} %copy-done.8, f32[32,64,64]{2,1,0:T(8,128)S(1)} %copy-done.2, f32[32,64]{1,0:T(8,128)S(1)} %copy-done.6, f32[32,64]{1,0:T(8,128)S(1)} %copy-done.5), custom_call_target="tpu_custom_call" | custom-call | tf_op jit(solution)/shard_map/fields/pallas_call | solution.py:307
  9.1 3.1 %collective-permute-start = (f32[9,8,128]{2,1,0:T(8,128)S(1)}, f32[9,8,128]{2,1,0:T(8,128)S(1)}, u32[]{:S(2)}, u32[]{:S(2)}) collective-permute-start(f32[9,8,128]{2,1,0:T(8,128)S(1)} %fields.1), channel_id=1, source_target_pairs={{0,1},{1,0},{2,3},{3,2},{4,5},{5,4},{6,7},{7,6},{8,9},{9,8},{10,11... | collective-permute-start | bytes 110600 | tf_op jit(solution)/shard_map/ppermute | solution.py:293
  12.1 1.9 %collective-permute-done = f32[9,8,128]{2,1,0:T(8,128)S(1)} collective-permute-done((f32[9,8,128]{2,1,0:T(8,128)S(1)}, f32[9,8,128]{2,1,0:T(8,128)S(1)}, u32[]{:S(2)}, u32[]{:S(2)}) %collective-permute-start) | collective-permute-done | bytes 36896 | tf_op jit(solution)/shard_map/ppermute | solution.py:293
  14.1 3.0 %collective-permute-start.1 = (f32[9,8,128]{2,1,0:T(8,128)S(1)}, f32[9,8,128]{2,1,0:T(8,128)S(1)}, u32[]{:S(2)}, u32[]{:S(2)}) collective-permute-start(f32[9,8,128]{2,1,0:T(8,128)S(1)} %add.3.mine), channel_id=1, source_target_pairs={{0,2},{1,3},{2,0},{3,1},{4,6},{5,7},{6,4},{7,5},{8,10},{9,11},{10,... | collective-permute-start | bytes 110600 | tf_op jit(solution)/shard_map/ppermute | solution.py:293
  17.1 1.9 %collective-permute-done.1.theirs = f32[9,8,128]{2,1,0:T(8,128)S(1)} collective-permute-done((f32[9,8,128]{2,1,0:T(8,128)S(1)}, f32[9,8,128]{2,1,0:T(8,128)S(1)}, u32[]{:S(2)}, u32[]{:S(2)}) %collective-permute-start.1) | collective-permute-done | bytes 36896 | tf_op jit(solution)/shard_map/ppermute | solution.py:293
  19.1 0.7 %combine.1 = f32[8,8,8,128]{3,2,1,0:T(8,128)} custom-call(f32[9,8,128]{2,1,0:T(8,128)S(1)} %add.3.mine, f32[9,8,128]{2,1,0:T(8,128)S(1)} %collective-permute-done.1.theirs), custom_call_target="tpu_custom_call" | custom-call | tf_op jit(solution)/shard_map/combine/pallas_call | solution.py:352
  19.8 4.1 %all-to-all-start = ((f32[8,8,8,128]{3,2,1,0:T(8,128)}), f32[8,8,8,128]{3,2,1,0:T(8,128)S(1)}, u32[]{:S(2)}, u32[]{:S(2)}) async-start(f32[8,8,8,128]{3,2,1,0:T(8,128)} %combine.1), calls=%async_computation | async-start | bytes 524288 | tf_op jit(solution)/shard_map/all_to_all | solution.py:360
  23.8 0.0 copy-done.3
  23.9 0.0 copy-done.7
  23.9 0.0 copy-start.1
  23.9 1.6 %copy-done.1 = f32[64,8,1024]{2,1,0:T(8,128)S(1)} copy-done((f32[64,8,1024]{2,1,0:T(8,128)S(1)}, f32[64,8,1024]{2,1,0:T(8,128)}, u32[]{:S(2)}) %copy-start.1) | copy-done | bytes 2097176
  25.5 4.8 %power.1 = (f32[8,512,128]{2,1,0:T(8,128)S(1)}, f32[4,8,64]{2,1,0:T(8,128)S(1)}) custom-call(f32[512,1024]{1,0:T(8,128)S(1)} %bitcast.1, f32[32,64,64]{2,1,0:T(8,128)S(1)} %copy-done.3, f32[32,64]{1,0:T(8,128)S(1)} %copy-done.7), custom_call_target="tpu_custom_call" | custom-call | flops 2000000000 | bytes 4194304 | tf_op jit(solution)/shard_map/power/pallas_call | solution.py:325
  30.2 0.5 %all-to-all-done.window = f32[8,8,8,128]{3,2,1,0:T(8,128)S(1)} async-done(((f32[8,8,8,128]{3,2,1,0:T(8,128)}), f32[8,8,8,128]{3,2,1,0:T(8,128)S(1)}, u32[]{:S(2)}, u32[]{:S(2)}) %all-to-all-start) | async-done | bytes 262176 | tf_op jit(solution)/shard_map/all_to_all | solution.py:360
  30.8 3.2 %finish.1 = (f32[64,8,1024]{2,1,0:T(8,128)}, f32[1,256]{1,0:T(1,128)}) custom-call(f32[8,8,8,128]{3,2,1,0:T(8,128)S(1)} %all-to-all-done.window, f32[8,512,128]{2,1,0:T(8,128)S(1)} %get-tuple-element.4.shells_hbm, f32[4,8,64]{2,1,0:T(8,128)S(1)} %get-tuple-element.5.columns), custom_call_target="tpu_custom_call" | custom-call | tf_op jit(solution)/shard_map/finish/pallas_call | solution.py:362
  (5 shorter events, 0.0 us)
Async XLA Ops:
  0.6 1.6 %copy-start = (f32[64,8,1024]{2,1,0:T(8,128)S(1)}, f32[64,8,1024]{2,1,0:T(8,128)}, u32[]{:S(2)}) copy-start(f32[64,8,1024]{2,1,0:T(8,128)} %melt_hbm.1) | copy-start | bytes 6291460
  2.2 1.2 %copy-start.2 = (f32[32,64,64]{2,1,0:T(8,128)S(1)}, f32[32,64,64]{2,1,0:T(8,128)}, u32[]{:S(2)}) copy-start(f32[32,64,64]{2,1,0:T(8,128)} %prop_hbm.3) | copy-start | bytes 1572868
  3.5 0.8 %copy-start.4 = (s32[8,1024]{1,0:T(8,128)S(1)}, s32[8,1024]{1,0:T(8,128)}, u32[]{:S(2)}) copy-start(s32[8,1024]{1,0:T(8,128)} %counts_hbm.1) | copy-start | bytes 98308
  4.2 0.7 %copy-start.5 = (f32[32,64]{1,0:T(8,128)S(1)}, f32[32,64]{1,0:T(8,128)}, u32[]{:S(2)}) copy-start(f32[32,64]{1,0:T(8,128)} %flux_hbm.1) | copy-start | bytes 24580
  4.9 0.7 %copy-start.6 = (f32[32,64]{1,0:T(8,128)S(1)}, f32[32,64]{1,0:T(8,128)}, u32[]{:S(2)}) copy-start(f32[32,64]{1,0:T(8,128)} %coup_hbm.3) | copy-start | bytes 24580
  5.6 0.7 %copy-start.8 = (f32[1,256]{1,0:T(1,128)S(1)}, f32[1,256]{1,0:T(1,128)}, u32[]{:S(2)}) copy-start(f32[1,256]{1,0:T(1,128)} %pressure_hbm.1) | copy-start | bytes 3076
  6.3 17.5 %copy-start.3 = (f32[32,64,64]{2,1,0:T(8,128)S(1)}, f32[32,64,64]{2,1,0:T(8,128)}, u32[]{:S(2)}) copy-start(f32[32,64,64]{2,1,0:T(8,128)} %prop_hbm.3) | copy-start | bytes 1572868
  6.3 17.5 %copy-start.7 = (f32[32,64]{1,0:T(8,128)S(1)}, f32[32,64]{1,0:T(8,128)}, u32[]{:S(2)}) copy-start(f32[32,64]{1,0:T(8,128)} %coup_hbm.3) | copy-start | bytes 24580
  9.1 5.0 %collective-permute-start = (f32[9,8,128]{2,1,0:T(8,128)S(1)}, f32[9,8,128]{2,1,0:T(8,128)S(1)}, u32[]{:S(2)}, u32[]{:S(2)}) collective-permute-start(f32[9,8,128]{2,1,0:T(8,128)S(1)} %fields.1), channel_id=1, source_target_pairs={{0,1},{1,0},{2,3},{3,2},{4,5},{5,4},{6,7},{7,6},{8,9},{9,8},{10,11... | collective-permute-start | bytes 110600 | tf_op jit(solution)/shard_map/ppermute | solution.py:293
  14.1 5.0 %collective-permute-start.1 = (f32[9,8,128]{2,1,0:T(8,128)S(1)}, f32[9,8,128]{2,1,0:T(8,128)S(1)}, u32[]{:S(2)}, u32[]{:S(2)}) collective-permute-start(f32[9,8,128]{2,1,0:T(8,128)S(1)} %add.3.mine), channel_id=1, source_target_pairs={{0,2},{1,3},{2,0},{3,1},{4,6},{5,7},{6,4},{7,5},{8,10},{9,11},{10,... | collective-permute-start | bytes 110600 | tf_op jit(solution)/shard_map/ppermute | solution.py:293
  19.8 11.0 %all-to-all-start = ((f32[8,8,8,128]{3,2,1,0:T(8,128)}), f32[8,8,8,128]{3,2,1,0:T(8,128)S(1)}, u32[]{:S(2)}, u32[]{:S(2)}) async-start(f32[8,8,8,128]{3,2,1,0:T(8,128)} %combine.1), calls=%async_computation | async-start | bytes 524288 | tf_op jit(solution)/shard_map/all_to_all | solution.py:360
  23.9 1.6 %copy-start.1 = (f32[64,8,1024]{2,1,0:T(8,128)S(1)}, f32[64,8,1024]{2,1,0:T(8,128)}, u32[]{:S(2)}) copy-start(f32[64,8,1024]{2,1,0:T(8,128)} %melt_hbm.1) | copy-start | bytes 6291460

commit v4 on v3

--- a/solution.py
+++ b/solution.py
@@ -117,23 +117,29 @@
                 value = melt[j, :, r * LANES : (r + 1) * LANES]
                 for t in range(SUBSTEPS):
                     sums[t][r] = sums[t][r] + weights[t] * value
-    out[2 * SUBSTEPS] = jnp.zeros((chunks, LANES), jnp.float32)
+    every = range(out.shape[0])
+    for n in every:
+        out[n, 2 * SUBSTEPS] = jnp.zeros((chunks, LANES), jnp.float32)
     for r in range(chunks):
         here = counts_n[:, r * LANES : (r + 1) * LANES]
         for t in range(SUBSTEPS):
-            out[t, r : r + 1, :] = jnp.sum(grow(here * sums[t][r], scale, t + 1), axis=0, keepdims=True)
+            row = jnp.sum(grow(here * sums[t][r], scale, t + 1), axis=0, keepdims=True)
+            for n in every:
+                out[n, t, r : r + 1, :] = row
         for d in range(SUBSTEPS):
-            out[SUBSTEPS + d, r : r + 1, :] = jnp.sum(here * spread[d], axis=0, keepdims=True)
+            row = jnp.sum(here * spread[d], axis=0, keepdims=True)
+            for n in every:
+                out[n, SUBSTEPS + d, r : r + 1, :] = row
     per = pressure.shape[1] // LANES
     tile = pressure.shape[0] * per
     at = lax.axis_index("cls") * tile
     for i in range(tile):
-        out[2 * SUBSTEPS, pl.ds(at + i, 1), :] = pressure[
-            i // per : i // per + 1, (i % per) * LANES : (i % per + 1) * LANES
-        ]
-
-
-def power_kernel(melt_hbm, prop_hbm, coup_hbm, out_hbm, columns, melt, out, prop, coup, sems, out_sems, param_sems):
+        row = pressure[i // per : i // per + 1, (i % per) * LANES : (i % per + 1) * LANES]
+        for n in every:
+            out[n, 2 * SUBSTEPS, pl.ds(at + i, 1), :] = row
+
+
+def power_kernel(melt_hbm, prop_hbm, coup_hbm, out_hbm, melt, out, columns, prop, coup, sems, out_sems, param_sems):
     chunks = out.shape[0]
     classes, nodes = prop.shape[:2]
     params = param_copies([(prop_hbm, prop), (coup_hbm, coup)], param_sems)
@@ -143,7 +149,16 @@
         pltpu.make_async_copy(melt_hbm.at[:, pl.ds(r * LANES, LANES)], melt.at[r], sems.at[r])
         for r in range(chunks)
     ]
-    stores = [pltpu.make_async_copy(out.at[r], out_hbm.at[r], out_sems.at[r]) for r in range(chunks)]
+    width = classes * nodes
+    stores = [
+        pltpu.make_async_copy(out.at[r], out_hbm.at[pl.ds(r * width, width)], out_sems.at[r])
+        for r in range(chunks)
+    ]
+    stores.append(
+        pltpu.make_async_copy(
+            columns, out_hbm.at[pl.ds(chunks * width, columns.shape[0])], out_sems.at[chunks]
+        )
+    )
     for load in loads:
         load.start()
     for copy in params:
@@ -152,7 +167,8 @@
     unit = [prop[k] / scale[k : k + 1, :] for k in range(classes)]
     table = jnp.concatenate(unit, axis=0)
     column = coup[...]
-    columns[0] = column
+    columns[:, nodes:] = jnp.zeros((columns.shape[0], LANES - nodes), jnp.float32)
+    columns[:classes, :nodes] = column
     for d in range(1, SUBSTEPS):
         pairs = lax.dot_general(
             column, table, (((1,), (1,)), ((), ())), precision=HIGHEST, preferred_element_type=jnp.float32
@@ -160,7 +176,8 @@
         column = jnp.concatenate(
             [pairs[k : k + 1, k * nodes : (k + 1) * nodes] for k in range(classes)], axis=0
         )
-        columns[d] = grow(column, scale, d)
+        columns[d * classes : (d + 1) * classes, :nodes] = grow(column, scale, d)
+    stores[chunks].start()
     lefts = []
     for k in range(classes):
         high, low = split2(square(square(unit[k])))
@@ -182,8 +199,10 @@
         store.wait()
 
 
-def combine_kernel(mine, theirs, out):
-    total = mine[...] + theirs[...]
+def combine_kernel(parts, _, out):
+    total = parts[0]
+    for n in range(1, parts.shape[0]):
+        total = total + parts[n]
     wall = 0.5 * total[2 * SUBSTEPS]
     for n in range(out.shape[0]):
         for t in range(SUBSTEPS):
@@ -213,7 +232,9 @@
     return total - 6.0 * x
 
 
-def finish_kernel(window, shells_hbm, columns, out_hbm, pressure_out, shells, out, walls_all, last, sems, out_sems):
+def finish_kernel(
+    window, shells_hbm, out_hbm, pressure_out, shells, out, columns, walls_all, last, sems, out_sems, column_sem
+):
     nodes, classes, cells = out.shape
     chunks = cells // LANES
     parts = nodes // GROUP
@@ -223,14 +244,19 @@
 
     loads = [
         pltpu.make_async_copy(
-            shells_hbm.at[:, pl.ds(g * GROUP * classes, GROUP * classes)],
-            shells.at[:, pl.ds(g * GROUP * classes, GROUP * classes)],
-            sems.at[g],
+            shells_hbm.at[pl.ds((r * nodes + g * GROUP) * classes, GROUP * classes)],
+            shells.at[r, pl.ds(g * GROUP * classes, GROUP * classes)],
+            sems.at[g, r],
         )
         for g in range(parts)
+        for r in range(chunks)
     ]
     for load in loads:
         load.start()
+    column_load = pltpu.make_async_copy(
+        shells_hbm.at[pl.ds(chunks * nodes * classes, columns.shape[0])], columns, column_sem
+    )
+    column_load.start()
     plane = pressure_out.shape[1]
     blocks = window.shape[0]
     rows = blocks * chunks
@@ -268,9 +294,13 @@
     stores = [
         pltpu.make_async_copy(out.at[piece(g)], out_hbm.at[piece(g)], out_sems.at[g]) for g in range(parts)
     ]
-    cols = [columns[SUBSTEPS - 1 - s] for s in range(SUBSTEPS)]
+    column_load.wait()
+    cols = [
+        columns[(SUBSTEPS - 1 - s) * classes : (SUBSTEPS - s) * classes, :] for s in range(SUBSTEPS)
+    ]
     for g in range(parts):
-        loads[g].wait()
+        for load in loads[g * chunks : (g + 1) * chunks]:
+            load.wait()
         for i in range(g * GROUP, (g + 1) * GROUP):
             weights = [jnp.broadcast_to(cols[s][:, i : i + 1], (classes, LANES)) for s in range(SUBSTEPS)]
             for r in range(chunks):
@@ -288,9 +318,8 @@
 DMA = pltpu.SemaphoreType.DMA
 
 
-def partner(value, axis, distance):
-    count = lax.axis_size(axis)
-    return lax.ppermute(value, axis, [(i, i ^ distance) for i in range(count)])
+def exchange(copies, axis):
+    return lax.all_to_all(copies, axis, split_axis=0, concat_axis=0, tiled=True)
 
 
 def shards(melt, counts, pressure, propagator, coupling, flux_weights):
@@ -298,7 +327,8 @@
     chunks = cells // LANES
     f32 = jnp.float32
     split = (chunks, nodes * classes, LANES)
-    params = pltpu.CompilerParams(vmem_limit_bytes=32 * 2**20)
+    whole = pltpu.CompilerParams(vmem_limit_bytes=60 * 2**20)
+    most = pltpu.CompilerParams(vmem_limit_bytes=52 * 2**20)
     cls_count = lax.axis_size("cls")
     cell_count = lax.axis_size("cell")
     prop_v = pltpu.VMEM((classes, nodes, nodes), f32)
@@ -306,7 +336,7 @@
     parts = nodes // GROUP
     packed = pl.pallas_call(
         fields_kernel,
-        out_shape=jax.ShapeDtypeStruct((FIELDS, chunks, LANES), f32),
+        out_shape=jax.ShapeDtypeStruct((cls_count, FIELDS, chunks, LANES), f32),
         in_specs=[HBM] * 6,
         out_specs=VMEM,
         scratch_shapes=[
@@ -319,62 +349,57 @@
             DMA((parts,)),
             DMA((5,)),
         ],
-        compiler_params=params,
+        compiler_params=whole,
         name="fields",
     )(melt, counts, pressure, propagator, coupling, flux_weights)
-    shells, columns = pl.pallas_call(
+    columns_v = pltpu.VMEM((SUBSTEPS * classes, LANES), f32)
+    shells = pl.pallas_call(
         power_kernel,
-        out_shape=[
-            jax.ShapeDtypeStruct(split, f32),
-            jax.ShapeDtypeStruct((SUBSTEPS, classes, nodes), f32),
-        ],
+        out_shape=jax.ShapeDtypeStruct(((chunks * nodes + SUBSTEPS) * classes, LANES), f32),
         in_specs=[HBM] * 3,
-        out_specs=[HBM, VMEM],
+        out_specs=HBM,
         scratch_shapes=[
             pltpu.VMEM(split, f32),
             pltpu.VMEM(split, f32),
+            columns_v,
             prop_v,
             small,
             DMA((chunks,)),
-            DMA((chunks,)),
+            DMA((chunks + 1,)),
             DMA((2,)),
         ],
-        compiler_params=params,
+        compiler_params=whole,
         cost_estimate=pl.CostEstimate(flops=2 * 10**9, bytes_accessed=2 * melt.size * 4, transcendentals=0),
         name="power",
     )(melt.reshape(nodes * classes, cells), propagator, coupling)
-    distance = 1
-    theirs = partner(packed, "cls", distance)
-    while 2 * distance < cls_count:
-        distance *= 2
-        packed = packed + theirs
-        theirs = partner(packed, "cls", distance)
     copies = pl.pallas_call(
         combine_kernel,
         out_shape=jax.ShapeDtypeStruct((cell_count, FIELDS - 1, chunks, LANES), f32),
-        in_specs=[VMEM, VMEM],
+        in_specs=[VMEM, HBM],
         out_specs=VMEM,
-        compiler_params=params,
+        compiler_params=most,
         name="combine",
-    )(packed, theirs)
-    window = lax.all_to_all(copies, "cell", split_axis=0, concat_axis=0, tiled=True)
+    )(exchange(packed, "cls"), shells)
+    window = exchange(copies, "cell")
     rows = cell_count * chunks
     return pl.pallas_call(
         finish_kernel,
         out_shape=[jax.ShapeDtypeStruct(melt.shape, f32), jax.ShapeDtypeStruct(pressure.shape, f32)],
-        in_specs=[VMEM, HBM, VMEM],
+        in_specs=[VMEM, HBM],
         out_specs=[HBM, VMEM],
         scratch_shapes=[
             pltpu.VMEM(split, f32),
             pltpu.VMEM(melt.shape, f32),
+            columns_v,
             pltpu.VMEM((SUBSTEPS, rows, LANES), f32),
             pltpu.VMEM((rows, LANES), f32),
+            DMA((parts, chunks)),
             DMA((parts,)),
-            DMA((parts,)),
+            DMA(()),
         ],
-        compiler_params=params,
+        compiler_params=most,
         name="finish",
-    )(window, shells, columns)
+    )(window, shells)
 
 
 def solution(mesh):

time: 34.5 us -> 34 us (0.986)
  blocking collectives: 0 us -> 10.5 us
  local copies, waits for them, and re-layouts: 7.27 us -> 0 us
  Pallas kernels: 11.5 us -> 16.2 us
  waiting for transfers between devices: 4.41 us -> 0.01 us
  starting transfers between devices: 10.2 us -> 6.33 us
    all_to_all x0 -> x1, blocking collectives: none -> 10.5 us  [exchange(): return lax.all_to_all(copies, axis, split_axis=0, concat_axis=0, tiled=True)]
    unnamed x18 -> x0, local copies, waits for them, and re-layouts: 7.27 us -> none
    ppermute x2 -> x0, starting transfers between devices: 6.12 us -> none  [partner(): return lax.ppermute(value, axis, [(i, i ^ distance) for i in range(count)])]
    ppermute x2 -> x0, waiting for transfers between devices: 3.87 us -> none  [partner(): return lax.ppermute(value, axis, [(i, i ^ distance) for i in range(count)])]
    pallas_call x2, Pallas kernels: 7.5 us -> 11.1 us  [the longest x1 6.64 us: shards(): pl.pallas_call(power_kernel, out_shape=jax.ShapeDtypeStruct(((chunks * no...]
    all_to_all x1, starting transfers between devices: 4.06 us -> 6.33 us  [exchange(): return lax.all_to_all(copies, axis, split_axis=0, concat_axis=0, tiled=True)]
    pallas_call x1, Pallas kernels: 3.25 us -> 5.01 us  [shards(): pl.pallas_call(finish_kernel, out_shape=[jax.ShapeDtypeStruct(melt.shape,...]
    pallas_call x1, Pallas kernels: 0.73 us -> 0.02 us  [shards(): pl.pallas_call(combine_kernel, out_shape=jax.ShapeDtypeStruct((cell_count...]
  transfers between devices with their start and end apart: 3 -> 1, of which waited for: 3 -> 0; matrix products, arithmetic and copies ran while one was open for 0% -> 0% of each run, Pallas kernels for 14% -> 20%
where the time goes in v4:
time: 34 us; the launch traced here: 33.6 us
  Pallas kernels  16.2 us (48%)
  blocking collectives  10.5 us (31%)
  starting transfers between devices  6.33 us (19%)
  between operations  0.66 us (2%)
    all_to_all x1, blocking collectives, exchange(): return lax.all_to_all(copies, axis, split_axis=0, concat_axis=0, tiled=True)  10.5 us
    pallas_call x1, Pallas kernels, shards(): pl.pallas_call(power_kernel, out_shape=jax.ShapeDtypeStruct(((chunks * no...  6.64 us
    all_to_all x1, starting transfers between devices, exchange(): return lax.all_to_all(copies, axis, split_axis=0, concat_axis=0, tiled=True)  6.33 us
    pallas_call x1, Pallas kernels, shards(): pl.pallas_call(finish_kernel, out_shape=[jax.ShapeDtypeStruct(melt.shape,...  5.01 us
    pallas_call x1, Pallas kernels, shards(): pl.pallas_call(fields_kernel, out_shape=jax.ShapeDtypeStruct((cls_count,...  4.48 us
  transfers between devices with their start and end apart: 1, of which 0 were waited for; matrix products, arithmetic and copies ran while one was open for 0% of the time, Pallas kernels for 20%

profile of v4, /device:TPU:0, one launch (start us, length us, event | category | flops | bytes accessed | tf_op | source)
XLA Modules:
  0.0 33.6 jit_solution(8671383649826574711)
XLA Ops:
  0.6 4.5 %fields.1 = f32[4,9,8,128]{3,2,1,0:T(8,128)} custom-call(f32[64,8,1024]{2,1,0:T(8,128)} %melt_hbm.1, s32[8,1024]{1,0:T(8,128)} %counts_hbm.1, f32[1,256]{1,0:T(1,128)} %pressure_hbm.1, f32[32,64,64]{2,1,0:T(8,128)} %prop_hbm.3, f32[32,64]{1,0:T(8,128)} %coup_hbm.3, f32[32,64]{1,0:T(8,128)} %flux_hbm.1), custom_call_target="tpu_custom_call" | custom-call | tf_op jit(solution)/shard_map/fields/pallas_call | solution.py:337
  5.1 6.3 %all-to-all-start = ((f32[4,9,8,128]{3,2,1,0:T(8,128)}), f32[4,9,8,128]{3,2,1,0:T(8,128)S(1)}, u32[]{:S(2)}, u32[]{:S(2)}) async-start(f32[4,9,8,128]{3,2,1,0:T(8,128)} %fields.1), calls=%async_computation | async-start | bytes 294912 | tf_op jit(solution)/shard_map/all_to_all | solution.py:322
  11.5 6.6 %power.1._.shells_hbm = f32[4128,128]{1,0:T(8,128)} custom-call(f32[512,1024]{1,0:T(8,128)} %bitcast.1, f32[32,64,64]{2,1,0:T(8,128)} %prop_hbm.3, f32[32,64]{1,0:T(8,128)} %coup_hbm.3), custom_call_target="tpu_custom_call" | custom-call | flops 2000000000 | bytes 4194304 | tf_op jit(solution)/shard_map/power/pallas_call | solution.py:356
  18.1 0.0 all-to-all-done.parts
  18.1 10.5 %all_to_all.10.window = f32[8,8,8,128]{3,2,1,0:T(8,128)S(1)} all-to-all(f32[8,8,8,128]{3,2,1,0:T(8,128)S(1)} %combine.1), channel_id=1, replica_groups=mesh['cell'=8,'cls'=4] {'cell'}, dimensions={0} | all-to-all | bytes 524288 | tf_op jit(solution)/shard_map/all_to_all | solution.py:322
  28.6 5.0 %finish.1 = (f32[64,8,1024]{2,1,0:T(8,128)}, f32[1,256]{1,0:T(1,128)}) custom-call(f32[8,8,8,128]{3,2,1,0:T(8,128)S(1)} %all_to_all.10.window, f32[4128,128]{1,0:T(8,128)} %power.1._.shells_hbm), custom_call_target="tpu_custom_call" | custom-call | tf_op jit(solution)/shard_map/finish/pallas_call | solution.py:385
  (1 shorter events, 0.0 us)
Async XLA Ops:
  5.1 13.0 %all-to-all-start = ((f32[4,9,8,128]{3,2,1,0:T(8,128)}), f32[4,9,8,128]{3,2,1,0:T(8,128)S(1)}, u32[]{:S(2)}, u32[]{:S(2)}) async-start(f32[4,9,8,128]{3,2,1,0:T(8,128)} %fields.1), calls=%async_computation | async-start | bytes 294912 | tf_op jit(solution)/shard_map/all_to_all | solution.py:322

commit v5 on v4

--- a/solution.py
+++ b/solution.py
@@ -139,49 +139,10 @@
             out[n, 2 * SUBSTEPS, pl.ds(at + i, 1), :] = row
 
 
-def power_kernel(melt_hbm, prop_hbm, coup_hbm, out_hbm, melt, out, columns, prop, coup, sems, out_sems, param_sems):
+def apply_power(lefts, scale, melt, out, loads, stores):
     chunks = out.shape[0]
-    classes, nodes = prop.shape[:2]
-    params = param_copies([(prop_hbm, prop), (coup_hbm, coup)], param_sems)
-    for copy in params:
-        copy.start()
-    loads = [
-        pltpu.make_async_copy(melt_hbm.at[:, pl.ds(r * LANES, LANES)], melt.at[r], sems.at[r])
-        for r in range(chunks)
-    ]
-    width = classes * nodes
-    stores = [
-        pltpu.make_async_copy(out.at[r], out_hbm.at[pl.ds(r * width, width)], out_sems.at[r])
-        for r in range(chunks)
-    ]
-    stores.append(
-        pltpu.make_async_copy(
-            columns, out_hbm.at[pl.ds(chunks * width, columns.shape[0])], out_sems.at[chunks]
-        )
-    )
-    for load in loads:
-        load.start()
-    for copy in params:
-        copy.wait()
-    scale = class_scale(prop)
-    unit = [prop[k] / scale[k : k + 1, :] for k in range(classes)]
-    table = jnp.concatenate(unit, axis=0)
-    column = coup[...]
-    columns[:, nodes:] = jnp.zeros((columns.shape[0], LANES - nodes), jnp.float32)
-    columns[:classes, :nodes] = column
-    for d in range(1, SUBSTEPS):
-        pairs = lax.dot_general(
-            column, table, (((1,), (1,)), ((), ())), precision=HIGHEST, preferred_element_type=jnp.float32
-        )
-        column = jnp.concatenate(
-            [pairs[k : k + 1, k * nodes : (k + 1) * nodes] for k in range(classes)], axis=0
-        )
-        columns[d * classes : (d + 1) * classes, :nodes] = grow(column, scale, d)
-    stores[chunks].start()
-    lefts = []
-    for k in range(classes):
-        high, low = split2(square(square(unit[k])))
-        lefts.append(jnp.concatenate([high, high, low], axis=1))
+    classes = scale.shape[0]
+    nodes = out.shape[1] // classes
     together = 2 if chunks % 2 == 0 else 1
     for r in range(0, chunks, together):
         for n in range(together):
@@ -190,13 +151,87 @@
             own = pl.ds(k, nodes, stride=classes)
             high, low = split2(jnp.concatenate([melt[r + n, own, :] for n in range(together)], axis=1))
             part = dot(lefts[k], jnp.concatenate([high, low, high], axis=0))
-            part = grow(part, scale[k : k + 1, :], SUBSTEPS)
+            part = grow(part, scale[k : k + 1, :1], SUBSTEPS)
             for n in range(together):
                 out[r + n, own, :] = part[:, n * LANES : (n + 1) * LANES]
         for n in range(together):
             stores[r + n].start()
     for store in stores:
         store.wait()
+
+
+def chunk_copies(first, melt_hbm, shells_hbm, melt, out, sems, out_sems):
+    chunks, width = out.shape[:2]
+    loads = [
+        pltpu.make_async_copy(
+            melt_hbm.at[:, pl.ds((first + r) * LANES, LANES)], melt.at[r], sems.at[r]
+        )
+        for r in range(chunks)
+    ]
+    stores = [
+        pltpu.make_async_copy(
+            out.at[r], shells_hbm.at[first + r, pl.ds(0, width)], out_sems.at[r]
+        )
+        for r in range(chunks)
+    ]
+    return loads, stores
+
+
+def power_kernel(
+    melt_hbm, prop_hbm, coup_hbm, shells_hbm, lefts_hbm, melt, out, extra, lefts, prop, coup, sems, out_sems, other_sems
+):
+    classes, nodes = prop.shape[:2]
+    params = param_copies([(prop_hbm, prop), (coup_hbm, coup)], other_sems)
+    for copy in params:
+        copy.start()
+    loads, stores = chunk_copies(0, melt_hbm, shells_hbm, melt, out, sems, out_sems)
+    for load in loads:
+        load.start()
+    extra_store = pltpu.make_async_copy(
+        extra, shells_hbm.at[0, pl.ds(classes * nodes, extra.shape[0])], other_sems.at[2]
+    )
+    lefts_store = pltpu.make_async_copy(lefts, lefts_hbm, other_sems.at[3])
+    for copy in params:
+        copy.wait()
+    scale = class_scale(prop)
+    unit = [prop[k] / scale[k : k + 1, :] for k in range(classes)]
+    for k in range(classes):
+        high, low = split2(square(square(unit[k])))
+        lefts[k] = jnp.concatenate([high, high, low], axis=1)
+    lefts_store.start()
+    table = jnp.concatenate(unit, axis=0)
+    column = coup[...]
+    extra[:, nodes:] = jnp.zeros((extra.shape[0], LANES - nodes), jnp.float32)
+    extra[:classes, :nodes] = column
+    for d in range(1, SUBSTEPS):
+        pairs = lax.dot_general(
+            column, table, (((1,), (1,)), ((), ())), precision=HIGHEST, preferred_element_type=jnp.float32
+        )
+        column = jnp.concatenate(
+            [pairs[k : k + 1, k * nodes : (k + 1) * nodes] for k in range(classes)], axis=0
+        )
+        extra[d * classes : (d + 1) * classes, :nodes] = grow(column, scale, d)
+    extra[SUBSTEPS * classes :, :] = jnp.broadcast_to(scale, (classes, LANES))
+    extra_store.start()
+    apply_power(lefts, scale, melt, out, loads, stores)
+    extra_store.wait()
+    lefts_store.wait()
+
+
+def rest_kernel(first, melt_hbm, lefts_hbm, shells_in, _, shells_hbm, melt, out, scale, lefts, sems, out_sems, other_sems):
+    classes, nodes = lefts.shape[:2]
+    params = [
+        pltpu.make_async_copy(lefts_hbm, lefts, other_sems.at[0]),
+        pltpu.make_async_copy(
+            shells_in.at[0, pl.ds((nodes + SUBSTEPS) * classes, classes)], scale, other_sems.at[1]
+        ),
+    ]
+    loads, stores = chunk_copies(first, melt_hbm, shells_hbm, melt, out, sems, out_sems)
+    for copy in params + loads:
+        copy.start()
+    for copy in params:
+        copy.wait()
+    apply_power(lefts, scale, melt, out, loads, stores)
 
 
 def combine_kernel(parts, _, out):
@@ -242,21 +277,21 @@
     def piece(g):
         return pl.ds(g * GROUP, GROUP)
 
+    width = GROUP * classes
     loads = [
         pltpu.make_async_copy(
-            shells_hbm.at[pl.ds((r * nodes + g * GROUP) * classes, GROUP * classes)],
-            shells.at[r, pl.ds(g * GROUP * classes, GROUP * classes)],
-            sems.at[g, r],
-        )
-        for g in range(parts)
-        for r in range(chunks)
-    ]
+            shells_hbm.at[:, pl.ds(g * 2 * width, 2 * width)],
+            shells.at[:, pl.ds(g * 2 * width, 2 * width)],
+            sems.at[g],
+        )
+        for g in range(parts // 2)
+    ]
+    column_load = pltpu.make_async_copy(
+        shells_hbm.at[0, pl.ds(nodes * classes, columns.shape[0])], columns, column_sem
+    )
+    column_load.start()
     for load in loads:
         load.start()
-    column_load = pltpu.make_async_copy(
-        shells_hbm.at[pl.ds(chunks * nodes * classes, columns.shape[0])], columns, column_sem
-    )
-    column_load.start()
     plane = pressure_out.shape[1]
     blocks = window.shape[0]
     rows = blocks * chunks
@@ -299,8 +334,8 @@
         columns[(SUBSTEPS - 1 - s) * classes : (SUBSTEPS - s) * classes, :] for s in range(SUBSTEPS)
     ]
     for g in range(parts):
-        for load in loads[g * chunks : (g + 1) * chunks]:
-            load.wait()
+        if g % 2 == 0:
+            loads[g // 2].wait()
         for i in range(g * GROUP, (g + 1) * GROUP):
             weights = [jnp.broadcast_to(cols[s][:, i : i + 1], (classes, LANES)) for s in range(SUBSTEPS)]
             for r in range(chunks):
@@ -352,26 +387,32 @@
         compiler_params=whole,
         name="fields",
     )(melt, counts, pressure, propagator, coupling, flux_weights)
-    columns_v = pltpu.VMEM((SUBSTEPS * classes, LANES), f32)
-    shells = pl.pallas_call(
+    height = (nodes + SUBSTEPS + 1) * classes
+    half = (chunks + 1) // 2
+    melt_flat = melt.reshape(nodes * classes, cells)
+    shells_shape = jax.ShapeDtypeStruct((chunks, height, LANES), f32)
+    lefts_shape = (classes, nodes, 3 * nodes)
+    cost = pl.CostEstimate(flops=10**9, bytes_accessed=melt.size * 4, transcendentals=0)
+    shells, lefts = pl.pallas_call(
         power_kernel,
-        out_shape=jax.ShapeDtypeStruct(((chunks * nodes + SUBSTEPS) * classes, LANES), f32),
+        out_shape=[shells_shape, jax.ShapeDtypeStruct(lefts_shape, jnp.bfloat16)],
         in_specs=[HBM] * 3,
-        out_specs=HBM,
+        out_specs=[HBM] * 2,
         scratch_shapes=[
-            pltpu.VMEM(split, f32),
-            pltpu.VMEM(split, f32),
-            columns_v,
+            pltpu.VMEM((half,) + split[1:], f32),
+            pltpu.VMEM((half,) + split[1:], f32),
+            pltpu.VMEM(((SUBSTEPS + 1) * classes, LANES), f32),
+            pltpu.VMEM(lefts_shape, jnp.bfloat16),
             prop_v,
             small,
-            DMA((chunks,)),
-            DMA((chunks + 1,)),
-            DMA((2,)),
+            DMA((half,)),
+            DMA((half,)),
+            DMA((4,)),
         ],
         compiler_params=whole,
-        cost_estimate=pl.CostEstimate(flops=2 * 10**9, bytes_accessed=2 * melt.size * 4, transcendentals=0),
+        cost_estimate=cost,
         name="power",
-    )(melt.reshape(nodes * classes, cells), propagator, coupling)
+    )(melt_flat, propagator, coupling)
     copies = pl.pallas_call(
         combine_kernel,
         out_shape=jax.ShapeDtypeStruct((cell_count, FIELDS - 1, chunks, LANES), f32),
@@ -380,6 +421,26 @@
         compiler_params=most,
         name="combine",
     )(exchange(packed, "cls"), shells)
+    left = chunks - half
+    shells = pl.pallas_call(
+        functools.partial(rest_kernel, half),
+        out_shape=shells_shape,
+        in_specs=[HBM] * 4,
+        out_specs=HBM,
+        scratch_shapes=[
+            pltpu.VMEM((left,) + split[1:], f32),
+            pltpu.VMEM((left,) + split[1:], f32),
+            pltpu.VMEM((classes, LANES), f32),
+            pltpu.VMEM(lefts_shape, jnp.bfloat16),
+            DMA((left,)),
+            DMA((left,)),
+            DMA((2,)),
+        ],
+        input_output_aliases={2: 0},
+        compiler_params=whole,
+        cost_estimate=cost,
+        name="rest",
+    )(melt_flat, lefts, shells, copies)
     window = exchange(copies, "cell")
     rows = cell_count * chunks
     return pl.pallas_call(
@@ -390,10 +451,10 @@
         scratch_shapes=[
             pltpu.VMEM(split, f32),
             pltpu.VMEM(melt.shape, f32),
-            columns_v,
+            pltpu.VMEM((SUBSTEPS * classes, LANES), f32),
             pltpu.VMEM((SUBSTEPS, rows, LANES), f32),
             pltpu.VMEM((rows, LANES), f32),
-            DMA((parts, chunks)),
+            DMA((parts // 2,)),
             DMA((parts,)),
             DMA(()),
         ],

time: 34 us -> 33.4 us (0.982)
  blocking collectives: 10.5 us -> 0 us
  waiting for transfers between devices: 0.01 us -> 4.9 us
  starting transfers between devices: 6.33 us -> 10.1 us
  Pallas kernels: 16.2 us -> 17.3 us
    all_to_all x1 -> x0, blocking collectives: 10.5 us -> none  [exchange(): return lax.all_to_all(copies, axis, split_axis=0, concat_axis=0, tiled=True)]
    all_to_all x1 -> x2, waiting for transfers between devices: 0.01 us -> 4.9 us  [exchange(): return lax.all_to_all(copies, axis, split_axis=0, concat_axis=0, tiled=True)]
    all_to_all x1 -> x2, starting transfers between devices: 6.33 us -> 10.1 us  [exchange(): return lax.all_to_all(copies, axis, split_axis=0, concat_axis=0, tiled=True)]
    pallas_call x1 -> x2, Pallas kernels: 6.64 us -> 8.27 us  [the longest x1 5.69 us: shards(): pl.pallas_call(power_kernel, out_shape=[shells_shape, jax.ShapeDtypeStruc...]
    pallas_call x1, Pallas kernels: 5.01 us -> 3.87 us  [shards(): pl.pallas_call(finish_kernel, out_shape=[jax.ShapeDtypeStruct(melt.shape,...]
    pallas_call x1, Pallas kernels: 0.02 us -> 0.73 us  [shards(): pl.pallas_call(combine_kernel, out_shape=jax.ShapeDtypeStruct((cell_count...]
  transfers between devices with their start and end apart: 1 -> 2, of which waited for: 0 -> 2; matrix products, arithmetic and copies ran while one was open for 0% -> 0% of each run, Pallas kernels for 20% -> 25%
where the time goes in v5:
time: 33.4 us; the launch traced here: 33 us
  Pallas kernels  17.3 us (52%)
  starting transfers between devices  10.1 us (30%)
  waiting for transfers between devices  4.9 us (15%)
  between operations  0.66 us (2%)
    all_to_all x2, starting transfers between devices, exchange(): return lax.all_to_all(copies, axis, split_axis=0, concat_axis=0, tiled=True)  10.1 us
    pallas_call x1, Pallas kernels, shards(): pl.pallas_call(power_kernel, out_shape=[shells_shape, jax.ShapeDtypeStruc...  5.69 us
    all_to_all x2, waiting for transfers between devices, exchange(): return lax.all_to_all(copies, axis, split_axis=0, concat_axis=0, tiled=True)  4.9 us
    pallas_call x1, Pallas kernels, shards(): pl.pallas_call(fields_kernel, out_shape=jax.ShapeDtypeStruct((cls_count,...  4.47 us
    pallas_call x1, Pallas kernels, shards(): pl.pallas_call(finish_kernel, out_shape=[jax.ShapeDtypeStruct(melt.shape,...  3.87 us
    pallas_call x1, Pallas kernels, shards(): pl.pallas_call(functools.partial(rest_kernel, half), out_shape=shells_sha...  2.58 us
    pallas_call x1, Pallas kernels, shards(): pl.pallas_call(combine_kernel, out_shape=jax.ShapeDtypeStruct((cell_count...  0.73 us
  transfers between devices with their start and end apart: 2, of which 2 were waited for; matrix products, arithmetic and copies ran while one was open for 0% of the time, Pallas kernels for 25%

profile of v5, /device:TPU:0, one launch (start us, length us, event | category | flops | bytes accessed | tf_op | source)
XLA Modules:
  0.0 33.0 jit_solution(18306805041654833698)
XLA Ops:
  0.6 4.5 %fields.1 = f32[4,9,8,128]{3,2,1,0:T(8,128)} custom-call(f32[64,8,1024]{2,1,0:T(8,128)} %melt_hbm.1, s32[8,1024]{1,0:T(8,128)} %counts_hbm.1, f32[1,256]{1,0:T(1,128)} %pressure_hbm.1, f32[32,64,64]{2,1,0:T(8,128)} %prop_hbm.3, f32[32,64]{1,0:T(8,128)} %coup_hbm.3, f32[32,64]{1,0:T(8,128)} %flux_hbm.1), custom_call_target="tpu_custom_call" | custom-call | tf_op jit(solution)/shard_map/fields/pallas_call | solution.py:372
  5.1 6.3 %all-to-all-start = ((f32[4,9,8,128]{3,2,1,0:T(8,128)}), f32[4,9,8,128]{3,2,1,0:T(8,128)S(1)}, u32[]{:S(2)}, u32[]{:S(2)}) async-start(f32[4,9,8,128]{3,2,1,0:T(8,128)} %fields.1), calls=%async_computation | async-start | bytes 294912 | tf_op jit(solution)/shard_map/all_to_all | solution.py:357
  11.4 5.7 %power.1 = (f32[8,552,128]{2,1,0:T(8,128)}, bf16[8,64,192]{2,1,0:T(8,128)(2,1)}) custom-call(f32[512,1024]{1,0:T(8,128)} %bitcast.1, f32[32,64,64]{2,1,0:T(8,128)} %prop_hbm.3, f32[32,64]{1,0:T(8,128)} %coup_hbm.3), custom_call_target="tpu_custom_call" | custom-call | flops 1000000000 | bytes 2097152 | tf_op jit(solution)/shard_map/power/pallas_call | solution.py:396
  17.1 0.5 %all-to-all-done.parts = f32[4,9,8,128]{3,2,1,0:T(8,128)S(1)} async-done(((f32[4,9,8,128]{3,2,1,0:T(8,128)}), f32[4,9,8,128]{3,2,1,0:T(8,128)S(1)}, u32[]{:S(2)}, u32[]{:S(2)}) %all-to-all-start) | async-done | bytes 147488 | tf_op jit(solution)/shard_map/all_to_all | solution.py:357
  17.7 0.7 %combine.1._ = f32[8,8,8,128]{3,2,1,0:T(8,128)} custom-call(f32[4,9,8,128]{3,2,1,0:T(8,128)S(1)} %all-to-all-done.parts, f32[8,552,128]{2,1,0:T(8,128)} %get-tuple-element.4._.shells_in), custom_call_target="tpu_custom_call" | custom-call | tf_op jit(solution)/shard_map/combine/pallas_call | solution.py:416
  18.4 3.7 %all-to-all-start.1 = ((f32[8,8,8,128]{3,2,1,0:T(8,128)}), f32[8,8,8,128]{3,2,1,0:T(8,128)S(1)}, u32[]{:S(2)}, u32[]{:S(2)}) async-start(f32[8,8,8,128]{3,2,1,0:T(8,128)} %combine.1._), calls=%async_computation.1 | async-start | bytes 524288 | tf_op jit(solution)/shard_map/all_to_all | solution.py:357
  22.1 2.6 %rest.1.shells_hbm = f32[8,552,128]{2,1,0:T(8,128)} custom-call(f32[512,1024]{1,0:T(8,128)} %bitcast.2, bf16[8,64,192]{2,1,0:T(8,128)(2,1)} %get-tuple-element.5.lefts_hbm, f32[8,552,128]{2,1,0:T(8,128)} %get-tuple-element.4._.shells_in, f32[8,8,8,128]{3,2,1,0:T(8,128)} %combine.1._), custom_call_target="tpu_custom_call", output_to_operand_aliasing={{}: (2, {})} | custom-call | flops 1000000000 | bytes 2097152 | tf_op jit(solution)/shard_map/rest/pallas_call | solution.py:425
  24.7 4.4 %all-to-all-done.1.window = f32[8,8,8,128]{3,2,1,0:T(8,128)S(1)} async-done(((f32[8,8,8,128]{3,2,1,0:T(8,128)}), f32[8,8,8,128]{3,2,1,0:T(8,128)S(1)}, u32[]{:S(2)}, u32[]{:S(2)}) %all-to-all-start.1) | async-done | bytes 262176 | tf_op jit(solution)/shard_map/all_to_all | solution.py:357
  29.1 3.9 %finish.1 = (f32[64,8,1024]{2,1,0:T(8,128)}, f32[1,256]{1,0:T(1,128)}) custom-call(f32[8,8,8,128]{3,2,1,0:T(8,128)S(1)} %all-to-all-done.1.window, f32[8,552,128]{2,1,0:T(8,128)} %rest.1.shells_hbm), custom_call_target="tpu_custom_call" | custom-call | tf_op jit(solution)/shard_map/finish/pallas_call | solution.py:446
Async XLA Ops:
  5.1 12.6 %all-to-all-start = ((f32[4,9,8,128]{3,2,1,0:T(8,128)}), f32[4,9,8,128]{3,2,1,0:T(8,128)S(1)}, u32[]{:S(2)}, u32[]{:S(2)}) async-start(f32[4,9,8,128]{3,2,1,0:T(8,128)} %fields.1), calls=%async_computation | async-start | bytes 294912 | tf_op jit(solution)/shard_map/all_to_all | solution.py:357
  18.4 10.7 %all-to-all-start.1 = ((f32[8,8,8,128]{3,2,1,0:T(8,128)}), f32[8,8,8,128]{3,2,1,0:T(8,128)S(1)}, u32[]{:S(2)}, u32[]{:S(2)}) async-start(f32[8,8,8,128]{3,2,1,0:T(8,128)} %combine.1._), calls=%async_computation.1 | async-start | bytes 524288 | tf_op jit(solution)/shard_map/all_to_all | solution.py:357

commit v6 on v4

--- a/solution.py
+++ b/solution.py
@@ -28,14 +28,6 @@
     return lax.broadcasted_iota(jnp.int32, shape, dim)
 
 
-def split3(x):
-    high = x.astype(jnp.bfloat16)
-    rest = x - high.astype(jnp.float32)
-    middle = rest.astype(jnp.bfloat16)
-    low = (rest - middle.astype(jnp.float32)).astype(jnp.bfloat16)
-    return high, middle, low
-
-
 def split2(x):
     high = x.astype(jnp.bfloat16)
     return high, (x - high.astype(jnp.float32)).astype(jnp.bfloat16)
@@ -45,11 +37,14 @@
     return jnp.dot(a, b, preferred_element_type=jnp.float32)
 
 
-def square(a):
-    high, middle, low = split3(a)
-    left = jnp.concatenate([high, high, middle, high, low, middle], axis=1)
-    right = jnp.concatenate([high, middle, high, low, high, middle], axis=0)
-    return dot(left, right)
+def left_of(x):
+    high, low = split2(x)
+    return jnp.concatenate([high, high, low], axis=1)
+
+
+def right_of(x):
+    high, low = split2(x)
+    return jnp.concatenate([high, low, high], axis=0)
 
 
 def class_scale(prop):
@@ -91,14 +86,15 @@
         copy.wait()
     scale = class_scale(prop)
     width = classes * nodes
-    table = jnp.concatenate(split3(prop[...].reshape(width, nodes)), axis=1)
+    table = jnp.concatenate(split2(prop[...].reshape(width, nodes)), axis=1)
+    inverse = 1.0 / scale
     mask = iota((classes, width), 1) // nodes == iota((classes, width), 0)
     rows = [flux[...]]
     for _ in range(SUBSTEPS):
         wide = jnp.where(mask, jnp.concatenate([rows[-1]] * classes, axis=1), 0.0)
-        pairs = dot(jnp.concatenate(split3(wide), axis=0), table)
-        row = pairs[:classes] + pairs[classes : 2 * classes] + pairs[2 * classes :]
-        rows.append((row[:, :nodes] + row[:, nodes : 2 * nodes] + row[:, 2 * nodes :]) / scale)
+        pairs = dot(jnp.concatenate(split2(wide), axis=0), table)
+        row = pairs[:classes] + pairs[classes:]
+        rows.append((row[:, :nodes] + row[:, nodes:]) * inverse)
     spread = [
         grow(jnp.sum(rows[d] * coup[...], axis=1, keepdims=True), scale, d) for d in range(SUBSTEPS)
     ]
@@ -139,8 +135,8 @@
             out[n, 2 * SUBSTEPS, pl.ds(at + i, 1), :] = row
 
 
-def power_kernel(melt_hbm, prop_hbm, coup_hbm, out_hbm, melt, out, columns, prop, coup, sems, out_sems, param_sems):
-    chunks = out.shape[0]
+def power_kernel(melt_hbm, prop_hbm, coup_hbm, out_hbm, melt, out, prop, coup, sems, out_sems, param_sems):
+    chunks = melt.shape[0]
     classes, nodes = prop.shape[:2]
     params = param_copies([(prop_hbm, prop), (coup_hbm, coup)], param_sems)
     for copy in params:
@@ -149,48 +145,53 @@
         pltpu.make_async_copy(melt_hbm.at[:, pl.ds(r * LANES, LANES)], melt.at[r], sems.at[r])
         for r in range(chunks)
     ]
-    width = classes * nodes
     stores = [
-        pltpu.make_async_copy(out.at[r], out_hbm.at[pl.ds(r * width, width)], out_sems.at[r])
-        for r in range(chunks)
-    ]
-    stores.append(
-        pltpu.make_async_copy(
-            columns, out_hbm.at[pl.ds(chunks * width, columns.shape[0])], out_sems.at[chunks]
-        )
-    )
+        pltpu.make_async_copy(out.at[r], out_hbm.at[r], out_sems.at[r]) for r in range(chunks + 1)
+    ]
     for load in loads:
         load.start()
     for copy in params:
         copy.wait()
     scale = class_scale(prop)
-    unit = [prop[k] / scale[k : k + 1, :] for k in range(classes)]
-    table = jnp.concatenate(unit, axis=0)
-    column = coup[...]
-    columns[:, nodes:] = jnp.zeros((columns.shape[0], LANES - nodes), jnp.float32)
-    columns[:classes, :nodes] = column
-    for d in range(1, SUBSTEPS):
-        pairs = lax.dot_general(
-            column, table, (((1,), (1,)), ((), ())), precision=HIGHEST, preferred_element_type=jnp.float32
-        )
-        column = jnp.concatenate(
-            [pairs[k : k + 1, k * nodes : (k + 1) * nodes] for k in range(classes)], axis=0
-        )
-        columns[d * classes : (d + 1) * classes, :nodes] = grow(column, scale, d)
+    inverse = 1.0 / scale
+    every = range(classes)
+    factors = [scale[k : k + 1, :] for k in every]
+    unit = [prop[k] * inverse[k : k + 1, :] for k in every]
+    first = [left_of(unit[k]) for k in every]
+    square = [dot(first[k], right_of(unit[k])) for k in every]
+    second = [left_of(square[k]) for k in every]
+    lefts = [left_of(dot(second[k], right_of(square[k]))) for k in every]
+    start = jnp.concatenate(
+        [jnp.transpose(coup[...]), jnp.zeros((nodes, LANES - classes), jnp.float32)], axis=1
+    )
+    once = [dot(first[k], right_of(start)) for k in every]
+    start = start[:, :classes]
+    twice = [
+        dot(second[k], right_of(jnp.concatenate([start, once[k][:, :classes]], axis=1))) for k in every
+    ]
+    lane = iota((nodes, LANES), 1)
+    for k in every:
+        powers = [
+            start[:, k : k + 1],
+            once[k][:, k : k + 1],
+            twice[k][:, k : k + 1],
+            twice[k][:, classes + k : classes + k + 1],
+        ]
+        value = jnp.zeros((nodes, LANES), jnp.float32)
+        for d in range(SUBSTEPS):
+            value = jnp.where(lane % SUBSTEPS == SUBSTEPS - 1 - d, grow(powers[d], factors[k], d), value)
+        high = value.astype(jnp.bfloat16).astype(jnp.float32)
+        value = jnp.where(lane < 2 * SUBSTEPS, high, jnp.where(lane < 3 * SUBSTEPS, value - high, 0.0))
+        out[chunks, pl.ds(k, nodes, stride=classes), :] = value
     stores[chunks].start()
-    lefts = []
-    for k in range(classes):
-        high, low = split2(square(square(unit[k])))
-        lefts.append(jnp.concatenate([high, high, low], axis=1))
     together = 2 if chunks % 2 == 0 else 1
     for r in range(0, chunks, together):
         for n in range(together):
             loads[r + n].wait()
-        for k in range(classes):
+        for k in every:
             own = pl.ds(k, nodes, stride=classes)
-            high, low = split2(jnp.concatenate([melt[r + n, own, :] for n in range(together)], axis=1))
-            part = dot(lefts[k], jnp.concatenate([high, low, high], axis=0))
-            part = grow(part, scale[k : k + 1, :], SUBSTEPS)
+            x = jnp.concatenate([melt[r + n, own, :] for n in range(together)], axis=1)
+            part = grow(dot(lefts[k], right_of(x)), factors[k], SUBSTEPS)
             for n in range(together):
                 out[r + n, own, :] = part[:, n * LANES : (n + 1) * LANES]
         for n in range(together):
@@ -238,25 +239,23 @@
     nodes, classes, cells = out.shape
     chunks = cells // LANES
     parts = nodes // GROUP
+    width = GROUP * classes
 
     def piece(g):
         return pl.ds(g * GROUP, GROUP)
 
+    column_load = pltpu.make_async_copy(shells_hbm.at[chunks], columns, column_sem)
+    column_load.start()
     loads = [
         pltpu.make_async_copy(
-            shells_hbm.at[pl.ds((r * nodes + g * GROUP) * classes, GROUP * classes)],
-            shells.at[r, pl.ds(g * GROUP * classes, GROUP * classes)],
-            sems.at[g, r],
+            shells_hbm.at[pl.ds(0, chunks), pl.ds(g * 2 * width, 2 * width)],
+            shells.at[:, pl.ds(g * 2 * width, 2 * width)],
+            sems.at[g],
         )
-        for g in range(parts)
-        for r in range(chunks)
+        for g in range(parts // 2)
     ]
     for load in loads:
         load.start()
-    column_load = pltpu.make_async_copy(
-        shells_hbm.at[pl.ds(chunks * nodes * classes, columns.shape[0])], columns, column_sem
-    )
-    column_load.start()
     plane = pressure_out.shape[1]
     blocks = window.shape[0]
     rows = blocks * chunks
@@ -284,30 +283,25 @@
         pressure_out[i // per : i // per + 1, (i % per) * LANES : (i % per + 1) * LANES] = last[
             pl.ds(at + i, 1), :
         ]
-    walls_here = [
-        [
-            jnp.broadcast_to(walls_all[s, pl.ds(first + r, 1), :], (classes, LANES))
-            for r in range(chunks)
-        ]
-        for s in range(SUBSTEPS)
-    ]
+    right = []
+    for r in range(chunks):
+        wall = jnp.concatenate([walls_all[s, pl.ds(first + r, 1), :] for s in range(SUBSTEPS)], axis=0)
+        high = wall.astype(jnp.bfloat16).astype(jnp.float32)
+        right.append(jnp.concatenate([high, wall - high, high, jnp.zeros_like(high)], axis=0))
+    right = jnp.concatenate(right, axis=1).astype(jnp.bfloat16)
     stores = [
         pltpu.make_async_copy(out.at[piece(g)], out_hbm.at[piece(g)], out_sems.at[g]) for g in range(parts)
     ]
     column_load.wait()
-    cols = [
-        columns[(SUBSTEPS - 1 - s) * classes : (SUBSTEPS - s) * classes, :] for s in range(SUBSTEPS)
-    ]
     for g in range(parts):
-        for load in loads[g * chunks : (g + 1) * chunks]:
-            load.wait()
-        for i in range(g * GROUP, (g + 1) * GROUP):
-            weights = [jnp.broadcast_to(cols[s][:, i : i + 1], (classes, LANES)) for s in range(SUBSTEPS)]
-            for r in range(chunks):
-                value = shells[r, i * classes : (i + 1) * classes, :]
-                for s in range(SUBSTEPS):
-                    value = value + weights[s] * walls_here[s][r]
-                out[i, :, r * LANES : (r + 1) * LANES] = value
+        here = slice(g * width, (g + 1) * width)
+        change = dot(columns[here, : 4 * SUBSTEPS].astype(jnp.bfloat16), right)
+        if g % 2 == 0:
+            loads[g // 2].wait()
+        for r in range(chunks):
+            lanes = slice(r * LANES, (r + 1) * LANES)
+            value = shells[r, here, :] + change[:, lanes]
+            out[g * GROUP : (g + 1) * GROUP, :, lanes] = value.reshape(GROUP, classes, LANES)
         stores[g].start()
     for store in stores:
         store.wait()
@@ -352,16 +346,14 @@
         compiler_params=whole,
         name="fields",
     )(melt, counts, pressure, propagator, coupling, flux_weights)
-    columns_v = pltpu.VMEM((SUBSTEPS * classes, LANES), f32)
     shells = pl.pallas_call(
         power_kernel,
-        out_shape=jax.ShapeDtypeStruct(((chunks * nodes + SUBSTEPS) * classes, LANES), f32),
+        out_shape=jax.ShapeDtypeStruct((chunks + 1,) + split[1:], f32),
         in_specs=[HBM] * 3,
         out_specs=HBM,
         scratch_shapes=[
             pltpu.VMEM(split, f32),
-            pltpu.VMEM(split, f32),
-            columns_v,
+            pltpu.VMEM((chunks + 1,) + split[1:], f32),
             prop_v,
             small,
             DMA((chunks,)),
@@ -390,10 +382,10 @@
         scratch_shapes=[
             pltpu.VMEM(split, f32),
             pltpu.VMEM(melt.shape, f32),
-            columns_v,
+            pltpu.VMEM(split[1:], f32),
             pltpu.VMEM((SUBSTEPS, rows, LANES), f32),
             pltpu.VMEM((rows, LANES), f32),
-            DMA((parts, chunks)),
+            DMA((parts // 2,)),
             DMA((parts,)),
             DMA(()),
         ],

time: 34 us -> 32.5 us (0.956)
  Pallas kernels: 16.2 us -> 13.3 us
  waiting for transfers between devices: 0.01 us -> 1.39 us
    pallas_call x1, Pallas kernels: 6.64 us -> 4.85 us  [shards(): pl.pallas_call(power_kernel, out_shape=jax.ShapeDtypeStruct((chunks + 1,)...]
    all_to_all x1, waiting for transfers between devices: 0.01 us -> 1.39 us  [exchange(): return lax.all_to_all(copies, axis, split_axis=0, concat_axis=0, tiled=True)]
    pallas_call x1, Pallas kernels: 5.01 us -> 4.14 us  [shards(): pl.pallas_call(finish_kernel, out_shape=[jax.ShapeDtypeStruct(melt.shape,...]
  transfers between devices with their start and end apart: 1 -> 1, of which waited for: 0 -> 1; matrix products, arithmetic and copies ran while one was open for 0% -> 0% of each run, Pallas kernels for 20% -> 15%
where the time goes in v6:
time: 32.5 us; the launch traced here: 32.2 us
  Pallas kernels  13.3 us (41%)
  blocking collectives  10.5 us (32%)
  starting transfers between devices  6.33 us (19%)
  waiting for transfers between devices  1.39 us (4%)
  between operations  0.65 us (2%)
    all_to_all x1, blocking collectives, exchange(): return lax.all_to_all(copies, axis, split_axis=0, concat_axis=0, tiled=True)  10.5 us
    all_to_all x1, starting transfers between devices, exchange(): return lax.all_to_all(copies, axis, split_axis=0, concat_axis=0, tiled=True)  6.33 us
    pallas_call x1, Pallas kernels, shards(): pl.pallas_call(power_kernel, out_shape=jax.ShapeDtypeStruct((chunks + 1,)...  4.85 us
    pallas_call x1, Pallas kernels, shards(): pl.pallas_call(fields_kernel, out_shape=jax.ShapeDtypeStruct((cls_count,...  4.34 us
    pallas_call x1, Pallas kernels, shards(): pl.pallas_call(finish_kernel, out_shape=[jax.ShapeDtypeStruct(melt.shape,...  4.14 us
    all_to_all x1, waiting for transfers between devices, exchange(): return lax.all_to_all(copies, axis, split_axis=0, concat_axis=0, tiled=True)  1.39 us
  transfers between devices with their start and end apart: 1, of which 1 were waited for; matrix products, arithmetic and copies ran while one was open for 0% of the time, Pallas kernels for 15%

profile of v6, /device:TPU:0, one launch (start us, length us, event | category | flops | bytes accessed | tf_op | source)
XLA Modules:
  0.0 32.2 jit_solution(16580085598911316147)
XLA Ops:
  0.6 4.3 %fields.1 = f32[4,9,8,128]{3,2,1,0:T(8,128)} custom-call(f32[64,8,1024]{2,1,0:T(8,128)} %melt_hbm.1, s32[8,1024]{1,0:T(8,128)} %counts_hbm.1, f32[1,256]{1,0:T(1,128)} %pressure_hbm.1, f32[32,64,64]{2,1,0:T(8,128)} %prop_hbm.3, f32[32,64]{1,0:T(8,128)} %coup_hbm.3, f32[32,64]{1,0:T(8,128)} %flux_hbm.1), custom_call_target="tpu_custom_call" | custom-call | tf_op jit(solution)/shard_map/fields/pallas_call | solution.py:331
  5.0 6.3 %all-to-all-start = ((f32[4,9,8,128]{3,2,1,0:T(8,128)}), f32[4,9,8,128]{3,2,1,0:T(8,128)S(1)}, u32[]{:S(2)}, u32[]{:S(2)}) async-start(f32[4,9,8,128]{3,2,1,0:T(8,128)} %fields.1), calls=%async_computation | async-start | bytes 294912 | tf_op jit(solution)/shard_map/all_to_all | solution.py:316
  11.3 4.9 %power.1._.shells_hbm = f32[9,512,128]{2,1,0:T(8,128)} custom-call(f32[512,1024]{1,0:T(8,128)} %bitcast.1, f32[32,64,64]{2,1,0:T(8,128)} %prop_hbm.3, f32[32,64]{1,0:T(8,128)} %coup_hbm.3), custom_call_target="tpu_custom_call" | custom-call | flops 2000000000 | bytes 4194304 | tf_op jit(solution)/shard_map/power/pallas_call | solution.py:349
  16.2 1.4 %all-to-all-done.parts = f32[4,9,8,128]{3,2,1,0:T(8,128)S(1)} async-done(((f32[4,9,8,128]{3,2,1,0:T(8,128)}), f32[4,9,8,128]{3,2,1,0:T(8,128)S(1)}, u32[]{:S(2)}, u32[]{:S(2)}) %all-to-all-start) | async-done | bytes 147488 | tf_op jit(solution)/shard_map/all_to_all | solution.py:316
  17.6 10.5 %all_to_all.10.window = f32[8,8,8,128]{3,2,1,0:T(8,128)S(1)} all-to-all(f32[8,8,8,128]{3,2,1,0:T(8,128)S(1)} %combine.1), channel_id=1, replica_groups=mesh['cell'=8,'cls'=4] {'cell'}, dimensions={0} | all-to-all | bytes 524288 | tf_op jit(solution)/shard_map/all_to_all | solution.py:316
  28.0 4.1 %finish.1 = (f32[64,8,1024]{2,1,0:T(8,128)}, f32[1,256]{1,0:T(1,128)}) custom-call(f32[8,8,8,128]{3,2,1,0:T(8,128)S(1)} %all_to_all.10.window, f32[9,512,128]{2,1,0:T(8,128)} %power.1._.shells_hbm), custom_call_target="tpu_custom_call" | custom-call | tf_op jit(solution)/shard_map/finish/pallas_call | solution.py:377
  (1 shorter events, 0.0 us)
Async XLA Ops:
  5.0 12.6 %all-to-all-start = ((f32[4,9,8,128]{3,2,1,0:T(8,128)}), f32[4,9,8,128]{3,2,1,0:T(8,128)S(1)}, u32[]{:S(2)}, u32[]{:S(2)}) async-start(f32[4,9,8,128]{3,2,1,0:T(8,128)} %fields.1), calls=%async_computation | async-start | bytes 294912 | tf_op jit(solution)/shard_map/all_to_all | solution.py:316

commit v7 on v6

--- a/solution.py
+++ b/solution.py
@@ -205,12 +205,16 @@
     for n in range(1, parts.shape[0]):
         total = total + parts[n]
     wall = 0.5 * total[2 * SUBSTEPS]
-    for n in range(out.shape[0]):
-        for t in range(SUBSTEPS):
-            out[n, t] = total[t] + total[SUBSTEPS + t] * wall
-        for d in range(SUBSTEPS - 1):
-            out[n, SUBSTEPS + d] = total[SUBSTEPS + d]
-        out[n, 2 * SUBSTEPS - 1] = total[2 * SUBSTEPS]
+    for t in range(SUBSTEPS):
+        out[t] = total[t] + total[SUBSTEPS + t] * wall
+    for d in range(SUBSTEPS - 1):
+        out[SUBSTEPS + d] = total[SUBSTEPS + d]
+    out[2 * SUBSTEPS - 1] = total[2 * SUBSTEPS]
+
+
+def total_of(x):
+    tiles = jnp.sum(x.reshape(-1, GROUP, LANES), axis=0)
+    return jnp.sum(jnp.sum(tiles, axis=1, keepdims=True), axis=0, keepdims=True)
 
 
 def laplacian(x, plane):
@@ -264,16 +268,26 @@
         return window[:, f].reshape(rows, LANES)
 
     field = field_of(2 * SUBSTEPS - 1)
+    answer = field_of(SUBSTEPS)
+    answer_total = total_of(answer)
+    chamber = None
     walls = []
     for t in range(SUBSTEPS):
+        gas = field_of(t)
+        for s in range(1, t):
+            gas = gas + field_of(SUBSTEPS + t - s) * walls[s]
+        if t:
+            gas = gas + answer * (0.5 * field)
+        total = total_of(gas)
+        if t:
+            field = field + 0.2 * chamber
+            gas = gas + answer * (0.1 * chamber)
+            total = total + answer_total * (0.1 * chamber)
         walls.append(0.5 * field)
         walls_all[t] = walls[t]
-        gas = field_of(t)
-        for s in range(1, t + 1):
-            gas = gas + field_of(SUBSTEPS + t - s) * walls[s]
-        chamber = 1.5 - 0.5 * jnp.sum(gas) / (rows * LANES)
-        field = field + 0.15 * laplacian(field, plane) + 0.1 * gas + 0.2 * (chamber - field)
-    last[...] = field
+        field = 0.8 * field + 0.15 * laplacian(field, plane) + 0.1 * gas
+        chamber = 1.5 - 0.5 * total / (rows * LANES)
+    last[...] = field + 0.2 * chamber
     cell = lax.axis_index("cell")
     first = cell * chunks
     tile = pressure_out.shape[0] * plane // LANES
@@ -364,15 +378,15 @@
         cost_estimate=pl.CostEstimate(flops=2 * 10**9, bytes_accessed=2 * melt.size * 4, transcendentals=0),
         name="power",
     )(melt.reshape(nodes * classes, cells), propagator, coupling)
-    copies = pl.pallas_call(
+    fields = pl.pallas_call(
         combine_kernel,
-        out_shape=jax.ShapeDtypeStruct((cell_count, FIELDS - 1, chunks, LANES), f32),
+        out_shape=jax.ShapeDtypeStruct((FIELDS - 1, chunks, LANES), f32),
         in_specs=[VMEM, HBM],
         out_specs=VMEM,
         compiler_params=most,
         name="combine",
     )(exchange(packed, "cls"), shells)
-    window = exchange(copies, "cell")
+    window = lax.all_gather(fields, "cell", axis=0)
     rows = cell_count * chunks
     return pl.pallas_call(
         finish_kernel,

time: 32.5 us -> 31.3 us (0.963)
  blocking collectives: 10.5 us -> 9.32 us
    all_to_all x1 -> x0, blocking collectives: 10.5 us -> none  [exchange(): return lax.all_to_all(copies, axis, split_axis=0, concat_axis=0, tiled=True)]
    all_gather x0 -> x1, blocking collectives: none -> 9.32 us  [shards(): window = lax.all_gather(fields, 'cell', axis=0)]
  transfers between devices with their start and end apart: 1 -> 1, of which waited for: 1 -> 1; matrix products, arithmetic and copies ran while one was open for 0% -> 0% of each run, Pallas kernels for 15% -> 16%
where the time goes in v7:
time: 31.3 us; the launch traced here: 31 us
  Pallas kernels  13.3 us (42%)
  blocking collectives  9.32 us (30%)
  starting transfers between devices  6.33 us (20%)
  waiting for transfers between devices  1.39 us (4%)
  between operations  0.65 us (2%)
    all_gather x1, blocking collectives, shards(): window = lax.all_gather(fields, 'cell', axis=0)  9.32 us
    all_to_all x1, starting transfers between devices, exchange(): return lax.all_to_all(copies, axis, split_axis=0, concat_axis=0, tiled=True)  6.33 us
    pallas_call x1, Pallas kernels, shards(): pl.pallas_call(power_kernel, out_shape=jax.ShapeDtypeStruct((chunks + 1,)...  4.85 us
    pallas_call x1, Pallas kernels, shards(): pl.pallas_call(fields_kernel, out_shape=jax.ShapeDtypeStruct((cls_count,...  4.34 us
    pallas_call x1, Pallas kernels, shards(): pl.pallas_call(finish_kernel, out_shape=[jax.ShapeDtypeStruct(melt.shape,...  4.11 us
    all_to_all x1, waiting for transfers between devices, exchange(): return lax.all_to_all(copies, axis, split_axis=0, concat_axis=0, tiled=True)  1.39 us
  transfers between devices with their start and end apart: 1, of which 1 were waited for; matrix products, arithmetic and copies ran while one was open for 0% of the time, Pallas kernels for 16%

profile of v7, /device:TPU:0, one launch (start us, length us, event | category | flops | bytes accessed | tf_op | source)
XLA Modules:
  0.0 31.0 jit_solution(3765514006646371297)
XLA Ops:
  0.6 4.3 %fields.1 = f32[4,9,8,128]{3,2,1,0:T(8,128)} custom-call(f32[64,8,1024]{2,1,0:T(8,128)} %melt_hbm.1, s32[8,1024]{1,0:T(8,128)} %counts_hbm.1, f32[1,256]{1,0:T(1,128)} %pressure_hbm.1, f32[32,64,64]{2,1,0:T(8,128)} %prop_hbm.3, f32[32,64]{1,0:T(8,128)} %coup_hbm.3, f32[32,64]{1,0:T(8,128)} %flux_hbm.1), custom_call_target="tpu_custom_call" | custom-call | tf_op jit(solution)/shard_map/fields/pallas_call | solution.py:345
  5.0 6.3 %all-to-all-start = ((f32[4,9,8,128]{3,2,1,0:T(8,128)}), f32[4,9,8,128]{3,2,1,0:T(8,128)S(1)}, u32[]{:S(2)}, u32[]{:S(2)}) async-start(f32[4,9,8,128]{3,2,1,0:T(8,128)} %fields.1), calls=%async_computation | async-start | bytes 294912 | tf_op jit(solution)/shard_map/all_to_all | solution.py:330
  11.3 4.9 %power.1._.shells_hbm = f32[9,512,128]{2,1,0:T(8,128)} custom-call(f32[512,1024]{1,0:T(8,128)} %bitcast.3, f32[32,64,64]{2,1,0:T(8,128)} %prop_hbm.3, f32[32,64]{1,0:T(8,128)} %coup_hbm.3), custom_call_target="tpu_custom_call" | custom-call | flops 2000000000 | bytes 4194304 | tf_op jit(solution)/shard_map/power/pallas_call | solution.py:363
  16.2 1.4 %all-to-all-done.parts = f32[4,9,8,128]{3,2,1,0:T(8,128)S(1)} async-done(((f32[4,9,8,128]{3,2,1,0:T(8,128)}), f32[4,9,8,128]{3,2,1,0:T(8,128)S(1)}, u32[]{:S(2)}, u32[]{:S(2)}) %all-to-all-start) | async-done | bytes 147488 | tf_op jit(solution)/shard_map/all_to_all | solution.py:330
  17.6 9.3 %all-gather = f32[64,8,128]{2,1,0:T(8,128)S(1)} all-gather(f32[8,8,128]{2,1,0:T(8,128)S(1)} %combine.1), channel_id=2, replica_groups=mesh['cell'=8,'cls'=4] {'cell'}, dimensions={0}, use_global_device_ids=true | all-gather | bytes 294912 | tf_op jit(solution)/shard_map/all_gather | solution.py:389
  26.9 4.1 %finish.1 = (f32[64,8,1024]{2,1,0:T(8,128)}, f32[1,256]{1,0:T(1,128)}) custom-call(f32[8,8,8,128]{3,2,1,0:T(8,128)S(1)} %bitcast.2, f32[9,512,128]{2,1,0:T(8,128)} %power.1._.shells_hbm), custom_call_target="tpu_custom_call" | custom-call | tf_op jit(solution)/shard_map/finish/pallas_call | solution.py:391
  (1 shorter events, 0.0 us)
Async XLA Ops:
  5.0 12.6 %all-to-all-start = ((f32[4,9,8,128]{3,2,1,0:T(8,128)}), f32[4,9,8,128]{3,2,1,0:T(8,128)S(1)}, u32[]{:S(2)}, u32[]{:S(2)}) async-start(f32[4,9,8,128]{3,2,1,0:T(8,128)} %fields.1), calls=%async_computation | async-start | bytes 294912 | tf_op jit(solution)/shard_map/all_to_all | solution.py:330

commit v8 on v7

--- a/solution.py
+++ b/solution.py
@@ -14,8 +14,6 @@
 LANES = 128
 GROUP = 8
 FIELDS = 2 * SUBSTEPS + 1
-
-HIGHEST = lax.Precision.HIGHEST
 
 
 def grow(value, factor, times):
@@ -135,7 +133,7 @@
             out[n, 2 * SUBSTEPS, pl.ds(at + i, 1), :] = row
 
 
-def power_kernel(melt_hbm, prop_hbm, coup_hbm, out_hbm, melt, out, prop, coup, sems, out_sems, param_sems):
+def power_kernel(melt_hbm, prop_hbm, coup_hbm, out_hbm, done, melt, out, prop, coup, sems, out_sems, param_sems):
     chunks = melt.shape[0]
     classes, nodes = prop.shape[:2]
     params = param_copies([(prop_hbm, prop), (coup_hbm, coup)], param_sems)
@@ -198,6 +196,7 @@
             stores[r + n].start()
     for store in stores:
         store.wait()
+    done[...] = jnp.zeros_like(done)
 
 
 def combine_kernel(parts, _, out):
@@ -238,7 +237,7 @@
 
 
 def finish_kernel(
-    window, shells_hbm, out_hbm, pressure_out, shells, out, columns, walls_all, last, sems, out_sems, column_sem
+    window, shells, out_hbm, pressure_out, out, walls_all, last, out_sems
 ):
     nodes, classes, cells = out.shape
     chunks = cells // LANES
@@ -248,18 +247,6 @@
     def piece(g):
         return pl.ds(g * GROUP, GROUP)
 
-    column_load = pltpu.make_async_copy(shells_hbm.at[chunks], columns, column_sem)
-    column_load.start()
-    loads = [
-        pltpu.make_async_copy(
-            shells_hbm.at[pl.ds(0, chunks), pl.ds(g * 2 * width, 2 * width)],
-            shells.at[:, pl.ds(g * 2 * width, 2 * width)],
-            sems.at[g],
-        )
-        for g in range(parts // 2)
-    ]
-    for load in loads:
-        load.start()
     plane = pressure_out.shape[1]
     blocks = window.shape[0]
     rows = blocks * chunks
@@ -306,12 +293,9 @@
     stores = [
         pltpu.make_async_copy(out.at[piece(g)], out_hbm.at[piece(g)], out_sems.at[g]) for g in range(parts)
     ]
-    column_load.wait()
     for g in range(parts):
         here = slice(g * width, (g + 1) * width)
-        change = dot(columns[here, : 4 * SUBSTEPS].astype(jnp.bfloat16), right)
-        if g % 2 == 0:
-            loads[g // 2].wait()
+        change = dot(shells[chunks, here, : 4 * SUBSTEPS].astype(jnp.bfloat16), right)
         for r in range(chunks):
             lanes = slice(r * LANES, (r + 1) * LANES)
             value = shells[r, here, :] + change[:, lanes]
@@ -336,7 +320,7 @@
     f32 = jnp.float32
     split = (chunks, nodes * classes, LANES)
     whole = pltpu.CompilerParams(vmem_limit_bytes=60 * 2**20)
-    most = pltpu.CompilerParams(vmem_limit_bytes=52 * 2**20)
+    little = pltpu.CompilerParams(vmem_limit_bytes=32 * 2**20)
     cls_count = lax.axis_size("cls")
     cell_count = lax.axis_size("cell")
     prop_v = pltpu.VMEM((classes, nodes, nodes), f32)
@@ -360,11 +344,14 @@
         compiler_params=whole,
         name="fields",
     )(melt, counts, pressure, propagator, coupling, flux_weights)
-    shells = pl.pallas_call(
+    shells, done = pl.pallas_call(
         power_kernel,
-        out_shape=jax.ShapeDtypeStruct((chunks + 1,) + split[1:], f32),
+        out_shape=[
+            jax.ShapeDtypeStruct((chunks + 1,) + split[1:], f32),
+            jax.ShapeDtypeStruct((GROUP, LANES), f32),
+        ],
         in_specs=[HBM] * 3,
-        out_specs=HBM,
+        out_specs=[HBM, VMEM],
         scratch_shapes=[
             pltpu.VMEM(split, f32),
             pltpu.VMEM((chunks + 1,) + split[1:], f32),
@@ -381,29 +368,25 @@
     fields = pl.pallas_call(
         combine_kernel,
         out_shape=jax.ShapeDtypeStruct((FIELDS - 1, chunks, LANES), f32),
-        in_specs=[VMEM, HBM],
+        in_specs=[VMEM, VMEM],
         out_specs=VMEM,
-        compiler_params=most,
+        compiler_params=little,
         name="combine",
-    )(exchange(packed, "cls"), shells)
+    )(exchange(packed, "cls"), done)
     window = lax.all_gather(fields, "cell", axis=0)
     rows = cell_count * chunks
     return pl.pallas_call(
         finish_kernel,
         out_shape=[jax.ShapeDtypeStruct(melt.shape, f32), jax.ShapeDtypeStruct(pressure.shape, f32)],
-        in_specs=[VMEM, HBM],
+        in_specs=[VMEM, VMEM],
         out_specs=[HBM, VMEM],
         scratch_shapes=[
-            pltpu.VMEM(split, f32),
             pltpu.VMEM(melt.shape, f32),
-            pltpu.VMEM(split[1:], f32),
             pltpu.VMEM((SUBSTEPS, rows, LANES), f32),
             pltpu.VMEM((rows, LANES), f32),
-            DMA((parts // 2,)),
             DMA((parts,)),
-            DMA(()),
         ],
-        compiler_params=most,
+        compiler_params=little,
         name="finish",
     )(window, shells)
 

time: 31.3 us -> 32.1 us (1.026)
  local copies, waits for them, and re-layouts: 0 us -> 2.35 us
  Pallas kernels: 13.3 us -> 12.3 us
  waiting for transfers between devices: 1.39 us -> 0.81 us
    unnamed x0 -> x4, local copies, waits for them, and re-layouts: none -> 2.35 us
    pallas_call x1, Pallas kernels: 4.11 us -> 2.5 us  [shards(): pl.pallas_call(finish_kernel, out_shape=[jax.ShapeDtypeStruct(melt.shape,...]
    pallas_call x1, Pallas kernels: 4.85 us -> 5.43 us  [shards(): pl.pallas_call(power_kernel, out_shape=[jax.ShapeDtypeStruct((chunks + 1,...]
    all_to_all x1, waiting for transfers between devices: 1.39 us -> 0.81 us  [exchange(): return lax.all_to_all(copies, axis, split_axis=0, concat_axis=0, tiled=True)]
  transfers between devices with their start and end apart: 1 -> 1, of which waited for: 1 -> 1; matrix products, arithmetic and copies ran while one was open for 0% -> 0% of each run, Pallas kernels for 16% -> 17%
where the time goes in v8:
time: 32.1 us; the launch traced here: 31.7 us
  Pallas kernels  12.3 us (38%)
  blocking collectives  9.32 us (29%)
  starting transfers between devices  6.33 us (20%)
  local copies, waits for them, and re-layouts  2.35 us (7%)
  waiting for transfers between devices  0.81 us (3%)
  between operations  0.65 us (2%)
    all_gather x1, blocking collectives, shards(): window = lax.all_gather(fields, 'cell', axis=0)  9.32 us
    all_to_all x1, starting transfers between devices, exchange(): return lax.all_to_all(copies, axis, split_axis=0, concat_axis=0, tiled=True)  6.33 us
    pallas_call x1, Pallas kernels, shards(): pl.pallas_call(power_kernel, out_shape=[jax.ShapeDtypeStruct((chunks + 1,...  5.43 us
    pallas_call x1, Pallas kernels, shards(): pl.pallas_call(fields_kernel, out_shape=jax.ShapeDtypeStruct((cls_count,...  4.34 us
    pallas_call x1, Pallas kernels, shards(): pl.pallas_call(finish_kernel, out_shape=[jax.ShapeDtypeStruct(melt.shape,...  2.5 us
    unnamed x4, local copies, waits for them, and re-layouts  2.35 us
    all_to_all x1, waiting for transfers between devices, exchange(): return lax.all_to_all(copies, axis, split_axis=0, concat_axis=0, tiled=True)  0.81 us
  transfers between devices with their start and end apart: 1, of which 1 were waited for; matrix products, arithmetic and copies ran while one was open for 0% of the time, Pallas kernels for 17%

profile of v8, /device:TPU:0, one launch (start us, length us, event | category | flops | bytes accessed | tf_op | source)
XLA Modules:
  0.0 31.7 jit_solution(7052521188117155143)
XLA Ops:
  0.6 4.3 %fields.1 = f32[4,9,8,128]{3,2,1,0:T(8,128)} custom-call(f32[64,8,1024]{2,1,0:T(8,128)} %melt_hbm.1, s32[8,1024]{1,0:T(8,128)} %counts_hbm.1, f32[1,256]{1,0:T(1,128)} %pressure_hbm.1, f32[32,64,64]{2,1,0:T(8,128)} %prop_hbm.3, f32[32,64]{1,0:T(8,128)} %coup_hbm.3, f32[32,64]{1,0:T(8,128)} %flux_hbm.1), custom_call_target="tpu_custom_call" | custom-call | tf_op jit(solution)/shard_map/fields/pallas_call | solution.py:329
  5.0 6.3 %all-to-all-start = ((f32[4,9,8,128]{3,2,1,0:T(8,128)}), f32[4,9,8,128]{3,2,1,0:T(8,128)S(1)}, u32[]{:S(2)}, u32[]{:S(2)}) async-start(f32[4,9,8,128]{3,2,1,0:T(8,128)} %fields.1), calls=%async_computation | async-start | bytes 294912 | tf_op jit(solution)/shard_map/all_to_all | solution.py:314
  11.3 5.4 %power.1 = (f32[9,512,128]{2,1,0:T(8,128)}, f32[8,128]{1,0:T(8,128)}) custom-call(f32[512,1024]{1,0:T(8,128)} %bitcast.3, f32[32,64,64]{2,1,0:T(8,128)} %prop_hbm.3, f32[32,64]{1,0:T(8,128)} %coup_hbm.3), custom_call_target="tpu_custom_call" | custom-call | flops 2000000000 | bytes 4194304 | tf_op jit(solution)/shard_map/power/pallas_call | solution.py:347
  16.7 0.8 %all-to-all-done.parts = f32[4,9,8,128]{3,2,1,0:T(8,128)S(1)} async-done(((f32[4,9,8,128]{3,2,1,0:T(8,128)}), f32[4,9,8,128]{3,2,1,0:T(8,128)S(1)}, u32[]{:S(2)}, u32[]{:S(2)}) %all-to-all-start) | async-done | bytes 147488 | tf_op jit(solution)/shard_map/all_to_all | solution.py:314
  17.6 0.0 copy-start.1
  17.6 0.7 %copy-done.1 = f32[8,128]{1,0:T(8,128)S(1)} copy-done((f32[8,128]{1,0:T(8,128)S(1)}, f32[8,128]{1,0:T(8,128)}, u32[]{:S(2)}) %copy-start.1) | copy-done | bytes 4120
  18.3 9.3 %all-gather = f32[64,8,128]{2,1,0:T(8,128)S(1)} all-gather(f32[8,8,128]{2,1,0:T(8,128)S(1)} %combine.1), channel_id=2, replica_groups=mesh['cell'=8,'cls'=4] {'cell'}, dimensions={0}, use_global_device_ids=true | all-gather | bytes 294912 | tf_op jit(solution)/shard_map/all_gather | solution.py:376
  27.6 0.0 copy-start
  27.6 1.7 %copy-done = f32[9,512,128]{2,1,0:T(8,128)S(1)} copy-done((f32[9,512,128]{2,1,0:T(8,128)S(1)}, f32[9,512,128]{2,1,0:T(8,128)}, u32[]{:S(2)}) %copy-start) | copy-done | bytes 2359320
  29.2 2.5 %finish.1 = (f32[64,8,1024]{2,1,0:T(8,128)}, f32[1,256]{1,0:T(1,128)}) custom-call(f32[8,8,8,128]{3,2,1,0:T(8,128)S(1)} %bitcast.2, f32[9,512,128]{2,1,0:T(8,128)S(1)} %copy-done), custom_call_target="tpu_custom_call" | custom-call | tf_op jit(solution)/shard_map/finish/pallas_call | solution.py:378
  (1 shorter events, 0.0 us)
Async XLA Ops:
  5.0 12.6 %all-to-all-start = ((f32[4,9,8,128]{3,2,1,0:T(8,128)}), f32[4,9,8,128]{3,2,1,0:T(8,128)S(1)}, u32[]{:S(2)}, u32[]{:S(2)}) async-start(f32[4,9,8,128]{3,2,1,0:T(8,128)} %fields.1), calls=%async_computation | async-start | bytes 294912 | tf_op jit(solution)/shard_map/all_to_all | solution.py:314
  17.6 0.7 %copy-start.1 = (f32[8,128]{1,0:T(8,128)S(1)}, f32[8,128]{1,0:T(8,128)}, u32[]{:S(2)}) copy-start(f32[8,128]{1,0:T(8,128)} %get-tuple-element.4._) | copy-start | bytes 12292
  27.6 1.7 %copy-start = (f32[9,512,128]{2,1,0:T(8,128)S(1)}, f32[9,512,128]{2,1,0:T(8,128)}, u32[]{:S(2)}) copy-start(f32[9,512,128]{2,1,0:T(8,128)} %get-tuple-element.5.shells) | copy-start | bytes 7077892

commit v9 on v8

--- a/solution.py
+++ b/solution.py
@@ -133,7 +133,7 @@
             out[n, 2 * SUBSTEPS, pl.ds(at + i, 1), :] = row
 
 
-def power_kernel(melt_hbm, prop_hbm, coup_hbm, out_hbm, done, melt, out, prop, coup, sems, out_sems, param_sems):
+def power_kernel(melt_hbm, prop_hbm, coup_hbm, out, melt, prop, coup, sems, param_sems):
     chunks = melt.shape[0]
     classes, nodes = prop.shape[:2]
     params = param_copies([(prop_hbm, prop), (coup_hbm, coup)], param_sems)
@@ -142,9 +142,6 @@
     loads = [
         pltpu.make_async_copy(melt_hbm.at[:, pl.ds(r * LANES, LANES)], melt.at[r], sems.at[r])
         for r in range(chunks)
-    ]
-    stores = [
-        pltpu.make_async_copy(out.at[r], out_hbm.at[r], out_sems.at[r]) for r in range(chunks + 1)
     ]
     for load in loads:
         load.start()
@@ -181,7 +178,6 @@
         high = value.astype(jnp.bfloat16).astype(jnp.float32)
         value = jnp.where(lane < 2 * SUBSTEPS, high, jnp.where(lane < 3 * SUBSTEPS, value - high, 0.0))
         out[chunks, pl.ds(k, nodes, stride=classes), :] = value
-    stores[chunks].start()
     together = 2 if chunks % 2 == 0 else 1
     for r in range(0, chunks, together):
         for n in range(together):
@@ -192,11 +188,6 @@
             part = grow(dot(lefts[k], right_of(x)), factors[k], SUBSTEPS)
             for n in range(together):
                 out[r + n, own, :] = part[:, n * LANES : (n + 1) * LANES]
-        for n in range(together):
-            stores[r + n].start()
-    for store in stores:
-        store.wait()
-    done[...] = jnp.zeros_like(done)
 
 
 def combine_kernel(parts, _, out):
@@ -320,6 +311,7 @@
     f32 = jnp.float32
     split = (chunks, nodes * classes, LANES)
     whole = pltpu.CompilerParams(vmem_limit_bytes=60 * 2**20)
+    most = pltpu.CompilerParams(vmem_limit_bytes=48 * 2**20)
     little = pltpu.CompilerParams(vmem_limit_bytes=32 * 2**20)
     cls_count = lax.axis_size("cls")
     cell_count = lax.axis_size("cell")
@@ -344,24 +336,19 @@
         compiler_params=whole,
         name="fields",
     )(melt, counts, pressure, propagator, coupling, flux_weights)
-    shells, done = pl.pallas_call(
+    shells = pl.pallas_call(
         power_kernel,
-        out_shape=[
-            jax.ShapeDtypeStruct((chunks + 1,) + split[1:], f32),
-            jax.ShapeDtypeStruct((GROUP, LANES), f32),
-        ],
+        out_shape=jax.ShapeDtypeStruct((chunks + 1,) + split[1:], f32),
         in_specs=[HBM] * 3,
-        out_specs=[HBM, VMEM],
+        out_specs=VMEM,
         scratch_shapes=[
             pltpu.VMEM(split, f32),
-            pltpu.VMEM((chunks + 1,) + split[1:], f32),
             prop_v,
             small,
             DMA((chunks,)),
-            DMA((chunks + 1,)),
             DMA((2,)),
         ],
-        compiler_params=whole,
+        compiler_params=most,
         cost_estimate=pl.CostEstimate(flops=2 * 10**9, bytes_accessed=2 * melt.size * 4, transcendentals=0),
         name="power",
     )(melt.reshape(nodes * classes, cells), propagator, coupling)
@@ -372,7 +359,7 @@
         out_specs=VMEM,
         compiler_params=little,
         name="combine",
-    )(exchange(packed, "cls"), done)
+    )(exchange(packed, "cls"), shells)
     window = lax.all_gather(fields, "cell", axis=0)
     rows = cell_count * chunks
     return pl.pallas_call(

time: 32.1 us -> 29.8 us (0.928)
  Pallas kernels: 12.3 us -> 9.69 us
  waiting for transfers between devices: 0.81 us -> 1.17 us
    pallas_call x1, Pallas kernels: 5.43 us -> 2.76 us  [shards(): pl.pallas_call(power_kernel, out_shape=jax.ShapeDtypeStruct((chunks + 1,)...]
    all_to_all x1, waiting for transfers between devices: 0.81 us -> 1.17 us  [exchange(): return lax.all_to_all(copies, axis, split_axis=0, concat_axis=0, tiled=True)]
    unnamed x4 -> x6, local copies, waits for them, and re-layouts: 2.35 us -> 2.31 us
  transfers between devices with their start and end apart: 1 -> 1, of which waited for: 1 -> 1; matrix products, arithmetic and copies ran while one was open for 0% -> 0% of each run, Pallas kernels for 17% -> 9%
where the time goes in v9:
time: 29.8 us; the launch traced here: 29.5 us
  Pallas kernels  9.69 us (33%)
  blocking collectives  9.32 us (31%)
  starting transfers between devices  6.33 us (21%)
  local copies, waits for them, and re-layouts  2.31 us (8%)
  waiting for transfers between devices  1.17 us (4%)
  between operations  0.66 us (2%)
    all_gather x1, blocking collectives, shards(): window = lax.all_gather(fields, 'cell', axis=0)  9.32 us
    all_to_all x1, starting transfers between devices, exchange(): return lax.all_to_all(copies, axis, split_axis=0, concat_axis=0, tiled=True)  6.33 us
    pallas_call x1, Pallas kernels, shards(): pl.pallas_call(fields_kernel, out_shape=jax.ShapeDtypeStruct((cls_count,...  4.42 us
    pallas_call x1, Pallas kernels, shards(): pl.pallas_call(power_kernel, out_shape=jax.ShapeDtypeStruct((chunks + 1,)...  2.76 us
    pallas_call x1, Pallas kernels, shards(): pl.pallas_call(finish_kernel, out_shape=[jax.ShapeDtypeStruct(melt.shape,...  2.5 us
    unnamed x6, local copies, waits for them, and re-layouts  2.31 us
    all_to_all x1, waiting for transfers between devices, exchange(): return lax.all_to_all(copies, axis, split_axis=0, concat_axis=0, tiled=True)  1.17 us
  transfers between devices with their start and end apart: 1, of which 1 were waited for; matrix products, arithmetic and copies ran while one was open for 0% of the time, Pallas kernels for 9%

profile of v9, /device:TPU:0, one launch (start us, length us, event | category | flops | bytes accessed | tf_op | source)
XLA Modules:
  0.0 29.5 jit_solution(7651231750429601245)
XLA Ops:
  0.6 0.0 copy-start.1
  0.6 4.4 %fields.1 = f32[4,9,8,128]{3,2,1,0:T(8,128)} custom-call(f32[64,8,1024]{2,1,0:T(8,128)} %melt_hbm.1, s32[8,1024]{1,0:T(8,128)} %counts_hbm.1, f32[1,256]{1,0:T(1,128)} %pressure_hbm.1, f32[32,64,64]{2,1,0:T(8,128)} %prop_hbm.3, f32[32,64]{1,0:T(8,128)} %coup_hbm.3, f32[32,64]{1,0:T(8,128)} %flux_hbm.1), custom_call_target="tpu_custom_call" | custom-call | tf_op jit(solution)/shard_map/fields/pallas_call | solution.py:321
  5.1 6.3 %all-to-all-start = ((f32[4,9,8,128]{3,2,1,0:T(8,128)}), f32[4,9,8,128]{3,2,1,0:T(8,128)S(1)}, u32[]{:S(2)}, u32[]{:S(2)}) async-start(f32[4,9,8,128]{3,2,1,0:T(8,128)} %fields.1), calls=%async_computation | async-start | bytes 294912 | tf_op jit(solution)/shard_map/all_to_all | solution.py:305
  11.4 0.0 copy-done.1
  11.4 0.0 copy-start
  11.4 1.6 %copy-done = f32[64,8,1024]{2,1,0:T(8,128)S(1)} copy-done((f32[64,8,1024]{2,1,0:T(8,128)S(1)}, f32[64,8,1024]{2,1,0:T(8,128)}, u32[]{:S(2)}) %copy-start) | copy-done | bytes 2097176
  13.0 0.0 copy-start.2
  13.0 0.7 %copy-done.2 = f32[32,64]{1,0:T(8,128)S(1)} copy-done((f32[32,64]{1,0:T(8,128)S(1)}, f32[32,64]{1,0:T(8,128)}, u32[]{:S(2)}) %copy-start.2) | copy-done | bytes 8216
  13.7 2.8 %power.1._.shells = f32[9,512,128]{2,1,0:T(8,128)S(1)} custom-call(f32[512,1024]{1,0:T(8,128)S(1)} %bitcast.2, f32[32,64,64]{2,1,0:T(8,128)S(1)} %copy-done.1, f32[32,64]{1,0:T(8,128)S(1)} %copy-done.2), custom_call_target="tpu_custom_call" | custom-call | flops 2000000000 | bytes 4194304 | tf_op jit(solution)/shard_map/power/pallas_call | solution.py:339
  16.5 1.2 %all-to-all-done.parts = f32[4,9,8,128]{3,2,1,0:T(8,128)S(1)} async-done(((f32[4,9,8,128]{3,2,1,0:T(8,128)}), f32[4,9,8,128]{3,2,1,0:T(8,128)S(1)}, u32[]{:S(2)}, u32[]{:S(2)}) %all-to-all-start) | async-done | bytes 147488 | tf_op jit(solution)/shard_map/all_to_all | solution.py:305
  17.7 9.3 %all-gather = f32[64,8,128]{2,1,0:T(8,128)S(1)} all-gather(f32[8,8,128]{2,1,0:T(8,128)S(1)} %combine.1), channel_id=2, replica_groups=mesh['cell'=8,'cls'=4] {'cell'}, dimensions={0}, use_global_device_ids=true | all-gather | bytes 294912 | tf_op jit(solution)/shard_map/all_gather | solution.py:363
  27.0 2.5 %finish.1 = (f32[64,8,1024]{2,1,0:T(8,128)}, f32[1,256]{1,0:T(1,128)}) custom-call(f32[8,8,8,128]{3,2,1,0:T(8,128)S(1)} %bitcast.3, f32[9,512,128]{2,1,0:T(8,128)S(1)} %power.1._.shells), custom_call_target="tpu_custom_call" | custom-call | tf_op jit(solution)/shard_map/finish/pallas_call | solution.py:365
  (1 shorter events, 0.0 us)
Async XLA Ops:
  0.6 10.8 %copy-start.1 = (f32[32,64,64]{2,1,0:T(8,128)S(1)}, f32[32,64,64]{2,1,0:T(8,128)}, u32[]{:S(2)}) copy-start(f32[32,64,64]{2,1,0:T(8,128)} %prop_hbm.3) | copy-start | bytes 1572868
  5.1 12.6 %all-to-all-start = ((f32[4,9,8,128]{3,2,1,0:T(8,128)}), f32[4,9,8,128]{3,2,1,0:T(8,128)S(1)}, u32[]{:S(2)}, u32[]{:S(2)}) async-start(f32[4,9,8,128]{3,2,1,0:T(8,128)} %fields.1), calls=%async_computation | async-start | bytes 294912 | tf_op jit(solution)/shard_map/all_to_all | solution.py:305
  11.4 1.6 %copy-start = (f32[64,8,1024]{2,1,0:T(8,128)S(1)}, f32[64,8,1024]{2,1,0:T(8,128)}, u32[]{:S(2)}) copy-start(f32[64,8,1024]{2,1,0:T(8,128)} %melt_hbm.1) | copy-start | bytes 6291460
  13.0 0.7 %copy-start.2 = (f32[32,64]{1,0:T(8,128)S(1)}, f32[32,64]{1,0:T(8,128)}, u32[]{:S(2)}) copy-start(f32[32,64]{1,0:T(8,128)} %coup_hbm.3) | copy-start | bytes 24580

commit v10 on v9

--- a/solution.py
+++ b/solution.py
@@ -59,7 +59,7 @@
 
 
 def fields_kernel(
-    melt_hbm, counts_hbm, pressure_hbm, prop_hbm, coup_hbm, flux_hbm, out, melt, counts, pressure, prop, coup, flux, sems, other_sems
+    melt_hbm, counts_hbm, pressure_hbm, prop_hbm, coup_hbm, flux_hbm, out, melt, highs, lows, counts, pressure, prop, coup, flux, sems, other_sems
 ):
     nodes, classes, cells = melt.shape
     first = param_copies([(prop_hbm, prop), (flux_hbm, flux), (coup_hbm, coup)], other_sems)
@@ -88,11 +88,27 @@
     inverse = 1.0 / scale
     mask = iota((classes, width), 1) // nodes == iota((classes, width), 0)
     rows = [flux[...]]
-    for _ in range(SUBSTEPS):
+    tall = GROUP * classes
+    each = parts // SUBSTEPS
+    for t in range(SUBSTEPS):
         wide = jnp.where(mask, jnp.concatenate([rows[-1]] * classes, axis=1), 0.0)
         pairs = dot(jnp.concatenate(split2(wide), axis=0), table)
         row = pairs[:classes] + pairs[classes:]
         rows.append((row[:, :nodes] + row[:, nodes:]) * inverse)
+        for g in range(t * each, parts if t == SUBSTEPS - 1 else (t + 1) * each):
+            pieces[g].wait()
+            here = slice(g * tall, (g + 1) * tall)
+            highs[here, :], lows[here, :] = split2(
+                melt[g * GROUP : (g + 1) * GROUP].reshape(tall, cells)
+            )
+    spread_out = (iota((nodes, width), 1) // classes == iota((nodes, width), 0)).astype(jnp.bfloat16)
+    parts_of_rows = jnp.concatenate(split2(jnp.concatenate(rows[1:], axis=0)), axis=0)
+    dense = dot(parts_of_rows, spread_out)
+    same = iota(dense.shape, 0) % classes == iota(dense.shape, 1) % classes
+    dense = jnp.where(same, dense, 0.0).astype(jnp.bfloat16)
+    count = SUBSTEPS * classes
+    fluxes = dot(dense, highs[...])
+    fluxes = fluxes[:count] + fluxes[count:] + dot(dense[:count], lows[...])
     spread = [
         grow(jnp.sum(rows[d] * coup[...], axis=1, keepdims=True), scale, d) for d in range(SUBSTEPS)
     ]
@@ -100,24 +116,14 @@
         copy.wait()
     counts_n = counts[...].astype(jnp.float32) / (COUNT_SCALE * CLASSES)
     chunks = cells // LANES
-    sums = [[jnp.zeros((classes, LANES), jnp.float32) for _ in range(chunks)] for _ in range(SUBSTEPS)]
-    for g in range(parts):
-        pieces[g].wait()
-        for j in range(g * GROUP, (g + 1) * GROUP):
-            weights = [
-                jnp.broadcast_to(rows[t + 1][:, j : j + 1], (classes, LANES)) for t in range(SUBSTEPS)
-            ]
-            for r in range(chunks):
-                value = melt[j, :, r * LANES : (r + 1) * LANES]
-                for t in range(SUBSTEPS):
-                    sums[t][r] = sums[t][r] + weights[t] * value
     every = range(out.shape[0])
     for n in every:
         out[n, 2 * SUBSTEPS] = jnp.zeros((chunks, LANES), jnp.float32)
     for r in range(chunks):
         here = counts_n[:, r * LANES : (r + 1) * LANES]
         for t in range(SUBSTEPS):
-            row = jnp.sum(grow(here * sums[t][r], scale, t + 1), axis=0, keepdims=True)
+            part = fluxes[t * classes : (t + 1) * classes, r * LANES : (r + 1) * LANES]
+            row = jnp.sum(grow(here * part, scale, t + 1), axis=0, keepdims=True)
             for n in every:
                 out[n, t, r : r + 1, :] = row
         for d in range(SUBSTEPS):
@@ -325,6 +331,8 @@
         out_specs=VMEM,
         scratch_shapes=[
             pltpu.VMEM(melt.shape, f32),
+            pltpu.VMEM((nodes * classes, cells), jnp.bfloat16),
+            pltpu.VMEM((nodes * classes, cells), jnp.bfloat16),
             pltpu.VMEM(counts.shape, counts.dtype),
             pltpu.VMEM(pressure.shape, f32),
             prop_v,

time: 29.8 us -> 29.3 us (0.983)
  Pallas kernels: 9.69 us -> 9.18 us
    pallas_call x1, Pallas kernels: 4.42 us -> 3.91 us  [shards(): pl.pallas_call(fields_kernel, out_shape=jax.ShapeDtypeStruct((cls_count,...]
where the time goes in v10:
time: 29.3 us; the launch traced here: 29 us
  blocking collectives  9.32 us (32%)
  Pallas kernels  9.18 us (31%)
  starting transfers between devices  6.33 us (22%)
  local copies, waits for them, and re-layouts  2.31 us (8%)
  waiting for transfers between devices  1.17 us (4%)
  between operations  0.66 us (2%)
    all_gather x1, blocking collectives, shards(): window = lax.all_gather(fields, 'cell', axis=0)  9.32 us
    all_to_all x1, starting transfers between devices, exchange(): return lax.all_to_all(copies, axis, split_axis=0, concat_axis=0, tiled=True)  6.33 us
    pallas_call x1, Pallas kernels, shards(): pl.pallas_call(fields_kernel, out_shape=jax.ShapeDtypeStruct((cls_count,...  3.91 us
    pallas_call x1, Pallas kernels, shards(): pl.pallas_call(power_kernel, out_shape=jax.ShapeDtypeStruct((chunks + 1,)...  2.75 us
    pallas_call x1, Pallas kernels, shards(): pl.pallas_call(finish_kernel, out_shape=[jax.ShapeDtypeStruct(melt.shape,...  2.5 us
    unnamed x6, local copies, waits for them, and re-layouts  2.31 us
    all_to_all x1, waiting for transfers between devices, exchange(): return lax.all_to_all(copies, axis, split_axis=0, concat_axis=0, tiled=True)  1.17 us
  transfers between devices with their start and end apart: 1, of which 1 were waited for; matrix products, arithmetic and copies ran while one was open for 0% of the time, Pallas kernels for 9%

profile of v10, /device:TPU:0, one launch (start us, length us, event | category | flops | bytes accessed | tf_op | source)
XLA Modules:
  0.0 29.0 jit_solution(5812977132161840499)
XLA Ops:
  0.6 0.0 copy-start.1
  0.6 3.9 %fields.1 = f32[4,9,8,128]{3,2,1,0:T(8,128)} custom-call(f32[64,8,1024]{2,1,0:T(8,128)} %melt_hbm.1, s32[8,1024]{1,0:T(8,128)} %counts_hbm.1, f32[1,256]{1,0:T(1,128)} %pressure_hbm.1, f32[32,64,64]{2,1,0:T(8,128)} %prop_hbm.3, f32[32,64]{1,0:T(8,128)} %coup_hbm.3, f32[32,64]{1,0:T(8,128)} %flux_hbm.1), custom_call_target="tpu_custom_call" | custom-call | tf_op jit(solution)/shard_map/fields/pallas_call | solution.py:327
  4.6 6.3 %all-to-all-start = ((f32[4,9,8,128]{3,2,1,0:T(8,128)}), f32[4,9,8,128]{3,2,1,0:T(8,128)S(1)}, u32[]{:S(2)}, u32[]{:S(2)}) async-start(f32[4,9,8,128]{3,2,1,0:T(8,128)} %fields.1), calls=%async_computation | async-start | bytes 294912 | tf_op jit(solution)/shard_map/all_to_all | solution.py:311
  10.9 0.0 copy-done.1
  10.9 0.0 copy-start
  10.9 1.6 %copy-done = f32[64,8,1024]{2,1,0:T(8,128)S(1)} copy-done((f32[64,8,1024]{2,1,0:T(8,128)S(1)}, f32[64,8,1024]{2,1,0:T(8,128)}, u32[]{:S(2)}) %copy-start) | copy-done | bytes 2097176
  12.5 0.0 copy-start.2
  12.5 0.7 %copy-done.2 = f32[32,64]{1,0:T(8,128)S(1)} copy-done((f32[32,64]{1,0:T(8,128)S(1)}, f32[32,64]{1,0:T(8,128)}, u32[]{:S(2)}) %copy-start.2) | copy-done | bytes 8216
  13.2 2.8 %power.1._.shells = f32[9,512,128]{2,1,0:T(8,128)S(1)} custom-call(f32[512,1024]{1,0:T(8,128)S(1)} %bitcast.2, f32[32,64,64]{2,1,0:T(8,128)S(1)} %copy-done.1, f32[32,64]{1,0:T(8,128)S(1)} %copy-done.2), custom_call_target="tpu_custom_call" | custom-call | flops 2000000000 | bytes 4194304 | tf_op jit(solution)/shard_map/power/pallas_call | solution.py:347
  16.0 1.2 %all-to-all-done.parts = f32[4,9,8,128]{3,2,1,0:T(8,128)S(1)} async-done(((f32[4,9,8,128]{3,2,1,0:T(8,128)}), f32[4,9,8,128]{3,2,1,0:T(8,128)S(1)}, u32[]{:S(2)}, u32[]{:S(2)}) %all-to-all-start) | async-done | bytes 147488 | tf_op jit(solution)/shard_map/all_to_all | solution.py:311
  17.2 9.3 %all-gather = f32[64,8,128]{2,1,0:T(8,128)S(1)} all-gather(f32[8,8,128]{2,1,0:T(8,128)S(1)} %combine.1), channel_id=2, replica_groups=mesh['cell'=8,'cls'=4] {'cell'}, dimensions={0}, use_global_device_ids=true | all-gather | bytes 294912 | tf_op jit(solution)/shard_map/all_gather | solution.py:371
  26.5 2.5 %finish.1 = (f32[64,8,1024]{2,1,0:T(8,128)}, f32[1,256]{1,0:T(1,128)}) custom-call(f32[8,8,8,128]{3,2,1,0:T(8,128)S(1)} %bitcast.3, f32[9,512,128]{2,1,0:T(8,128)S(1)} %power.1._.shells), custom_call_target="tpu_custom_call" | custom-call | tf_op jit(solution)/shard_map/finish/pallas_call | solution.py:373
  (1 shorter events, 0.0 us)
Async XLA Ops:
  0.6 10.3 %copy-start.1 = (f32[32,64,64]{2,1,0:T(8,128)S(1)}, f32[32,64,64]{2,1,0:T(8,128)}, u32[]{:S(2)}) copy-start(f32[32,64,64]{2,1,0:T(8,128)} %prop_hbm.3) | copy-start | bytes 1572868
  4.6 12.6 %all-to-all-start = ((f32[4,9,8,128]{3,2,1,0:T(8,128)}), f32[4,9,8,128]{3,2,1,0:T(8,128)S(1)}, u32[]{:S(2)}, u32[]{:S(2)}) async-start(f32[4,9,8,128]{3,2,1,0:T(8,128)} %fields.1), calls=%async_computation | async-start | bytes 294912 | tf_op jit(solution)/shard_map/all_to_all | solution.py:311
  10.9 1.6 %copy-start = (f32[64,8,1024]{2,1,0:T(8,128)S(1)}, f32[64,8,1024]{2,1,0:T(8,128)}, u32[]{:S(2)}) copy-start(f32[64,8,1024]{2,1,0:T(8,128)} %melt_hbm.1) | copy-start | bytes 6291460
  12.5 0.7 %copy-start.2 = (f32[32,64]{1,0:T(8,128)S(1)}, f32[32,64]{1,0:T(8,128)}, u32[]{:S(2)}) copy-start(f32[32,64]{1,0:T(8,128)} %coup_hbm.3) | copy-start | bytes 24580

commit v11 on v10

--- a/solution.py
+++ b/solution.py
@@ -13,7 +13,7 @@
 COUNT_SCALE = 400.0
 LANES = 128
 GROUP = 8
-FIELDS = 2 * SUBSTEPS + 1
+FIELDS = 2 * SUBSTEPS
 
 
 def grow(value, factor, times):
@@ -116,27 +116,35 @@
         copy.wait()
     counts_n = counts[...].astype(jnp.float32) / (COUNT_SCALE * CLASSES)
     chunks = cells // LANES
-    every = range(out.shape[0])
-    for n in every:
-        out[n, 2 * SUBSTEPS] = jnp.zeros((chunks, LANES), jnp.float32)
+    targets = range(out.shape[0])
+    per = pressure.shape[1] // LANES
+    tile = pressure.shape[0] * per
+    tail = out.shape[1] - 1
+    total = jnp.zeros((1, LANES), jnp.float32)
+    for n in targets:
+        out[n, tail] = jnp.zeros((chunks, LANES), jnp.float32)
     for r in range(chunks):
         here = counts_n[:, r * LANES : (r + 1) * LANES]
         for t in range(SUBSTEPS):
             part = fluxes[t * classes : (t + 1) * classes, r * LANES : (r + 1) * LANES]
             row = jnp.sum(grow(here * part, scale, t + 1), axis=0, keepdims=True)
-            for n in every:
-                out[n, t, r : r + 1, :] = row
+            if t < SUBSTEPS - 1:
+                for n in targets:
+                    out[n, t, r : r + 1, :] = row
+            else:
+                out[r // tile, tail, r % tile : r % tile + 1, :] = row
+                total = total + row
         for d in range(SUBSTEPS):
             row = jnp.sum(here * spread[d], axis=0, keepdims=True)
-            for n in every:
-                out[n, SUBSTEPS + d, r : r + 1, :] = row
-    per = pressure.shape[1] // LANES
-    tile = pressure.shape[0] * per
-    at = lax.axis_index("cls") * tile
-    for i in range(tile):
-        row = pressure[i // per : i // per + 1, (i % per) * LANES : (i % per + 1) * LANES]
-        for n in every:
-            out[n, 2 * SUBSTEPS, pl.ds(at + i, 1), :] = row
+            for n in targets:
+                out[n, SUBSTEPS - 1 + d, r : r + 1, :] = row
+    total = jnp.broadcast_to(jnp.sum(total, axis=1, keepdims=True), (1, LANES))
+    for n in targets:
+        for i in range(tile):
+            out[n, tail, tile + i : tile + i + 1, :] = pressure[
+                i // per : i // per + 1, (i % per) * LANES : (i % per + 1) * LANES
+            ]
+        out[n, tail, 2 * tile : 2 * tile + 1, :] = total
 
 
 def power_kernel(melt_hbm, prop_hbm, coup_hbm, out, melt, prop, coup, sems, param_sems):
@@ -196,16 +204,25 @@
                 out[r + n, own, :] = part[:, n * LANES : (n + 1) * LANES]
 
 
-def combine_kernel(parts, _, out):
+def combine_kernel(parts, _, out, kept):
+    senders, fields = parts.shape[:2]
+    tail = fields - 1
+    tile = out.shape[1] // senders
     total = parts[0]
-    for n in range(1, parts.shape[0]):
+    for n in range(1, senders):
         total = total + parts[n]
-    wall = 0.5 * total[2 * SUBSTEPS]
-    for t in range(SUBSTEPS):
-        out[t] = total[t] + total[SUBSTEPS + t] * wall
-    for d in range(SUBSTEPS - 1):
-        out[SUBSTEPS + d] = total[SUBSTEPS + d]
-    out[2 * SUBSTEPS - 1] = total[2 * SUBSTEPS]
+    pressure = jnp.concatenate([parts[n, tail, tile : 2 * tile, :] for n in range(senders)], axis=0)
+    wall = 0.5 * pressure
+    for t in range(SUBSTEPS - 1):
+        out[t] = total[t] + total[SUBSTEPS - 1 + t] * wall
+        out[SUBSTEPS - 1 + t] = total[SUBSTEPS - 1 + t]
+    out[tail - 1] = pressure
+    change = total[tail - 1] * wall
+    kept[...] = change
+    own = kept[pl.ds(lax.axis_index("cls") * tile, tile), :]
+    out[tail] = jnp.zeros_like(pressure)
+    out[tail, :tile, :] = total[tail, :tile, :] + own
+    out[tail, tile : tile + 1, :] = total[tail, 2 * tile : 2 * tile + 1, :] + total_of(change)
 
 
 def total_of(x):
@@ -247,22 +264,26 @@
     plane = pressure_out.shape[1]
     blocks = window.shape[0]
     rows = blocks * chunks
+    per = plane // LANES
+    tile = pressure_out.shape[0] * per
 
     def field_of(f):
         return window[:, f].reshape(rows, LANES)
 
-    field = field_of(2 * SUBSTEPS - 1)
-    answer = field_of(SUBSTEPS)
+    field = field_of(2 * SUBSTEPS - 2)
+    answer = field_of(SUBSTEPS - 1)
     answer_total = total_of(answer)
     chamber = None
     walls = []
     for t in range(SUBSTEPS):
-        gas = field_of(t)
+        gas = answer * (0.5 * field) if t else field_of(0)
         for s in range(1, t):
-            gas = gas + field_of(SUBSTEPS + t - s) * walls[s]
-        if t:
-            gas = gas + answer * (0.5 * field)
+            gas = gas + field_of(SUBSTEPS - 1 + t - s) * walls[s]
+        if 0 < t < SUBSTEPS - 1:
+            gas = gas + field_of(t)
         total = total_of(gas)
+        if t == SUBSTEPS - 1:
+            total = total + jnp.sum(window[:, 2 * SUBSTEPS - 1], axis=0)[tile : tile + 1, :1]
         if t:
             field = field + 0.2 * chamber
             gas = gas + answer * (0.1 * chamber)
@@ -274,13 +295,11 @@
     last[...] = field + 0.2 * chamber
     cell = lax.axis_index("cell")
     first = cell * chunks
-    tile = pressure_out.shape[0] * plane // LANES
-    per = plane // LANES
     at = first + lax.axis_index("cls") * tile
     for i in range(tile):
-        pressure_out[i // per : i // per + 1, (i % per) * LANES : (i % per + 1) * LANES] = last[
-            pl.ds(at + i, 1), :
-        ]
+        pressure_out[i // per : i // per + 1, (i % per) * LANES : (i % per + 1) * LANES] = (
+            last[pl.ds(at + i, 1), :] + 0.1 * window[cell, 2 * SUBSTEPS - 1, i : i + 1, :]
+        )
     right = []
     for r in range(chunks):
         wall = jnp.concatenate([walls_all[s, pl.ds(first + r, 1), :] for s in range(SUBSTEPS)], axis=0)
@@ -362,9 +381,10 @@
     )(melt.reshape(nodes * classes, cells), propagator, coupling)
     fields = pl.pallas_call(
         combine_kernel,
-        out_shape=jax.ShapeDtypeStruct((FIELDS - 1, chunks, LANES), f32),
+        out_shape=jax.ShapeDtypeStruct((FIELDS, chunks, LANES), f32),
         in_specs=[VMEM, VMEM],
         out_specs=VMEM,
+        scratch_shapes=[pltpu.VMEM((chunks, LANES), f32)],
         compiler_params=little,
         name="combine",
     )(exchange(packed, "cls"), shells)

time: 29.3 us -> 29.2 us (level)
  local copies, waits for them, and re-layouts: 2.31 us -> 1.59 us
  waiting for transfers between devices: 1.17 us -> 1.71 us
    unnamed x6, local copies, waits for them, and re-layouts: 2.31 us -> 1.59 us
    all_to_all x1, waiting for transfers between devices: 1.17 us -> 1.71 us  [exchange(): return lax.all_to_all(copies, axis, split_axis=0, concat_axis=0, tiled=True)]
  transfers between devices with their start and end apart: 1 -> 1, of which waited for: 1 -> 1; matrix products, arithmetic and copies ran while one was open for 0% -> 0% of each run, Pallas kernels for 9% -> 10%
where the time goes in v11:
time: 29.2 us; the launch traced here: 29 us
  Pallas kernels  9.39 us (32%)
  blocking collectives  9.3 us (32%)
  starting transfers between devices  6.28 us (22%)
  waiting for transfers between devices  1.71 us (6%)
  local copies, waits for them, and re-layouts  1.59 us (5%)
  between operations  0.67 us (2%)
    all_gather x1, blocking collectives, shards(): window = lax.all_gather(fields, 'cell', axis=0)  9.3 us
    all_to_all x1, starting transfers between devices, exchange(): return lax.all_to_all(copies, axis, split_axis=0, concat_axis=0, tiled=True)  6.28 us
    pallas_call x1, Pallas kernels, shards(): pl.pallas_call(fields_kernel, out_shape=jax.ShapeDtypeStruct((cls_count,...  4.03 us
    pallas_call x1, Pallas kernels, shards(): pl.pallas_call(power_kernel, out_shape=jax.ShapeDtypeStruct((chunks + 1,)...  2.76 us
    pallas_call x1, Pallas kernels, shards(): pl.pallas_call(finish_kernel, out_shape=[jax.ShapeDtypeStruct(melt.shape,...  2.51 us
    all_to_all x1, waiting for transfers between devices, exchange(): return lax.all_to_all(copies, axis, split_axis=0, concat_axis=0, tiled=True)  1.71 us
    unnamed x6, local copies, waits for them, and re-layouts  1.59 us
  transfers between devices with their start and end apart: 1, of which 1 were waited for; matrix products, arithmetic and copies ran while one was open for 0% of the time, Pallas kernels for 10%

profile of v11, /device:TPU:0, one launch (start us, length us, event | category | flops | bytes accessed | tf_op | source)
XLA Modules:
  0.0 29.0 jit_solution(3179305512390968511)
XLA Ops:
  0.6 0.0 copy-start.2
  0.6 0.0 copy-start.1
  0.7 4.0 %fields.1 = f32[4,8,8,128]{3,2,1,0:T(8,128)} custom-call(f32[64,8,1024]{2,1,0:T(8,128)} %melt_hbm.1, s32[8,1024]{1,0:T(8,128)} %counts_hbm.1, f32[1,256]{1,0:T(1,128)} %pressure_hbm.1, f32[32,64,64]{2,1,0:T(8,128)} %prop_hbm.3, f32[32,64]{1,0:T(8,128)} %coup_hbm.3, f32[32,64]{1,0:T(8,128)} %flux_hbm.1), custom_call_target="tpu_custom_call" | custom-call | tf_op jit(solution)/shard_map/fields/pallas_call | solution.py:346
  4.7 6.3 %all-to-all-start = ((f32[4,8,8,128]{3,2,1,0:T(8,128)}), f32[4,8,8,128]{3,2,1,0:T(8,128)S(1)}, u32[]{:S(2)}, u32[]{:S(2)}) async-start(f32[4,8,8,128]{3,2,1,0:T(8,128)} %fields.1), calls=%async_computation | async-start | bytes 262144 | tf_op jit(solution)/shard_map/all_to_all | solution.py:330
  11.0 0.0 copy-done.2
  11.0 0.0 copy-done.1
  11.0 0.0 copy-start
  11.0 1.6 %copy-done = f32[64,8,1024]{2,1,0:T(8,128)S(1)} copy-done((f32[64,8,1024]{2,1,0:T(8,128)S(1)}, f32[64,8,1024]{2,1,0:T(8,128)}, u32[]{:S(2)}) %copy-start) | copy-done | bytes 2097176
  12.6 2.8 %power.1._.shells = f32[9,512,128]{2,1,0:T(8,128)S(1)} custom-call(f32[512,1024]{1,0:T(8,128)S(1)} %bitcast.2, f32[32,64,64]{2,1,0:T(8,128)S(1)} %copy-done.1, f32[32,64]{1,0:T(8,128)S(1)} %copy-done.2), custom_call_target="tpu_custom_call" | custom-call | flops 2000000000 | bytes 4194304 | tf_op jit(solution)/shard_map/power/pallas_call | solution.py:366
  15.3 1.7 %all-to-all-done.parts = f32[4,8,8,128]{3,2,1,0:T(8,128)S(1)} async-done(((f32[4,8,8,128]{3,2,1,0:T(8,128)}), f32[4,8,8,128]{3,2,1,0:T(8,128)S(1)}, u32[]{:S(2)}, u32[]{:S(2)}) %all-to-all-start) | async-done | bytes 131104 | tf_op jit(solution)/shard_map/all_to_all | solution.py:330
  17.0 0.1 combine.1
  17.1 9.3 %all-gather = f32[64,8,128]{2,1,0:T(8,128)S(1)} all-gather(f32[8,8,128]{2,1,0:T(8,128)S(1)} %combine.1), channel_id=2, replica_groups=mesh['cell'=8,'cls'=4] {'cell'}, dimensions={0}, use_global_device_ids=true | all-gather | bytes 294912 | tf_op jit(solution)/shard_map/all_gather | solution.py:391
  26.4 2.5 %finish.1 = (f32[64,8,1024]{2,1,0:T(8,128)}, f32[1,256]{1,0:T(1,128)}) custom-call(f32[8,8,8,128]{3,2,1,0:T(8,128)S(1)} %bitcast.3, f32[9,512,128]{2,1,0:T(8,128)S(1)} %power.1._.shells), custom_call_target="tpu_custom_call" | custom-call | tf_op jit(solution)/shard_map/finish/pallas_call | solution.py:393
Async XLA Ops:
  0.6 10.3 %copy-start.2 = (f32[32,64]{1,0:T(8,128)S(1)}, f32[32,64]{1,0:T(8,128)}, u32[]{:S(2)}) copy-start(f32[32,64]{1,0:T(8,128)} %coup_hbm.3) | copy-start | bytes 24580
  0.6 10.3 %copy-start.1 = (f32[32,64,64]{2,1,0:T(8,128)S(1)}, f32[32,64,64]{2,1,0:T(8,128)}, u32[]{:S(2)}) copy-start(f32[32,64,64]{2,1,0:T(8,128)} %prop_hbm.3) | copy-start | bytes 1572868
  4.7 12.4 %all-to-all-start = ((f32[4,8,8,128]{3,2,1,0:T(8,128)}), f32[4,8,8,128]{3,2,1,0:T(8,128)S(1)}, u32[]{:S(2)}, u32[]{:S(2)}) async-start(f32[4,8,8,128]{3,2,1,0:T(8,128)} %fields.1), calls=%async_computation | async-start | bytes 262144 | tf_op jit(solution)/shard_map/all_to_all | solution.py:330
  11.0 1.6 %copy-start = (f32[64,8,1024]{2,1,0:T(8,128)S(1)}, f32[64,8,1024]{2,1,0:T(8,128)}, u32[]{:S(2)}) copy-start(f32[64,8,1024]{2,1,0:T(8,128)} %melt_hbm.1) | copy-start | bytes 6291460

commit v12 on v11

--- a/solution.py
+++ b/solution.py
@@ -116,38 +116,24 @@
         copy.wait()
     counts_n = counts[...].astype(jnp.float32) / (COUNT_SCALE * CLASSES)
     chunks = cells // LANES
-    targets = range(out.shape[0])
-    per = pressure.shape[1] // LANES
-    tile = pressure.shape[0] * per
-    tail = out.shape[1] - 1
-    total = jnp.zeros((1, LANES), jnp.float32)
-    for n in targets:
-        out[n, tail] = jnp.zeros((chunks, LANES), jnp.float32)
     for r in range(chunks):
         here = counts_n[:, r * LANES : (r + 1) * LANES]
         for t in range(SUBSTEPS):
             part = fluxes[t * classes : (t + 1) * classes, r * LANES : (r + 1) * LANES]
-            row = jnp.sum(grow(here * part, scale, t + 1), axis=0, keepdims=True)
-            if t < SUBSTEPS - 1:
-                for n in targets:
-                    out[n, t, r : r + 1, :] = row
-            else:
-                out[r // tile, tail, r % tile : r % tile + 1, :] = row
-                total = total + row
+            out[t, r : r + 1, :] = jnp.sum(grow(here * part, scale, t + 1), axis=0, keepdims=True)
         for d in range(SUBSTEPS):
-            row = jnp.sum(here * spread[d], axis=0, keepdims=True)
-            for n in targets:
-                out[n, SUBSTEPS - 1 + d, r : r + 1, :] = row
-    total = jnp.broadcast_to(jnp.sum(total, axis=1, keepdims=True), (1, LANES))
-    for n in targets:
-        for i in range(tile):
-            out[n, tail, tile + i : tile + i + 1, :] = pressure[
-                i // per : i // per + 1, (i % per) * LANES : (i % per + 1) * LANES
-            ]
-        out[n, tail, 2 * tile : 2 * tile + 1, :] = total
-
-
-def power_kernel(melt_hbm, prop_hbm, coup_hbm, out, melt, prop, coup, sems, param_sems):
+            out[SUBSTEPS + d, r : r + 1, :] = jnp.sum(here * spread[d], axis=0, keepdims=True)
+    out[2 * SUBSTEPS] = jnp.zeros((chunks, LANES), jnp.float32)
+    per = pressure.shape[1] // LANES
+    tile = pressure.shape[0] * per
+    at = lax.axis_index("cls") * tile
+    for i in range(tile):
+        out[2 * SUBSTEPS, pl.ds(at + i, 1), :] = pressure[
+            i // per : i // per + 1, (i % per) * LANES : (i % per + 1) * LANES
+        ]
+
+
+def power_kernel(melt_hbm, prop_hbm, coup_hbm, _, out, melt, prop, coup, sems, param_sems):
     chunks = melt.shape[0]
     classes, nodes = prop.shape[:2]
     params = param_copies([(prop_hbm, prop), (coup_hbm, coup)], param_sems)
@@ -204,25 +190,20 @@
                 out[r + n, own, :] = part[:, n * LANES : (n + 1) * LANES]
 
 
-def combine_kernel(parts, _, out, kept):
-    senders, fields = parts.shape[:2]
-    tail = fields - 1
+def combine_kernel(senders, mine, theirs, _, out, kept):
+    total = mine[...] + theirs[...]
+    tail = out.shape[0] - 1
     tile = out.shape[1] // senders
-    total = parts[0]
-    for n in range(1, senders):
-        total = total + parts[n]
-    pressure = jnp.concatenate([parts[n, tail, tile : 2 * tile, :] for n in range(senders)], axis=0)
+    pressure = total[2 * SUBSTEPS]
     wall = 0.5 * pressure
     for t in range(SUBSTEPS - 1):
-        out[t] = total[t] + total[SUBSTEPS - 1 + t] * wall
-        out[SUBSTEPS - 1 + t] = total[SUBSTEPS - 1 + t]
+        out[t] = total[t] + total[SUBSTEPS + t] * wall
+        out[SUBSTEPS - 1 + t] = total[SUBSTEPS + t]
     out[tail - 1] = pressure
-    change = total[tail - 1] * wall
-    kept[...] = change
-    own = kept[pl.ds(lax.axis_index("cls") * tile, tile), :]
-    out[tail] = jnp.zeros_like(pressure)
-    out[tail, :tile, :] = total[tail, :tile, :] + own
-    out[tail, tile : tile + 1, :] = total[tail, 2 * tile : 2 * tile + 1, :] + total_of(change)
+    gas = total[SUBSTEPS - 1] + total[2 * SUBSTEPS - 1] * wall
+    kept[...] = gas
+    out[tail] = jnp.broadcast_to(total_of(gas), gas.shape)
+    out[tail, :tile, :] = kept[pl.ds(lax.axis_index("cls") * tile, tile), :]
 
 
 def total_of(x):
@@ -326,8 +307,8 @@
 DMA = pltpu.SemaphoreType.DMA
 
 
-def exchange(copies, axis):
-    return lax.all_to_all(copies, axis, split_axis=0, concat_axis=0, tiled=True)
+def partner(value, axis, distance):
+    return lax.ppermute(value, axis, [(i, i ^ distance) for i in range(lax.axis_size(axis))])
 
 
 def shards(melt, counts, pressure, propagator, coupling, flux_weights):
@@ -345,7 +326,7 @@
     parts = nodes // GROUP
     packed = pl.pallas_call(
         fields_kernel,
-        out_shape=jax.ShapeDtypeStruct((cls_count, FIELDS, chunks, LANES), f32),
+        out_shape=jax.ShapeDtypeStruct((FIELDS + 1, chunks, LANES), f32),
         in_specs=[HBM] * 6,
         out_specs=VMEM,
         scratch_shapes=[
@@ -363,10 +344,16 @@
         compiler_params=whole,
         name="fields",
     )(melt, counts, pressure, propagator, coupling, flux_weights)
+    distance = 1
+    theirs = partner(packed, "cls", distance)
+    while 2 * distance < cls_count:
+        distance *= 2
+        packed = packed + theirs
+        theirs = partner(packed, "cls", distance)
     shells = pl.pallas_call(
         power_kernel,
         out_shape=jax.ShapeDtypeStruct((chunks + 1,) + split[1:], f32),
-        in_specs=[HBM] * 3,
+        in_specs=[HBM] * 4,
         out_specs=VMEM,
         scratch_shapes=[
             pltpu.VMEM(split, f32),
@@ -378,16 +365,16 @@
         compiler_params=most,
         cost_estimate=pl.CostEstimate(flops=2 * 10**9, bytes_accessed=2 * melt.size * 4, transcendentals=0),
         name="power",
-    )(melt.reshape(nodes * classes, cells), propagator, coupling)
+    )(melt.reshape(nodes * classes, cells), propagator, coupling, packed)
     fields = pl.pallas_call(
-        combine_kernel,
+        functools.partial(combine_kernel, cls_count),
         out_shape=jax.ShapeDtypeStruct((FIELDS, chunks, LANES), f32),
-        in_specs=[VMEM, VMEM],
+        in_specs=[VMEM, VMEM, VMEM],
         out_specs=VMEM,
         scratch_shapes=[pltpu.VMEM((chunks, LANES), f32)],
         compiler_params=little,
         name="combine",
-    )(exchange(packed, "cls"), shells)
+    )(packed, theirs, shells)
     window = lax.all_gather(fields, "cell", axis=0)
     rows = cell_count * chunks
     return pl.pallas_call(

time: 29.2 us -> 28.5 us (0.976)
  local copies, waits for them, and re-layouts: 1.59 us -> 0.01 us
  other arithmetic: 0 us -> 0.78 us
  waiting for transfers between devices: 1.71 us -> 2.15 us
    all_to_all x1 -> x0, starting transfers between devices: 6.28 us -> none  [exchange(): return lax.all_to_all(copies, axis, split_axis=0, concat_axis=0, tiled=True)]
    ppermute x0 -> x2, starting transfers between devices: none -> 6.11 us  [partner(): lax.ppermute(value, axis, [(i, i ^ distance) for i in range(lax.axis_size...]
    ppermute x0 -> x2, waiting for transfers between devices: none -> 2.15 us  [partner(): lax.ppermute(value, axis, [(i, i ^ distance) for i in range(lax.axis_size...]
    all_to_all x1 -> x0, waiting for transfers between devices: 1.71 us -> none  [exchange(): return lax.all_to_all(copies, axis, split_axis=0, concat_axis=0, tiled=True)]
    unnamed x6, local copies, waits for them, and re-layouts: 1.59 us -> 0.01 us
    add x0 -> x1, other arithmetic: none -> 0.78 us  [shards(): packed = packed + theirs]
  transfers between devices with their start and end apart: 1 -> 2, of which waited for: 1 -> 1; matrix products, arithmetic and copies ran while one was open for 0% -> 0% of each run, Pallas kernels for 10% -> 10%
where the time goes in v12:
time: 28.5 us; the launch traced here: 28.3 us
  Pallas kernels  9.31 us (33%)
  blocking collectives  9.3 us (33%)
  starting transfers between devices  6.11 us (21%)
  waiting for transfers between devices  2.15 us (8%)
  other arithmetic  0.78 us (3%)
  between operations  0.68 us (2%)
    all_gather x1, blocking collectives, shards(): window = lax.all_gather(fields, 'cell', axis=0)  9.3 us
    ppermute x2, starting transfers between devices, partner(): lax.ppermute(value, axis, [(i, i ^ distance) for i in range(lax.axis_size...  6.11 us
    pallas_call x1, Pallas kernels, shards(): pl.pallas_call(fields_kernel, out_shape=jax.ShapeDtypeStruct((FIELDS + 1,...  3.95 us
    pallas_call x1, Pallas kernels, shards(): pl.pallas_call(power_kernel, out_shape=jax.ShapeDtypeStruct((chunks + 1,)...  2.77 us
    pallas_call x1, Pallas kernels, shards(): pl.pallas_call(finish_kernel, out_shape=[jax.ShapeDtypeStruct(melt.shape,...  2.5 us
    ppermute x2, waiting for transfers between devices, partner(): lax.ppermute(value, axis, [(i, i ^ distance) for i in range(lax.axis_size...  2.15 us
    add x1, other arithmetic, shards(): packed = packed + theirs  0.78 us
  transfers between devices with their start and end apart: 2, of which 1 were waited for; matrix products, arithmetic and copies ran while one was open for 0% of the time, Pallas kernels for 10%

profile of v12, /device:TPU:0, one launch (start us, length us, event | category | flops | bytes accessed | tf_op | source)
XLA Modules:
  0.0 28.3 jit_solution(4001063263706713811)
XLA Ops:
  0.6 0.0 copy-start.2
  0.6 0.0 copy-start.1
  0.7 0.0 copy-start
  0.7 3.9 %fields.1 = f32[9,8,128]{2,1,0:T(8,128)} custom-call(f32[64,8,1024]{2,1,0:T(8,128)} %melt_hbm.1, s32[8,1024]{1,0:T(8,128)} %counts_hbm.1, f32[1,256]{1,0:T(1,128)} %pressure_hbm.1, f32[32,64,64]{2,1,0:T(8,128)} %prop_hbm.3, f32[32,64]{1,0:T(8,128)} %coup_hbm.3, f32[32,64]{1,0:T(8,128)} %flux_hbm.1), custom_call_target="tpu_custom_call" | custom-call | tf_op jit(solution)/shard_map/fields/pallas_call | solution.py:327
  4.6 3.1 %collective-permute-start = (f32[9,8,128]{2,1,0:T(8,128)}, f32[9,8,128]{2,1,0:T(8,128)S(1)}, u32[]{:S(2)}, u32[]{:S(2)}) collective-permute-start(f32[9,8,128]{2,1,0:T(8,128)} %fields.1), channel_id=1, source_target_pairs={{0,1},{1,0},{2,3},{3,2},{4,5},{5,4},{6,7},{7,6},{8,9},{9,8},{10,11... | collective-permute-start | bytes 110600 | tf_op jit(solution)/shard_map/ppermute | solution.py:311
  7.7 2.1 %collective-permute-done = f32[9,8,128]{2,1,0:T(8,128)S(1)} collective-permute-done((f32[9,8,128]{2,1,0:T(8,128)}, f32[9,8,128]{2,1,0:T(8,128)S(1)}, u32[]{:S(2)}, u32[]{:S(2)}) %collective-permute-start) | collective-permute-done | bytes 36896 | tf_op jit(solution)/shard_map/ppermute | solution.py:311
  9.8 0.8 %add.3._.mine = f32[9,8,128]{2,1,0:T(8,128)S(1)} add(f32[9,8,128]{2,1,0:T(8,128)} %fields.1, f32[9,8,128]{2,1,0:T(8,128)S(1)} %collective-permute-done) | non-fusion elementwise | flops 9216 | bytes 110592 | tf_op jit(solution)/shard_map/add | solution.py:351
  10.6 3.0 %collective-permute-start.1 = (f32[9,8,128]{2,1,0:T(8,128)S(1)}, f32[9,8,128]{2,1,0:T(8,128)S(1)}, u32[]{:S(2)}, u32[]{:S(2)}) collective-permute-start(f32[9,8,128]{2,1,0:T(8,128)S(1)} %add.3._.mine), channel_id=1, source_target_pairs={{0,2},{1,3},{2,0},{3,1},{4,6},{5,7},{6,4},{7,5},{8,10},{9,11},{10,... | collective-permute-start | bytes 110600 | tf_op jit(solution)/shard_map/ppermute | solution.py:311
  13.6 0.0 copy-done.2
  13.7 0.0 copy-done.1
  13.7 0.0 copy-done
  13.7 2.8 %power.1._.shells = f32[9,512,128]{2,1,0:T(8,128)S(1)} custom-call(f32[512,1024]{1,0:T(8,128)S(1)} %bitcast.2, f32[32,64,64]{2,1,0:T(8,128)S(1)} %copy-done.1, f32[32,64]{1,0:T(8,128)S(1)} %copy-done.2, f32[9,8,128]{2,1,0:T(8,128)S(1)} %add.3._.mine), custom_call_target="tpu_custom_call" | custom-call | flops 2000000000 | bytes 4194304 | tf_op jit(solution)/shard_map/power/pallas_call | solution.py:353
  16.4 0.0 collective-permute-done.1.theirs
  16.4 0.1 combine.1
  16.5 9.3 %all-gather = f32[64,8,128]{2,1,0:T(8,128)S(1)} all-gather(f32[8,8,128]{2,1,0:T(8,128)S(1)} %combine.1), channel_id=2, replica_groups=mesh['cell'=8,'cls'=4] {'cell'}, dimensions={0}, use_global_device_ids=true | all-gather | bytes 294912 | tf_op jit(solution)/shard_map/all_gather | solution.py:378
  25.8 2.5 %finish.1 = (f32[64,8,1024]{2,1,0:T(8,128)}, f32[1,256]{1,0:T(1,128)}) custom-call(f32[8,8,8,128]{3,2,1,0:T(8,128)S(1)} %bitcast.3, f32[9,512,128]{2,1,0:T(8,128)S(1)} %power.1._.shells), custom_call_target="tpu_custom_call" | custom-call | tf_op jit(solution)/shard_map/finish/pallas_call | solution.py:380
Async XLA Ops:
  0.6 13.0 %copy-start.2 = (f32[32,64]{1,0:T(8,128)S(1)}, f32[32,64]{1,0:T(8,128)}, u32[]{:S(2)}) copy-start(f32[32,64]{1,0:T(8,128)} %coup_hbm.3) | copy-start | bytes 24580
  0.6 13.0 %copy-start.1 = (f32[32,64,64]{2,1,0:T(8,128)S(1)}, f32[32,64,64]{2,1,0:T(8,128)}, u32[]{:S(2)}) copy-start(f32[32,64,64]{2,1,0:T(8,128)} %prop_hbm.3) | copy-start | bytes 1572868
  0.7 13.0 %copy-start = (f32[64,8,1024]{2,1,0:T(8,128)S(1)}, f32[64,8,1024]{2,1,0:T(8,128)}, u32[]{:S(2)}) copy-start(f32[64,8,1024]{2,1,0:T(8,128)} %melt_hbm.1) | copy-start | bytes 6291460
  4.6 5.2 %collective-permute-start = (f32[9,8,128]{2,1,0:T(8,128)}, f32[9,8,128]{2,1,0:T(8,128)S(1)}, u32[]{:S(2)}, u32[]{:S(2)}) collective-permute-start(f32[9,8,128]{2,1,0:T(8,128)} %fields.1), channel_id=1, source_target_pairs={{0,1},{1,0},{2,3},{3,2},{4,5},{5,4},{6,7},{7,6},{8,9},{9,8},{10,11... | collective-permute-start | bytes 110600 | tf_op jit(solution)/shard_map/ppermute | solution.py:311
  10.6 5.8 %collective-permute-start.1 = (f32[9,8,128]{2,1,0:T(8,128)S(1)}, f32[9,8,128]{2,1,0:T(8,128)S(1)}, u32[]{:S(2)}, u32[]{:S(2)}) collective-permute-start(f32[9,8,128]{2,1,0:T(8,128)S(1)} %add.3._.mine), channel_id=1, source_target_pairs={{0,2},{1,3},{2,0},{3,1},{4,6},{5,7},{6,4},{7,5},{8,10},{9,11},{10,... | collective-permute-start | bytes 110600 | tf_op jit(solution)/shard_map/ppermute | solution.py:311

commit v13 on v12

--- a/solution.py
+++ b/solution.py
@@ -133,29 +133,23 @@
         ]
 
 
-def power_kernel(melt_hbm, prop_hbm, coup_hbm, _, out, melt, prop, coup, sems, param_sems):
-    chunks = melt.shape[0]
+def powers_kernel(prop_hbm, coup_hbm, _, lefts, columns, factors, prop, coup, param_sems):
     classes, nodes = prop.shape[:2]
     params = param_copies([(prop_hbm, prop), (coup_hbm, coup)], param_sems)
     for copy in params:
         copy.start()
-    loads = [
-        pltpu.make_async_copy(melt_hbm.at[:, pl.ds(r * LANES, LANES)], melt.at[r], sems.at[r])
-        for r in range(chunks)
-    ]
-    for load in loads:
-        load.start()
     for copy in params:
         copy.wait()
     scale = class_scale(prop)
+    factors[...] = jnp.broadcast_to(scale, factors.shape)
     inverse = 1.0 / scale
     every = range(classes)
-    factors = [scale[k : k + 1, :] for k in every]
     unit = [prop[k] * inverse[k : k + 1, :] for k in every]
     first = [left_of(unit[k]) for k in every]
     square = [dot(first[k], right_of(unit[k])) for k in every]
     second = [left_of(square[k]) for k in every]
-    lefts = [left_of(dot(second[k], right_of(square[k]))) for k in every]
+    for k in every:
+        lefts[k] = left_of(dot(second[k], right_of(square[k])))
     start = jnp.concatenate(
         [jnp.transpose(coup[...]), jnp.zeros((nodes, LANES - classes), jnp.float32)], axis=1
     )
@@ -174,20 +168,36 @@
         ]
         value = jnp.zeros((nodes, LANES), jnp.float32)
         for d in range(SUBSTEPS):
-            value = jnp.where(lane % SUBSTEPS == SUBSTEPS - 1 - d, grow(powers[d], factors[k], d), value)
+            grown = grow(powers[d], scale[k : k + 1, :], d)
+            value = jnp.where(lane % SUBSTEPS == SUBSTEPS - 1 - d, grown, value)
         high = value.astype(jnp.bfloat16).astype(jnp.float32)
         value = jnp.where(lane < 2 * SUBSTEPS, high, jnp.where(lane < 3 * SUBSTEPS, value - high, 0.0))
-        out[chunks, pl.ds(k, nodes, stride=classes), :] = value
+        columns[pl.ds(k, nodes, stride=classes), :] = value
+
+
+def apply_kernel(melt_hbm, lefts, factors, _, out, melt, sems):
+    chunks = melt.shape[0]
+    classes, nodes = lefts.shape[:2]
+    loads = [
+        pltpu.make_async_copy(melt_hbm.at[:, pl.ds(r * LANES, LANES)], melt.at[r], sems.at[r])
+        for r in range(chunks)
+    ]
+    for load in loads:
+        load.start()
     together = 2 if chunks % 2 == 0 else 1
     for r in range(0, chunks, together):
         for n in range(together):
             loads[r + n].wait()
-        for k in every:
+        for k in range(classes):
             own = pl.ds(k, nodes, stride=classes)
             x = jnp.concatenate([melt[r + n, own, :] for n in range(together)], axis=1)
-            part = grow(dot(lefts[k], right_of(x)), factors[k], SUBSTEPS)
+            part = grow(dot(lefts[k], right_of(x)), factors[k : k + 1, :1], SUBSTEPS)
             for n in range(together):
                 out[r + n, own, :] = part[:, n * LANES : (n + 1) * LANES]
+
+
+def add_kernel(mine, theirs, _, out):
+    out[...] = mine[...] + theirs[...]
 
 
 def combine_kernel(senders, mine, theirs, _, out, kept):
@@ -232,7 +242,7 @@
 
 
 def finish_kernel(
-    window, shells, out_hbm, pressure_out, out, walls_all, last, out_sems
+    window, shells, columns, out_hbm, pressure_out, out, walls_all, last, out_sems
 ):
     nodes, classes, cells = out.shape
     chunks = cells // LANES
@@ -292,7 +302,7 @@
     ]
     for g in range(parts):
         here = slice(g * width, (g + 1) * width)
-        change = dot(shells[chunks, here, : 4 * SUBSTEPS].astype(jnp.bfloat16), right)
+        change = dot(columns[here, : 4 * SUBSTEPS].astype(jnp.bfloat16), right)
         for r in range(chunks):
             lanes = slice(r * LANES, (r + 1) * LANES)
             value = shells[r, here, :] + change[:, lanes]
@@ -344,28 +354,45 @@
         compiler_params=whole,
         name="fields",
     )(melt, counts, pressure, propagator, coupling, flux_weights)
+    lefts_shape = (classes, nodes, 3 * nodes)
+    theirs = partner(packed, "cls", 1)
+    lefts, columns, factors = pl.pallas_call(
+        powers_kernel,
+        out_shape=[
+            jax.ShapeDtypeStruct(lefts_shape, jnp.bfloat16),
+            jax.ShapeDtypeStruct(split[1:], f32),
+            jax.ShapeDtypeStruct((classes, LANES), f32),
+        ],
+        in_specs=[HBM, HBM, VMEM],
+        out_specs=[VMEM] * 3,
+        scratch_shapes=[prop_v, small, DMA((2,))],
+        compiler_params=most,
+        cost_estimate=pl.CostEstimate(flops=10**9, bytes_accessed=10**6, transcendentals=0),
+        name="powers",
+    )(propagator, coupling, packed)
     distance = 1
-    theirs = partner(packed, "cls", distance)
+    after = factors
     while 2 * distance < cls_count:
         distance *= 2
-        packed = packed + theirs
+        packed = pl.pallas_call(
+            add_kernel,
+            out_shape=jax.ShapeDtypeStruct(packed.shape, f32),
+            in_specs=[VMEM] * 3,
+            out_specs=VMEM,
+            compiler_params=little,
+            name="add",
+        )(packed, theirs, after)
         theirs = partner(packed, "cls", distance)
     shells = pl.pallas_call(
-        power_kernel,
-        out_shape=jax.ShapeDtypeStruct((chunks + 1,) + split[1:], f32),
-        in_specs=[HBM] * 4,
+        apply_kernel,
+        out_shape=jax.ShapeDtypeStruct(split, f32),
+        in_specs=[HBM, VMEM, VMEM, VMEM],
         out_specs=VMEM,
-        scratch_shapes=[
-            pltpu.VMEM(split, f32),
-            prop_v,
-            small,
-            DMA((chunks,)),
-            DMA((2,)),
-        ],
+        scratch_shapes=[pltpu.VMEM(split, f32), DMA((chunks,))],
         compiler_params=most,
-        cost_estimate=pl.CostEstimate(flops=2 * 10**9, bytes_accessed=2 * melt.size * 4, transcendentals=0),
-        name="power",
-    )(melt.reshape(nodes * classes, cells), propagator, coupling, packed)
+        cost_estimate=pl.CostEstimate(flops=10**9, bytes_accessed=melt.size * 4, transcendentals=0),
+        name="apply",
+    )(melt.reshape(nodes * classes, cells), lefts, factors, packed)
     fields = pl.pallas_call(
         functools.partial(combine_kernel, cls_count),
         out_shape=jax.ShapeDtypeStruct((FIELDS, chunks, LANES), f32),
@@ -380,7 +407,7 @@
     return pl.pallas_call(
         finish_kernel,
         out_shape=[jax.ShapeDtypeStruct(melt.shape, f32), jax.ShapeDtypeStruct(pressure.shape, f32)],
-        in_specs=[VMEM, VMEM],
+        in_specs=[VMEM, VMEM, VMEM],
         out_specs=[HBM, VMEM],
         scratch_shapes=[
             pltpu.VMEM(melt.shape, f32),
@@ -390,7 +417,7 @@
         ],
         compiler_params=little,
         name="finish",
-    )(window, shells)
+    )(window, shells, columns)
 
 
 def solution(mesh):

time: 28.5 us -> 27.3 us (0.958)
  waiting for transfers between devices: 2.15 us -> 0.5 us
  local copies, waits for them, and re-layouts: 0.01 us -> 0.81 us
  other arithmetic: 0.78 us -> 0 us
  blocking collectives: 9.3 us -> 9.68 us
    ppermute x2, waiting for transfers between devices: 2.15 us -> 0.5 us  [partner(): lax.ppermute(value, axis, [(i, i ^ distance) for i in range(lax.axis_size...]
    unnamed x6 -> x10, local copies, waits for them, and re-layouts: 0.01 us -> 0.81 us
    add x1 -> x0, other arithmetic: 0.78 us -> none  [shards(): packed = packed + theirs]
    all_gather x1, blocking collectives: 9.3 us -> 9.68 us  [shards(): window = lax.all_gather(fields, 'cell', axis=0)]
    pallas_call x1 -> x3, Pallas kernels: 2.77 us -> 2.77 us  [the longest x1 1.51 us: shards(): pl.pallas_call(apply_kernel, out_shape=jax.ShapeDtypeStruct(split, f32),...]
  transfers between devices with their start and end apart: 2 -> 2, of which waited for: 1 -> 2; matrix products, arithmetic and copies ran while one was open for 0% -> 0% of each run, Pallas kernels for 10% -> 10%
where the time goes in v13:
time: 27.3 us; the launch traced here: 27.1 us
  blocking collectives  9.68 us (35%)
  Pallas kernels  9.28 us (34%)
  starting transfers between devices  6.14 us (22%)
  local copies, waits for them, and re-layouts  0.81 us (3%)
  between operations  0.69 us (3%)
  waiting for transfers between devices  0.5 us (2%)
    all_gather x1, blocking collectives, shards(): window = lax.all_gather(fields, 'cell', axis=0)  9.68 us
    ppermute x2, starting transfers between devices, partner(): lax.ppermute(value, axis, [(i, i ^ distance) for i in range(lax.axis_size...  6.14 us
    pallas_call x1, Pallas kernels, shards(): pl.pallas_call(fields_kernel, out_shape=jax.ShapeDtypeStruct((FIELDS + 1,...  3.92 us
    pallas_call x1, Pallas kernels, shards(): pl.pallas_call(finish_kernel, out_shape=[jax.ShapeDtypeStruct(melt.shape,...  2.51 us
    pallas_call x1, Pallas kernels, shards(): pl.pallas_call(apply_kernel, out_shape=jax.ShapeDtypeStruct(split, f32),...  1.51 us
    pallas_call x1, Pallas kernels, shards(): pl.pallas_call(powers_kernel, out_shape=[jax.ShapeDtypeStruct(lefts_shape...  1.25 us
    unnamed x10, local copies, waits for them, and re-layouts  0.81 us
  transfers between devices with their start and end apart: 2, of which 2 were waited for; matrix products, arithmetic and copies ran while one was open for 0% of the time, Pallas kernels for 10%

profile of v13, /device:TPU:0, one launch (start us, length us, event | category | flops | bytes accessed | tf_op | source)
XLA Modules:
  0.0 27.1 jit_solution(16084877637007450412)
XLA Ops:
  0.6 0.0 copy-start.4
  0.6 0.0 copy-start.1
  0.7 3.9 %fields.1._.mine = f32[9,8,128]{2,1,0:T(8,128)} custom-call(f32[64,8,1024]{2,1,0:T(8,128)} %melt_hbm.1, s32[8,1024]{1,0:T(8,128)} %counts_hbm.1, f32[1,256]{1,0:T(1,128)} %pressure_hbm.1, f32[32,64,64]{2,1,0:T(8,128)} %prop_hbm.3, f32[32,64]{1,0:T(8,128)} %coup_hbm.3, f32[32,64]{1,0:T(8,128)} %flux_hbm.1), custom_call_target="tpu_custom_call" | custom-call | tf_op jit(solution)/shard_map/fields/pallas_call | solution.py:337
  4.6 0.0 copy-start
  4.6 3.0 %collective-permute-start = (f32[9,8,128]{2,1,0:T(8,128)}, f32[9,8,128]{2,1,0:T(8,128)S(1)}, u32[]{:S(2)}, u32[]{:S(2)}) collective-permute-start(f32[9,8,128]{2,1,0:T(8,128)} %fields.1._.mine), channel_id=1, source_target_pairs={{0,1},{1,0},{2,3},{3,2},{4,5},{5,4},{6,7},{7,6},{8,9},{9,8},{10,11... | collective-permute-start | bytes 110600 | tf_op jit(solution)/shard_map/ppermute | solution.py:321
  7.6 0.0 copy-done.4
  7.6 0.0 copy-done.1
  7.6 0.0 copy-start.2
  7.6 0.8 %copy-done.2 = f32[9,8,128]{2,1,0:T(8,128)S(1)} copy-done((f32[9,8,128]{2,1,0:T(8,128)S(1)}, f32[9,8,128]{2,1,0:T(8,128)}, u32[]{:S(2)}) %copy-start.2) | copy-done | bytes 36888
  8.4 0.0 copy-start.3
  8.4 1.3 %powers.1 = (bf16[8,64,192]{2,1,0:T(8,128)(2,1)S(1)}, f32[512,128]{1,0:T(8,128)S(1)}, f32[8,128]{1,0:T(8,128)S(1)}) custom-call(f32[32,64,64]{2,1,0:T(8,128)S(1)} %copy-done.1, f32[32,64]{1,0:T(8,128)S(1)} %copy-done.4, f32[9,8,128]{2,1,0:T(8,128)S(1)} %copy-done.2), custom_call_target="tpu_custom_call" | custom-call | flops 1000000000 | bytes 1000000 | tf_op jit(solution)/shard_map/powers/pallas_call | solution.py:359
  9.7 0.1 collective-permute-done.theirs
  9.8 0.0 copy-done.3
  9.8 3.1 %collective-permute-start.1 = (f32[9,8,128]{2,1,0:T(8,128)S(1)}, f32[9,8,128]{2,1,0:T(8,128)S(1)}, u32[]{:S(2)}, u32[]{:S(2)}) collective-permute-start(f32[9,8,128]{2,1,0:T(8,128)S(1)} %add.1._.mine), channel_id=1, source_target_pairs={{0,2},{1,3},{2,0},{3,1},{4,6},{5,7},{6,4},{7,5},{8,10},{9,11},{10,... | collective-permute-start | bytes 110600 | tf_op jit(solution)/shard_map/ppermute | solution.py:321
  12.9 0.0 copy-done
  12.9 1.5 %apply.1._.shells = f32[8,512,128]{2,1,0:T(8,128)S(1)} custom-call(f32[512,1024]{1,0:T(8,128)S(1)} %bitcast.2, bf16[8,64,192]{2,1,0:T(8,128)(2,1)S(1)} %get-tuple-element.6.lefts, f32[8,128]{1,0:T(8,128)S(1)} %get-tuple-element.5._.factors, f32[9,8,128]{2,1,0:T(8,128)S(1)} %add.1._.mine), custom_call_target="tpu_custom_call" | custom-call | flops 1000000000 | bytes 2097152 | tf_op jit(solution)/shard_map/apply/pallas_call | solution.py:386
  14.4 0.4 %collective-permute-done.1.theirs = f32[9,8,128]{2,1,0:T(8,128)S(1)} collective-permute-done((f32[9,8,128]{2,1,0:T(8,128)S(1)}, f32[9,8,128]{2,1,0:T(8,128)S(1)}, u32[]{:S(2)}, u32[]{:S(2)}) %collective-permute-start.1) | collective-permute-done | bytes 36896 | tf_op jit(solution)/shard_map/ppermute | solution.py:321
  14.8 0.1 combine.1
  14.9 9.7 %all-gather = f32[64,8,128]{2,1,0:T(8,128)S(1)} all-gather(f32[8,8,128]{2,1,0:T(8,128)S(1)} %combine.1), channel_id=2, replica_groups=mesh['cell'=8,'cls'=4] {'cell'}, dimensions={0}, use_global_device_ids=true | all-gather | bytes 294912 | tf_op jit(solution)/shard_map/all_gather | solution.py:405
  24.6 2.5 %finish.1 = (f32[64,8,1024]{2,1,0:T(8,128)}, f32[1,256]{1,0:T(1,128)}) custom-call(f32[8,8,8,128]{3,2,1,0:T(8,128)S(1)} %bitcast.3, f32[8,512,128]{2,1,0:T(8,128)S(1)} %apply.1._.shells, f32[512,128]{1,0:T(8,128)S(1)} %get-tuple-element.7.columns), custom_call_target="tpu_custom_call" | custom-call | tf_op jit(solution)/shard_map/finish/pallas_call | solution.py:407
  (1 shorter events, 0.0 us)
Async XLA Ops:
  0.6 7.0 %copy-start.4 = (f32[32,64]{1,0:T(8,128)S(1)}, f32[32,64]{1,0:T(8,128)}, u32[]{:S(2)}) copy-start(f32[32,64]{1,0:T(8,128)} %coup_hbm.3) | copy-start | bytes 24580
  0.6 7.0 %copy-start.1 = (f32[32,64,64]{2,1,0:T(8,128)S(1)}, f32[32,64,64]{2,1,0:T(8,128)}, u32[]{:S(2)}) copy-start(f32[32,64,64]{2,1,0:T(8,128)} %prop_hbm.3) | copy-start | bytes 1572868
  4.6 8.3 %copy-start = (f32[64,8,1024]{2,1,0:T(8,128)S(1)}, f32[64,8,1024]{2,1,0:T(8,128)}, u32[]{:S(2)}) copy-start(f32[64,8,1024]{2,1,0:T(8,128)} %melt_hbm.1) | copy-start | bytes 6291460
  4.6 5.2 %collective-permute-start = (f32[9,8,128]{2,1,0:T(8,128)}, f32[9,8,128]{2,1,0:T(8,128)S(1)}, u32[]{:S(2)}, u32[]{:S(2)}) collective-permute-start(f32[9,8,128]{2,1,0:T(8,128)} %fields.1._.mine), channel_id=1, source_target_pairs={{0,1},{1,0},{2,3},{3,2},{4,5},{5,4},{6,7},{7,6},{8,9},{9,8},{10,11... | collective-permute-start | bytes 110600 | tf_op jit(solution)/shard_map/ppermute | solution.py:321
  7.6 0.8 %copy-start.2 = (f32[9,8,128]{2,1,0:T(8,128)S(1)}, f32[9,8,128]{2,1,0:T(8,128)}, u32[]{:S(2)}) copy-start(f32[9,8,128]{2,1,0:T(8,128)} %fields.1._.mine) | copy-start | bytes 110596
  8.4 1.3 %copy-start.3 = (f32[9,8,128]{2,1,0:T(8,128)S(1)}, f32[9,8,128]{2,1,0:T(8,128)}, u32[]{:S(2)}) copy-start(f32[9,8,128]{2,1,0:T(8,128)} %fields.1._.mine) | copy-start | bytes 110596
  9.8 5.0 %collective-permute-start.1 = (f32[9,8,128]{2,1,0:T(8,128)S(1)}, f32[9,8,128]{2,1,0:T(8,128)S(1)}, u32[]{:S(2)}, u32[]{:S(2)}) collective-permute-start(f32[9,8,128]{2,1,0:T(8,128)S(1)} %add.1._.mine), channel_id=1, source_target_pairs={{0,2},{1,3},{2,0},{3,1},{4,6},{5,7},{6,4},{7,5},{8,10},{9,11},{10,... | collective-permute-start | bytes 110600 | tf_op jit(solution)/shard_map/ppermute | solution.py:321

commit v14 on v13

--- a/solution.py
+++ b/solution.py
@@ -242,7 +242,7 @@
 
 
 def finish_kernel(
-    window, shells, columns, out_hbm, pressure_out, out, walls_all, last, out_sems
+    mine, theirs, shells, columns, out_hbm, pressure_out, out, walls_all, last, out_sems
 ):
     nodes, classes, cells = out.shape
     chunks = cells // LANES
@@ -253,13 +253,17 @@
         return pl.ds(g * GROUP, GROUP)
 
     plane = pressure_out.shape[1]
-    blocks = window.shape[0]
+    cell = lax.axis_index("cell")
+    even = cell % 2 == 0
+    blocks = 2 * mine.shape[0]
     rows = blocks * chunks
     per = plane // LANES
     tile = pressure_out.shape[0] * per
 
     def field_of(f):
-        return window[:, f].reshape(rows, LANES)
+        first, second = mine[:, f], theirs[:, f]
+        low, high = jnp.where(even, first, second), jnp.where(even, second, first)
+        return jnp.stack([low, high], axis=1).reshape(rows, LANES)
 
     field = field_of(2 * SUBSTEPS - 2)
     answer = field_of(SUBSTEPS - 1)
@@ -274,7 +278,8 @@
             gas = gas + field_of(t)
         total = total_of(gas)
         if t == SUBSTEPS - 1:
-            total = total + jnp.sum(window[:, 2 * SUBSTEPS - 1], axis=0)[tile : tile + 1, :1]
+            rest = jnp.sum(mine[:, 2 * SUBSTEPS - 1] + theirs[:, 2 * SUBSTEPS - 1], axis=0)
+            total = total + rest[tile : tile + 1, :1]
         if t:
             field = field + 0.2 * chamber
             gas = gas + answer * (0.1 * chamber)
@@ -284,12 +289,11 @@
         field = 0.8 * field + 0.15 * laplacian(field, plane) + 0.1 * gas
         chamber = 1.5 - 0.5 * total / (rows * LANES)
     last[...] = field + 0.2 * chamber
-    cell = lax.axis_index("cell")
     first = cell * chunks
     at = first + lax.axis_index("cls") * tile
     for i in range(tile):
         pressure_out[i // per : i // per + 1, (i % per) * LANES : (i % per + 1) * LANES] = (
-            last[pl.ds(at + i, 1), :] + 0.1 * window[cell, 2 * SUBSTEPS - 1, i : i + 1, :]
+            last[pl.ds(at + i, 1), :] + 0.1 * mine[cell // 2, 2 * SUBSTEPS - 1, i : i + 1, :]
         )
     right = []
     for r in range(chunks):
@@ -402,12 +406,14 @@
         compiler_params=little,
         name="combine",
     )(packed, theirs, shells)
-    window = lax.all_gather(fields, "cell", axis=0)
+    groups = [list(range(core, cell_count, 2)) for core in range(2)]
+    own = lax.all_gather(fields, "cell", axis=0, axis_index_groups=groups)
+    other = partner(own, "cell", 1)
     rows = cell_count * chunks
     return pl.pallas_call(
         finish_kernel,
         out_shape=[jax.ShapeDtypeStruct(melt.shape, f32), jax.ShapeDtypeStruct(pressure.shape, f32)],
-        in_specs=[VMEM, VMEM, VMEM],
+        in_specs=[VMEM] * 4,
         out_specs=[HBM, VMEM],
         scratch_shapes=[
             pltpu.VMEM(melt.shape, f32),
@@ -417,7 +423,7 @@
         ],
         compiler_params=little,
         name="finish",
-    )(window, shells, columns)
+    )(own, other, shells, columns)
 
 
 def solution(mesh):

time: 27.3 us -> 27.8 us (1.018)
  waiting for transfers between devices: 0.5 us -> 1.84 us
  blocking collectives: 9.68 us -> 8.84 us
    ppermute x2 -> x3, waiting for transfers between devices: 0.5 us -> 1.84 us  [partner(): lax.ppermute(value, axis, [(i, i ^ distance) for i in range(lax.axis_size...]
    all_gather x1, blocking collectives: 9.68 us -> 8.84 us  [shards(): own = lax.all_gather(fields, 'cell', axis=0, axis_index_groups=groups)]
    ppermute x2 -> x3, starting transfers between devices: 6.14 us -> 6.08 us  [partner(): lax.ppermute(value, axis, [(i, i ^ distance) for i in range(lax.axis_size...]
    unnamed x10 -> x8, local copies, waits for them, and re-layouts: 0.81 us -> 0.81 us
  transfers between devices with their start and end apart: 2 -> 3, of which waited for: 2 -> 3; matrix products, arithmetic and copies ran while one was open for 0% -> 0% of each run, Pallas kernels for 10% -> 10%
where the time goes in v14:
time: 27.8 us; the launch traced here: 27.6 us
  Pallas kernels  9.3 us (33%)
  blocking collectives  8.84 us (32%)
  starting transfers between devices  6.08 us (22%)
  waiting for transfers between devices  1.84 us (7%)
  local copies, waits for them, and re-layouts  0.81 us (3%)
  between operations  0.69 us (2%)
    all_gather x1, blocking collectives, shards(): own = lax.all_gather(fields, 'cell', axis=0, axis_index_groups=groups)  8.84 us
    ppermute x3, starting transfers between devices, partner(): lax.ppermute(value, axis, [(i, i ^ distance) for i in range(lax.axis_size...  6.08 us
    pallas_call x1, Pallas kernels, shards(): pl.pallas_call(fields_kernel, out_shape=jax.ShapeDtypeStruct((FIELDS + 1,...  3.92 us
    pallas_call x1, Pallas kernels, shards(): pl.pallas_call(finish_kernel, out_shape=[jax.ShapeDtypeStruct(melt.shape,...  2.52 us
    ppermute x3, waiting for transfers between devices, partner(): lax.ppermute(value, axis, [(i, i ^ distance) for i in range(lax.axis_size...  1.84 us
    pallas_call x1, Pallas kernels, shards(): pl.pallas_call(apply_kernel, out_shape=jax.ShapeDtypeStruct(split, f32),...  1.51 us
    pallas_call x1, Pallas kernels, shards(): pl.pallas_call(powers_kernel, out_shape=[jax.ShapeDtypeStruct(lefts_shape...  1.25 us
    unnamed x8, local copies, waits for them, and re-layouts  0.81 us
  transfers between devices with their start and end apart: 3, of which 3 were waited for; matrix products, arithmetic and copies ran while one was open for 0% of the time, Pallas kernels for 10%

profile of v14, /device:TPU:0, one launch (start us, length us, event | category | flops | bytes accessed | tf_op | source)
XLA Modules:
  0.0 27.6 jit_solution(14858512081667926293)
XLA Ops:
  0.6 0.0 copy-start.3
  0.6 0.0 copy-start.1
  0.7 3.9 %fields.1._.mine = f32[9,8,128]{2,1,0:T(8,128)} custom-call(f32[64,8,1024]{2,1,0:T(8,128)} %melt_hbm.1, s32[8,1024]{1,0:T(8,128)} %counts_hbm.1, f32[1,256]{1,0:T(1,128)} %pressure_hbm.1, f32[32,64,64]{2,1,0:T(8,128)} %prop_hbm.3, f32[32,64]{1,0:T(8,128)} %coup_hbm.3, f32[32,64]{1,0:T(8,128)} %flux_hbm.1), custom_call_target="tpu_custom_call" | custom-call | tf_op jit(solution)/shard_map/fields/pallas_call | solution.py:341
  4.6 0.0 copy-start
  4.6 3.0 %collective-permute-start = (f32[9,8,128]{2,1,0:T(8,128)}, f32[9,8,128]{2,1,0:T(8,128)S(1)}, u32[]{:S(2)}, u32[]{:S(2)}) collective-permute-start(f32[9,8,128]{2,1,0:T(8,128)} %fields.1._.mine), channel_id=1, source_target_pairs={{0,1},{1,0},{2,3},{3,2},{4,5},{5,4},{6,7},{7,6},{8,9},{9,8},{10,11... | collective-permute-start | bytes 110600 | tf_op jit(solution)/shard_map/ppermute | solution.py:325
  7.6 0.0 copy-done.3
  7.6 0.0 copy-done.1
  7.6 0.0 copy-start.2
  7.6 0.8 %copy-done.2 = f32[9,8,128]{2,1,0:T(8,128)S(1)} copy-done((f32[9,8,128]{2,1,0:T(8,128)S(1)}, f32[9,8,128]{2,1,0:T(8,128)}, u32[]{:S(2)}) %copy-start.2) | copy-done | bytes 36888
  8.4 1.3 %powers.1 = (bf16[8,64,192]{2,1,0:T(8,128)(2,1)S(1)}, f32[512,128]{1,0:T(8,128)S(1)}, f32[8,128]{1,0:T(8,128)S(1)}) custom-call(f32[32,64,64]{2,1,0:T(8,128)S(1)} %copy-done.1, f32[32,64]{1,0:T(8,128)S(1)} %copy-done.3, f32[9,8,128]{2,1,0:T(8,128)S(1)} %copy-done.2), custom_call_target="tpu_custom_call" | custom-call | flops 1000000000 | bytes 1000000 | tf_op jit(solution)/shard_map/powers/pallas_call | solution.py:363
  9.7 0.1 collective-permute-done.theirs
  9.8 3.0 %collective-permute-start.1 = (f32[9,8,128]{2,1,0:T(8,128)S(1)}, f32[9,8,128]{2,1,0:T(8,128)S(1)}, u32[]{:S(2)}, u32[]{:S(2)}) collective-permute-start(f32[9,8,128]{2,1,0:T(8,128)S(1)} %add.1._.mine), channel_id=1, source_target_pairs={{0,2},{1,3},{2,0},{3,1},{4,6},{5,7},{6,4},{7,5},{8,10},{9,11},{10,... | collective-permute-start | bytes 110600 | tf_op jit(solution)/shard_map/ppermute | solution.py:325
  12.8 0.0 copy-done
  12.8 1.5 %apply.1._.shells = f32[8,512,128]{2,1,0:T(8,128)S(1)} custom-call(f32[512,1024]{1,0:T(8,128)S(1)} %bitcast.2, bf16[8,64,192]{2,1,0:T(8,128)(2,1)S(1)} %get-tuple-element.6.lefts, f32[8,128]{1,0:T(8,128)S(1)} %get-tuple-element.5._.factors, f32[9,8,128]{2,1,0:T(8,128)S(1)} %add.1._.mine), custom_call_target="tpu_custom_call" | custom-call | flops 1000000000 | bytes 2097152 | tf_op jit(solution)/shard_map/apply/pallas_call | solution.py:390
  14.3 0.4 %collective-permute-done.1.theirs = f32[9,8,128]{2,1,0:T(8,128)S(1)} collective-permute-done((f32[9,8,128]{2,1,0:T(8,128)S(1)}, f32[9,8,128]{2,1,0:T(8,128)S(1)}, u32[]{:S(2)}, u32[]{:S(2)}) %collective-permute-start.1) | collective-permute-done | bytes 36896 | tf_op jit(solution)/shard_map/ppermute | solution.py:325
  14.8 0.1 combine.1
  14.8 8.8 %all-gather = f32[32,8,128]{2,1,0:T(8,128)S(1)} all-gather(f32[8,8,128]{2,1,0:T(8,128)S(1)} %combine.1), channel_id=2, replica_groups={{0,8,16,24},{4,12,20,28},{1,9,17,25},{5,13,21,29},{2,10,18,26},{6,14,22..., dimensions={0}, use_global_device_ids=true | all-gather | bytes 163840 | tf_op jit(solution)/shard_map/all_gather | solution.py:410
  23.7 0.0 collective-permute-start.2
  23.7 1.3 %collective-permute-done.2.theirs = f32[4,8,8,128]{3,2,1,0:T(8,128)S(1)} collective-permute-done((f32[4,8,8,128]{3,2,1,0:T(8,128)S(1)}, f32[4,8,8,128]{3,2,1,0:T(8,128)S(1)}, u32[]{:S(2)}, u32[]{:S(2)}) %collective-permute-start.2) | collective-permute-done | bytes 131104 | tf_op jit(solution)/shard_map/ppermute | solution.py:325
  25.0 2.5 %finish.1 = (f32[64,8,1024]{2,1,0:T(8,128)}, f32[1,256]{1,0:T(1,128)}) custom-call(f32[4,8,8,128]{3,2,1,0:T(8,128)S(1)} %bitcast.4, f32[4,8,8,128]{3,2,1,0:T(8,128)S(1)} %collective-permute-done.2.theirs, f32[8,512,128]{2,1,0:T(8,128)S(1)} %apply.1._.shells, f32[512,128]{1,0:T(8,128)S(1)} %get-tuple-element.7.columns), custom_call_target="tpu_custom_call" | custom-call | tf_op jit(solution)/shard_map/finish/pallas_call | solution.py:413
  (1 shorter events, 0.0 us)
Async XLA Ops:
  0.6 7.0 %copy-start.3 = (f32[32,64]{1,0:T(8,128)S(1)}, f32[32,64]{1,0:T(8,128)}, u32[]{:S(2)}) copy-start(f32[32,64]{1,0:T(8,128)} %coup_hbm.3) | copy-start | bytes 24580
  0.6 7.0 %copy-start.1 = (f32[32,64,64]{2,1,0:T(8,128)S(1)}, f32[32,64,64]{2,1,0:T(8,128)}, u32[]{:S(2)}) copy-start(f32[32,64,64]{2,1,0:T(8,128)} %prop_hbm.3) | copy-start | bytes 1572868
  4.6 8.2 %copy-start = (f32[64,8,1024]{2,1,0:T(8,128)S(1)}, f32[64,8,1024]{2,1,0:T(8,128)}, u32[]{:S(2)}) copy-start(f32[64,8,1024]{2,1,0:T(8,128)} %melt_hbm.1) | copy-start | bytes 6291460
  4.6 5.2 %collective-permute-start = (f32[9,8,128]{2,1,0:T(8,128)}, f32[9,8,128]{2,1,0:T(8,128)S(1)}, u32[]{:S(2)}, u32[]{:S(2)}) collective-permute-start(f32[9,8,128]{2,1,0:T(8,128)} %fields.1._.mine), channel_id=1, source_target_pairs={{0,1},{1,0},{2,3},{3,2},{4,5},{5,4},{6,7},{7,6},{8,9},{9,8},{10,11... | collective-permute-start | bytes 110600 | tf_op jit(solution)/shard_map/ppermute | solution.py:325
  7.6 0.8 %copy-start.2 = (f32[9,8,128]{2,1,0:T(8,128)S(1)}, f32[9,8,128]{2,1,0:T(8,128)}, u32[]{:S(2)}) copy-start(f32[9,8,128]{2,1,0:T(8,128)} %fields.1._.mine) | copy-start | bytes 110596
  9.8 5.0 %collective-permute-start.1 = (f32[9,8,128]{2,1,0:T(8,128)S(1)}, f32[9,8,128]{2,1,0:T(8,128)S(1)}, u32[]{:S(2)}, u32[]{:S(2)}) collective-permute-start(f32[9,8,128]{2,1,0:T(8,128)S(1)} %add.1._.mine), channel_id=1, source_target_pairs={{0,2},{1,3},{2,0},{3,1},{4,6},{5,7},{6,4},{7,5},{8,10},{9,11},{10,... | collective-permute-start | bytes 110600 | tf_op jit(solution)/shard_map/ppermute | solution.py:325
  23.7 1.4 %collective-permute-start.2 = (f32[4,8,8,128]{3,2,1,0:T(8,128)S(1)}, f32[4,8,8,128]{3,2,1,0:T(8,128)S(1)}, u32[]{:S(2)}, u32[]{:S(2)}) collective-permute-start(f32[4,8,8,128]{3,2,1,0:T(8,128)S(1)} %bitcast.3), channel_id=1, source_target_pairs={{0,4},{4,0},{8,12},{12,8},{16,20},{20,16},{24,28},{28,24},{1,5},{5... | collective-permute-start | bytes 393224 | tf_op jit(solution)/shard_map/ppermute | solution.py:325

commit v15 on v13

--- a/solution.py
+++ b/solution.py
@@ -200,7 +200,8 @@
     out[...] = mine[...] + theirs[...]
 
 
-def combine_kernel(senders, mine, theirs, _, out, kept):
+def combine_kernel(senders, mine, theirs, _, out_ref, kept):
+    out = out_ref.at[0]
     total = mine[...] + theirs[...]
     tail = out.shape[0] - 1
     tile = out.shape[1] // senders
@@ -242,7 +243,7 @@
 
 
 def finish_kernel(
-    window, shells, columns, out_hbm, pressure_out, out, walls_all, last, out_sems
+    mine, theirs, shells, columns, out_hbm, pressure_out, out, window, walls_all, last, out_sems
 ):
     nodes, classes, cells = out.shape
     chunks = cells // LANES
@@ -253,7 +254,13 @@
         return pl.ds(g * GROUP, GROUP)
 
     plane = pressure_out.shape[1]
+    cell = lax.axis_index("cell")
+    even = cell % 2 == 0
     blocks = window.shape[0]
+    bits = chip_bits(blocks)
+    for n, (first, second) in enumerate(zip(offsets(bits), offsets(bits[::-1]))):
+        window[cell ^ jnp.where(even, first, second)] = mine[n]
+        window[cell ^ 1 ^ jnp.where(even, second, first)] = theirs[n]
     rows = blocks * chunks
     per = plane // LANES
     tile = pressure_out.shape[0] * per
@@ -274,7 +281,8 @@
             gas = gas + field_of(t)
         total = total_of(gas)
         if t == SUBSTEPS - 1:
-            total = total + jnp.sum(window[:, 2 * SUBSTEPS - 1], axis=0)[tile : tile + 1, :1]
+            rest = jnp.sum(window[:, 2 * SUBSTEPS - 1], axis=0)
+            total = total + rest[tile : tile + 1, :1]
         if t:
             field = field + 0.2 * chamber
             gas = gas + answer * (0.1 * chamber)
@@ -284,12 +292,11 @@
         field = 0.8 * field + 0.15 * laplacian(field, plane) + 0.1 * gas
         chamber = 1.5 - 0.5 * total / (rows * LANES)
     last[...] = field + 0.2 * chamber
-    cell = lax.axis_index("cell")
     first = cell * chunks
     at = first + lax.axis_index("cls") * tile
     for i in range(tile):
         pressure_out[i // per : i // per + 1, (i % per) * LANES : (i % per + 1) * LANES] = (
-            last[pl.ds(at + i, 1), :] + 0.1 * window[cell, 2 * SUBSTEPS - 1, i : i + 1, :]
+            last[pl.ds(at + i, 1), :] + 0.1 * mine[0, 2 * SUBSTEPS - 1, i : i + 1, :]
         )
     right = []
     for r in range(chunks):
@@ -315,6 +322,17 @@
 HBM = pl.BlockSpec(memory_space=pltpu.HBM)
 VMEM = pl.BlockSpec(memory_space=pltpu.VMEM)
 DMA = pltpu.SemaphoreType.DMA
+
+
+def chip_bits(count):
+    return [1 << b for b in reversed(range(1, count.bit_length() - 1))]
+
+
+def offsets(bits):
+    found = [0]
+    for bit in bits:
+        found = found + [m ^ bit for m in found]
+    return found
 
 
 def partner(value, axis, distance):
@@ -395,29 +413,35 @@
     )(melt.reshape(nodes * classes, cells), lefts, factors, packed)
     fields = pl.pallas_call(
         functools.partial(combine_kernel, cls_count),
-        out_shape=jax.ShapeDtypeStruct((FIELDS, chunks, LANES), f32),
+        out_shape=jax.ShapeDtypeStruct((1, FIELDS, chunks, LANES), f32),
         in_specs=[VMEM, VMEM, VMEM],
         out_specs=VMEM,
         scratch_shapes=[pltpu.VMEM((chunks, LANES), f32)],
         compiler_params=little,
         name="combine",
     )(packed, theirs, shells)
-    window = lax.all_gather(fields, "cell", axis=0)
+    bits = chip_bits(cell_count)
+    held = fields
+    for even, odd in zip(bits, reversed(bits)):
+        pairs = [(i, i ^ (odd if i % 2 else even)) for i in range(cell_count)]
+        held = jnp.concatenate([held, lax.ppermute(held, "cell", pairs)], axis=0)
+    other = partner(held, "cell", 1)
     rows = cell_count * chunks
     return pl.pallas_call(
         finish_kernel,
         out_shape=[jax.ShapeDtypeStruct(melt.shape, f32), jax.ShapeDtypeStruct(pressure.shape, f32)],
-        in_specs=[VMEM, VMEM, VMEM],
+        in_specs=[VMEM] * 4,
         out_specs=[HBM, VMEM],
         scratch_shapes=[
             pltpu.VMEM(melt.shape, f32),
+            pltpu.VMEM((cell_count, FIELDS, chunks, LANES), f32),
             pltpu.VMEM((SUBSTEPS, rows, LANES), f32),
             pltpu.VMEM((rows, LANES), f32),
             DMA((parts,)),
         ],
         compiler_params=little,
         name="finish",
-    )(window, shells, columns)
+    )(held, other, shells, columns)
 
 
 def solution(mesh):

time: 27.3 us -> 27.5 us (level)
  blocking collectives: 9.68 us -> 0 us
  waiting for transfers between devices: 0.5 us -> 6.28 us
  starting transfers between devices: 6.14 us -> 10.1 us
    all_gather x1 -> x0, blocking collectives: 9.68 us -> none  [shards(): window = lax.all_gather(fields, 'cell', axis=0)]
    ppermute x0 -> x2, waiting for transfers between devices: none -> 4.44 us  [shards(): held = jnp.concatenate([held, lax.ppermute(held, 'cell', pairs)], axis=0)]
    ppermute x0 -> x2, starting transfers between devices: none -> 3.93 us  [shards(): held = jnp.concatenate([held, lax.ppermute(held, 'cell', pairs)], axis=0)]
    ppermute x2 -> x3, waiting for transfers between devices: 0.5 us -> 1.84 us  [partner(): lax.ppermute(value, axis, [(i, i ^ distance) for i in range(lax.axis_size...]
    ppermute x2 -> x3, starting transfers between devices: 6.14 us -> 6.21 us  [partner(): lax.ppermute(value, axis, [(i, i ^ distance) for i in range(lax.axis_size...]
  transfers between devices with their start and end apart: 2 -> 5, of which waited for: 2 -> 5; matrix products, arithmetic and copies ran while one was open for 0% -> 0% of each run, Pallas kernels for 10% -> 10%
where the time goes in v15:
time: 27.5 us; the launch traced here: 27.3 us
  starting transfers between devices  10.1 us (37%)
  Pallas kernels  9.32 us (34%)
  waiting for transfers between devices  6.28 us (23%)
  local copies, waits for them, and re-layouts  0.81 us (3%)
  between operations  0.7 us (3%)
    ppermute x3, starting transfers between devices, partner(): lax.ppermute(value, axis, [(i, i ^ distance) for i in range(lax.axis_size...  6.21 us
    ppermute x2, waiting for transfers between devices, shards(): held = jnp.concatenate([held, lax.ppermute(held, 'cell', pairs)], axis=0)  4.44 us
    ppermute x2, starting transfers between devices, shards(): held = jnp.concatenate([held, lax.ppermute(held, 'cell', pairs)], axis=0)  3.93 us
    pallas_call x1, Pallas kernels, shards(): pl.pallas_call(fields_kernel, out_shape=jax.ShapeDtypeStruct((FIELDS + 1,...  3.92 us
    pallas_call x1, Pallas kernels, shards(): pl.pallas_call(finish_kernel, out_shape=[jax.ShapeDtypeStruct(melt.shape,...  2.55 us
    ppermute x3, waiting for transfers between devices, partner(): lax.ppermute(value, axis, [(i, i ^ distance) for i in range(lax.axis_size...  1.84 us
    pallas_call x1, Pallas kernels, shards(): pl.pallas_call(apply_kernel, out_shape=jax.ShapeDtypeStruct(split, f32),...  1.51 us
    pallas_call x1, Pallas kernels, shards(): pl.pallas_call(powers_kernel, out_shape=[jax.ShapeDtypeStruct(lefts_shape...  1.25 us
  transfers between devices with their start and end apart: 5, of which 5 were waited for; matrix products, arithmetic and copies ran while one was open for 0% of the time, Pallas kernels for 10%

profile of v15, /device:TPU:0, one launch (start us, length us, event | category | flops | bytes accessed | tf_op | source)
XLA Modules:
  0.0 27.3 jit_solution(9489409016219199887)
XLA Ops:
  0.6 0.0 copy-start.4
  0.6 0.0 copy-start.1
  0.7 3.9 %fields.1._.mine = f32[9,8,128]{2,1,0:T(8,128)} custom-call(f32[64,8,1024]{2,1,0:T(8,128)} %melt_hbm.1, s32[8,1024]{1,0:T(8,128)} %counts_hbm.1, f32[1,256]{1,0:T(1,128)} %pressure_hbm.1, f32[32,64,64]{2,1,0:T(8,128)} %prop_hbm.3, f32[32,64]{1,0:T(8,128)} %coup_hbm.3, f32[32,64]{1,0:T(8,128)} %flux_hbm.1), custom_call_target="tpu_custom_call" | custom-call | tf_op jit(solution)/shard_map/fields/pallas_call | solution.py:355
  4.6 0.0 copy-start
  4.6 3.0 %collective-permute-start = (f32[9,8,128]{2,1,0:T(8,128)}, f32[9,8,128]{2,1,0:T(8,128)S(1)}, u32[]{:S(2)}, u32[]{:S(2)}) collective-permute-start(f32[9,8,128]{2,1,0:T(8,128)} %fields.1._.mine), channel_id=1, source_target_pairs={{0,1},{1,0},{2,3},{3,2},{4,5},{5,4},{6,7},{7,6},{8,9},{9,8},{10,11... | collective-permute-start | bytes 110600 | tf_op jit(solution)/shard_map/ppermute | solution.py:339
  7.6 0.0 copy-done.4
  7.6 0.0 copy-done.1
  7.6 0.0 copy-start.2
  7.6 0.8 %copy-done.2 = f32[9,8,128]{2,1,0:T(8,128)S(1)} copy-done((f32[9,8,128]{2,1,0:T(8,128)S(1)}, f32[9,8,128]{2,1,0:T(8,128)}, u32[]{:S(2)}) %copy-start.2) | copy-done | bytes 36888
  8.4 1.3 %powers.1 = (bf16[8,64,192]{2,1,0:T(8,128)(2,1)S(1)}, f32[512,128]{1,0:T(8,128)S(1)}, f32[8,128]{1,0:T(8,128)S(1)}) custom-call(f32[32,64,64]{2,1,0:T(8,128)S(1)} %copy-done.1, f32[32,64]{1,0:T(8,128)S(1)} %copy-done.4, f32[9,8,128]{2,1,0:T(8,128)S(1)} %copy-done.2), custom_call_target="tpu_custom_call" | custom-call | flops 1000000000 | bytes 1000000 | tf_op jit(solution)/shard_map/powers/pallas_call | solution.py:377
  9.7 0.1 collective-permute-done.theirs
  9.8 0.0 copy-done.3
  9.8 3.1 %collective-permute-start.1 = (f32[9,8,128]{2,1,0:T(8,128)S(1)}, f32[9,8,128]{2,1,0:T(8,128)S(1)}, u32[]{:S(2)}, u32[]{:S(2)}) collective-permute-start(f32[9,8,128]{2,1,0:T(8,128)S(1)} %add.1._.mine), channel_id=1, source_target_pairs={{0,2},{1,3},{2,0},{3,1},{4,6},{5,7},{6,4},{7,5},{8,10},{9,11},{10,... | collective-permute-start | bytes 110600 | tf_op jit(solution)/shard_map/ppermute | solution.py:339
  12.9 0.0 copy-done
  12.9 1.5 %apply.1._.shells = f32[8,512,128]{2,1,0:T(8,128)S(1)} custom-call(f32[512,1024]{1,0:T(8,128)S(1)} %bitcast.1, bf16[8,64,192]{2,1,0:T(8,128)(2,1)S(1)} %get-tuple-element.6.lefts, f32[8,128]{1,0:T(8,128)S(1)} %get-tuple-element.5._.factors, f32[9,8,128]{2,1,0:T(8,128)S(1)} %add.1._.mine), custom_call_target="tpu_custom_call" | custom-call | flops 1000000000 | bytes 2097152 | tf_op jit(solution)/shard_map/apply/pallas_call | solution.py:404
  14.4 0.4 %collective-permute-done.1.theirs = f32[9,8,128]{2,1,0:T(8,128)S(1)} collective-permute-done((f32[9,8,128]{2,1,0:T(8,128)S(1)}, f32[9,8,128]{2,1,0:T(8,128)S(1)}, u32[]{:S(2)}, u32[]{:S(2)}) %collective-permute-start.1) | collective-permute-done | bytes 36896 | tf_op jit(solution)/shard_map/ppermute | solution.py:339
  14.8 0.1 combine.1
  14.9 1.9 %collective-permute-start.2 = (f32[1,8,8,128]{3,2,1,0:T(8,128)S(1)}, f32[1,8,8,128]{3,2,1,0:T(8,128)S(1)}, u32[]{:S(2)}, u32[]{:S(2)}) collective-permute-start(f32[1,8,8,128]{3,2,1,0:T(8,128)S(1)} %combine.1), channel_id=1, source_target_pairs={{0,16},{4,12},{8,24},{12,4},{16,0},{20,28},{24,8},{28,20},{1,17},{... | collective-permute-start | bytes 98312 | tf_op jit(solution)/shard_map/ppermute | solution.py:427
  16.8 2.2 %collective-permute-done.2 = f32[1,8,8,128]{3,2,1,0:T(8,128)S(1)} collective-permute-done((f32[1,8,8,128]{3,2,1,0:T(8,128)S(1)}, f32[1,8,8,128]{3,2,1,0:T(8,128)S(1)}, u32[]{:S(2)}, u32[]{:S(2)}) %collective-permute-start.2) | collective-permute-done | bytes 32800 | tf_op jit(solution)/shard_map/ppermute | solution.py:427
  19.0 2.0 %collective-permute-start.3 = (f32[2,8,8,128]{3,2,1,0:T(8,128)S(1)}, f32[2,8,8,128]{3,2,1,0:T(8,128)S(1)}, u32[]{:S(2)}, u32[]{:S(2)}) collective-permute-start(f32[2,8,8,128]{3,2,1,0:T(8,128)S(1)} %pad_maximum_fusion.1), channel_id=1, source_target_pairs={{0,8},{4,20},{8,0},{12,28},{16,24},{20,4},{24,16},{28,12},{1,9},{5... | collective-permute-start | bytes 196616 | tf_op jit(solution)/shard_map/ppermute | solution.py:427
  21.1 2.2 %collective-permute-done.3 = f32[2,8,8,128]{3,2,1,0:T(8,128)S(1)} collective-permute-done((f32[2,8,8,128]{3,2,1,0:T(8,128)S(1)}, f32[2,8,8,128]{3,2,1,0:T(8,128)S(1)}, u32[]{:S(2)}, u32[]{:S(2)}) %collective-permute-start.3) | collective-permute-done | bytes 65568 | tf_op jit(solution)/shard_map/ppermute | solution.py:427
  23.3 0.1 collective-permute-start.4
  23.4 1.3 %collective-permute-done.4.theirs = f32[4,8,8,128]{3,2,1,0:T(8,128)S(1)} collective-permute-done((f32[4,8,8,128]{3,2,1,0:T(8,128)S(1)}, f32[4,8,8,128]{3,2,1,0:T(8,128)S(1)}, u32[]{:S(2)}, u32[]{:S(2)}) %collective-permute-start.4) | collective-permute-done | bytes 131104 | tf_op jit(solution)/shard_map/ppermute | solution.py:339
  24.7 2.5 %finish.1 = (f32[64,8,1024]{2,1,0:T(8,128)}, f32[1,256]{1,0:T(1,128)}) custom-call(f32[4,8,8,128]{3,2,1,0:T(8,128)S(1)} %pad_maximum_fusion.mine, f32[4,8,8,128]{3,2,1,0:T(8,128)S(1)} %collective-permute-done.4.theirs, f32[8,512,128]{2,1,0:T(8,128)S(1)} %apply.1._.shells, f32[512,128]{1,0:T(8,128)S(1)} %get-tuple-element.7.columns), custom_call_target="tpu_custom_call" | custom-call | tf_op jit(solution)/shard_map/finish/pallas_call | solution.py:430
  (4 shorter events, 0.0 us)
Async XLA Ops:
  0.6 7.0 %copy-start.4 = (f32[32,64]{1,0:T(8,128)S(1)}, f32[32,64]{1,0:T(8,128)}, u32[]{:S(2)}) copy-start(f32[32,64]{1,0:T(8,128)} %coup_hbm.3) | copy-start | bytes 24580
  0.6 7.0 %copy-start.1 = (f32[32,64,64]{2,1,0:T(8,128)S(1)}, f32[32,64,64]{2,1,0:T(8,128)}, u32[]{:S(2)}) copy-start(f32[32,64,64]{2,1,0:T(8,128)} %prop_hbm.3) | copy-start | bytes 1572868
  4.6 8.3 %copy-start = (f32[64,8,1024]{2,1,0:T(8,128)S(1)}, f32[64,8,1024]{2,1,0:T(8,128)}, u32[]{:S(2)}) copy-start(f32[64,8,1024]{2,1,0:T(8,128)} %melt_hbm.1) | copy-start | bytes 6291460
  4.6 5.2 %collective-permute-start = (f32[9,8,128]{2,1,0:T(8,128)}, f32[9,8,128]{2,1,0:T(8,128)S(1)}, u32[]{:S(2)}, u32[]{:S(2)}) collective-permute-start(f32[9,8,128]{2,1,0:T(8,128)} %fields.1._.mine), channel_id=1, source_target_pairs={{0,1},{1,0},{2,3},{3,2},{4,5},{5,4},{6,7},{7,6},{8,9},{9,8},{10,11... | collective-permute-start | bytes 110600 | tf_op jit(solution)/shard_map/ppermute | solution.py:339
  7.6 0.8 %copy-start.2 = (f32[9,8,128]{2,1,0:T(8,128)S(1)}, f32[9,8,128]{2,1,0:T(8,128)}, u32[]{:S(2)}) copy-start(f32[9,8,128]{2,1,0:T(8,128)} %fields.1._.mine) | copy-start | bytes 110596
  8.4 1.3 %copy-start.3 = (f32[9,8,128]{2,1,0:T(8,128)S(1)}, f32[9,8,128]{2,1,0:T(8,128)}, u32[]{:S(2)}) copy-start(f32[9,8,128]{2,1,0:T(8,128)} %fields.1._.mine) | copy-start | bytes 110596
  9.8 5.0 %collective-permute-start.1 = (f32[9,8,128]{2,1,0:T(8,128)S(1)}, f32[9,8,128]{2,1,0:T(8,128)S(1)}, u32[]{:S(2)}, u32[]{:S(2)}) collective-permute-start(f32[9,8,128]{2,1,0:T(8,128)S(1)} %add.1._.mine), channel_id=1, source_target_pairs={{0,2},{1,3},{2,0},{3,1},{4,6},{5,7},{6,4},{7,5},{8,10},{9,11},{10,... | collective-permute-start | bytes 110600 | tf_op jit(solution)/shard_map/ppermute | solution.py:339
  14.9 4.1 %collective-permute-start.2 = (f32[1,8,8,128]{3,2,1,0:T(8,128)S(1)}, f32[1,8,8,128]{3,2,1,0:T(8,128)S(1)}, u32[]{:S(2)}, u32[]{:S(2)}) collective-permute-start(f32[1,8,8,128]{3,2,1,0:T(8,128)S(1)} %combine.1), channel_id=1, source_target_pairs={{0,16},{4,12},{8,24},{12,4},{16,0},{20,28},{24,8},{28,20},{1,17},{... | collective-permute-start | bytes 98312 | tf_op jit(solution)/shard_map/ppermute | solution.py:427
  19.0 4.3 %collective-permute-start.3 = (f32[2,8,8,128]{3,2,1,0:T(8,128)S(1)}, f32[2,8,8,128]{3,2,1,0:T(8,128)S(1)}, u32[]{:S(2)}, u32[]{:S(2)}) collective-permute-start(f32[2,8,8,128]{3,2,1,0:T(8,128)S(1)} %pad_maximum_fusion.1), channel_id=1, source_target_pairs={{0,8},{4,20},{8,0},{12,28},{16,24},{20,4},{24,16},{28,12},{1,9},{5... | collective-permute-start | bytes 196616 | tf_op jit(solution)/shard_map/ppermute | solution.py:427
  23.3 1.4 %collective-permute-start.4 = (f32[4,8,8,128]{3,2,1,0:T(8,128)S(1)}, f32[4,8,8,128]{3,2,1,0:T(8,128)S(1)}, u32[]{:S(2)}, u32[]{:S(2)}) collective-permute-start(f32[4,8,8,128]{3,2,1,0:T(8,128)S(1)} %pad_maximum_fusion.mine), channel_id=1, source_target_pairs={{0,4},{4,0},{8,12},{12,8},{16,20},{20,16},{24,28},{28,24},{1,5},{5... | collective-permute-start | bytes 393224 | tf_op jit(solution)/shard_map/ppermute | solution.py:339

commit v16 on v15

--- a/solution.py
+++ b/solution.py
@@ -200,21 +200,30 @@
     out[...] = mine[...] + theirs[...]
 
 
-def combine_kernel(senders, mine, theirs, _, out_ref, kept):
-    out = out_ref.at[0]
-    total = mine[...] + theirs[...]
-    tail = out.shape[0] - 1
-    tile = out.shape[1] // senders
-    pressure = total[2 * SUBSTEPS]
-    wall = 0.5 * pressure
-    for t in range(SUBSTEPS - 1):
-        out[t] = total[t] + total[SUBSTEPS + t] * wall
-        out[SUBSTEPS - 1 + t] = total[SUBSTEPS + t]
-    out[tail - 1] = pressure
-    gas = total[SUBSTEPS - 1] + total[2 * SUBSTEPS - 1] * wall
-    kept[...] = gas
-    out[tail] = jnp.broadcast_to(total_of(gas), gas.shape)
-    out[tail, :tile, :] = kept[pl.ds(lax.axis_index("cls") * tile, tile), :]
+def lift_kernel(value, out):
+    out[...] = value[...]
+
+
+def join_kernel(mine, theirs, out):
+    out[0] = mine[...]
+    out[1] = theirs[...]
+
+
+def combine_kernel(senders, mine, theirs, _, out, kept):
+    tail = out.shape[1] - 1
+    tile = out.shape[2] // senders
+    for n in range(out.shape[0]):
+        total = mine[n] + theirs[n]
+        pressure = total[2 * SUBSTEPS]
+        wall = 0.5 * pressure
+        for t in range(SUBSTEPS - 1):
+            out[n, t] = total[t] + total[SUBSTEPS + t] * wall
+            out[n, SUBSTEPS - 1 + t] = total[SUBSTEPS + t]
+        out[n, tail - 1] = pressure
+        gas = total[SUBSTEPS - 1] + total[2 * SUBSTEPS - 1] * wall
+        kept[n] = gas
+        out[n, tail] = jnp.broadcast_to(total_of(gas), gas.shape)
+        out[n, tail, :tile, :] = kept[n, pl.ds(lax.axis_index("cls") * tile, tile), :]
 
 
 def total_of(x):
@@ -257,10 +266,10 @@
     cell = lax.axis_index("cell")
     even = cell % 2 == 0
     blocks = window.shape[0]
-    bits = chip_bits(blocks)
-    for n, (first, second) in enumerate(zip(offsets(bits), offsets(bits[::-1]))):
-        window[cell ^ jnp.where(even, first, second)] = mine[n]
-        window[cell ^ 1 ^ jnp.where(even, second, first)] = theirs[n]
+    for n, offset in enumerate(offsets(chip_bits(blocks))):
+        for core in range(2):
+            at = (cell | 1) ^ (offset + core)
+            window[at] = jnp.where(even, theirs[2 * n + core], mine[2 * n + core])
     rows = blocks * chunks
     per = plane // LANES
     tile = pressure_out.shape[0] * per
@@ -296,7 +305,7 @@
     at = first + lax.axis_index("cls") * tile
     for i in range(tile):
         pressure_out[i // per : i // per + 1, (i % per) * LANES : (i % per + 1) * LANES] = (
-            last[pl.ds(at + i, 1), :] + 0.1 * mine[0, 2 * SUBSTEPS - 1, i : i + 1, :]
+            last[pl.ds(at + i, 1), :] + 0.1 * window[cell, 2 * SUBSTEPS - 1, i : i + 1, :]
         )
     right = []
     for r in range(chunks):
@@ -335,8 +344,19 @@
     return found
 
 
-def partner(value, axis, distance):
-    return lax.ppermute(value, axis, [(i, i ^ distance) for i in range(lax.axis_size(axis))])
+def hand(value, odd):
+    count = lax.axis_size("cell")
+    return lax.ppermute(value, "cell", [(i, i ^ 1) for i in range(count) if i % 2 == odd])
+
+
+def swap(value, cell_bit, cls_bit):
+    cells, classes = lax.axis_size("cell"), lax.axis_size("cls")
+    pairs = [
+        (i * classes + k, (i ^ cell_bit) * classes + (k ^ cls_bit))
+        for i in range(1, cells, 2)
+        for k in range(classes)
+    ]
+    return lax.ppermute(value, ("cell", "cls"), pairs)
 
 
 def shards(melt, counts, pressure, propagator, coupling, flux_weights):
@@ -373,7 +393,25 @@
         name="fields",
     )(melt, counts, pressure, propagator, coupling, flux_weights)
     lefts_shape = (classes, nodes, 3 * nodes)
-    theirs = partner(packed, "cls", 1)
+    handed = hand(packed, 0)
+    packed = pl.pallas_call(
+        lift_kernel,
+        out_shape=jax.ShapeDtypeStruct(packed.shape, f32),
+        in_specs=[VMEM],
+        out_specs=VMEM,
+        compiler_params=little,
+        cost_estimate=pl.CostEstimate(flops=10**8, bytes_accessed=10**6, transcendentals=0),
+        name="lift",
+    )(packed)
+    packed = pl.pallas_call(
+        join_kernel,
+        out_shape=jax.ShapeDtypeStruct((2,) + packed.shape, f32),
+        in_specs=[VMEM] * 2,
+        out_specs=VMEM,
+        compiler_params=little,
+        name="join",
+    )(packed, handed)
+    theirs = swap(packed, 0, 1)
     lefts, columns, factors = pl.pallas_call(
         powers_kernel,
         out_shape=[
@@ -400,7 +438,7 @@
             compiler_params=little,
             name="add",
         )(packed, theirs, after)
-        theirs = partner(packed, "cls", distance)
+        theirs = swap(packed, 0, distance)
     shells = pl.pallas_call(
         apply_kernel,
         out_shape=jax.ShapeDtypeStruct(split, f32),
@@ -413,19 +451,17 @@
     )(melt.reshape(nodes * classes, cells), lefts, factors, packed)
     fields = pl.pallas_call(
         functools.partial(combine_kernel, cls_count),
-        out_shape=jax.ShapeDtypeStruct((1, FIELDS, chunks, LANES), f32),
+        out_shape=jax.ShapeDtypeStruct((2, FIELDS, chunks, LANES), f32),
         in_specs=[VMEM, VMEM, VMEM],
         out_specs=VMEM,
-        scratch_shapes=[pltpu.VMEM((chunks, LANES), f32)],
+        scratch_shapes=[pltpu.VMEM((2, chunks, LANES), f32)],
         compiler_params=little,
         name="combine",
     )(packed, theirs, shells)
-    bits = chip_bits(cell_count)
     held = fields
-    for even, odd in zip(bits, reversed(bits)):
-        pairs = [(i, i ^ (odd if i % 2 else even)) for i in range(cell_count)]
-        held = jnp.concatenate([held, lax.ppermute(held, "cell", pairs)], axis=0)
-    other = partner(held, "cell", 1)
+    for bit in chip_bits(cell_count):
+        held = jnp.concatenate([held, swap(held, bit, 0)], axis=0)
+    other = hand(held, 1)
     rows = cell_count * chunks
     return pl.pallas_call(
         finish_kernel,

time: 27.5 us -> 36.2 us (1.32)
  waiting for transfers between devices: 6.28 us -> 18.5 us
  starting transfers between devices: 10.1 us -> 6.42 us
    ppermute x5 -> x6, waiting for transfers between devices: 6.28 us -> 18.5 us  [the longest x2 18.5 us: hand(): lax.ppermute(value, 'cell', [(i, i ^ 1) for i in range(count) if i % 2 ==...]
    ppermute x5 -> x6, starting transfers between devices: 10.1 us -> 6.42 us  [the longest x2 3.65 us: hand(): lax.ppermute(value, 'cell', [(i, i ^ 1) for i in range(count) if i % 2 ==...]
    unnamed x10 -> x8, local copies, waits for them, and re-layouts: 0.81 us -> 0.78 us
  transfers between devices with their start and end apart: 5 -> 6, of which waited for: 5 -> 2; matrix products, arithmetic and copies ran while one was open for 0% -> 0% of each run, Pallas kernels for 10% -> 8%
where the time goes in v16:
time: 36.2 us; the launch traced here: 35.9 us
  waiting for transfers between devices  18.5 us (51%)
  Pallas kernels  9.36 us (26%)
  starting transfers between devices  6.42 us (18%)
  between operations  0.81 us (2%)
  local copies, waits for them, and re-layouts  0.78 us (2%)
    ppermute x2, waiting for transfers between devices, hand(): lax.ppermute(value, 'cell', [(i, i ^ 1) for i in range(count) if i % 2 ==...  18.5 us
    pallas_call x1, Pallas kernels, shards(): pl.pallas_call(fields_kernel, out_shape=jax.ShapeDtypeStruct((FIELDS + 1,...  3.92 us
    ppermute x2, starting transfers between devices, hand(): lax.ppermute(value, 'cell', [(i, i ^ 1) for i in range(count) if i % 2 ==...  3.65 us
    ppermute x4, starting transfers between devices, swap(): return lax.ppermute(value, ('cell', 'cls'), pairs)  2.77 us
    pallas_call x1, Pallas kernels, shards(): pl.pallas_call(finish_kernel, out_shape=[jax.ShapeDtypeStruct(melt.shape,...  2.56 us
    pallas_call x1, Pallas kernels, shards(): pl.pallas_call(apply_kernel, out_shape=jax.ShapeDtypeStruct(split, f32),...  1.51 us
    pallas_call x1, Pallas kernels, shards(): pl.pallas_call(powers_kernel, out_shape=[jax.ShapeDtypeStruct(lefts_shape...  1.26 us
    unnamed x8, local copies, waits for them, and re-layouts  0.78 us
  transfers between devices with their start and end apart: 6, of which 2 were waited for; matrix products, arithmetic and copies ran while one was open for 0% of the time, Pallas kernels for 8%

profile of v16, /device:TPU:0, one launch (start us, length us, event | category | flops | bytes accessed | tf_op | source)
XLA Modules:
  0.0 35.9 jit_solution(17248631303108109388)
XLA Ops:
  0.6 0.0 copy-start.3
  0.6 0.0 copy-start.1
  0.7 3.9 %fields.1.value = f32[9,8,128]{2,1,0:T(8,128)} custom-call(f32[64,8,1024]{2,1,0:T(8,128)} %melt_hbm.1, s32[8,1024]{1,0:T(8,128)} %counts_hbm.1, f32[1,256]{1,0:T(1,128)} %pressure_hbm.1, f32[32,64,64]{2,1,0:T(8,128)} %prop_hbm.3, f32[32,64]{1,0:T(8,128)} %coup_hbm.3, f32[32,64]{1,0:T(8,128)} %flux_hbm.1), custom_call_target="tpu_custom_call" | custom-call | tf_op jit(solution)/shard_map/fields/pallas_call | solution.py:375
  4.6 2.4 %collective-permute-start = (f32[9,8,128]{2,1,0:T(8,128)}, f32[9,8,128]{2,1,0:T(8,128)S(1)}, u32[]{:S(2)}, u32[]{:S(2)}) collective-permute-start(f32[9,8,128]{2,1,0:T(8,128)} %fields.1.value), channel_id=1, source_target_pairs={{0,4},{8,12},{16,20},{24,28},{1,5},{9,13},{17,21},{25,29},{2,6},{1... | collective-permute-start | bytes 110600 | tf_op jit(solution)/shard_map/ppermute | solution.py:349
  6.9 0.0 copy-start.2
  7.0 0.8 %copy-done.2 = f32[9,8,128]{2,1,0:T(8,128)S(1)} copy-done((f32[9,8,128]{2,1,0:T(8,128)S(1)}, f32[9,8,128]{2,1,0:T(8,128)}, u32[]{:S(2)}) %copy-start.2) | copy-done | bytes 36888
  7.7 0.3 collective-permute-done.theirs
  8.0 0.8 %collective-permute-start.1 = (f32[2,9,8,128]{3,2,1,0:T(8,128)S(1)}, f32[2,9,8,128]{3,2,1,0:T(8,128)S(1)}, u32[]{:S(2)}, u32[]{:S(2)}) collective-permute-start(f32[2,9,8,128]{3,2,1,0:T(8,128)S(1)} %join.1._.mine), channel_id=1, source_target_pairs={{4,5},{5,4},{6,7},{7,6},{12,13},{13,12},{14,15},{15,14},{20,21},{2... | collective-permute-start | bytes 221192 | tf_op jit(solution)/shard_map/ppermute | solution.py:359
  8.8 0.0 copy-done.3
  8.8 0.0 copy-done.1
  8.8 1.3 %powers.1 = (bf16[8,64,192]{2,1,0:T(8,128)(2,1)S(1)}, f32[512,128]{1,0:T(8,128)S(1)}, f32[8,128]{1,0:T(8,128)S(1)}) custom-call(f32[32,64,64]{2,1,0:T(8,128)S(1)} %copy-done.1, f32[32,64]{1,0:T(8,128)S(1)} %copy-done.3, f32[2,9,8,128]{3,2,1,0:T(8,128)S(1)} %join.1._.mine), custom_call_target="tpu_custom_call" | custom-call | flops 1000000000 | bytes 1000000 | tf_op jit(solution)/shard_map/powers/pallas_call | solution.py:415
  10.1 0.0 collective-permute-done.1.theirs
  10.1 0.7 %collective-permute-start.2 = (f32[2,9,8,128]{3,2,1,0:T(8,128)S(1)}, f32[2,9,8,128]{3,2,1,0:T(8,128)S(1)}, u32[]{:S(2)}, u32[]{:S(2)}) collective-permute-start(f32[2,9,8,128]{3,2,1,0:T(8,128)S(1)} %add.1._.mine), channel_id=1, source_target_pairs={{4,6},{5,7},{6,4},{7,5},{12,14},{13,15},{14,12},{15,13},{20,22},{2... | collective-permute-start | bytes 221192 | tf_op jit(solution)/shard_map/ppermute | solution.py:359
  10.8 0.0 copy-done
  10.8 1.5 %apply.1._.shells = f32[8,512,128]{2,1,0:T(8,128)S(1)} custom-call(f32[512,1024]{1,0:T(8,128)S(1)} %bitcast.1, bf16[8,64,192]{2,1,0:T(8,128)(2,1)S(1)} %get-tuple-element.6.lefts, f32[8,128]{1,0:T(8,128)S(1)} %get-tuple-element.5._.factors, f32[2,9,8,128]{3,2,1,0:T(8,128)S(1)} %add.1._.mine), custom_call_target="tpu_custom_call" | custom-call | flops 1000000000 | bytes 2097152 | tf_op jit(solution)/shard_map/apply/pallas_call | solution.py:442
  12.3 0.0 collective-permute-done.2.theirs
  12.3 0.1 combine.1
  12.4 0.7 %collective-permute-start.3 = (f32[2,8,8,128]{3,2,1,0:T(8,128)S(1)}, f32[2,8,8,128]{3,2,1,0:T(8,128)S(1)}, u32[]{:S(2)}, u32[]{:S(2)}) collective-permute-start(f32[2,8,8,128]{3,2,1,0:T(8,128)S(1)} %combine.1), channel_id=1, source_target_pairs={{4,20},{5,21},{6,22},{7,23},{12,28},{13,29},{14,30},{15,31},{20,4}... | collective-permute-start | bytes 196616 | tf_op jit(solution)/shard_map/ppermute | solution.py:359
  13.1 0.0 collective-permute-done.3
  13.1 0.7 %collective-permute-start.4 = (f32[4,8,8,128]{3,2,1,0:T(8,128)S(1)}, f32[4,8,8,128]{3,2,1,0:T(8,128)S(1)}, u32[]{:S(2)}, u32[]{:S(2)}) collective-permute-start(f32[4,8,8,128]{3,2,1,0:T(8,128)S(1)} %pad_maximum_fusion.1), channel_id=1, source_target_pairs={{4,12},{5,13},{6,14},{7,15},{12,4},{13,5},{14,6},{15,7},{20,28},{2... | collective-permute-start | bytes 393224 | tf_op jit(solution)/shard_map/ppermute | solution.py:359
  13.8 0.0 collective-permute-done.4
  13.8 1.3 %collective-permute-start.5 = (f32[8,8,8,128]{3,2,1,0:T(8,128)S(1)}, f32[8,8,8,128]{3,2,1,0:T(8,128)S(1)}, u32[]{:S(2)}, u32[]{:S(2)}) collective-permute-start(f32[8,8,8,128]{3,2,1,0:T(8,128)S(1)} %pad_maximum_fusion.mine), channel_id=1, source_target_pairs={{4,0},{12,8},{20,16},{28,24},{5,1},{13,9},{21,17},{29,25},{6,2},{1... | collective-permute-start | bytes 786440 | tf_op jit(solution)/shard_map/ppermute | solution.py:349
  15.1 18.2 %collective-permute-done.5.theirs = f32[8,8,8,128]{3,2,1,0:T(8,128)S(1)} collective-permute-done((f32[8,8,8,128]{3,2,1,0:T(8,128)S(1)}, f32[8,8,8,128]{3,2,1,0:T(8,128)S(1)}, u32[]{:S(2)}, u32[]{:S(2)}) %collective-permute-start.5) | collective-permute-done | bytes 262176 | tf_op jit(solution)/shard_map/ppermute | solution.py:349
  33.3 2.6 %finish.1 = (f32[64,8,1024]{2,1,0:T(8,128)}, f32[1,256]{1,0:T(1,128)}) custom-call(f32[8,8,8,128]{3,2,1,0:T(8,128)S(1)} %pad_maximum_fusion.mine, f32[8,8,8,128]{3,2,1,0:T(8,128)S(1)} %collective-permute-done.5.theirs, f32[8,512,128]{2,1,0:T(8,128)S(1)} %apply.1._.shells, f32[512,128]{1,0:T(8,128)S(1)} %get-tuple-element.7.columns), custom_call_target="tpu_custom_call" | custom-call | tf_op jit(solution)/shard_map/finish/pallas_call | solution.py:466
  (6 shorter events, 0.1 us)
Async XLA Ops:
  0.6 8.2 %copy-start.3 = (f32[32,64]{1,0:T(8,128)S(1)}, f32[32,64]{1,0:T(8,128)}, u32[]{:S(2)}) copy-start(f32[32,64]{1,0:T(8,128)} %coup_hbm.3) | copy-start | bytes 24580
  0.6 8.2 %copy-start.1 = (f32[32,64,64]{2,1,0:T(8,128)S(1)}, f32[32,64,64]{2,1,0:T(8,128)}, u32[]{:S(2)}) copy-start(f32[32,64,64]{2,1,0:T(8,128)} %prop_hbm.3) | copy-start | bytes 1572868
  4.6 3.4 %collective-permute-start = (f32[9,8,128]{2,1,0:T(8,128)}, f32[9,8,128]{2,1,0:T(8,128)S(1)}, u32[]{:S(2)}, u32[]{:S(2)}) collective-permute-start(f32[9,8,128]{2,1,0:T(8,128)} %fields.1.value), channel_id=1, source_target_pairs={{0,4},{8,12},{16,20},{24,28},{1,5},{9,13},{17,21},{25,29},{2,6},{1... | collective-permute-start | bytes 110600 | tf_op jit(solution)/shard_map/ppermute | solution.py:349
  6.9 0.8 %copy-start.2 = (f32[9,8,128]{2,1,0:T(8,128)S(1)}, f32[9,8,128]{2,1,0:T(8,128)}, u32[]{:S(2)}) copy-start(f32[9,8,128]{2,1,0:T(8,128)} %fields.1.value) | copy-start | bytes 110596
  7.7 3.1 %copy-start = (f32[64,8,1024]{2,1,0:T(8,128)S(1)}, f32[64,8,1024]{2,1,0:T(8,128)}, u32[]{:S(2)}) copy-start(f32[64,8,1024]{2,1,0:T(8,128)} %melt_hbm.1) | copy-start | bytes 6291460
  8.0 2.1 %collective-permute-start.1 = (f32[2,9,8,128]{3,2,1,0:T(8,128)S(1)}, f32[2,9,8,128]{3,2,1,0:T(8,128)S(1)}, u32[]{:S(2)}, u32[]{:S(2)}) collective-permute-start(f32[2,9,8,128]{3,2,1,0:T(8,128)S(1)} %join.1._.mine), channel_id=1, source_target_pairs={{4,5},{5,4},{6,7},{7,6},{12,13},{13,12},{14,15},{15,14},{20,21},{2... | collective-permute-start | bytes 221192 | tf_op jit(solution)/shard_map/ppermute | solution.py:359
  10.1 2.2 %collective-permute-start.2 = (f32[2,9,8,128]{3,2,1,0:T(8,128)S(1)}, f32[2,9,8,128]{3,2,1,0:T(8,128)S(1)}, u32[]{:S(2)}, u32[]{:S(2)}) collective-permute-start(f32[2,9,8,128]{3,2,1,0:T(8,128)S(1)} %add.1._.mine), channel_id=1, source_target_pairs={{4,6},{5,7},{6,4},{7,5},{12,14},{13,15},{14,12},{15,13},{20,22},{2... | collective-permute-start | bytes 221192 | tf_op jit(solution)/shard_map/ppermute | solution.py:359
  12.4 0.7 %collective-permute-start.3 = (f32[2,8,8,128]{3,2,1,0:T(8,128)S(1)}, f32[2,8,8,128]{3,2,1,0:T(8,128)S(1)}, u32[]{:S(2)}, u32[]{:S(2)}) collective-permute-start(f32[2,8,8,128]{3,2,1,0:T(8,128)S(1)} %combine.1), channel_id=1, source_target_pairs={{4,20},{5,21},{6,22},{7,23},{12,28},{13,29},{14,30},{15,31},{20,4}... | collective-permute-start | bytes 196616 | tf_op jit(solution)/shard_map/ppermute | solution.py:359
  13.1 0.7 %collective-permute-start.4 = (f32[4,8,8,128]{3,2,1,0:T(8,128)S(1)}, f32[4,8,8,128]{3,2,1,0:T(8,128)S(1)}, u32[]{:S(2)}, u32[]{:S(2)}) collective-permute-start(f32[4,8,8,128]{3,2,1,0:T(8,128)S(1)} %pad_maximum_fusion.1), channel_id=1, source_target_pairs={{4,12},{5,13},{6,14},{7,15},{12,4},{13,5},{14,6},{15,7},{20,28},{2... | collective-permute-start | bytes 393224 | tf_op jit(solution)/shard_map/ppermute | solution.py:359
  13.8 19.5 %collective-permute-start.5 = (f32[8,8,8,128]{3,2,1,0:T(8,128)S(1)}, f32[8,8,8,128]{3,2,1,0:T(8,128)S(1)}, u32[]{:S(2)}, u32[]{:S(2)}) collective-permute-start(f32[8,8,8,128]{3,2,1,0:T(8,128)S(1)} %pad_maximum_fusion.mine), channel_id=1, source_target_pairs={{4,0},{12,8},{20,16},{28,24},{5,1},{13,9},{21,17},{29,25},{6,2},{1... | collective-permute-start | bytes 786440 | tf_op jit(solution)/shard_map/ppermute | solution.py:349

commit v17 on v16

--- a/solution.py
+++ b/solution.py
@@ -344,16 +344,15 @@
     return found
 
 
-def hand(value, odd):
-    count = lax.axis_size("cell")
-    return lax.ppermute(value, "cell", [(i, i ^ 1) for i in range(count) if i % 2 == odd])
+def swap_cores(value):
+    return lax.ppermute(value, "cell", [(i, i ^ 1) for i in range(lax.axis_size("cell"))])
 
 
 def swap(value, cell_bit, cls_bit):
     cells, classes = lax.axis_size("cell"), lax.axis_size("cls")
     pairs = [
-        (i * classes + k, (i ^ cell_bit) * classes + (k ^ cls_bit))
-        for i in range(1, cells, 2)
+        (i * classes + k, (i ^ cell_bit if i % 2 else i) * classes + (k ^ cls_bit if i % 2 else k))
+        for i in range(cells)
         for k in range(classes)
     ]
     return lax.ppermute(value, ("cell", "cls"), pairs)
@@ -393,7 +392,7 @@
         name="fields",
     )(melt, counts, pressure, propagator, coupling, flux_weights)
     lefts_shape = (classes, nodes, 3 * nodes)
-    handed = hand(packed, 0)
+    handed = swap_cores(packed)
     packed = pl.pallas_call(
         lift_kernel,
         out_shape=jax.ShapeDtypeStruct(packed.shape, f32),
@@ -461,7 +460,7 @@
     held = fields
     for bit in chip_bits(cell_count):
         held = jnp.concatenate([held, swap(held, bit, 0)], axis=0)
-    other = hand(held, 1)
+    other = swap_cores(held)
     rows = cell_count * chunks
     return pl.pallas_call(
         finish_kernel,

time: 36.2 us -> 33.7 us (0.931)
  waiting for transfers between devices: 18.5 us -> 1.47 us
  starting transfers between devices: 6.42 us -> 21 us
    ppermute x2, waiting for transfers between devices: 18.5 us -> 1.46 us  [swap_cores(): lax.ppermute(value, 'cell', [(i, i ^ 1) for i in range(lax.axis_size('cel...]
    ppermute x2, starting transfers between devices: 3.65 us -> 18.2 us  [swap_cores(): lax.ppermute(value, 'cell', [(i, i ^ 1) for i in range(lax.axis_size('cel...]
where the time goes in v17:
time: 33.7 us; the launch traced here: 33.5 us
  starting transfers between devices  21 us (62%)
  Pallas kernels  9.37 us (28%)
  waiting for transfers between devices  1.47 us (4%)
  between operations  0.79 us (2%)
  local copies, waits for them, and re-layouts  0.78 us (2%)
    ppermute x2, starting transfers between devices, swap_cores(): lax.ppermute(value, 'cell', [(i, i ^ 1) for i in range(lax.axis_size('cel...  18.2 us
    pallas_call x1, Pallas kernels, shards(): pl.pallas_call(fields_kernel, out_shape=jax.ShapeDtypeStruct((FIELDS + 1,...  3.92 us
    ppermute x4, starting transfers between devices, swap(): return lax.ppermute(value, ('cell', 'cls'), pairs)  2.77 us
    pallas_call x1, Pallas kernels, shards(): pl.pallas_call(finish_kernel, out_shape=[jax.ShapeDtypeStruct(melt.shape,...  2.57 us
    pallas_call x1, Pallas kernels, shards(): pl.pallas_call(apply_kernel, out_shape=jax.ShapeDtypeStruct(split, f32),...  1.51 us
    ppermute x2, waiting for transfers between devices, swap_cores(): lax.ppermute(value, 'cell', [(i, i ^ 1) for i in range(lax.axis_size('cel...  1.46 us
    pallas_call x1, Pallas kernels, shards(): pl.pallas_call(powers_kernel, out_shape=[jax.ShapeDtypeStruct(lefts_shape...  1.26 us
    unnamed x8, local copies, waits for them, and re-layouts  0.78 us
  transfers between devices with their start and end apart: 6, of which 2 were waited for; matrix products, arithmetic and copies ran while one was open for 0% of the time, Pallas kernels for 8%

profile of v17, /device:TPU:0, one launch (start us, length us, event | category | flops | bytes accessed | tf_op | source)
XLA Modules:
  0.0 33.5 jit_solution(16107718142423530777)
XLA Ops:
  0.6 0.0 copy-start.3
  0.6 0.0 copy-start.1
  0.7 3.9 %fields.1.value = f32[9,8,128]{2,1,0:T(8,128)} custom-call(f32[64,8,1024]{2,1,0:T(8,128)} %melt_hbm.1, s32[8,1024]{1,0:T(8,128)} %counts_hbm.1, f32[1,256]{1,0:T(1,128)} %pressure_hbm.1, f32[32,64,64]{2,1,0:T(8,128)} %prop_hbm.3, f32[32,64]{1,0:T(8,128)} %coup_hbm.3, f32[32,64]{1,0:T(8,128)} %flux_hbm.1), custom_call_target="tpu_custom_call" | custom-call | tf_op jit(solution)/shard_map/fields/pallas_call | solution.py:374
  4.6 0.5 %collective-permute-start = (f32[9,8,128]{2,1,0:T(8,128)}, f32[9,8,128]{2,1,0:T(8,128)S(1)}, u32[]{:S(2)}, u32[]{:S(2)}) collective-permute-start(f32[9,8,128]{2,1,0:T(8,128)} %fields.1.value), channel_id=1, source_target_pairs={{0,4},{4,0},{8,12},{12,8},{16,20},{20,16},{24,28},{28,24},{1,5},{5... | collective-permute-start | bytes 110600 | tf_op jit(solution)/shard_map/ppermute | solution.py:348
  5.1 0.0 copy-start.2
  5.1 0.8 %copy-done.2 = f32[9,8,128]{2,1,0:T(8,128)S(1)} copy-done((f32[9,8,128]{2,1,0:T(8,128)S(1)}, f32[9,8,128]{2,1,0:T(8,128)}, u32[]{:S(2)}) %copy-start.2) | copy-done | bytes 36888
  5.9 0.3 collective-permute-done.theirs
  6.2 0.8 %collective-permute-start.1 = (f32[2,9,8,128]{3,2,1,0:T(8,128)S(1)}, f32[2,9,8,128]{3,2,1,0:T(8,128)S(1)}, u32[]{:S(2)}, u32[]{:S(2)}) collective-permute-start(f32[2,9,8,128]{3,2,1,0:T(8,128)S(1)} %join.1._.mine), channel_id=1, source_target_pairs={{0,0},{1,1},{2,2},{3,3},{4,5},{5,4},{6,7},{7,6},{8,8},{9,9},{10,10... | collective-permute-start | bytes 221192 | tf_op jit(solution)/shard_map/ppermute | solution.py:358
  7.0 0.0 copy-done.3
  7.0 0.0 copy-done.1
  7.0 1.3 %powers.1 = (bf16[8,64,192]{2,1,0:T(8,128)(2,1)S(1)}, f32[512,128]{1,0:T(8,128)S(1)}, f32[8,128]{1,0:T(8,128)S(1)}) custom-call(f32[32,64,64]{2,1,0:T(8,128)S(1)} %copy-done.1, f32[32,64]{1,0:T(8,128)S(1)} %copy-done.3, f32[2,9,8,128]{3,2,1,0:T(8,128)S(1)} %join.1._.mine), custom_call_target="tpu_custom_call" | custom-call | flops 1000000000 | bytes 1000000 | tf_op jit(solution)/shard_map/powers/pallas_call | solution.py:414
  8.3 0.0 collective-permute-done.1.theirs
  8.3 0.7 %collective-permute-start.2 = (f32[2,9,8,128]{3,2,1,0:T(8,128)S(1)}, f32[2,9,8,128]{3,2,1,0:T(8,128)S(1)}, u32[]{:S(2)}, u32[]{:S(2)}) collective-permute-start(f32[2,9,8,128]{3,2,1,0:T(8,128)S(1)} %add.1._.mine), channel_id=1, source_target_pairs={{0,0},{1,1},{2,2},{3,3},{4,6},{5,7},{6,4},{7,5},{8,8},{9,9},{10,10... | collective-permute-start | bytes 221192 | tf_op jit(solution)/shard_map/ppermute | solution.py:358
  9.0 0.0 copy-done
  9.0 1.5 %apply.1._.shells = f32[8,512,128]{2,1,0:T(8,128)S(1)} custom-call(f32[512,1024]{1,0:T(8,128)S(1)} %bitcast.1, bf16[8,64,192]{2,1,0:T(8,128)(2,1)S(1)} %get-tuple-element.6.lefts, f32[8,128]{1,0:T(8,128)S(1)} %get-tuple-element.5._.factors, f32[2,9,8,128]{3,2,1,0:T(8,128)S(1)} %add.1._.mine), custom_call_target="tpu_custom_call" | custom-call | flops 1000000000 | bytes 2097152 | tf_op jit(solution)/shard_map/apply/pallas_call | solution.py:441
  10.5 0.0 collective-permute-done.2.theirs
  10.5 0.1 combine.1
  10.6 0.7 %collective-permute-start.3 = (f32[2,8,8,128]{3,2,1,0:T(8,128)S(1)}, f32[2,8,8,128]{3,2,1,0:T(8,128)S(1)}, u32[]{:S(2)}, u32[]{:S(2)}) collective-permute-start(f32[2,8,8,128]{3,2,1,0:T(8,128)S(1)} %combine.1), channel_id=1, source_target_pairs={{0,0},{1,1},{2,2},{3,3},{4,20},{5,21},{6,22},{7,23},{8,8},{9,9},{1... | collective-permute-start | bytes 196616 | tf_op jit(solution)/shard_map/ppermute | solution.py:358
  11.3 0.0 collective-permute-done.3
  11.3 0.7 %collective-permute-start.4 = (f32[4,8,8,128]{3,2,1,0:T(8,128)S(1)}, f32[4,8,8,128]{3,2,1,0:T(8,128)S(1)}, u32[]{:S(2)}, u32[]{:S(2)}) collective-permute-start(f32[4,8,8,128]{3,2,1,0:T(8,128)S(1)} %pad_maximum_fusion.1), channel_id=1, source_target_pairs={{0,0},{1,1},{2,2},{3,3},{4,12},{5,13},{6,14},{7,15},{8,8},{9,9},{1... | collective-permute-start | bytes 393224 | tf_op jit(solution)/shard_map/ppermute | solution.py:358
  12.0 0.0 collective-permute-done.4
  12.0 17.7 %collective-permute-start.5 = (f32[8,8,8,128]{3,2,1,0:T(8,128)S(1)}, f32[8,8,8,128]{3,2,1,0:T(8,128)S(1)}, u32[]{:S(2)}, u32[]{:S(2)}) collective-permute-start(f32[8,8,8,128]{3,2,1,0:T(8,128)S(1)} %pad_maximum_fusion.mine), channel_id=1, source_target_pairs={{0,4},{4,0},{8,12},{12,8},{16,20},{20,16},{24,28},{28,24},{1,5},{5... | collective-permute-start | bytes 786440 | tf_op jit(solution)/shard_map/ppermute | solution.py:348
  29.7 1.2 %collective-permute-done.5.theirs = f32[8,8,8,128]{3,2,1,0:T(8,128)S(1)} collective-permute-done((f32[8,8,8,128]{3,2,1,0:T(8,128)S(1)}, f32[8,8,8,128]{3,2,1,0:T(8,128)S(1)}, u32[]{:S(2)}, u32[]{:S(2)}) %collective-permute-start.5) | collective-permute-done | bytes 262176 | tf_op jit(solution)/shard_map/ppermute | solution.py:348
  30.9 2.6 %finish.1 = (f32[64,8,1024]{2,1,0:T(8,128)}, f32[1,256]{1,0:T(1,128)}) custom-call(f32[8,8,8,128]{3,2,1,0:T(8,128)S(1)} %pad_maximum_fusion.mine, f32[8,8,8,128]{3,2,1,0:T(8,128)S(1)} %collective-permute-done.5.theirs, f32[8,512,128]{2,1,0:T(8,128)S(1)} %apply.1._.shells, f32[512,128]{1,0:T(8,128)S(1)} %get-tuple-element.7.columns), custom_call_target="tpu_custom_call" | custom-call | tf_op jit(solution)/shard_map/finish/pallas_call | solution.py:465
  (6 shorter events, 0.1 us)
Async XLA Ops:
  0.6 6.3 %copy-start.3 = (f32[32,64]{1,0:T(8,128)S(1)}, f32[32,64]{1,0:T(8,128)}, u32[]{:S(2)}) copy-start(f32[32,64]{1,0:T(8,128)} %coup_hbm.3) | copy-start | bytes 24580
  0.6 6.3 %copy-start.1 = (f32[32,64,64]{2,1,0:T(8,128)S(1)}, f32[32,64,64]{2,1,0:T(8,128)}, u32[]{:S(2)}) copy-start(f32[32,64,64]{2,1,0:T(8,128)} %prop_hbm.3) | copy-start | bytes 1572868
  4.6 1.6 %collective-permute-start = (f32[9,8,128]{2,1,0:T(8,128)}, f32[9,8,128]{2,1,0:T(8,128)S(1)}, u32[]{:S(2)}, u32[]{:S(2)}) collective-permute-start(f32[9,8,128]{2,1,0:T(8,128)} %fields.1.value), channel_id=1, source_target_pairs={{0,4},{4,0},{8,12},{12,8},{16,20},{20,16},{24,28},{28,24},{1,5},{5... | collective-permute-start | bytes 110600 | tf_op jit(solution)/shard_map/ppermute | solution.py:348
  5.1 0.8 %copy-start.2 = (f32[9,8,128]{2,1,0:T(8,128)S(1)}, f32[9,8,128]{2,1,0:T(8,128)}, u32[]{:S(2)}) copy-start(f32[9,8,128]{2,1,0:T(8,128)} %fields.1.value) | copy-start | bytes 110596
  5.9 3.1 %copy-start = (f32[64,8,1024]{2,1,0:T(8,128)S(1)}, f32[64,8,1024]{2,1,0:T(8,128)}, u32[]{:S(2)}) copy-start(f32[64,8,1024]{2,1,0:T(8,128)} %melt_hbm.1) | copy-start | bytes 6291460
  6.2 2.1 %collective-permute-start.1 = (f32[2,9,8,128]{3,2,1,0:T(8,128)S(1)}, f32[2,9,8,128]{3,2,1,0:T(8,128)S(1)}, u32[]{:S(2)}, u32[]{:S(2)}) collective-permute-start(f32[2,9,8,128]{3,2,1,0:T(8,128)S(1)} %join.1._.mine), channel_id=1, source_target_pairs={{0,0},{1,1},{2,2},{3,3},{4,5},{5,4},{6,7},{7,6},{8,8},{9,9},{10,10... | collective-permute-start | bytes 221192 | tf_op jit(solution)/shard_map/ppermute | solution.py:358
  8.3 2.2 %collective-permute-start.2 = (f32[2,9,8,128]{3,2,1,0:T(8,128)S(1)}, f32[2,9,8,128]{3,2,1,0:T(8,128)S(1)}, u32[]{:S(2)}, u32[]{:S(2)}) collective-permute-start(f32[2,9,8,128]{3,2,1,0:T(8,128)S(1)} %add.1._.mine), channel_id=1, source_target_pairs={{0,0},{1,1},{2,2},{3,3},{4,6},{5,7},{6,4},{7,5},{8,8},{9,9},{10,10... | collective-permute-start | bytes 221192 | tf_op jit(solution)/shard_map/ppermute | solution.py:358
  10.6 0.7 %collective-permute-start.3 = (f32[2,8,8,128]{3,2,1,0:T(8,128)S(1)}, f32[2,8,8,128]{3,2,1,0:T(8,128)S(1)}, u32[]{:S(2)}, u32[]{:S(2)}) collective-permute-start(f32[2,8,8,128]{3,2,1,0:T(8,128)S(1)} %combine.1), channel_id=1, source_target_pairs={{0,0},{1,1},{2,2},{3,3},{4,20},{5,21},{6,22},{7,23},{8,8},{9,9},{1... | collective-permute-start | bytes 196616 | tf_op jit(solution)/shard_map/ppermute | solution.py:358
  11.3 0.7 %collective-permute-start.4 = (f32[4,8,8,128]{3,2,1,0:T(8,128)S(1)}, f32[4,8,8,128]{3,2,1,0:T(8,128)S(1)}, u32[]{:S(2)}, u32[]{:S(2)}) collective-permute-start(f32[4,8,8,128]{3,2,1,0:T(8,128)S(1)} %pad_maximum_fusion.1), channel_id=1, source_target_pairs={{0,0},{1,1},{2,2},{3,3},{4,12},{5,13},{6,14},{7,15},{8,8},{9,9},{1... | collective-permute-start | bytes 393224 | tf_op jit(solution)/shard_map/ppermute | solution.py:358
  12.0 18.9 %collective-permute-start.5 = (f32[8,8,8,128]{3,2,1,0:T(8,128)S(1)}, f32[8,8,8,128]{3,2,1,0:T(8,128)S(1)}, u32[]{:S(2)}, u32[]{:S(2)}) collective-permute-start(f32[8,8,8,128]{3,2,1,0:T(8,128)S(1)} %pad_maximum_fusion.mine), channel_id=1, source_target_pairs={{0,4},{4,0},{8,12},{12,8},{16,20},{20,16},{24,28},{28,24},{1,5},{5... | collective-permute-start | bytes 786440 | tf_op jit(solution)/shard_map/ppermute | solution.py:348

commit v18 on v14

--- a/solution.py
+++ b/solution.py
@@ -202,18 +202,21 @@
 
 def combine_kernel(senders, mine, theirs, _, out, kept):
     total = mine[...] + theirs[...]
-    tail = out.shape[0] - 1
-    tile = out.shape[1] // senders
+    tail = out.shape[1] - 1
+    tile = out.shape[2] // senders
     pressure = total[2 * SUBSTEPS]
     wall = 0.5 * pressure
-    for t in range(SUBSTEPS - 1):
-        out[t] = total[t] + total[SUBSTEPS + t] * wall
-        out[SUBSTEPS - 1 + t] = total[SUBSTEPS + t]
-    out[tail - 1] = pressure
     gas = total[SUBSTEPS - 1] + total[2 * SUBSTEPS - 1] * wall
     kept[...] = gas
-    out[tail] = jnp.broadcast_to(total_of(gas), gas.shape)
-    out[tail, :tile, :] = kept[pl.ds(lax.axis_index("cls") * tile, tile), :]
+    own = kept[pl.ds(lax.axis_index("cls") * tile, tile), :]
+    gas_total = jnp.broadcast_to(total_of(gas), gas.shape)
+    for n in range(out.shape[0]):
+        for t in range(SUBSTEPS - 1):
+            out[n, t] = total[t] + total[SUBSTEPS + t] * wall
+            out[n, SUBSTEPS - 1 + t] = total[SUBSTEPS + t]
+        out[n, tail - 1] = pressure
+        out[n, tail] = gas_total
+        out[n, tail, :tile, :] = own
 
 
 def total_of(x):
@@ -399,7 +402,7 @@
     )(melt.reshape(nodes * classes, cells), lefts, factors, packed)
     fields = pl.pallas_call(
         functools.partial(combine_kernel, cls_count),
-        out_shape=jax.ShapeDtypeStruct((FIELDS, chunks, LANES), f32),
+        out_shape=jax.ShapeDtypeStruct((cell_count // 2, FIELDS, chunks, LANES), f32),
         in_specs=[VMEM, VMEM, VMEM],
         out_specs=VMEM,
         scratch_shapes=[pltpu.VMEM((chunks, LANES), f32)],
@@ -407,7 +410,9 @@
         name="combine",
     )(packed, theirs, shells)
     groups = [list(range(core, cell_count, 2)) for core in range(2)]
-    own = lax.all_gather(fields, "cell", axis=0, axis_index_groups=groups)
+    own = lax.all_to_all(
+        fields, "cell", split_axis=0, concat_axis=0, tiled=True, axis_index_groups=groups
+    )
     other = partner(own, "cell", 1)
     rows = cell_count * chunks
     return pl.pallas_call(

time: 27.8 us -> 27.9 us (level)
    all_to_all x0 -> x1, blocking collectives: none -> 8.9 us  [shards(): lax.all_to_all(fields, 'cell', split_axis=0, concat_axis=0, tiled=True, a...]
    all_gather x1 -> x0, blocking collectives: 8.84 us -> none  [shards(): own = lax.all_gather(fields, 'cell', axis=0, axis_index_groups=groups)]
    unnamed x8 -> x10, local copies, waits for them, and re-layouts: 0.81 us -> 0.81 us
where the time goes in v18:
time: 27.9 us; the launch traced here: 27.7 us
  Pallas kernels  9.3 us (33%)
  blocking collectives  8.9 us (32%)
  starting transfers between devices  6.14 us (22%)
  waiting for transfers between devices  1.85 us (7%)
  local copies, waits for them, and re-layouts  0.81 us (3%)
  between operations  0.69 us (2%)
    all_to_all x1, blocking collectives, shards(): lax.all_to_all(fields, 'cell', split_axis=0, concat_axis=0, tiled=True, a...  8.9 us
    ppermute x3, starting transfers between devices, partner(): lax.ppermute(value, axis, [(i, i ^ distance) for i in range(lax.axis_size...  6.14 us
    pallas_call x1, Pallas kernels, shards(): pl.pallas_call(fields_kernel, out_shape=jax.ShapeDtypeStruct((FIELDS + 1,...  3.92 us
    pallas_call x1, Pallas kernels, shards(): pl.pallas_call(finish_kernel, out_shape=[jax.ShapeDtypeStruct(melt.shape,...  2.52 us
    ppermute x3, waiting for transfers between devices, partner(): lax.ppermute(value, axis, [(i, i ^ distance) for i in range(lax.axis_size...  1.85 us
    pallas_call x1, Pallas kernels, shards(): pl.pallas_call(apply_kernel, out_shape=jax.ShapeDtypeStruct(split, f32),...  1.51 us
    pallas_call x1, Pallas kernels, shards(): pl.pallas_call(powers_kernel, out_shape=[jax.ShapeDtypeStruct(lefts_shape...  1.25 us
    unnamed x10, local copies, waits for them, and re-layouts  0.81 us
  transfers between devices with their start and end apart: 3, of which 3 were waited for; matrix products, arithmetic and copies ran while one was open for 0% of the time, Pallas kernels for 10%

profile of v18, /device:TPU:0, one launch (start us, length us, event | category | flops | bytes accessed | tf_op | source)
XLA Modules:
  0.0 27.7 jit_solution(3892404234595916145)
XLA Ops:
  0.6 0.0 copy-start.4
  0.6 0.0 copy-start.1
  0.7 3.9 %fields.1._.mine = f32[9,8,128]{2,1,0:T(8,128)} custom-call(f32[64,8,1024]{2,1,0:T(8,128)} %melt_hbm.1, s32[8,1024]{1,0:T(8,128)} %counts_hbm.1, f32[1,256]{1,0:T(1,128)} %pressure_hbm.1, f32[32,64,64]{2,1,0:T(8,128)} %prop_hbm.3, f32[32,64]{1,0:T(8,128)} %coup_hbm.3, f32[32,64]{1,0:T(8,128)} %flux_hbm.1), custom_call_target="tpu_custom_call" | custom-call | tf_op jit(solution)/shard_map/fields/pallas_call | solution.py:344
  4.6 0.0 copy-start
  4.6 3.0 %collective-permute-start = (f32[9,8,128]{2,1,0:T(8,128)}, f32[9,8,128]{2,1,0:T(8,128)S(1)}, u32[]{:S(2)}, u32[]{:S(2)}) collective-permute-start(f32[9,8,128]{2,1,0:T(8,128)} %fields.1._.mine), channel_id=1, source_target_pairs={{0,1},{1,0},{2,3},{3,2},{4,5},{5,4},{6,7},{7,6},{8,9},{9,8},{10,11... | collective-permute-start | bytes 110600 | tf_op jit(solution)/shard_map/ppermute | solution.py:328
  7.6 0.0 copy-done.4
  7.6 0.0 copy-done.1
  7.6 0.0 copy-start.2
  7.6 0.8 %copy-done.2 = f32[9,8,128]{2,1,0:T(8,128)S(1)} copy-done((f32[9,8,128]{2,1,0:T(8,128)S(1)}, f32[9,8,128]{2,1,0:T(8,128)}, u32[]{:S(2)}) %copy-start.2) | copy-done | bytes 36888
  8.4 0.0 copy-start.3
  8.4 1.3 %powers.1 = (bf16[8,64,192]{2,1,0:T(8,128)(2,1)S(1)}, f32[512,128]{1,0:T(8,128)S(1)}, f32[8,128]{1,0:T(8,128)S(1)}) custom-call(f32[32,64,64]{2,1,0:T(8,128)S(1)} %copy-done.1, f32[32,64]{1,0:T(8,128)S(1)} %copy-done.4, f32[9,8,128]{2,1,0:T(8,128)S(1)} %copy-done.2), custom_call_target="tpu_custom_call" | custom-call | flops 1000000000 | bytes 1000000 | tf_op jit(solution)/shard_map/powers/pallas_call | solution.py:366
  9.7 0.1 collective-permute-done.theirs
  9.8 0.0 copy-done.3
  9.8 3.1 %collective-permute-start.1 = (f32[9,8,128]{2,1,0:T(8,128)S(1)}, f32[9,8,128]{2,1,0:T(8,128)S(1)}, u32[]{:S(2)}, u32[]{:S(2)}) collective-permute-start(f32[9,8,128]{2,1,0:T(8,128)S(1)} %add.1._.mine), channel_id=1, source_target_pairs={{0,2},{1,3},{2,0},{3,1},{4,6},{5,7},{6,4},{7,5},{8,10},{9,11},{10,... | collective-permute-start | bytes 110600 | tf_op jit(solution)/shard_map/ppermute | solution.py:328
  12.9 0.0 copy-done
  12.9 1.5 %apply.1._.shells = f32[8,512,128]{2,1,0:T(8,128)S(1)} custom-call(f32[512,1024]{1,0:T(8,128)S(1)} %bitcast.1, bf16[8,64,192]{2,1,0:T(8,128)(2,1)S(1)} %get-tuple-element.6.lefts, f32[8,128]{1,0:T(8,128)S(1)} %get-tuple-element.5._.factors, f32[9,8,128]{2,1,0:T(8,128)S(1)} %add.1._.mine), custom_call_target="tpu_custom_call" | custom-call | flops 1000000000 | bytes 2097152 | tf_op jit(solution)/shard_map/apply/pallas_call | solution.py:393
  14.4 0.4 %collective-permute-done.1.theirs = f32[9,8,128]{2,1,0:T(8,128)S(1)} collective-permute-done((f32[9,8,128]{2,1,0:T(8,128)S(1)}, f32[9,8,128]{2,1,0:T(8,128)S(1)}, u32[]{:S(2)}, u32[]{:S(2)}) %collective-permute-start.1) | collective-permute-done | bytes 36896 | tf_op jit(solution)/shard_map/ppermute | solution.py:328
  14.8 0.1 combine.1
  14.9 8.9 %all_to_all.5.mine = f32[4,8,8,128]{3,2,1,0:T(8,128)S(1)} all-to-all(f32[4,8,8,128]{3,2,1,0:T(8,128)S(1)} %combine.1), channel_id=1, replica_groups={{0,8,16,24},{4,12,20,28},{1,9,17,25},{5,13,21,29},{2,10,18,26},{6,14,22..., dimensions={0} | all-to-all | bytes 262144 | tf_op jit(solution)/shard_map/all_to_all | solution.py:413
  23.8 0.0 collective-permute-start.2
  23.8 1.3 %collective-permute-done.2.theirs = f32[4,8,8,128]{3,2,1,0:T(8,128)S(1)} collective-permute-done((f32[4,8,8,128]{3,2,1,0:T(8,128)S(1)}, f32[4,8,8,128]{3,2,1,0:T(8,128)S(1)}, u32[]{:S(2)}, u32[]{:S(2)}) %collective-permute-start.2) | collective-permute-done | bytes 131104 | tf_op jit(solution)/shard_map/ppermute | solution.py:328
  25.2 2.5 %finish.1 = (f32[64,8,1024]{2,1,0:T(8,128)}, f32[1,256]{1,0:T(1,128)}) custom-call(f32[4,8,8,128]{3,2,1,0:T(8,128)S(1)} %all_to_all.5.mine, f32[4,8,8,128]{3,2,1,0:T(8,128)S(1)} %collective-permute-done.2.theirs, f32[8,512,128]{2,1,0:T(8,128)S(1)} %apply.1._.shells, f32[512,128]{1,0:T(8,128)S(1)} %get-tuple-element.7.columns), custom_call_target="tpu_custom_call" | custom-call | tf_op jit(solution)/shard_map/finish/pallas_call | solution.py:418
  (1 shorter events, 0.0 us)
Async XLA Ops:
  0.6 7.0 %copy-start.4 = (f32[32,64]{1,0:T(8,128)S(1)}, f32[32,64]{1,0:T(8,128)}, u32[]{:S(2)}) copy-start(f32[32,64]{1,0:T(8,128)} %coup_hbm.3) | copy-start | bytes 24580
  0.6 7.0 %copy-start.1 = (f32[32,64,64]{2,1,0:T(8,128)S(1)}, f32[32,64,64]{2,1,0:T(8,128)}, u32[]{:S(2)}) copy-start(f32[32,64,64]{2,1,0:T(8,128)} %prop_hbm.3) | copy-start | bytes 1572868
  4.6 8.3 %copy-start = (f32[64,8,1024]{2,1,0:T(8,128)S(1)}, f32[64,8,1024]{2,1,0:T(8,128)}, u32[]{:S(2)}) copy-start(f32[64,8,1024]{2,1,0:T(8,128)} %melt_hbm.1) | copy-start | bytes 6291460
  4.6 5.2 %collective-permute-start = (f32[9,8,128]{2,1,0:T(8,128)}, f32[9,8,128]{2,1,0:T(8,128)S(1)}, u32[]{:S(2)}, u32[]{:S(2)}) collective-permute-start(f32[9,8,128]{2,1,0:T(8,128)} %fields.1._.mine), channel_id=1, source_target_pairs={{0,1},{1,0},{2,3},{3,2},{4,5},{5,4},{6,7},{7,6},{8,9},{9,8},{10,11... | collective-permute-start | bytes 110600 | tf_op jit(solution)/shard_map/ppermute | solution.py:328
  7.6 0.8 %copy-start.2 = (f32[9,8,128]{2,1,0:T(8,128)S(1)}, f32[9,8,128]{2,1,0:T(8,128)}, u32[]{:S(2)}) copy-start(f32[9,8,128]{2,1,0:T(8,128)} %fields.1._.mine) | copy-start | bytes 110596
  8.4 1.3 %copy-start.3 = (f32[9,8,128]{2,1,0:T(8,128)S(1)}, f32[9,8,128]{2,1,0:T(8,128)}, u32[]{:S(2)}) copy-start(f32[9,8,128]{2,1,0:T(8,128)} %fields.1._.mine) | copy-start | bytes 110596
  9.8 5.0 %collective-permute-start.1 = (f32[9,8,128]{2,1,0:T(8,128)S(1)}, f32[9,8,128]{2,1,0:T(8,128)S(1)}, u32[]{:S(2)}, u32[]{:S(2)}) collective-permute-start(f32[9,8,128]{2,1,0:T(8,128)S(1)} %add.1._.mine), channel_id=1, source_target_pairs={{0,2},{1,3},{2,0},{3,1},{4,6},{5,7},{6,4},{7,5},{8,10},{9,11},{10,... | collective-permute-start | bytes 110600 | tf_op jit(solution)/shard_map/ppermute | solution.py:328
  23.8 1.3 %collective-permute-start.2 = (f32[4,8,8,128]{3,2,1,0:T(8,128)S(1)}, f32[4,8,8,128]{3,2,1,0:T(8,128)S(1)}, u32[]{:S(2)}, u32[]{:S(2)}) collective-permute-start(f32[4,8,8,128]{3,2,1,0:T(8,128)S(1)} %all_to_all.5.mine), channel_id=1, source_target_pairs={{0,4},{4,0},{8,12},{12,8},{16,20},{20,16},{24,28},{28,24},{1,5},{5... | collective-permute-start | bytes 393224 | tf_op jit(solution)/shard_map/ppermute | solution.py:328

commit v19 on v15

--- a/solution.py
+++ b/solution.py
@@ -255,12 +255,10 @@
 
     plane = pressure_out.shape[1]
     cell = lax.axis_index("cell")
-    even = cell % 2 == 0
     blocks = window.shape[0]
-    bits = chip_bits(blocks)
-    for n, (first, second) in enumerate(zip(offsets(bits), offsets(bits[::-1]))):
-        window[cell ^ jnp.where(even, first, second)] = mine[n]
-        window[cell ^ 1 ^ jnp.where(even, second, first)] = theirs[n]
+    for n, offset in enumerate(offsets(blocks)):
+        window[cell ^ offset] = mine[n]
+        window[cell ^ 1 ^ offset] = theirs[n]
     rows = blocks * chunks
     per = plane // LANES
     tile = pressure_out.shape[0] * per
@@ -324,14 +322,16 @@
 DMA = pltpu.SemaphoreType.DMA
 
 
-def chip_bits(count):
-    return [1 << b for b in reversed(range(1, count.bit_length() - 1))]
-
-
-def offsets(bits):
+def stages(count):
+    bits = [1 << b for b in range(1, count.bit_length() - 1)]
+    pairs = [bits[n : n + 2] for n in range(0, len(bits), 2)]
+    return [[sum(pair)] + pair[::-1] if len(pair) > 1 else pair for pair in pairs]
+
+
+def offsets(count):
     found = [0]
-    for bit in bits:
-        found = found + [m ^ bit for m in found]
+    for stage in stages(count):
+        found = found + [m ^ offset for offset in stage[::-1] for m in found]
     return found
 
 
@@ -420,11 +420,10 @@
         compiler_params=little,
         name="combine",
     )(packed, theirs, shells)
-    bits = chip_bits(cell_count)
     held = fields
-    for even, odd in zip(bits, reversed(bits)):
-        pairs = [(i, i ^ (odd if i % 2 else even)) for i in range(cell_count)]
-        held = jnp.concatenate([held, lax.ppermute(held, "cell", pairs)], axis=0)
+    for stage in stages(cell_count):
+        arrived = [partner(held, "cell", offset) for offset in stage]
+        held = jnp.concatenate([held] + arrived[::-1], axis=0)
     other = partner(held, "cell", 1)
     rows = cell_count * chunks
     return pl.pallas_call(

time: 27.5 us -> 26.3 us (0.956)
  waiting for transfers between devices: 6.28 us -> 5.59 us
  starting transfers between devices: 10.1 us -> 9.7 us
    ppermute x2 -> x0, waiting for transfers between devices: 4.44 us -> none  [shards(): held = jnp.concatenate([held, lax.ppermute(held, 'cell', pairs)], axis=0)]
    ppermute x2 -> x0, starting transfers between devices: 3.93 us -> none  [shards(): held = jnp.concatenate([held, lax.ppermute(held, 'cell', pairs)], axis=0)]
    ppermute x3 -> x6, waiting for transfers between devices: 1.84 us -> 5.59 us  [partner(): lax.ppermute(value, axis, [(i, i ^ distance) for i in range(lax.axis_size...]
    ppermute x3 -> x6, starting transfers between devices: 6.21 us -> 9.7 us  [partner(): lax.ppermute(value, axis, [(i, i ^ distance) for i in range(lax.axis_size...]
  transfers between devices with their start and end apart: 5 -> 6, of which waited for: 5 -> 6; matrix products, arithmetic and copies ran while one was open for 0% -> 0% of each run, Pallas kernels for 10% -> 11%
where the time goes in v19:
time: 26.3 us; the launch traced here: 26.1 us
  starting transfers between devices  9.7 us (37%)
  Pallas kernels  9.32 us (35%)
  waiting for transfers between devices  5.59 us (21%)
  local copies, waits for them, and re-layouts  0.81 us (3%)
  between operations  0.7 us (3%)
    ppermute x6, starting transfers between devices, partner(): lax.ppermute(value, axis, [(i, i ^ distance) for i in range(lax.axis_size...  9.7 us
    ppermute x6, waiting for transfers between devices, partner(): lax.ppermute(value, axis, [(i, i ^ distance) for i in range(lax.axis_size...  5.59 us
    pallas_call x1, Pallas kernels, shards(): pl.pallas_call(fields_kernel, out_shape=jax.ShapeDtypeStruct((FIELDS + 1,...  3.92 us
    pallas_call x1, Pallas kernels, shards(): pl.pallas_call(finish_kernel, out_shape=[jax.ShapeDtypeStruct(melt.shape,...  2.54 us
    pallas_call x1, Pallas kernels, shards(): pl.pallas_call(apply_kernel, out_shape=jax.ShapeDtypeStruct(split, f32),...  1.51 us
    pallas_call x1, Pallas kernels, shards(): pl.pallas_call(powers_kernel, out_shape=[jax.ShapeDtypeStruct(lefts_shape...  1.25 us
    unnamed x10, local copies, waits for them, and re-layouts  0.81 us
  transfers between devices with their start and end apart: 6, of which 6 were waited for; matrix products, arithmetic and copies ran while one was open for 0% of the time, Pallas kernels for 11%

profile of v19, /device:TPU:0, one launch (start us, length us, event | category | flops | bytes accessed | tf_op | source)
XLA Modules:
  0.0 26.1 jit_solution(4280679236651582737)
XLA Ops:
  0.6 0.0 copy-start.4
  0.6 0.0 copy-start.1
  0.7 3.9 %fields.1._.mine = f32[9,8,128]{2,1,0:T(8,128)} custom-call(f32[64,8,1024]{2,1,0:T(8,128)} %melt_hbm.1, s32[8,1024]{1,0:T(8,128)} %counts_hbm.1, f32[1,256]{1,0:T(1,128)} %pressure_hbm.1, f32[32,64,64]{2,1,0:T(8,128)} %prop_hbm.3, f32[32,64]{1,0:T(8,128)} %coup_hbm.3, f32[32,64]{1,0:T(8,128)} %flux_hbm.1), custom_call_target="tpu_custom_call" | custom-call | tf_op jit(solution)/shard_map/fields/pallas_call | solution.py:355
  4.6 0.0 copy-start
  4.6 3.0 %collective-permute-start = (f32[9,8,128]{2,1,0:T(8,128)}, f32[9,8,128]{2,1,0:T(8,128)S(1)}, u32[]{:S(2)}, u32[]{:S(2)}) collective-permute-start(f32[9,8,128]{2,1,0:T(8,128)} %fields.1._.mine), channel_id=1, source_target_pairs={{0,1},{1,0},{2,3},{3,2},{4,5},{5,4},{6,7},{7,6},{8,9},{9,8},{10,11... | collective-permute-start | bytes 110600 | tf_op jit(solution)/shard_map/ppermute | solution.py:339
  7.6 0.0 copy-done.4
  7.6 0.0 copy-done.1
  7.6 0.8 %copy-done.2 = f32[9,8,128]{2,1,0:T(8,128)S(1)} copy-done((f32[9,8,128]{2,1,0:T(8,128)S(1)}, f32[9,8,128]{2,1,0:T(8,128)}, u32[]{:S(2)}) %copy-start.2) | copy-done | bytes 36888
  8.4 1.3 %powers.1 = (bf16[8,64,192]{2,1,0:T(8,128)(2,1)S(1)}, f32[512,128]{1,0:T(8,128)S(1)}, f32[8,128]{1,0:T(8,128)S(1)}) custom-call(f32[32,64,64]{2,1,0:T(8,128)S(1)} %copy-done.1, f32[32,64]{1,0:T(8,128)S(1)} %copy-done.4, f32[9,8,128]{2,1,0:T(8,128)S(1)} %copy-done.2), custom_call_target="tpu_custom_call" | custom-call | flops 1000000000 | bytes 1000000 | tf_op jit(solution)/shard_map/powers/pallas_call | solution.py:377
  9.7 0.1 collective-permute-done.theirs
  9.8 0.0 copy-done.3
  9.8 3.1 %collective-permute-start.1 = (f32[9,8,128]{2,1,0:T(8,128)S(1)}, f32[9,8,128]{2,1,0:T(8,128)S(1)}, u32[]{:S(2)}, u32[]{:S(2)}) collective-permute-start(f32[9,8,128]{2,1,0:T(8,128)S(1)} %add.1._.mine), channel_id=1, source_target_pairs={{0,2},{1,3},{2,0},{3,1},{4,6},{5,7},{6,4},{7,5},{8,10},{9,11},{10,... | collective-permute-start | bytes 110600 | tf_op jit(solution)/shard_map/ppermute | solution.py:339
  12.9 1.5 %apply.1._.shells = f32[8,512,128]{2,1,0:T(8,128)S(1)} custom-call(f32[512,1024]{1,0:T(8,128)S(1)} %bitcast.1, bf16[8,64,192]{2,1,0:T(8,128)(2,1)S(1)} %get-tuple-element.6.lefts, f32[8,128]{1,0:T(8,128)S(1)} %get-tuple-element.5._.factors, f32[9,8,128]{2,1,0:T(8,128)S(1)} %add.1._.mine), custom_call_target="tpu_custom_call" | custom-call | flops 1000000000 | bytes 2097152 | tf_op jit(solution)/shard_map/apply/pallas_call | solution.py:404
  14.4 0.4 %collective-permute-done.1.theirs = f32[9,8,128]{2,1,0:T(8,128)S(1)} collective-permute-done((f32[9,8,128]{2,1,0:T(8,128)S(1)}, f32[9,8,128]{2,1,0:T(8,128)S(1)}, u32[]{:S(2)}, u32[]{:S(2)}) %collective-permute-start.1) | collective-permute-done | bytes 36896 | tf_op jit(solution)/shard_map/ppermute | solution.py:339
  14.8 0.1 combine.1
  14.9 2.8 %collective-permute-start.4 = (f32[1,8,8,128]{3,2,1,0:T(8,128)S(1)}, f32[1,8,8,128]{3,2,1,0:T(8,128)S(1)}, u32[]{:S(2)}, u32[]{:S(2)}) collective-permute-start(f32[1,8,8,128]{3,2,1,0:T(8,128)S(1)} %combine.1), channel_id=1, source_target_pairs={{0,24},{4,28},{8,16},{12,20},{16,8},{20,12},{24,0},{28,4},{1,25},{... | collective-permute-start | bytes 98312 | tf_op jit(solution)/shard_map/ppermute | solution.py:339
  17.7 0.5 %collective-permute-start.3 = (f32[1,8,8,128]{3,2,1,0:T(8,128)S(1)}, f32[1,8,8,128]{3,2,1,0:T(8,128)S(1)}, u32[]{:S(2)}, u32[]{:S(2)}) collective-permute-start(f32[1,8,8,128]{3,2,1,0:T(8,128)S(1)} %combine.1), channel_id=1, source_target_pairs={{0,16},{4,20},{8,24},{12,28},{16,0},{20,4},{24,8},{28,12},{1,17},{... | collective-permute-start | bytes 98312 | tf_op jit(solution)/shard_map/ppermute | solution.py:339
  18.2 0.2 collective-permute-start.2
  18.4 1.5 %collective-permute-done.4 = f32[1,8,8,128]{3,2,1,0:T(8,128)S(1)} collective-permute-done((f32[1,8,8,128]{3,2,1,0:T(8,128)S(1)}, f32[1,8,8,128]{3,2,1,0:T(8,128)S(1)}, u32[]{:S(2)}, u32[]{:S(2)}) %collective-permute-start.4) | collective-permute-done | bytes 32800 | tf_op jit(solution)/shard_map/ppermute | solution.py:339
  19.9 1.7 %collective-permute-done.3 = f32[1,8,8,128]{3,2,1,0:T(8,128)S(1)} collective-permute-done((f32[1,8,8,128]{3,2,1,0:T(8,128)S(1)}, f32[1,8,8,128]{3,2,1,0:T(8,128)S(1)}, u32[]{:S(2)}, u32[]{:S(2)}) %collective-permute-start.3) | collective-permute-done | bytes 32800 | tf_op jit(solution)/shard_map/ppermute | solution.py:339
  21.7 0.5 %collective-permute-done.2 = f32[1,8,8,128]{3,2,1,0:T(8,128)S(1)} collective-permute-done((f32[1,8,8,128]{3,2,1,0:T(8,128)S(1)}, f32[1,8,8,128]{3,2,1,0:T(8,128)S(1)}, u32[]{:S(2)}, u32[]{:S(2)}) %collective-permute-start.2) | collective-permute-done | bytes 32800 | tf_op jit(solution)/shard_map/ppermute | solution.py:339
  22.2 0.1 collective-permute-start.5
  22.3 1.3 %collective-permute-done.5.theirs = f32[4,8,8,128]{3,2,1,0:T(8,128)S(1)} collective-permute-done((f32[4,8,8,128]{3,2,1,0:T(8,128)S(1)}, f32[4,8,8,128]{3,2,1,0:T(8,128)S(1)}, u32[]{:S(2)}, u32[]{:S(2)}) %collective-permute-start.5) | collective-permute-done | bytes 131104 | tf_op jit(solution)/shard_map/ppermute | solution.py:339
  23.6 2.5 %finish.1 = (f32[64,8,1024]{2,1,0:T(8,128)}, f32[1,256]{1,0:T(1,128)}) custom-call(f32[4,8,8,128]{3,2,1,0:T(8,128)S(1)} %pad_maximum_fusion.mine, f32[4,8,8,128]{3,2,1,0:T(8,128)S(1)} %collective-permute-done.5.theirs, f32[8,512,128]{2,1,0:T(8,128)S(1)} %apply.1._.shells, f32[512,128]{1,0:T(8,128)S(1)} %get-tuple-element.7.columns), custom_call_target="tpu_custom_call" | custom-call | tf_op jit(solution)/shard_map/finish/pallas_call | solution.py:429
  (5 shorter events, 0.0 us)
Async XLA Ops:
  0.6 7.0 %copy-start.4 = (f32[32,64]{1,0:T(8,128)S(1)}, f32[32,64]{1,0:T(8,128)}, u32[]{:S(2)}) copy-start(f32[32,64]{1,0:T(8,128)} %coup_hbm.3) | copy-start | bytes 24580
  0.6 7.0 %copy-start.1 = (f32[32,64,64]{2,1,0:T(8,128)S(1)}, f32[32,64,64]{2,1,0:T(8,128)}, u32[]{:S(2)}) copy-start(f32[32,64,64]{2,1,0:T(8,128)} %prop_hbm.3) | copy-start | bytes 1572868
  4.6 8.3 %copy-start = (f32[64,8,1024]{2,1,0:T(8,128)S(1)}, f32[64,8,1024]{2,1,0:T(8,128)}, u32[]{:S(2)}) copy-start(f32[64,8,1024]{2,1,0:T(8,128)} %melt_hbm.1) | copy-start | bytes 6291460
  4.6 5.2 %collective-permute-start = (f32[9,8,128]{2,1,0:T(8,128)}, f32[9,8,128]{2,1,0:T(8,128)S(1)}, u32[]{:S(2)}, u32[]{:S(2)}) collective-permute-start(f32[9,8,128]{2,1,0:T(8,128)} %fields.1._.mine), channel_id=1, source_target_pairs={{0,1},{1,0},{2,3},{3,2},{4,5},{5,4},{6,7},{7,6},{8,9},{9,8},{10,11... | collective-permute-start | bytes 110600 | tf_op jit(solution)/shard_map/ppermute | solution.py:339
  7.6 0.8 %copy-start.2 = (f32[9,8,128]{2,1,0:T(8,128)S(1)}, f32[9,8,128]{2,1,0:T(8,128)}, u32[]{:S(2)}) copy-start(f32[9,8,128]{2,1,0:T(8,128)} %fields.1._.mine) | copy-start | bytes 110596
  8.4 1.3 %copy-start.3 = (f32[9,8,128]{2,1,0:T(8,128)S(1)}, f32[9,8,128]{2,1,0:T(8,128)}, u32[]{:S(2)}) copy-start(f32[9,8,128]{2,1,0:T(8,128)} %fields.1._.mine) | copy-start | bytes 110596
  9.8 5.0 %collective-permute-start.1 = (f32[9,8,128]{2,1,0:T(8,128)S(1)}, f32[9,8,128]{2,1,0:T(8,128)S(1)}, u32[]{:S(2)}, u32[]{:S(2)}) collective-permute-start(f32[9,8,128]{2,1,0:T(8,128)S(1)} %add.1._.mine), channel_id=1, source_target_pairs={{0,2},{1,3},{2,0},{3,1},{4,6},{5,7},{6,4},{7,5},{8,10},{9,11},{10,... | collective-permute-start | bytes 110600 | tf_op jit(solution)/shard_map/ppermute | solution.py:339
  14.9 5.0 %collective-permute-start.4 = (f32[1,8,8,128]{3,2,1,0:T(8,128)S(1)}, f32[1,8,8,128]{3,2,1,0:T(8,128)S(1)}, u32[]{:S(2)}, u32[]{:S(2)}) collective-permute-start(f32[1,8,8,128]{3,2,1,0:T(8,128)S(1)} %combine.1), channel_id=1, source_target_pairs={{0,24},{4,28},{8,16},{12,20},{16,8},{20,12},{24,0},{28,4},{1,25},{... | collective-permute-start | bytes 98312 | tf_op jit(solution)/shard_map/ppermute | solution.py:339
  17.7 3.9 %collective-permute-start.3 = (f32[1,8,8,128]{3,2,1,0:T(8,128)S(1)}, f32[1,8,8,128]{3,2,1,0:T(8,128)S(1)}, u32[]{:S(2)}, u32[]{:S(2)}) collective-permute-start(f32[1,8,8,128]{3,2,1,0:T(8,128)S(1)} %combine.1), channel_id=1, source_target_pairs={{0,16},{4,20},{8,24},{12,28},{16,0},{20,4},{24,8},{28,12},{1,17},{... | collective-permute-start | bytes 98312 | tf_op jit(solution)/shard_map/ppermute | solution.py:339
  18.2 3.9 %collective-permute-start.2 = (f32[1,8,8,128]{3,2,1,0:T(8,128)S(1)}, f32[1,8,8,128]{3,2,1,0:T(8,128)S(1)}, u32[]{:S(2)}, u32[]{:S(2)}) collective-permute-start(f32[1,8,8,128]{3,2,1,0:T(8,128)S(1)} %combine.1), channel_id=1, source_target_pairs={{0,8},{4,12},{8,0},{12,4},{16,24},{20,28},{24,16},{28,20},{1,9},{5... | collective-permute-start | bytes 98312 | tf_op jit(solution)/shard_map/ppermute | solution.py:339
  22.2 1.4 %collective-permute-start.5 = (f32[4,8,8,128]{3,2,1,0:T(8,128)S(1)}, f32[4,8,8,128]{3,2,1,0:T(8,128)S(1)}, u32[]{:S(2)}, u32[]{:S(2)}) collective-permute-start(f32[4,8,8,128]{3,2,1,0:T(8,128)S(1)} %pad_maximum_fusion.mine), channel_id=1, source_target_pairs={{0,4},{4,0},{8,12},{12,8},{16,20},{20,16},{24,28},{28,24},{1,5},{5... | collective-permute-start | bytes 393224 | tf_op jit(solution)/shard_map/ppermute | solution.py:339

commit v20 on v19

--- a/solution.py
+++ b/solution.py
@@ -325,13 +325,13 @@
 def stages(count):
     bits = [1 << b for b in range(1, count.bit_length() - 1)]
     pairs = [bits[n : n + 2] for n in range(0, len(bits), 2)]
-    return [[sum(pair)] + pair[::-1] if len(pair) > 1 else pair for pair in pairs]
+    return [pair + [sum(pair)] if len(pair) > 1 else pair for pair in pairs]
 
 
 def offsets(count):
     found = [0]
     for stage in stages(count):
-        found = found + [m ^ offset for offset in stage[::-1] for m in found]
+        found = found + [m ^ offset for offset in stage for m in found]
     return found
 
 
@@ -423,7 +423,7 @@
     held = fields
     for stage in stages(cell_count):
         arrived = [partner(held, "cell", offset) for offset in stage]
-        held = jnp.concatenate([held] + arrived[::-1], axis=0)
+        held = jnp.concatenate([held] + arrived, axis=0)
     other = partner(held, "cell", 1)
     rows = cell_count * chunks
     return pl.pallas_call(

time: 26.3 us -> 26.3 us (level)
  no operation moved by 1% of the time
where the time goes in v20:
time: 26.3 us; the launch traced here: 26.1 us
  starting transfers between devices  9.7 us (37%)
  Pallas kernels  9.32 us (35%)
  waiting for transfers between devices  5.59 us (21%)
  local copies, waits for them, and re-layouts  0.81 us (3%)
  between operations  0.7 us (3%)
    ppermute x6, starting transfers between devices, partner(): lax.ppermute(value, axis, [(i, i ^ distance) for i in range(lax.axis_size...  9.7 us
    ppermute x6, waiting for transfers between devices, partner(): lax.ppermute(value, axis, [(i, i ^ distance) for i in range(lax.axis_size...  5.59 us
    pallas_call x1, Pallas kernels, shards(): pl.pallas_call(fields_kernel, out_shape=jax.ShapeDtypeStruct((FIELDS + 1,...  3.92 us
    pallas_call x1, Pallas kernels, shards(): pl.pallas_call(finish_kernel, out_shape=[jax.ShapeDtypeStruct(melt.shape,...  2.54 us
    pallas_call x1, Pallas kernels, shards(): pl.pallas_call(apply_kernel, out_shape=jax.ShapeDtypeStruct(split, f32),...  1.51 us
    pallas_call x1, Pallas kernels, shards(): pl.pallas_call(powers_kernel, out_shape=[jax.ShapeDtypeStruct(lefts_shape...  1.25 us
    unnamed x10, local copies, waits for them, and re-layouts  0.81 us
  transfers between devices with their start and end apart: 6, of which 6 were waited for; matrix products, arithmetic and copies ran while one was open for 0% of the time, Pallas kernels for 11%

profile of v20, /device:TPU:0, one launch (start us, length us, event | category | flops | bytes accessed | tf_op | source)
XLA Modules:
  0.0 26.1 jit_solution(4280679236651582737)
XLA Ops:
  0.6 0.0 copy-start.4
  0.6 0.0 copy-start.1
  0.7 3.9 %fields.1._.mine = f32[9,8,128]{2,1,0:T(8,128)} custom-call(f32[64,8,1024]{2,1,0:T(8,128)} %melt_hbm.1, s32[8,1024]{1,0:T(8,128)} %counts_hbm.1, f32[1,256]{1,0:T(1,128)} %pressure_hbm.1, f32[32,64,64]{2,1,0:T(8,128)} %prop_hbm.3, f32[32,64]{1,0:T(8,128)} %coup_hbm.3, f32[32,64]{1,0:T(8,128)} %flux_hbm.1), custom_call_target="tpu_custom_call" | custom-call | tf_op jit(solution)/shard_map/fields/pallas_call | solution.py:355
  4.6 0.0 copy-start
  4.6 3.0 %collective-permute-start = (f32[9,8,128]{2,1,0:T(8,128)}, f32[9,8,128]{2,1,0:T(8,128)S(1)}, u32[]{:S(2)}, u32[]{:S(2)}) collective-permute-start(f32[9,8,128]{2,1,0:T(8,128)} %fields.1._.mine), channel_id=1, source_target_pairs={{0,1},{1,0},{2,3},{3,2},{4,5},{5,4},{6,7},{7,6},{8,9},{9,8},{10,11... | collective-permute-start | bytes 110600 | tf_op jit(solution)/shard_map/ppermute | solution.py:339
  7.6 0.0 copy-done.4
  7.6 0.0 copy-done.1
  7.6 0.8 %copy-done.2 = f32[9,8,128]{2,1,0:T(8,128)S(1)} copy-done((f32[9,8,128]{2,1,0:T(8,128)S(1)}, f32[9,8,128]{2,1,0:T(8,128)}, u32[]{:S(2)}) %copy-start.2) | copy-done | bytes 36888
  8.4 1.3 %powers.1 = (bf16[8,64,192]{2,1,0:T(8,128)(2,1)S(1)}, f32[512,128]{1,0:T(8,128)S(1)}, f32[8,128]{1,0:T(8,128)S(1)}) custom-call(f32[32,64,64]{2,1,0:T(8,128)S(1)} %copy-done.1, f32[32,64]{1,0:T(8,128)S(1)} %copy-done.4, f32[9,8,128]{2,1,0:T(8,128)S(1)} %copy-done.2), custom_call_target="tpu_custom_call" | custom-call | flops 1000000000 | bytes 1000000 | tf_op jit(solution)/shard_map/powers/pallas_call | solution.py:377
  9.7 0.1 collective-permute-done.theirs
  9.8 0.0 copy-done.3
  9.8 3.1 %collective-permute-start.1 = (f32[9,8,128]{2,1,0:T(8,128)S(1)}, f32[9,8,128]{2,1,0:T(8,128)S(1)}, u32[]{:S(2)}, u32[]{:S(2)}) collective-permute-start(f32[9,8,128]{2,1,0:T(8,128)S(1)} %add.1._.mine), channel_id=1, source_target_pairs={{0,2},{1,3},{2,0},{3,1},{4,6},{5,7},{6,4},{7,5},{8,10},{9,11},{10,... | collective-permute-start | bytes 110600 | tf_op jit(solution)/shard_map/ppermute | solution.py:339
  12.9 1.5 %apply.1._.shells = f32[8,512,128]{2,1,0:T(8,128)S(1)} custom-call(f32[512,1024]{1,0:T(8,128)S(1)} %bitcast.1, bf16[8,64,192]{2,1,0:T(8,128)(2,1)S(1)} %get-tuple-element.6.lefts, f32[8,128]{1,0:T(8,128)S(1)} %get-tuple-element.5._.factors, f32[9,8,128]{2,1,0:T(8,128)S(1)} %add.1._.mine), custom_call_target="tpu_custom_call" | custom-call | flops 1000000000 | bytes 2097152 | tf_op jit(solution)/shard_map/apply/pallas_call | solution.py:404
  14.4 0.4 %collective-permute-done.1.theirs = f32[9,8,128]{2,1,0:T(8,128)S(1)} collective-permute-done((f32[9,8,128]{2,1,0:T(8,128)S(1)}, f32[9,8,128]{2,1,0:T(8,128)S(1)}, u32[]{:S(2)}, u32[]{:S(2)}) %collective-permute-start.1) | collective-permute-done | bytes 36896 | tf_op jit(solution)/shard_map/ppermute | solution.py:339
  14.8 0.1 combine.1
  14.9 2.8 %collective-permute-start.4 = (f32[1,8,8,128]{3,2,1,0:T(8,128)S(1)}, f32[1,8,8,128]{3,2,1,0:T(8,128)S(1)}, u32[]{:S(2)}, u32[]{:S(2)}) collective-permute-start(f32[1,8,8,128]{3,2,1,0:T(8,128)S(1)} %combine.1), channel_id=1, source_target_pairs={{0,24},{4,28},{8,16},{12,20},{16,8},{20,12},{24,0},{28,4},{1,25},{... | collective-permute-start | bytes 98312 | tf_op jit(solution)/shard_map/ppermute | solution.py:339
  17.7 0.5 %collective-permute-start.3 = (f32[1,8,8,128]{3,2,1,0:T(8,128)S(1)}, f32[1,8,8,128]{3,2,1,0:T(8,128)S(1)}, u32[]{:S(2)}, u32[]{:S(2)}) collective-permute-start(f32[1,8,8,128]{3,2,1,0:T(8,128)S(1)} %combine.1), channel_id=1, source_target_pairs={{0,16},{4,20},{8,24},{12,28},{16,0},{20,4},{24,8},{28,12},{1,17},{... | collective-permute-start | bytes 98312 | tf_op jit(solution)/shard_map/ppermute | solution.py:339
  18.2 0.2 collective-permute-start.2
  18.4 1.5 %collective-permute-done.4 = f32[1,8,8,128]{3,2,1,0:T(8,128)S(1)} collective-permute-done((f32[1,8,8,128]{3,2,1,0:T(8,128)S(1)}, f32[1,8,8,128]{3,2,1,0:T(8,128)S(1)}, u32[]{:S(2)}, u32[]{:S(2)}) %collective-permute-start.4) | collective-permute-done | bytes 32800 | tf_op jit(solution)/shard_map/ppermute | solution.py:339
  19.9 1.7 %collective-permute-done.3 = f32[1,8,8,128]{3,2,1,0:T(8,128)S(1)} collective-permute-done((f32[1,8,8,128]{3,2,1,0:T(8,128)S(1)}, f32[1,8,8,128]{3,2,1,0:T(8,128)S(1)}, u32[]{:S(2)}, u32[]{:S(2)}) %collective-permute-start.3) | collective-permute-done | bytes 32800 | tf_op jit(solution)/shard_map/ppermute | solution.py:339
  21.7 0.5 %collective-permute-done.2 = f32[1,8,8,128]{3,2,1,0:T(8,128)S(1)} collective-permute-done((f32[1,8,8,128]{3,2,1,0:T(8,128)S(1)}, f32[1,8,8,128]{3,2,1,0:T(8,128)S(1)}, u32[]{:S(2)}, u32[]{:S(2)}) %collective-permute-start.2) | collective-permute-done | bytes 32800 | tf_op jit(solution)/shard_map/ppermute | solution.py:339
  22.2 0.1 collective-permute-start.5
  22.3 1.3 %collective-permute-done.5.theirs = f32[4,8,8,128]{3,2,1,0:T(8,128)S(1)} collective-permute-done((f32[4,8,8,128]{3,2,1,0:T(8,128)S(1)}, f32[4,8,8,128]{3,2,1,0:T(8,128)S(1)}, u32[]{:S(2)}, u32[]{:S(2)}) %collective-permute-start.5) | collective-permute-done | bytes 131104 | tf_op jit(solution)/shard_map/ppermute | solution.py:339
  23.6 2.5 %finish.1 = (f32[64,8,1024]{2,1,0:T(8,128)}, f32[1,256]{1,0:T(1,128)}) custom-call(f32[4,8,8,128]{3,2,1,0:T(8,128)S(1)} %pad_maximum_fusion.mine, f32[4,8,8,128]{3,2,1,0:T(8,128)S(1)} %collective-permute-done.5.theirs, f32[8,512,128]{2,1,0:T(8,128)S(1)} %apply.1._.shells, f32[512,128]{1,0:T(8,128)S(1)} %get-tuple-element.7.columns), custom_call_target="tpu_custom_call" | custom-call | tf_op jit(solution)/shard_map/finish/pallas_call | solution.py:429
  (5 shorter events, 0.0 us)
Async XLA Ops:
  0.6 7.0 %copy-start.4 = (f32[32,64]{1,0:T(8,128)S(1)}, f32[32,64]{1,0:T(8,128)}, u32[]{:S(2)}) copy-start(f32[32,64]{1,0:T(8,128)} %coup_hbm.3) | copy-start | bytes 24580
  0.6 7.0 %copy-start.1 = (f32[32,64,64]{2,1,0:T(8,128)S(1)}, f32[32,64,64]{2,1,0:T(8,128)}, u32[]{:S(2)}) copy-start(f32[32,64,64]{2,1,0:T(8,128)} %prop_hbm.3) | copy-start | bytes 1572868
  4.6 8.3 %copy-start = (f32[64,8,1024]{2,1,0:T(8,128)S(1)}, f32[64,8,1024]{2,1,0:T(8,128)}, u32[]{:S(2)}) copy-start(f32[64,8,1024]{2,1,0:T(8,128)} %melt_hbm.1) | copy-start | bytes 6291460
  4.6 5.2 %collective-permute-start = (f32[9,8,128]{2,1,0:T(8,128)}, f32[9,8,128]{2,1,0:T(8,128)S(1)}, u32[]{:S(2)}, u32[]{:S(2)}) collective-permute-start(f32[9,8,128]{2,1,0:T(8,128)} %fields.1._.mine), channel_id=1, source_target_pairs={{0,1},{1,0},{2,3},{3,2},{4,5},{5,4},{6,7},{7,6},{8,9},{9,8},{10,11... | collective-permute-start | bytes 110600 | tf_op jit(solution)/shard_map/ppermute | solution.py:339
  7.6 0.8 %copy-start.2 = (f32[9,8,128]{2,1,0:T(8,128)S(1)}, f32[9,8,128]{2,1,0:T(8,128)}, u32[]{:S(2)}) copy-start(f32[9,8,128]{2,1,0:T(8,128)} %fields.1._.mine) | copy-start | bytes 110596
  8.4 1.3 %copy-start.3 = (f32[9,8,128]{2,1,0:T(8,128)S(1)}, f32[9,8,128]{2,1,0:T(8,128)}, u32[]{:S(2)}) copy-start(f32[9,8,128]{2,1,0:T(8,128)} %fields.1._.mine) | copy-start | bytes 110596
  9.8 5.0 %collective-permute-start.1 = (f32[9,8,128]{2,1,0:T(8,128)S(1)}, f32[9,8,128]{2,1,0:T(8,128)S(1)}, u32[]{:S(2)}, u32[]{:S(2)}) collective-permute-start(f32[9,8,128]{2,1,0:T(8,128)S(1)} %add.1._.mine), channel_id=1, source_target_pairs={{0,2},{1,3},{2,0},{3,1},{4,6},{5,7},{6,4},{7,5},{8,10},{9,11},{10,... | collective-permute-start | bytes 110600 | tf_op jit(solution)/shard_map/ppermute | solution.py:339
  14.9 5.0 %collective-permute-start.4 = (f32[1,8,8,128]{3,2,1,0:T(8,128)S(1)}, f32[1,8,8,128]{3,2,1,0:T(8,128)S(1)}, u32[]{:S(2)}, u32[]{:S(2)}) collective-permute-start(f32[1,8,8,128]{3,2,1,0:T(8,128)S(1)} %combine.1), channel_id=1, source_target_pairs={{0,24},{4,28},{8,16},{12,20},{16,8},{20,12},{24,0},{28,4},{1,25},{... | collective-permute-start | bytes 98312 | tf_op jit(solution)/shard_map/ppermute | solution.py:339
  17.7 3.9 %collective-permute-start.3 = (f32[1,8,8,128]{3,2,1,0:T(8,128)S(1)}, f32[1,8,8,128]{3,2,1,0:T(8,128)S(1)}, u32[]{:S(2)}, u32[]{:S(2)}) collective-permute-start(f32[1,8,8,128]{3,2,1,0:T(8,128)S(1)} %combine.1), channel_id=1, source_target_pairs={{0,16},{4,20},{8,24},{12,28},{16,0},{20,4},{24,8},{28,12},{1,17},{... | collective-permute-start | bytes 98312 | tf_op jit(solution)/shard_map/ppermute | solution.py:339
  18.2 3.9 %collective-permute-start.2 = (f32[1,8,8,128]{3,2,1,0:T(8,128)S(1)}, f32[1,8,8,128]{3,2,1,0:T(8,128)S(1)}, u32[]{:S(2)}, u32[]{:S(2)}) collective-permute-start(f32[1,8,8,128]{3,2,1,0:T(8,128)S(1)} %combine.1), channel_id=1, source_target_pairs={{0,8},{4,12},{8,0},{12,4},{16,24},{20,28},{24,16},{28,20},{1,9},{5... | collective-permute-start | bytes 98312 | tf_op jit(solution)/shard_map/ppermute | solution.py:339
  22.2 1.4 %collective-permute-start.5 = (f32[4,8,8,128]{3,2,1,0:T(8,128)S(1)}, f32[4,8,8,128]{3,2,1,0:T(8,128)S(1)}, u32[]{:S(2)}, u32[]{:S(2)}) collective-permute-start(f32[4,8,8,128]{3,2,1,0:T(8,128)S(1)} %pad_maximum_fusion.mine), channel_id=1, source_target_pairs={{0,4},{4,0},{8,12},{12,8},{16,20},{20,16},{24,28},{28,24},{1,5},{5... | collective-permute-start | bytes 393224 | tf_op jit(solution)/shard_map/ppermute | solution.py:339

commit v21 on v19

--- a/solution.py
+++ b/solution.py
@@ -242,9 +242,9 @@
     return total - 6.0 * x
 
 
-def finish_kernel(
-    mine, theirs, shells, columns, out_hbm, pressure_out, out, window, walls_all, last, out_sems
-):
+def finish_kernel(count, *refs):
+    mine, theirs = refs[:count], refs[count : 2 * count]
+    shells, columns, out_hbm, pressure_out, out, window, walls_all, last, out_sems = refs[2 * count :]
     nodes, classes, cells = out.shape
     chunks = cells // LANES
     parts = nodes // GROUP
@@ -257,8 +257,9 @@
     cell = lax.axis_index("cell")
     blocks = window.shape[0]
     for n, offset in enumerate(offsets(blocks)):
-        window[cell ^ offset] = mine[n]
-        window[cell ^ 1 ^ offset] = theirs[n]
+        part, slot = n // mine[0].shape[0], n % mine[0].shape[0]
+        window[cell ^ offset] = mine[part][slot]
+        window[cell ^ 1 ^ offset] = theirs[part][slot]
     rows = blocks * chunks
     per = plane // LANES
     tile = pressure_out.shape[0] * per
@@ -294,7 +295,7 @@
     at = first + lax.axis_index("cls") * tile
     for i in range(tile):
         pressure_out[i // per : i // per + 1, (i % per) * LANES : (i % per + 1) * LANES] = (
-            last[pl.ds(at + i, 1), :] + 0.1 * mine[0, 2 * SUBSTEPS - 1, i : i + 1, :]
+            last[pl.ds(at + i, 1), :] + 0.1 * mine[0][0, 2 * SUBSTEPS - 1, i : i + 1, :]
         )
     right = []
     for r in range(chunks):
@@ -420,16 +421,16 @@
         compiler_params=little,
         name="combine",
     )(packed, theirs, shells)
-    held = fields
+    pieces = [fields]
     for stage in stages(cell_count):
-        arrived = [partner(held, "cell", offset) for offset in stage]
-        held = jnp.concatenate([held] + arrived[::-1], axis=0)
-    other = partner(held, "cell", 1)
+        held = jnp.concatenate(pieces, axis=0) if len(pieces) > 1 else pieces[0]
+        pieces = [held] + [partner(held, "cell", offset) for offset in stage][::-1]
+    pieces = pieces + [partner(piece, "cell", 1) for piece in pieces]
     rows = cell_count * chunks
     return pl.pallas_call(
-        finish_kernel,
+        functools.partial(finish_kernel, len(pieces) // 2),
         out_shape=[jax.ShapeDtypeStruct(melt.shape, f32), jax.ShapeDtypeStruct(pressure.shape, f32)],
-        in_specs=[VMEM] * 4,
+        in_specs=[VMEM] * (len(pieces) + 2),
         out_specs=[HBM, VMEM],
         scratch_shapes=[
             pltpu.VMEM(melt.shape, f32),
@@ -440,7 +441,7 @@
         ],
         compiler_params=little,
         name="finish",
-    )(held, other, shells, columns)
+    )(*pieces, shells, columns)
 
 
 def solution(mesh):

time: 26.3 us -> 26 us (0.989)
    ppermute x6 -> x9, waiting for transfers between devices: 5.59 us -> 5.45 us  [partner(): lax.ppermute(value, axis, [(i, i ^ distance) for i in range(lax.axis_size...]
    ppermute x6 -> x9, starting transfers between devices: 9.7 us -> 9.58 us  [partner(): lax.ppermute(value, axis, [(i, i ^ distance) for i in range(lax.axis_size...]
    unnamed x10 -> x8, local copies, waits for them, and re-layouts: 0.81 us -> 0.81 us
  transfers between devices with their start and end apart: 6 -> 9, of which waited for: 6 -> 7; matrix products, arithmetic and copies ran while one was open for 0% -> 0% of each run, Pallas kernels for 11% -> 11%
where the time goes in v21:
time: 26 us; the launch traced here: 25.8 us
  starting transfers between devices  9.58 us (37%)
  Pallas kernels  9.32 us (36%)
  waiting for transfers between devices  5.45 us (21%)
  local copies, waits for them, and re-layouts  0.81 us (3%)
  between operations  0.69 us (3%)
    ppermute x9, starting transfers between devices, partner(): lax.ppermute(value, axis, [(i, i ^ distance) for i in range(lax.axis_size...  9.58 us
    ppermute x9, waiting for transfers between devices, partner(): lax.ppermute(value, axis, [(i, i ^ distance) for i in range(lax.axis_size...  5.45 us
    pallas_call x1, Pallas kernels, shards(): pl.pallas_call(fields_kernel, out_shape=jax.ShapeDtypeStruct((FIELDS + 1,...  3.92 us
    pallas_call x1, Pallas kernels, shards(): pl.pallas_call(functools.partial(finish_kernel, len(pieces) // 2), out_sh...  2.55 us
    pallas_call x1, Pallas kernels, shards(): pl.pallas_call(apply_kernel, out_shape=jax.ShapeDtypeStruct(split, f32),...  1.51 us
    pallas_call x1, Pallas kernels, shards(): pl.pallas_call(powers_kernel, out_shape=[jax.ShapeDtypeStruct(lefts_shape...  1.25 us
    unnamed x8, local copies, waits for them, and re-layouts  0.81 us
  transfers between devices with their start and end apart: 9, of which 7 were waited for; matrix products, arithmetic and copies ran while one was open for 0% of the time, Pallas kernels for 11%

profile of v21, /device:TPU:0, one launch (start us, length us, event | category | flops | bytes accessed | tf_op | source)
XLA Modules:
  0.0 25.8 jit_solution(2503143694500264073)
XLA Ops:
  0.7 3.9 %fields.1._.mine = f32[9,8,128]{2,1,0:T(8,128)} custom-call(f32[64,8,1024]{2,1,0:T(8,128)} %melt_hbm.1, s32[8,1024]{1,0:T(8,128)} %counts_hbm.1, f32[1,256]{1,0:T(1,128)} %pressure_hbm.1, f32[32,64,64]{2,1,0:T(8,128)} %prop_hbm.3, f32[32,64]{1,0:T(8,128)} %coup_hbm.3, f32[32,64]{1,0:T(8,128)} %flux_hbm.1), custom_call_target="tpu_custom_call" | custom-call | tf_op jit(solution)/shard_map/fields/pallas_call | solution.py:356
  4.6 0.0 copy-start
  4.6 3.0 %collective-permute-start = (f32[9,8,128]{2,1,0:T(8,128)}, f32[9,8,128]{2,1,0:T(8,128)S(1)}, u32[]{:S(2)}, u32[]{:S(2)}) collective-permute-start(f32[9,8,128]{2,1,0:T(8,128)} %fields.1._.mine), channel_id=1, source_target_pairs={{0,1},{1,0},{2,3},{3,2},{4,5},{5,4},{6,7},{7,6},{8,9},{9,8},{10,11... | collective-permute-start | bytes 110600 | tf_op jit(solution)/shard_map/ppermute | solution.py:340
  7.6 0.8 %copy-done.2 = f32[9,8,128]{2,1,0:T(8,128)S(1)} copy-done((f32[9,8,128]{2,1,0:T(8,128)S(1)}, f32[9,8,128]{2,1,0:T(8,128)}, u32[]{:S(2)}) %copy-start.2) | copy-done | bytes 36888
  8.4 1.3 %powers.1 = (bf16[8,64,192]{2,1,0:T(8,128)(2,1)S(1)}, f32[512,128]{1,0:T(8,128)S(1)}, f32[8,128]{1,0:T(8,128)S(1)}) custom-call(f32[32,64,64]{2,1,0:T(8,128)S(1)} %copy-done.1, f32[32,64]{1,0:T(8,128)S(1)} %copy-done.3, f32[9,8,128]{2,1,0:T(8,128)S(1)} %copy-done.2), custom_call_target="tpu_custom_call" | custom-call | flops 1000000000 | bytes 1000000 | tf_op jit(solution)/shard_map/powers/pallas_call | solution.py:378
  9.7 0.1 collective-permute-done.theirs
  9.8 3.0 %collective-permute-start.1 = (f32[9,8,128]{2,1,0:T(8,128)S(1)}, f32[9,8,128]{2,1,0:T(8,128)S(1)}, u32[]{:S(2)}, u32[]{:S(2)}) collective-permute-start(f32[9,8,128]{2,1,0:T(8,128)S(1)} %add.1._.mine), channel_id=1, source_target_pairs={{0,2},{1,3},{2,0},{3,1},{4,6},{5,7},{6,4},{7,5},{8,10},{9,11},{10,... | collective-permute-start | bytes 110600 | tf_op jit(solution)/shard_map/ppermute | solution.py:340
  12.8 1.5 %apply.1._.refs_8_ = f32[8,512,128]{2,1,0:T(8,128)S(1)} custom-call(f32[512,1024]{1,0:T(8,128)S(1)} %bitcast.1, bf16[8,64,192]{2,1,0:T(8,128)(2,1)S(1)} %get-tuple-element.6.lefts, f32[8,128]{1,0:T(8,128)S(1)} %get-tuple-element.5._.factors, f32[9,8,128]{2,1,0:T(8,128)S(1)} %add.1._.mine), custom_call_target="tpu_custom_call" | custom-call | flops 1000000000 | bytes 2097152 | tf_op jit(solution)/shard_map/apply/pallas_call | solution.py:405
  14.3 0.4 %collective-permute-done.1.theirs = f32[9,8,128]{2,1,0:T(8,128)S(1)} collective-permute-done((f32[9,8,128]{2,1,0:T(8,128)S(1)}, f32[9,8,128]{2,1,0:T(8,128)S(1)}, u32[]{:S(2)}, u32[]{:S(2)}) %collective-permute-start.1) | collective-permute-done | bytes 36896 | tf_op jit(solution)/shard_map/ppermute | solution.py:340
  14.8 0.1 combine.1.refs_0_
  14.8 2.8 %collective-permute-start.4 = (f32[1,8,8,128]{3,2,1,0:T(8,128)S(1)}, f32[1,8,8,128]{3,2,1,0:T(8,128)S(1)}, u32[]{:S(2)}, u32[]{:S(2)}) collective-permute-start(f32[1,8,8,128]{3,2,1,0:T(8,128)S(1)} %combine.1.refs_0_), channel_id=1, source_target_pairs={{0,24},{4,28},{8,16},{12,20},{16,8},{20,12},{24,0},{28,4},{1,25},{... | collective-permute-start | bytes 98312 | tf_op jit(solution)/shard_map/ppermute | solution.py:340
  17.7 0.5 %collective-permute-start.3 = (f32[1,8,8,128]{3,2,1,0:T(8,128)S(1)}, f32[1,8,8,128]{3,2,1,0:T(8,128)S(1)}, u32[]{:S(2)}, u32[]{:S(2)}) collective-permute-start(f32[1,8,8,128]{3,2,1,0:T(8,128)S(1)} %combine.1.refs_0_), channel_id=1, source_target_pairs={{0,16},{4,20},{8,24},{12,28},{16,0},{20,4},{24,8},{28,12},{1,17},{... | collective-permute-start | bytes 98312 | tf_op jit(solution)/shard_map/ppermute | solution.py:340
  18.2 0.2 collective-permute-start.2
  18.3 0.0 collective-permute-start.5
  18.3 1.6 %collective-permute-done.4.refs_3_ = f32[1,8,8,128]{3,2,1,0:T(8,128)S(1)} collective-permute-done((f32[1,8,8,128]{3,2,1,0:T(8,128)S(1)}, f32[1,8,8,128]{3,2,1,0:T(8,128)S(1)}, u32[]{:S(2)}, u32[]{:S(2)}) %collective-permute-start.4) | collective-permute-done | bytes 32800 | tf_op jit(solution)/shard_map/ppermute | solution.py:340
  19.9 0.0 collective-permute-start.8
  19.9 1.7 %collective-permute-done.3.refs_2_ = f32[1,8,8,128]{3,2,1,0:T(8,128)S(1)} collective-permute-done((f32[1,8,8,128]{3,2,1,0:T(8,128)S(1)}, f32[1,8,8,128]{3,2,1,0:T(8,128)S(1)}, u32[]{:S(2)}, u32[]{:S(2)}) %collective-permute-start.3) | collective-permute-done | bytes 32800 | tf_op jit(solution)/shard_map/ppermute | solution.py:340
  21.6 0.0 collective-permute-start.7
  21.6 0.5 %collective-permute-done.2.refs_1_ = f32[1,8,8,128]{3,2,1,0:T(8,128)S(1)} collective-permute-done((f32[1,8,8,128]{3,2,1,0:T(8,128)S(1)}, f32[1,8,8,128]{3,2,1,0:T(8,128)S(1)}, u32[]{:S(2)}, u32[]{:S(2)}) %collective-permute-start.2) | collective-permute-done | bytes 32800 | tf_op jit(solution)/shard_map/ppermute | solution.py:340
  22.1 0.0 collective-permute-start.6
  22.1 0.0 collective-permute-done.5.refs_4_
  22.1 0.7 %collective-permute-done.7.refs_6_ = f32[1,8,8,128]{3,2,1,0:T(8,128)S(1)} collective-permute-done((f32[1,8,8,128]{3,2,1,0:T(8,128)S(1)}, f32[1,8,8,128]{3,2,1,0:T(8,128)S(1)}, u32[]{:S(2)}, u32[]{:S(2)}) %collective-permute-start.7) | collective-permute-done | bytes 32800 | tf_op jit(solution)/shard_map/ppermute | solution.py:340
  22.8 0.5 %collective-permute-done.6.refs_5_ = f32[1,8,8,128]{3,2,1,0:T(8,128)S(1)} collective-permute-done((f32[1,8,8,128]{3,2,1,0:T(8,128)S(1)}, f32[1,8,8,128]{3,2,1,0:T(8,128)S(1)}, u32[]{:S(2)}, u32[]{:S(2)}) %collective-permute-start.6) | collective-permute-done | bytes 32800 | tf_op jit(solution)/shard_map/ppermute | solution.py:340
  23.3 2.5 %finish.1 = (f32[64,8,1024]{2,1,0:T(8,128)}, f32[1,256]{1,0:T(1,128)}) custom-call(f32[1,8,8,128]{3,2,1,0:T(8,128)S(1)} %combine.1.refs_0_, f32[1,8,8,128]{3,2,1,0:T(8,128)S(1)} %collective-permute-done.2.refs_1_, f32[1,8,8,128]{3,2,1,0:T(8,128)S(1)} %collective-permute-done.3.refs_2_, f32[1,8,8,128]{3,2,1,0:T(8,128)S(1)} %collective-permute-done.4.refs_3_, ...), custom_call_target="tpu_custom_call" | custom-call | tf_op jit(solution)/shard_map/finish/pallas_call | solution.py:430
  (8 shorter events, 0.0 us)
Async XLA Ops:
  0.6 7.0 %copy-start.3 = (f32[32,64]{1,0:T(8,128)S(1)}, f32[32,64]{1,0:T(8,128)}, u32[]{:S(2)}) copy-start(f32[32,64]{1,0:T(8,128)} %coup_hbm.3) | copy-start | bytes 24580
  0.6 7.0 %copy-start.1 = (f32[32,64,64]{2,1,0:T(8,128)S(1)}, f32[32,64,64]{2,1,0:T(8,128)}, u32[]{:S(2)}) copy-start(f32[32,64,64]{2,1,0:T(8,128)} %prop_hbm.3) | copy-start | bytes 1572868
  4.6 8.2 %copy-start = (f32[64,8,1024]{2,1,0:T(8,128)S(1)}, f32[64,8,1024]{2,1,0:T(8,128)}, u32[]{:S(2)}) copy-start(f32[64,8,1024]{2,1,0:T(8,128)} %melt_hbm.1) | copy-start | bytes 6291460
  4.6 5.2 %collective-permute-start = (f32[9,8,128]{2,1,0:T(8,128)}, f32[9,8,128]{2,1,0:T(8,128)S(1)}, u32[]{:S(2)}, u32[]{:S(2)}) collective-permute-start(f32[9,8,128]{2,1,0:T(8,128)} %fields.1._.mine), channel_id=1, source_target_pairs={{0,1},{1,0},{2,3},{3,2},{4,5},{5,4},{6,7},{7,6},{8,9},{9,8},{10,11... | collective-permute-start | bytes 110600 | tf_op jit(solution)/shard_map/ppermute | solution.py:340
  7.6 0.8 %copy-start.2 = (f32[9,8,128]{2,1,0:T(8,128)S(1)}, f32[9,8,128]{2,1,0:T(8,128)}, u32[]{:S(2)}) copy-start(f32[9,8,128]{2,1,0:T(8,128)} %fields.1._.mine) | copy-start | bytes 110596
  9.8 5.0 %collective-permute-start.1 = (f32[9,8,128]{2,1,0:T(8,128)S(1)}, f32[9,8,128]{2,1,0:T(8,128)S(1)}, u32[]{:S(2)}, u32[]{:S(2)}) collective-permute-start(f32[9,8,128]{2,1,0:T(8,128)S(1)} %add.1._.mine), channel_id=1, source_target_pairs={{0,2},{1,3},{2,0},{3,1},{4,6},{5,7},{6,4},{7,5},{8,10},{9,11},{10,... | collective-permute-start | bytes 110600 | tf_op jit(solution)/shard_map/ppermute | solution.py:340
  14.8 5.1 %collective-permute-start.4 = (f32[1,8,8,128]{3,2,1,0:T(8,128)S(1)}, f32[1,8,8,128]{3,2,1,0:T(8,128)S(1)}, u32[]{:S(2)}, u32[]{:S(2)}) collective-permute-start(f32[1,8,8,128]{3,2,1,0:T(8,128)S(1)} %combine.1.refs_0_), channel_id=1, source_target_pairs={{0,24},{4,28},{8,16},{12,20},{16,8},{20,12},{24,0},{28,4},{1,25},{... | collective-permute-start | bytes 98312 | tf_op jit(solution)/shard_map/ppermute | solution.py:340
  17.7 3.9 %collective-permute-start.3 = (f32[1,8,8,128]{3,2,1,0:T(8,128)S(1)}, f32[1,8,8,128]{3,2,1,0:T(8,128)S(1)}, u32[]{:S(2)}, u32[]{:S(2)}) collective-permute-start(f32[1,8,8,128]{3,2,1,0:T(8,128)S(1)} %combine.1.refs_0_), channel_id=1, source_target_pairs={{0,16},{4,20},{8,24},{12,28},{16,0},{20,4},{24,8},{28,12},{1,17},{... | collective-permute-start | bytes 98312 | tf_op jit(solution)/shard_map/ppermute | solution.py:340
  18.2 3.9 %collective-permute-start.2 = (f32[1,8,8,128]{3,2,1,0:T(8,128)S(1)}, f32[1,8,8,128]{3,2,1,0:T(8,128)S(1)}, u32[]{:S(2)}, u32[]{:S(2)}) collective-permute-start(f32[1,8,8,128]{3,2,1,0:T(8,128)S(1)} %combine.1.refs_0_), channel_id=1, source_target_pairs={{0,8},{4,12},{8,0},{12,4},{16,24},{20,28},{24,16},{28,20},{1,9},{5... | collective-permute-start | bytes 98312 | tf_op jit(solution)/shard_map/ppermute | solution.py:340
  18.3 3.8 %collective-permute-start.5 = (f32[1,8,8,128]{3,2,1,0:T(8,128)S(1)}, f32[1,8,8,128]{3,2,1,0:T(8,128)S(1)}, u32[]{:S(2)}, u32[]{:S(2)}) collective-permute-start(f32[1,8,8,128]{3,2,1,0:T(8,128)S(1)} %combine.1.refs_0_), channel_id=1, source_target_pairs={{0,4},{4,0},{8,12},{12,8},{16,20},{20,16},{24,28},{28,24},{1,5},{5... | collective-permute-start | bytes 98312 | tf_op jit(solution)/shard_map/ppermute | solution.py:340
  19.9 2.2 %collective-permute-start.8 = (f32[1,8,8,128]{3,2,1,0:T(8,128)S(1)}, f32[1,8,8,128]{3,2,1,0:T(8,128)S(1)}, u32[]{:S(2)}, u32[]{:S(2)}) collective-permute-start(f32[1,8,8,128]{3,2,1,0:T(8,128)S(1)} %collective-permute-done.4.refs_3_), channel_id=1, source_target_pairs={{0,4},{4,0},{8,12},{12,8},{16,20},{20,16},{24,28},{28,24},{1,5},{5... | collective-permute-start | bytes 98312 | tf_op jit(solution)/shard_map/ppermute | solution.py:340
  21.6 1.2 %collective-permute-start.7 = (f32[1,8,8,128]{3,2,1,0:T(8,128)S(1)}, f32[1,8,8,128]{3,2,1,0:T(8,128)S(1)}, u32[]{:S(2)}, u32[]{:S(2)}) collective-permute-start(f32[1,8,8,128]{3,2,1,0:T(8,128)S(1)} %collective-permute-done.3.refs_2_), channel_id=1, source_target_pairs={{0,4},{4,0},{8,12},{12,8},{16,20},{20,16},{24,28},{28,24},{1,5},{5... | collective-permute-start | bytes 98312 | tf_op jit(solution)/shard_map/ppermute | solution.py:340
  22.1 1.2 %collective-permute-start.6 = (f32[1,8,8,128]{3,2,1,0:T(8,128)S(1)}, f32[1,8,8,128]{3,2,1,0:T(8,128)S(1)}, u32[]{:S(2)}, u32[]{:S(2)}) collective-permute-start(f32[1,8,8,128]{3,2,1,0:T(8,128)S(1)} %collective-permute-done.2.refs_1_), channel_id=1, source_target_pairs={{0,4},{4,0},{8,12},{12,8},{16,20},{20,16},{24,28},{28,24},{1,5},{5... | collective-permute-start | bytes 98312 | tf_op jit(solution)/shard_map/ppermute | solution.py:340

commit v22 on v21

--- a/solution.py
+++ b/solution.py
@@ -95,7 +95,7 @@
         pairs = dot(jnp.concatenate(split2(wide), axis=0), table)
         row = pairs[:classes] + pairs[classes:]
         rows.append((row[:, :nodes] + row[:, nodes:]) * inverse)
-        for g in range(t * each, parts if t == SUBSTEPS - 1 else (t + 1) * each):
+        for g in range(max(t - 1, 0) * each, parts if t == SUBSTEPS - 1 else t * each):
             pieces[g].wait()
             here = slice(g * tall, (g + 1) * tall)
             highs[here, :], lows[here, :] = split2(

time: 26 us -> 26.1 us (level)
  no operation moved by 1% of the time
where the time goes in v22:
time: 26.1 us; the launch traced here: 25.9 us
  starting transfers between devices  9.58 us (37%)
  Pallas kernels  9.39 us (36%)
  waiting for transfers between devices  5.45 us (21%)
  local copies, waits for them, and re-layouts  0.81 us (3%)
  between operations  0.69 us (3%)
    ppermute x9, starting transfers between devices, partner(): lax.ppermute(value, axis, [(i, i ^ distance) for i in range(lax.axis_size...  9.58 us
    ppermute x9, waiting for transfers between devices, partner(): lax.ppermute(value, axis, [(i, i ^ distance) for i in range(lax.axis_size...  5.45 us
    pallas_call x1, Pallas kernels, shards(): pl.pallas_call(fields_kernel, out_shape=jax.ShapeDtypeStruct((FIELDS + 1,...  3.99 us
    pallas_call x1, Pallas kernels, shards(): pl.pallas_call(functools.partial(finish_kernel, len(pieces) // 2), out_sh...  2.54 us
    pallas_call x1, Pallas kernels, shards(): pl.pallas_call(apply_kernel, out_shape=jax.ShapeDtypeStruct(split, f32),...  1.51 us
    pallas_call x1, Pallas kernels, shards(): pl.pallas_call(powers_kernel, out_shape=[jax.ShapeDtypeStruct(lefts_shape...  1.25 us
    unnamed x8, local copies, waits for them, and re-layouts  0.81 us
  transfers between devices with their start and end apart: 9, of which 7 were waited for; matrix products, arithmetic and copies ran while one was open for 0% of the time, Pallas kernels for 11%

profile of v22, /device:TPU:0, one launch (start us, length us, event | category | flops | bytes accessed | tf_op | source)
XLA Modules:
  0.0 25.9 jit_solution(13583286677750043742)
XLA Ops:
  0.7 4.0 %fields.1._.mine = f32[9,8,128]{2,1,0:T(8,128)} custom-call(f32[64,8,1024]{2,1,0:T(8,128)} %melt_hbm.1, s32[8,1024]{1,0:T(8,128)} %counts_hbm.1, f32[1,256]{1,0:T(1,128)} %pressure_hbm.1, f32[32,64,64]{2,1,0:T(8,128)} %prop_hbm.3, f32[32,64]{1,0:T(8,128)} %coup_hbm.3, f32[32,64]{1,0:T(8,128)} %flux_hbm.1), custom_call_target="tpu_custom_call" | custom-call | tf_op jit(solution)/shard_map/fields/pallas_call | solution.py:356
  4.6 0.0 copy-start
  4.7 3.0 %collective-permute-start = (f32[9,8,128]{2,1,0:T(8,128)}, f32[9,8,128]{2,1,0:T(8,128)S(1)}, u32[]{:S(2)}, u32[]{:S(2)}) collective-permute-start(f32[9,8,128]{2,1,0:T(8,128)} %fields.1._.mine), channel_id=1, source_target_pairs={{0,1},{1,0},{2,3},{3,2},{4,5},{5,4},{6,7},{7,6},{8,9},{9,8},{10,11... | collective-permute-start | bytes 110600 | tf_op jit(solution)/shard_map/ppermute | solution.py:340
  7.7 0.8 %copy-done.2 = f32[9,8,128]{2,1,0:T(8,128)S(1)} copy-done((f32[9,8,128]{2,1,0:T(8,128)S(1)}, f32[9,8,128]{2,1,0:T(8,128)}, u32[]{:S(2)}) %copy-start.2) | copy-done | bytes 36888
  8.5 1.3 %powers.1 = (bf16[8,64,192]{2,1,0:T(8,128)(2,1)S(1)}, f32[512,128]{1,0:T(8,128)S(1)}, f32[8,128]{1,0:T(8,128)S(1)}) custom-call(f32[32,64,64]{2,1,0:T(8,128)S(1)} %copy-done.1, f32[32,64]{1,0:T(8,128)S(1)} %copy-done.3, f32[9,8,128]{2,1,0:T(8,128)S(1)} %copy-done.2), custom_call_target="tpu_custom_call" | custom-call | flops 1000000000 | bytes 1000000 | tf_op jit(solution)/shard_map/powers/pallas_call | solution.py:378
  9.8 0.1 collective-permute-done.theirs
  9.9 3.0 %collective-permute-start.1 = (f32[9,8,128]{2,1,0:T(8,128)S(1)}, f32[9,8,128]{2,1,0:T(8,128)S(1)}, u32[]{:S(2)}, u32[]{:S(2)}) collective-permute-start(f32[9,8,128]{2,1,0:T(8,128)S(1)} %add.1._.mine), channel_id=1, source_target_pairs={{0,2},{1,3},{2,0},{3,1},{4,6},{5,7},{6,4},{7,5},{8,10},{9,11},{10,... | collective-permute-start | bytes 110600 | tf_op jit(solution)/shard_map/ppermute | solution.py:340
  12.9 1.5 %apply.1._.refs_8_ = f32[8,512,128]{2,1,0:T(8,128)S(1)} custom-call(f32[512,1024]{1,0:T(8,128)S(1)} %bitcast.1, bf16[8,64,192]{2,1,0:T(8,128)(2,1)S(1)} %get-tuple-element.6.lefts, f32[8,128]{1,0:T(8,128)S(1)} %get-tuple-element.5._.factors, f32[9,8,128]{2,1,0:T(8,128)S(1)} %add.1._.mine), custom_call_target="tpu_custom_call" | custom-call | flops 1000000000 | bytes 2097152 | tf_op jit(solution)/shard_map/apply/pallas_call | solution.py:405
  14.4 0.4 %collective-permute-done.1.theirs = f32[9,8,128]{2,1,0:T(8,128)S(1)} collective-permute-done((f32[9,8,128]{2,1,0:T(8,128)S(1)}, f32[9,8,128]{2,1,0:T(8,128)S(1)}, u32[]{:S(2)}, u32[]{:S(2)}) %collective-permute-start.1) | collective-permute-done | bytes 36896 | tf_op jit(solution)/shard_map/ppermute | solution.py:340
  14.8 0.1 combine.1.refs_0_
  14.9 2.8 %collective-permute-start.4 = (f32[1,8,8,128]{3,2,1,0:T(8,128)S(1)}, f32[1,8,8,128]{3,2,1,0:T(8,128)S(1)}, u32[]{:S(2)}, u32[]{:S(2)}) collective-permute-start(f32[1,8,8,128]{3,2,1,0:T(8,128)S(1)} %combine.1.refs_0_), channel_id=1, source_target_pairs={{0,24},{4,28},{8,16},{12,20},{16,8},{20,12},{24,0},{28,4},{1,25},{... | collective-permute-start | bytes 98312 | tf_op jit(solution)/shard_map/ppermute | solution.py:340
  17.7 0.5 %collective-permute-start.3 = (f32[1,8,8,128]{3,2,1,0:T(8,128)S(1)}, f32[1,8,8,128]{3,2,1,0:T(8,128)S(1)}, u32[]{:S(2)}, u32[]{:S(2)}) collective-permute-start(f32[1,8,8,128]{3,2,1,0:T(8,128)S(1)} %combine.1.refs_0_), channel_id=1, source_target_pairs={{0,16},{4,20},{8,24},{12,28},{16,0},{20,4},{24,8},{28,12},{1,17},{... | collective-permute-start | bytes 98312 | tf_op jit(solution)/shard_map/ppermute | solution.py:340
  18.3 0.2 collective-permute-start.2
  18.4 0.0 collective-permute-start.5
  18.4 1.6 %collective-permute-done.4.refs_3_ = f32[1,8,8,128]{3,2,1,0:T(8,128)S(1)} collective-permute-done((f32[1,8,8,128]{3,2,1,0:T(8,128)S(1)}, f32[1,8,8,128]{3,2,1,0:T(8,128)S(1)}, u32[]{:S(2)}, u32[]{:S(2)}) %collective-permute-start.4) | collective-permute-done | bytes 32800 | tf_op jit(solution)/shard_map/ppermute | solution.py:340
  20.0 0.0 collective-permute-start.8
  20.0 1.7 %collective-permute-done.3.refs_2_ = f32[1,8,8,128]{3,2,1,0:T(8,128)S(1)} collective-permute-done((f32[1,8,8,128]{3,2,1,0:T(8,128)S(1)}, f32[1,8,8,128]{3,2,1,0:T(8,128)S(1)}, u32[]{:S(2)}, u32[]{:S(2)}) %collective-permute-start.3) | collective-permute-done | bytes 32800 | tf_op jit(solution)/shard_map/ppermute | solution.py:340
  21.7 0.0 collective-permute-start.7
  21.7 0.5 %collective-permute-done.2.refs_1_ = f32[1,8,8,128]{3,2,1,0:T(8,128)S(1)} collective-permute-done((f32[1,8,8,128]{3,2,1,0:T(8,128)S(1)}, f32[1,8,8,128]{3,2,1,0:T(8,128)S(1)}, u32[]{:S(2)}, u32[]{:S(2)}) %collective-permute-start.2) | collective-permute-done | bytes 32800 | tf_op jit(solution)/shard_map/ppermute | solution.py:340
  22.2 0.0 collective-permute-start.6
  22.2 0.0 collective-permute-done.5.refs_4_
  22.2 0.7 %collective-permute-done.7.refs_6_ = f32[1,8,8,128]{3,2,1,0:T(8,128)S(1)} collective-permute-done((f32[1,8,8,128]{3,2,1,0:T(8,128)S(1)}, f32[1,8,8,128]{3,2,1,0:T(8,128)S(1)}, u32[]{:S(2)}, u32[]{:S(2)}) %collective-permute-start.7) | collective-permute-done | bytes 32800 | tf_op jit(solution)/shard_map/ppermute | solution.py:340
  22.9 0.5 %collective-permute-done.6.refs_5_ = f32[1,8,8,128]{3,2,1,0:T(8,128)S(1)} collective-permute-done((f32[1,8,8,128]{3,2,1,0:T(8,128)S(1)}, f32[1,8,8,128]{3,2,1,0:T(8,128)S(1)}, u32[]{:S(2)}, u32[]{:S(2)}) %collective-permute-start.6) | collective-permute-done | bytes 32800 | tf_op jit(solution)/shard_map/ppermute | solution.py:340
  23.4 2.5 %finish.1 = (f32[64,8,1024]{2,1,0:T(8,128)}, f32[1,256]{1,0:T(1,128)}) custom-call(f32[1,8,8,128]{3,2,1,0:T(8,128)S(1)} %combine.1.refs_0_, f32[1,8,8,128]{3,2,1,0:T(8,128)S(1)} %collective-permute-done.2.refs_1_, f32[1,8,8,128]{3,2,1,0:T(8,128)S(1)} %collective-permute-done.3.refs_2_, f32[1,8,8,128]{3,2,1,0:T(8,128)S(1)} %collective-permute-done.4.refs_3_, ...), custom_call_target="tpu_custom_call" | custom-call | tf_op jit(solution)/shard_map/finish/pallas_call | solution.py:430
  (8 shorter events, 0.0 us)
Async XLA Ops:
  0.6 7.1 %copy-start.3 = (f32[32,64]{1,0:T(8,128)S(1)}, f32[32,64]{1,0:T(8,128)}, u32[]{:S(2)}) copy-start(f32[32,64]{1,0:T(8,128)} %coup_hbm.3) | copy-start | bytes 24580
  0.6 7.1 %copy-start.1 = (f32[32,64,64]{2,1,0:T(8,128)S(1)}, f32[32,64,64]{2,1,0:T(8,128)}, u32[]{:S(2)}) copy-start(f32[32,64,64]{2,1,0:T(8,128)} %prop_hbm.3) | copy-start | bytes 1572868
  4.6 8.2 %copy-start = (f32[64,8,1024]{2,1,0:T(8,128)S(1)}, f32[64,8,1024]{2,1,0:T(8,128)}, u32[]{:S(2)}) copy-start(f32[64,8,1024]{2,1,0:T(8,128)} %melt_hbm.1) | copy-start | bytes 6291460
  4.7 5.2 %collective-permute-start = (f32[9,8,128]{2,1,0:T(8,128)}, f32[9,8,128]{2,1,0:T(8,128)S(1)}, u32[]{:S(2)}, u32[]{:S(2)}) collective-permute-start(f32[9,8,128]{2,1,0:T(8,128)} %fields.1._.mine), channel_id=1, source_target_pairs={{0,1},{1,0},{2,3},{3,2},{4,5},{5,4},{6,7},{7,6},{8,9},{9,8},{10,11... | collective-permute-start | bytes 110600 | tf_op jit(solution)/shard_map/ppermute | solution.py:340
  7.7 0.8 %copy-start.2 = (f32[9,8,128]{2,1,0:T(8,128)S(1)}, f32[9,8,128]{2,1,0:T(8,128)}, u32[]{:S(2)}) copy-start(f32[9,8,128]{2,1,0:T(8,128)} %fields.1._.mine) | copy-start | bytes 110596
  9.9 5.0 %collective-permute-start.1 = (f32[9,8,128]{2,1,0:T(8,128)S(1)}, f32[9,8,128]{2,1,0:T(8,128)S(1)}, u32[]{:S(2)}, u32[]{:S(2)}) collective-permute-start(f32[9,8,128]{2,1,0:T(8,128)S(1)} %add.1._.mine), channel_id=1, source_target_pairs={{0,2},{1,3},{2,0},{3,1},{4,6},{5,7},{6,4},{7,5},{8,10},{9,11},{10,... | collective-permute-start | bytes 110600 | tf_op jit(solution)/shard_map/ppermute | solution.py:340
  14.9 5.1 %collective-permute-start.4 = (f32[1,8,8,128]{3,2,1,0:T(8,128)S(1)}, f32[1,8,8,128]{3,2,1,0:T(8,128)S(1)}, u32[]{:S(2)}, u32[]{:S(2)}) collective-permute-start(f32[1,8,8,128]{3,2,1,0:T(8,128)S(1)} %combine.1.refs_0_), channel_id=1, source_target_pairs={{0,24},{4,28},{8,16},{12,20},{16,8},{20,12},{24,0},{28,4},{1,25},{... | collective-permute-start | bytes 98312 | tf_op jit(solution)/shard_map/ppermute | solution.py:340
  17.7 3.9 %collective-permute-start.3 = (f32[1,8,8,128]{3,2,1,0:T(8,128)S(1)}, f32[1,8,8,128]{3,2,1,0:T(8,128)S(1)}, u32[]{:S(2)}, u32[]{:S(2)}) collective-permute-start(f32[1,8,8,128]{3,2,1,0:T(8,128)S(1)} %combine.1.refs_0_), channel_id=1, source_target_pairs={{0,16},{4,20},{8,24},{12,28},{16,0},{20,4},{24,8},{28,12},{1,17},{... | collective-permute-start | bytes 98312 | tf_op jit(solution)/shard_map/ppermute | solution.py:340
  18.3 3.9 %collective-permute-start.2 = (f32[1,8,8,128]{3,2,1,0:T(8,128)S(1)}, f32[1,8,8,128]{3,2,1,0:T(8,128)S(1)}, u32[]{:S(2)}, u32[]{:S(2)}) collective-permute-start(f32[1,8,8,128]{3,2,1,0:T(8,128)S(1)} %combine.1.refs_0_), channel_id=1, source_target_pairs={{0,8},{4,12},{8,0},{12,4},{16,24},{20,28},{24,16},{28,20},{1,9},{5... | collective-permute-start | bytes 98312 | tf_op jit(solution)/shard_map/ppermute | solution.py:340
  18.4 3.8 %collective-permute-start.5 = (f32[1,8,8,128]{3,2,1,0:T(8,128)S(1)}, f32[1,8,8,128]{3,2,1,0:T(8,128)S(1)}, u32[]{:S(2)}, u32[]{:S(2)}) collective-permute-start(f32[1,8,8,128]{3,2,1,0:T(8,128)S(1)} %combine.1.refs_0_), channel_id=1, source_target_pairs={{0,4},{4,0},{8,12},{12,8},{16,20},{20,16},{24,28},{28,24},{1,5},{5... | collective-permute-start | bytes 98312 | tf_op jit(solution)/shard_map/ppermute | solution.py:340
  20.0 2.2 %collective-permute-start.8 = (f32[1,8,8,128]{3,2,1,0:T(8,128)S(1)}, f32[1,8,8,128]{3,2,1,0:T(8,128)S(1)}, u32[]{:S(2)}, u32[]{:S(2)}) collective-permute-start(f32[1,8,8,128]{3,2,1,0:T(8,128)S(1)} %collective-permute-done.4.refs_3_), channel_id=1, source_target_pairs={{0,4},{4,0},{8,12},{12,8},{16,20},{20,16},{24,28},{28,24},{1,5},{5... | collective-permute-start | bytes 98312 | tf_op jit(solution)/shard_map/ppermute | solution.py:340
  21.7 1.2 %collective-permute-start.7 = (f32[1,8,8,128]{3,2,1,0:T(8,128)S(1)}, f32[1,8,8,128]{3,2,1,0:T(8,128)S(1)}, u32[]{:S(2)}, u32[]{:S(2)}) collective-permute-start(f32[1,8,8,128]{3,2,1,0:T(8,128)S(1)} %collective-permute-done.3.refs_2_), channel_id=1, source_target_pairs={{0,4},{4,0},{8,12},{12,8},{16,20},{20,16},{24,28},{28,24},{1,5},{5... | collective-permute-start | bytes 98312 | tf_op jit(solution)/shard_map/ppermute | solution.py:340
  22.2 1.2 %collective-permute-start.6 = (f32[1,8,8,128]{3,2,1,0:T(8,128)S(1)}, f32[1,8,8,128]{3,2,1,0:T(8,128)S(1)}, u32[]{:S(2)}, u32[]{:S(2)}) collective-permute-start(f32[1,8,8,128]{3,2,1,0:T(8,128)S(1)} %collective-permute-done.2.refs_1_), channel_id=1, source_target_pairs={{0,4},{4,0},{8,12},{12,8},{16,20},{20,16},{24,28},{28,24},{1,5},{5... | collective-permute-start | bytes 98312 | tf_op jit(solution)/shard_map/ppermute | solution.py:340
